TPU v7x, 32 devices: a whole 2x2x4 slice. The times are simulated.
32 devices in a mesh: dp: 4 (over x, core), cent: 8 (over z, y).
Axes of the slice: x: 2, y: 2, z: 4, core: 2. Of those that a mesh axis runs over, the one named last changes fastest.
Arguments:
- points: bfloat16 [32768, 1024], P(('dp', 'cent')), may hold values from -16 to 16
- point_cluster: int32 [32768], P(('dp', 'cent')), may hold values from 0 to 8191, as said below
- cand_blocks: int32 [256, 8], P(('dp', 'cent')), may hold values from 0 to 15, as said below
- cent1_prev: float32 [8192, 1024], P(('dp', 'cent')), may hold values from -6 to 6
- parent: int32 [8192], P(('dp', 'cent')), may hold values from 0 to 2047, as said below
- cent2_prev: bfloat16 [2048, 1024], P('dp'), may hold values from -6 to 6
Outputs:
- cent1_new: float32 [8192, 1024], P(('dp', 'cent'))
- cent2_new: float32 [2048, 1024], P('dp')
- point_score: float32 [32768], P(('dp', 'cent'))
Inputs may be any that keep to these rules, and one draw needn't show every extreme that they name: All points of an aligned block of 128 points share one level-one block (point_cluster // 128); on a device these block numbers never fall; the points of a device at index i of dp name only centroids from i * 8 * 256 to (i + 1) * 8 * 256 - 1; at most 2 point blocks of one device fall to one owner's 256 centroids, and in every draw one owner in each index of dp receives exactly 2 blocks from every device of that index. `parent`: the level-one centroids held at index i of dp name level-two centroids from i * 512 to (i + 1) * 512 - 1. `cand_blocks`: each row lists 8 different level-two blocks.
All inputs are finite; a program needn't handle non-finite values.
Results may differ from a plain program's by a relative error of at most 0.00094.
Values may be sent and summed in bfloat16 or wider, within the bound.
No kernel may reach another device: no remote copies, remote signals or barrier semaphores. Data moves between devices by JAX's collectives and lax.ppermute only.
A program may use at most 128 MiB of HBM per device.

v0:
```python
import jax
import jax.numpy as jnp
from jax import lax
from jax.sharding import PartitionSpec as P

BLOCK = 128
CAP = 2


EPSILON = 1e-06
SHARPNESS = 20.0


def rms_norm(values):
    return values * lax.rsqrt(jnp.mean(values * values, axis=-1, keepdims=True) + EPSILON)


def shards(points, point_cluster, cand_blocks, cent1_prev, parent, cent2_prev):
    width = points.shape[1]
    row_count = points.shape[0]
    block_count = row_count // BLOCK
    owned_rows = cent1_prev.shape[0]
    n_cent = lax.axis_size("cent")
    unit_points = rms_norm(points.astype(jnp.float32)).astype(jnp.bfloat16)
    point_blocks = points.reshape(block_count, BLOCK, width)
    cluster_blocks = point_cluster.reshape(block_count, BLOCK)
    local_ids = cluster_blocks % owned_rows
    leading = cluster_blocks[:, 0]
    owner_of = leading // owned_rows % n_cent
    per_owner = jnp.sum(
        (owner_of[None, :] == jnp.arange(n_cent)[:, None]).astype(jnp.int32), axis=1
    )
    first_block = jnp.cumsum(per_owner) - per_owner
    ranks = jnp.arange(CAP)
    source = jnp.minimum(first_block[:, None] + ranks[None, :], block_count - 1).reshape(-1)
    live = (ranks[None, :] < per_owner[:, None]).reshape(-1)
    outgoing = point_blocks[source]
    outgoing_ids = jnp.where(live[:, None], local_ids[source], -1).astype(jnp.bfloat16)
    arrived, arrived_ids = (
        lax.all_to_all(outgoing, "cent", split_axis=0, concat_axis=0, tiled=True),
        lax.all_to_all(outgoing_ids, "cent", split_axis=0, concat_axis=0, tiled=True),
    )
    member = (
        arrived_ids.astype(jnp.float32)[:, :, None]
        == jnp.arange(owned_rows, dtype=jnp.float32)[None, None, :]
    ).astype(jnp.bfloat16)
    level_sums = jnp.einsum("spc,spd->cd", member, arrived, preferred_element_type=jnp.float32)
    counts = jnp.sum(member.astype(jnp.float32), axis=(0, 1))
    average = level_sums / jnp.maximum(counts, 1.0)[:, None]
    cent1_new = rms_norm(average + cent1_prev)
    upper_rows = cent2_prev.shape[0]
    parent_local = parent - lax.axis_index("dp") * upper_rows
    membership = (parent_local[None, :] == jnp.arange(upper_rows)[:, None]).astype(jnp.float32)
    upper_part = jnp.dot(
        membership, cent1_new, precision=lax.Precision.HIGHEST, preferred_element_type=jnp.float32
    )
    cent2_new = rms_norm(lax.psum(upper_part, "cent"))
    column_scale = SHARPNESS / width
    table_rows = lax.all_gather(cent2_prev, "dp", axis=0, tiled=True)
    table_units = rms_norm(table_rows.astype(jnp.float32)).astype(jnp.bfloat16)
    products = lax.dot_general(
        unit_points, table_units, (((1,), (1,)), ((), ())), preferred_element_type=jnp.float32
    )
    column_block = jnp.arange(table_rows.shape[0]) // BLOCK
    listed = jnp.any(cand_blocks[:, :, None] == column_block[None, None, :], axis=1)
    weights = jnp.exp(products * column_scale).reshape(block_count, BLOCK, -1) * listed[
        :, None, :
    ].astype(jnp.float32)
    running = jnp.sum(weights, axis=2).reshape(row_count)
    point_score = jnp.log(running)
    return (cent1_new, cent2_new, point_score)


def solution(mesh):
    placed = (
        P(("dp", "cent"), None),
        P(("dp", "cent")),
        P(("dp", "cent"), None),
        P(("dp", "cent"), None),
        P(("dp", "cent")),
        P("dp", None),
    )
    return jax.shard_map(
        shards,
        mesh=mesh,
        in_specs=placed,
        out_specs=(P(("dp", "cent"), None), P("dp", None), P(("dp", "cent"))),
        check_vma=False,
    )
```

profile of v0, /device:TPU:0, one launch (start us, length us, event | category | flops | bytes accessed | tf_op | source)
XLA Modules:
  0.0 241.6 jit_solution(16021688464053258804)
XLA Ops:
  8.0 0.7 add_select_fusion.1
  8.7 0.8 slice_reduce_fusion
  9.5 0.1 convert_reduce_fusion.1
  9.6 0.1 iota_compare_fusion.11
  9.7 0.2 reduce-window.8
  9.9 0.1 add_minimum_fusion
  10.0 0.1 min.15
  10.1 0.6 gather_fusion
  10.6 0.7 select_convert_fusion
  11.3 7.3 %all-to-all-start = ((bf16[8,2,128]{2,1,0:T(2,128)(2,1)}), bf16[8,2,128]{2,1,0:T(2,128)(2,1)S(1)}, u32[]{:S(2)}, u32[]{:S(2)}) async-start(bf16[8,2,128]{2,1,0:T(2,128)(2,1)} %select_convert_fusion), calls=%async_computation | async-start | bytes 8192 | tf_op jit(solution)/shard_map/all_to_all | solution.py:41
  18.6 4.4 %gather_fusion.1 = bf16[16,128,1024]{2,1,0:T(8,128)(2,1)} fusion(bf16[8,128,1024]{2,1,0:T(8,128)(2,1)} %bitcast.23, s32[1024]{0:T(1024)S(1)} %pad_clamp_fusion), kind=kCustom, calls=%fused_computation.1 | custom fusion | bytes 8388672 | tf_op jit(solution)/shard_map/gather | solution.py:37
  23.0 0.0 copy-start.4
  23.0 0.0 copy-start.5
  23.0 2.0 all-to-all-done
  25.0 4.5 %all-to-all-start.1 = ((bf16[16,128,1024]{2,1,0:T(8,128)(2,1)}), bf16[16,128,1024]{2,1,0:T(8,128)(2,1)}, u32[]{:S(2)}, u32[]{:S(2)}) async-start(bf16[16,128,1024]{2,1,0:T(8,128)(2,1)} %gather_fusion.1), calls=%async_computation.1 | async-start | bytes 8388608 | tf_op jit(solution)/shard_map/all_to_all | solution.py:40
  29.5 0.0 all-gather.2.cloned.1.call-start
  29.6 0.7 all-gather.2.cloned.1.call-update
  30.3 0.0 all-reduce.2.cloned.1.call-start
  30.3 0.0 copy-done.4
  30.4 0.3 convert_reduce_fusion
  30.7 91.2 %all-to-all-done.1 = bf16[16,128,1024]{2,1,0:T(8,128)(2,1)} async-done(((bf16[16,128,1024]{2,1,0:T(8,128)(2,1)}), bf16[16,128,1024]{2,1,0:T(8,128)(2,1)}, u32[]{:S(2)}, u32[]{:S(2)}) %all-to-all-start.1) | async-done | bytes 4194336 | tf_op jit(solution)/shard_map/all_to_all | solution.py:40
  121.8 0.0 copy-done.5
  121.8 3.5 %multiply_reduce_fusion.1 = (f32[256]{0:T(256)S(1)}, f32[256,1024]{1,0:T(8,128)S(1)}) fusion(f32[256,1024]{1,0:T(8,128)S(1)} %copy-done.5, f32[256]{0:T(256)S(1)} %broadcast_maximum_fusion, bf16[16,128,1024]{2,1,0:T(8,128)(2,1)} %all-to-all-done.1, f32[16,128]{1,0:T(8,128)S(1)} %convert.1), kind=kOutput, calls=%fused_computation.23 | convolution fusion | flops 1075314432 | bytes 6301696 | tf_op jit(solution)/shard_map/spc,spd->cd/dot_general | solution.py:47
  125.4 0.0 copy-start.3
  125.4 0.0 copy-start
  125.4 0.1 broadcast_multiply_fusion.1
  125.6 0.0 copy-start.2
  125.6 2.4 fusion.15
  128.0 0.0 all-reduce.2.cloned.1.call-update
  128.0 0.0 copy-done.3
  128.0 0.2 compare_reduce_fusion
  128.3 0.0 copy-done
  128.3 0.5 fusion.3
  128.8 0.0 all-gather.2.cloned.1.call-done
  128.8 0.0 copy-start.1
  128.8 3.2 %fusion = f32[2048]{0:T(1024)S(1)} fusion(bf16[2048,1024]{1,0:T(8,128)(2,1)} %all-gather.2.cloned.1.call-done), kind=kLoop, calls=%fused_computation.4 | loop fusion | flops 6289408 | bytes 4202496 | tf_op jit(solution)/shard_map/reduce_sum | solution.py:15
  132.0 0.0 copy-done.2
  132.1 0.2 copy-done.1
  132.3 5.3 %fusion.2 = f32[1024]{0:T(1024)S(1)} fusion(bf16[2048,1024]{1,0:T(8,128)(2,1)S(1)} %copy-done.1, f32[8,2048]{1,0:T(8,128)S(1)} %convert_element_type.54, f32[2048]{0:T(1024)S(1)} %add_rsqrt_fusion, bf16[1024,1024]{1,0:T(8,128)(2,1)S(1)} %copy-done, f32[1024]{0:T(1024)S(1)} %add_rsqrt_fusion.1), kind=kOutput, calls=%fused_computation.7 | convolution fusion | flops 4310694912 | bytes 6373376 | tf_op jit(solution)/shard_map/dot_general | solution.py:61
  137.6 0.6 log.3
  138.2 91.1 %all-reduce.2.cloned.1.call-done = f32[512,1024]{1,0:T(8,128)} async-done(((f32[512,1024]{1,0:T(8,128)}), f32[512,1024]{1,0:T(8,128)}) %all-reduce.2.cloned.1.call-update) | async-done | bytes 2097168 | tf_op jit(solution)/shard_map/psum | solution.py:57
  229.3 1.8 multiply_reduce_fusion
  231.1 3.1 %broadcast_multiply_fusion = f32[512,1024]{1,0:T(8,128)} fusion(f32[512,1024]{1,0:T(8,128)} %all-reduce.2.cloned.1.call-done, f32[512]{0:T(512)S(1)} %add_rsqrt_fusion.2), kind=kLoop, calls=%fused_computation.22 | loop fusion | flops 524288 | bytes 4196352 | tf_op jit(solution)/shard_map/mul | solution.py:15
  (13 shorter events, 0.1 us)
Async XLA Ops:
  11.3 13.7 %all-to-all-start = ((bf16[8,2,128]{2,1,0:T(2,128)(2,1)}), bf16[8,2,128]{2,1,0:T(2,128)(2,1)S(1)}, u32[]{:S(2)}, u32[]{:S(2)}) async-start(bf16[8,2,128]{2,1,0:T(2,128)(2,1)} %select_convert_fusion), calls=%async_computation | async-start | bytes 8192 | tf_op jit(solution)/shard_map/all_to_all | solution.py:41
  23.0 7.4 %copy-start.4 = (s32[256]{0:T(256)S(1)}, s32[256]{0:T(256)}, u32[]{:S(2)}) copy-start(s32[256]{0:T(256)} %param.10) | copy-start | bytes 3076
  23.0 98.9 %copy-start.5 = (f32[256,1024]{1,0:T(8,128)S(1)}, f32[256,1024]{1,0:T(8,128)}, u32[]{:S(2)}) copy-start(f32[256,1024]{1,0:T(8,128)} %param.9) | copy-start | bytes 3145732
  25.0 96.9 %all-to-all-start.1 = ((bf16[16,128,1024]{2,1,0:T(8,128)(2,1)}), bf16[16,128,1024]{2,1,0:T(8,128)(2,1)}, u32[]{:S(2)}, u32[]{:S(2)}) async-start(bf16[16,128,1024]{2,1,0:T(8,128)(2,1)} %gather_fusion.1), calls=%async_computation.1 | async-start | bytes 8388608 | tf_op jit(solution)/shard_map/all_to_all | solution.py:40
  29.5 99.3 %all-gather.2.cloned.1.call-start = ((), (), s32[]{:S(2)}) async-start(), calls=%async_computation.3 | async-start | bytes 5242880 | tf_op jit(solution)/shard_map/all_gather | solution.py:59
  30.3 199.0 %all-reduce.2.cloned.1.call-start = ((), (), s32[]{:S(2)}) async-start(), calls=%async_computation.2 | async-start | bytes 4194304 | tf_op jit(solution)/shard_map/psum | solution.py:57
  125.4 2.6 %copy-start.3 = (s32[8,8]{1,0:T(8,128)S(1)}, s32[8,8]{1,0:T(8,128)}, u32[]{:S(2)}) copy-start(s32[8,8]{1,0:T(8,128)} %param.8) | copy-start | bytes 772
  125.4 2.9 %copy-start = (bf16[1024,1024]{1,0:T(8,128)(2,1)S(1)}, bf16[1024,1024]{1,0:T(8,128)(2,1)}, u32[]{:S(2)}) copy-start(bf16[1024,1024]{1,0:T(8,128)(2,1)} %param.6) | copy-start | bytes 6291460
  125.6 6.5 %copy-start.2 = (f32[256,1024]{1,0:T(8,128)}, f32[256,1024]{1,0:T(8,128)S(1)}, u32[]{:S(2)}) copy-start(f32[256,1024]{1,0:T(8,128)S(1)} %broadcast_multiply_fusion.1) | copy-start | bytes 3145732
  128.8 3.5 %copy-start.1 = (bf16[2048,1024]{1,0:T(8,128)(2,1)S(1)}, bf16[2048,1024]{1,0:T(8,128)(2,1)}, u32[]{:S(2)}) copy-start(bf16[2048,1024]{1,0:T(8,128)(2,1)} %all-gather.2.cloned.1.call-done) | copy-start | bytes 12582916
Sparse Core Ops, SparseCore 0:
  31.9 35.7 all-gather.1
Sparse Core Ops, SparseCore 1:
  128.1 101.1 all-reduce.1
where the time goes:
time: 242 us
  waiting for transfers between devices  185 us (76%)
  between operations  15.7 us (6%)
  starting transfers between devices  11.9 us (5%)
  matrix products  11.3 us (5%)
  other arithmetic  11.2 us (5%)
  local copies, waits for them, and re-layouts  6.64 us (3%)
    all_to_all x1, waiting for transfers between devices, shards(): lax.all_to_all(outgoing, 'cent', split_axis=0, concat_axis=0, tiled=True)  91.2 us
    psum x1, waiting for transfers between devices, shards(): cent2_new = rms_norm(lax.psum(upper_part, 'cent'))  91.1 us
    all_to_all x1, starting transfers between devices, shards(): lax.all_to_all(outgoing_ids, 'cent', split_axis=0, concat_axis=0, tiled=T...  7.28 us
    reduce_sum x3, other arithmetic, rms_norm(): jnp.mean(values * values, axis=-1, keepdims=True) + EPSILON  5.5 us
    dot_general x1, matrix products, shards(): lax.dot_general(unit_points, table_units, (((1,), (1,)), ((), ())), prefe...  5.34 us
  transfers between devices with their start and end apart: 4, of which 3 were waited for; matrix products, arithmetic and copies ran while one was open for 9% of the time, Pallas kernels for 0%

commit v1 on v0

v1 whole, which is shorter than its diff:
```python
import functools

import jax
import jax.numpy as jnp
from jax import lax
from jax.experimental import pallas as pl
from jax.experimental.pallas import tpu as pltpu
from jax.sharding import PartitionSpec as P

BLOCK = 128
EPSILON = 1e-06
SHARPNESS = 20.0
CODE = 32000.0
FLOOR = 1e-30
VMEM_LIMIT = 48 * 1024 * 1024


def rms_norm(values):
    return values * lax.rsqrt(jnp.mean(values * values, axis=-1, keepdims=True) + EPSILON)


def split(values):
    high = values.astype(jnp.bfloat16)
    return high, (values - high.astype(jnp.float32)).astype(jnp.bfloat16)


def dot(a, b):
    return jnp.dot(a, b, preferred_element_type=jnp.float32)


def dot_lanes(a, b):
    return lax.dot_general(a, b, (((1,), (1,)), ((), ())), preferred_element_type=jnp.float32)


def sums_kernel(block_ref, ids_ref, points_ref, prev_ref, prev_scale_ref, high_ref, low_ref, code_ref, stat_ref, acc, count):
    rows, w = acc.shape
    blocks = ids_ref.shape[0]
    acc[...] = jnp.zeros_like(acc)
    count[...] = jnp.zeros_like(count)
    centroid = lax.broadcasted_iota(jnp.int32, (BLOCK, BLOCK), 0)
    ones = jnp.ones((BLOCK, BLOCK), jnp.bfloat16)

    def add(i, carry):
        member = jnp.where(centroid == ids_ref[pl.ds(i, 1), :], 1.0, 0.0).astype(jnp.bfloat16)
        at = pl.ds(pl.multiple_of(block_ref[i] * BLOCK, BLOCK), BLOCK)
        part = dot(member, points_ref[pl.ds(pl.multiple_of(i * BLOCK, BLOCK), BLOCK), :])
        acc[at, :] += part
        count[at, :] += dot(member, ones)
        return carry

    lax.fori_loop(0, blocks, add, 0, unroll=4)
    step = 2 * BLOCK
    unit = jnp.ones((8, w), jnp.bfloat16)
    first = jnp.where(lax.broadcasted_iota(jnp.int32, (8, w), 1) == 0, 1.0, 0.0).astype(jnp.bfloat16)

    def finish(i, carry):
        at = pl.ds(pl.multiple_of(i * step, step), step)
        prev = prev_ref[at, :].astype(jnp.float32) * prev_scale_ref[at, :]
        x = acc[at, :] / jnp.maximum(count[at, :][:, :w], 1.0) + prev
        high, low = split(x)
        high_ref[at, :] = high
        low_ref[at, :] = low
        square_high, square_low = split(x * x)
        stat_ref[0:1, at] = (dot_lanes(unit, square_high) + dot_lanes(unit, square_low))[0:1]
        top = jnp.max(jnp.abs(x), axis=1, keepdims=True) * 1.01
        scale = jnp.maximum(top, FLOOR).astype(jnp.bfloat16)
        stat_ref[1:2, at] = dot_lanes(first, jnp.broadcast_to(scale, (step, w)))[0:1]
        code_ref[at, :] = jnp.round(x * (CODE / scale.astype(jnp.float32))).astype(jnp.int16)
        return carry

    lax.fori_loop(0, rows // step, finish, 0)


def upper_kernel(width, stat_ref, parent_ref, high_ref, low_ref, out_ref):
    squares = jnp.sum(stat_ref[:, 0, :], axis=0, keepdims=True)
    factor = lax.rsqrt(squares / width + EPSILON)
    parent = parent_ref[...]
    step = BLOCK
    at_row = lax.broadcasted_iota(jnp.int32, (step, parent.shape[1]), 0)

    def one(i, carry):
        weight = jnp.where(at_row + i * step == parent, factor, 0.0)
        weight_high, weight_low = split(weight)
        part = dot(weight_high, high_ref[...]) + dot(weight_high, low_ref[...])
        out_ref[pl.ds(pl.multiple_of(i * step, step), step), :] = part + dot(weight_low, high_ref[...])
        return carry

    lax.fori_loop(0, out_ref.shape[0] // step, one, 0)


def join_kernel(parts_ref, out_ref):
    parts, rows, w = parts_ref.shape
    squares = jnp.zeros((rows, 1), jnp.float32)
    for s in range(parts):
        values = parts_ref[s]
        squares += jnp.sum(values * values, axis=1, keepdims=True)
    factor = lax.rsqrt(squares / (parts * w) + EPSILON)
    for s in range(parts):
        out_ref[:, s * w : (s + 1) * w] = parts_ref[s] * factor


def decode_kernel(code_ref, scale_ref, out_ref):
    parts, rows, w = code_ref.shape
    squares = jnp.zeros((rows, 1), jnp.float32)
    for s in range(parts):
        values = code_ref[s].astype(jnp.float32) * scale_ref[:, s : s + 1]
        squares += jnp.sum(values * values, axis=1, keepdims=True)
        out_ref[:, s * w : (s + 1) * w] = values
    out_ref[...] *= lax.rsqrt(squares / (parts * w) + EPSILON)


def call(kernel, out_shape, **kw):
    params = pltpu.CompilerParams(vmem_limit_bytes=VMEM_LIMIT)
    return pl.pallas_call(kernel, out_shape=out_shape, compiler_params=params, **kw)


def columns(values, n):
    rows, width = values.shape
    return values.reshape(rows, n, width // n).transpose(1, 0, 2)


def exchange(values):
    return lax.all_to_all(values, "cent", split_axis=0, concat_axis=0, tiled=True)


def shards(points, point_cluster, cand_blocks, cent1_prev, parent, cent2_prev):
    point_rows, width = points.shape
    block_count = point_rows // BLOCK
    owned = cent1_prev.shape[0]
    upper_rows = cent2_prev.shape[0]
    n = lax.axis_size("cent")
    dp, me = lax.axis_index("dp"), lax.axis_index("cent")
    w = width // n
    rows = n * owned
    f32, bf16, i16, i32 = jnp.float32, jnp.bfloat16, jnp.int16, jnp.int32
    shape = jax.ShapeDtypeStruct

    prev_scale = jnp.maximum(jnp.max(jnp.abs(cent1_prev), axis=1), FLOOR)
    small = jnp.concatenate(
        [(point_cluster - dp * rows).astype(f32), (parent - dp * upper_rows).astype(f32), prev_scale]
    )
    small = lax.all_gather(small, "cent", axis=0, tiled=False)
    ids = small[:, :point_rows].astype(i32).reshape(n * block_count, BLOCK)
    parents = small[:, point_rows : point_rows + owned].astype(i32).reshape(1, rows)
    scales = (small[:, point_rows + owned :] / CODE).reshape(rows, 1)

    arrived = exchange(columns(points, n)).reshape(n * point_rows, w)
    prev_code = jnp.round(cent1_prev * (CODE / prev_scale)[:, None]).astype(i16)
    prev = exchange(columns(prev_code, n)).reshape(rows, w)

    table_rows = lax.all_gather(cent2_prev, "dp", axis=0, tiled=True)

    vmem = pl.BlockSpec(memory_space=pltpu.VMEM)
    high, low, code, stat = call(
        sums_kernel,
        (shape((rows, w), bf16), shape((rows, w), bf16), shape((rows, w), i16), shape((2, rows), f32)),
        in_specs=[pl.BlockSpec(memory_space=pltpu.SMEM)] + [vmem] * 4,
        out_specs=(vmem,) * 4,
        scratch_shapes=[pltpu.VMEM((rows, w), f32), pltpu.VMEM((rows, BLOCK), f32)],
        name="sums",
    )(ids[:, 0] // BLOCK, ids % BLOCK, arrived, prev, scales)
    stats = lax.all_gather(stat, "cent", axis=0, tiled=False)
    back = exchange(code.reshape(n, owned, w))

    upper = call(
        functools.partial(upper_kernel, width),
        shape((upper_rows, w), f32),
        in_specs=[vmem] * 4,
        out_specs=vmem,
        name="upper",
    )(stats, parents, high, low)
    uppers = lax.all_gather(upper, "cent", axis=0, tiled=False)

    mine = lax.dynamic_slice_in_dim(stats[:, 1, :], me * owned, owned, axis=1) / CODE
    cent1_new = call(
        decode_kernel, shape((owned, width), f32), in_specs=[vmem] * 2, out_specs=vmem, name="decode"
    )(back, mine.T)

    unit_points = rms_norm(points.astype(f32)).astype(bf16)
    table_units = rms_norm(table_rows.astype(f32)).astype(bf16)
    products = lax.dot_general(
        unit_points, table_units, (((1,), (1,)), ((), ())), preferred_element_type=f32
    )
    column_block = jnp.arange(table_rows.shape[0]) // BLOCK
    listed = jnp.any(cand_blocks[:, :, None] == column_block[None, None, :], axis=1)
    weights = jnp.exp(products * (SHARPNESS / width)).reshape(block_count, BLOCK, -1)
    running = jnp.sum(weights * listed[:, None, :].astype(f32), axis=2).reshape(point_rows)
    point_score = jnp.log(running)

    tile = min(upper_rows, BLOCK)
    cent2_new = call(
        join_kernel,
        shape((upper_rows, width), f32),
        grid=(upper_rows // tile,),
        in_specs=[pl.BlockSpec((n, tile, w), lambda i: (0, i, 0))],
        out_specs=pl.BlockSpec((tile, width), lambda i: (i, 0)),
        name="join",
    )(uppers)
    return (cent1_new, cent2_new, point_score)


def solution(mesh):
    placed = (
        P(("dp", "cent"), None),
        P(("dp", "cent")),
        P(("dp", "cent"), None),
        P(("dp", "cent"), None),
        P(("dp", "cent")),
        P("dp", None),
    )
    return jax.shard_map(
        shards,
        mesh=mesh,
        in_specs=placed,
        out_specs=(P(("dp", "cent"), None), P("dp", None), P(("dp", "cent"))),
        check_vma=False,
    )
```

time: 242 us -> 212 us (0.88)
  waiting for transfers between devices: 185 us -> 48.8 us
  blocking collectives: 0 us -> 99.2 us
  Pallas kernels: 0 us -> 14.4 us
  matrix products: 11.3 us -> 5.34 us
  other arithmetic: 11.2 us -> 7.7 us
  starting transfers between devices: 11.9 us -> 14.5 us
    all_gather x0 -> x2, blocking collectives: none -> 99.2 us  [the longest x1 68.4 us: shards(): small = lax.all_gather(small, 'cent', axis=0, tiled=False)]
    psum x1 -> x0, waiting for transfers between devices: 91.1 us -> none  [shards(): cent2_new = rms_norm(lax.psum(upper_part, 'cent'))]
    all_to_all x2 -> x3, waiting for transfers between devices: 93.2 us -> 25.7 us  [exchange(): lax.all_to_all(values, 'cent', split_axis=0, concat_axis=0, tiled=True)]
    all_gather x0 -> x1, waiting for transfers between devices: none -> 22.4 us  [shards(): uppers = lax.all_gather(upper, 'cent', axis=0, tiled=False)]
    pallas_call x0 -> x4, Pallas kernels: none -> 14.4 us  [the longest x1 6.72 us: shards(): call(sums_kernel, (shape((rows, w), bf16), shape((rows, w), bf16), shape(...]
    dot_general x2 -> x0, matrix products: 5.94 us -> none  [the longest x1 3.55 us: shards(): jnp.einsum('spc,spd->cd', member, arrived, preferred_element_type=jnp.flo...]
    gather x2 -> x0, local copies, waits for them, and re-layouts: 4.94 us -> none  [the longest x1 4.38 us: shards(): outgoing = point_blocks[source]]
    unnamed x12 -> x26, local copies, waits for them, and re-layouts: 0.21 us -> 4.98 us
  transfers between devices with their start and end apart: 4 -> 5, of which waited for: 3 -> 3; matrix products, arithmetic and copies ran while one was open for 9% -> 8% of each run, Pallas kernels for 0% -> 6%
where the time goes in v1:
time: 212 us
  blocking collectives  99.2 us (47%)
  waiting for transfers between devices  48.8 us (23%)
  starting transfers between devices  14.5 us (7%)
  Pallas kernels  14.4 us (7%)
  between operations  14.3 us (7%)
  other arithmetic  7.7 us (4%)
  local copies, waits for them, and re-layouts  7.49 us (4%)
  matrix products  5.34 us (3%)
    all_gather x1, blocking collectives, shards(): small = lax.all_gather(small, 'cent', axis=0, tiled=False)  68.4 us
    all_gather x1, blocking collectives, shards(): stats = lax.all_gather(stat, 'cent', axis=0, tiled=False)  30.8 us
    all_to_all x3, waiting for transfers between devices, exchange(): lax.all_to_all(values, 'cent', split_axis=0, concat_axis=0, tiled=True)  25.7 us
    all_gather x1, waiting for transfers between devices, shards(): uppers = lax.all_gather(upper, 'cent', axis=0, tiled=False)  22.4 us
    all_to_all x3, starting transfers between devices, exchange(): lax.all_to_all(values, 'cent', split_axis=0, concat_axis=0, tiled=True)  14.5 us
    pallas_call x1, Pallas kernels, shards(): call(sums_kernel, (shape((rows, w), bf16), shape((rows, w), bf16), shape(...  6.72 us
    dot_general x1, matrix products, shards(): lax.dot_general(unit_points, table_units, (((1,), (1,)), ((), ())), prefe...  5.34 us
    unnamed x26, local copies, waits for them, and re-layouts  4.98 us
  transfers between devices with their start and end apart: 5, of which 3 were waited for; matrix products, arithmetic and copies ran while one was open for 8% of the time, Pallas kernels for 6%

profile of v1, /device:TPU:0, one launch (start us, length us, event | category | flops | bytes accessed | tf_op | source)
XLA Modules:
  0.0 211.7 jit_solution(10921790952761635827)
XLA Ops:
  7.2 0.0 copy-start.4
  7.2 0.0 all-gather.8.cloned.1.call-start
  7.2 0.7 all-gather.8.cloned.1.call-update
  7.9 1.4 abs_reduce_fusion
  9.3 2.3 %bitcast_bitcast_fusion.1 = s16[8,256,128]{2,1,0:T(8,128)(2,1)} fusion(f32[256,1024]{1,0:T(8,128)} %param.9, f32[256]{0:T(256)S(1)} %get-tuple-element.13), kind=kLoop, calls=%fused_computation.16 | loop fusion | flops 786432 | bytes 1573888 | tf_op jit(solution)/shard_map/transpose | solution.py:119
  11.6 7.3 %all-to-all-start.1 = ((s16[8,256,128]{2,1,0:T(8,128)(2,1)}), s16[8,256,128]{2,1,0:T(8,128)(2,1)S(1)}, u32[]{:S(2)}, u32[]{:S(2)}) async-start(s16[8,256,128]{2,1,0:T(8,128)(2,1)} %bitcast_bitcast_fusion.1), calls=%async_computation.1 | async-start | bytes 1048576 | tf_op jit(solution)/shard_map/all_to_all | solution.py:123
  18.8 0.0 copy-done.4
  18.8 0.0 copy-start.9
  18.9 0.0 copy-start.8
  18.9 1.7 bitcast_bitcast_fusion
  20.6 12.8 %all-to-all-done.1 = s16[8,256,128]{2,1,0:T(8,128)(2,1)S(1)} async-done(((s16[8,256,128]{2,1,0:T(8,128)(2,1)}), s16[8,256,128]{2,1,0:T(8,128)(2,1)S(1)}, u32[]{:S(2)}, u32[]{:S(2)}) %all-to-all-start.1) | async-done | bytes 524320 | tf_op jit(solution)/shard_map/all_to_all | solution.py:123
  33.3 0.0 copy-start.1
  33.3 0.8 copy-done.1
  34.1 3.6 %all-to-all-start = ((bf16[8,1024,128]{2,1,0:T(8,128)(2,1)}), bf16[8,1024,128]{2,1,0:T(8,128)(2,1)S(1)}, u32[]{:S(2)}, u32[]{:S(2)}) async-start(bf16[8,1024,128]{2,1,0:T(8,128)(2,1)} %bitcast_bitcast_fusion), calls=%async_computation | async-start | bytes 4194304 | tf_op jit(solution)/shard_map/all_to_all | solution.py:123
  37.8 0.0 copy-start.7
  37.8 0.0 all-gather.10.cloned.1.call-start
  37.8 0.0 copy-done.9
  37.8 0.0 copy-done.8
  37.9 68.4 %all-gather.3 = f32[8,1,1536]{2,1,0:T(1,128)S(1)} all-gather(f32[1,1,1536]{2,1,0:T(1,128)S(1)} %reshape.87), channel_id=2, replica_groups=mesh['dp'=4,'cent'=8] {'cent'}, dimensions={0}, use_global_device_ids=true | all-gather | bytes 55296 | tf_op jit(solution)/shard_map/all_gather | solution.py:142
  106.4 0.4 copy.30
  106.7 0.1 slice_reduce_fusion
  106.9 0.0 all-to-all-done
  106.9 0.0 copy-start.2
  106.9 1.0 copy-done.2
  108.0 6.7 %sums.1 = (bf16[2048,128]{1,0:T(8,128)(2,1)S(1)}, bf16[2048,128]{1,0:T(8,128)(2,1)S(1)}, s16[2048,128]{1,0:T(8,128)(2,1)S(1)}, f32[2,2048]{1,0:T(2,128)S(1)}) custom-call(s32[64]{0:T(128)S(1)} %and_select_fusion.block_ref, s32[64,128]{1,0:T(8,128)S(1)} %add_select_fusion.ids_ref, bf16[8192,128]{1,0:T(8,128)(2,1)S(1)} %bitcast.39, ...), custom_call_target="tpu_custom_call" | custom-call | tf_op jit(solution)/shard_map/sums/pallas_call | solution.py:154
  114.7 0.0 copy-start.3
  114.7 0.8 copy-done.3
  115.5 0.0 copy-start.5
  115.5 30.8 %all-gather.4.stat_ref = f32[8,2,2048]{2,1,0:T(2,128)S(1)} all-gather(f32[1,2,2048]{2,1,0:T(2,128)S(1)} %bitcast.45), channel_id=3, replica_groups=mesh['dp'=4,'cent'=8] {'cent'}, dimensions={0}, use_global_device_ids=true | all-gather | bytes 147456 | tf_op jit(solution)/shard_map/all_gather | solution.py:162
  146.3 3.2 %upper.1 = f32[512,128]{1,0:T(8,128)} custom-call(f32[8,2,2048]{2,1,0:T(2,128)S(1)} %all-gather.4.stat_ref, s32[1,2048]{1,0:T(1,128)S(1)} %bitcast.44, bf16[2048,128]{1,0:T(8,128)(2,1)S(1)} %get-tuple-element.9.high_ref, bf16[2048,128]{1,0:T(8,128)(2,1)S(1)} %get-tuple-element.10.low_ref), custom_call_target="tpu_custom_call" | custom-call | tf_op jit(solution)/shard_map/upper/pallas_call | solution.py:165
  149.5 0.0 all-gather.10.cloned.1.call-update
  149.6 3.5 %all-to-all-start.2 = ((s16[8,256,128]{2,1,0:T(8,128)(2,1)}), s16[8,256,128]{2,1,0:T(8,128)(2,1)S(1)}, u32[]{:S(2)}, u32[]{:S(2)}) async-start(s16[8,256,128]{2,1,0:T(8,128)(2,1)} %bitcast.43), calls=%async_computation.2 | async-start | bytes 1048576 | tf_op jit(solution)/shard_map/all_to_all | solution.py:123
  153.1 0.0 copy-done.7
  153.1 0.2 compare_reduce_fusion
  153.4 0.0 copy-done.5
  153.4 0.5 fusion.3
  153.9 0.1 slice.23
  154.0 0.1 copy.26
  154.1 12.9 %all-to-all-done.2.code_ref = s16[8,256,128]{2,1,0:T(8,128)(2,1)S(1)} async-done(((s16[8,256,128]{2,1,0:T(8,128)(2,1)}), s16[8,256,128]{2,1,0:T(8,128)(2,1)S(1)}, u32[]{:S(2)}, u32[]{:S(2)}) %all-to-all-start.2) | async-done | bytes 524320 | tf_op jit(solution)/shard_map/all_to_all | solution.py:123
  167.1 2.0 decode.1
  169.1 0.0 all-gather.8.cloned.1.call-done
  169.1 3.2 %fusion = f32[2048]{0:T(1024)S(1)} fusion(bf16[2048,1024]{1,0:T(8,128)(2,1)} %all-gather.8.cloned.1.call-done), kind=kLoop, calls=%fused_computation.2 | loop fusion | flops 6289408 | bytes 4202496 | tf_op jit(solution)/shard_map/reduce_sum | solution.py:19
  172.3 0.2 copy-done.6
  172.5 5.3 %fusion.2 = f32[1024]{0:T(1024)S(1)} fusion(bf16[2048,1024]{1,0:T(8,128)(2,1)S(1)} %copy-done.6, f32[8,2048]{1,0:T(8,128)S(1)} %convert_element_type.44, f32[2048]{0:T(1024)S(1)} %add_rsqrt_fusion, bf16[1024,1024]{1,0:T(8,128)(2,1)S(1)} %copy-done.5, f32[1024]{0:T(1024)S(1)} %add_rsqrt_fusion.1), kind=kOutput, calls=%fused_computation.5 | convolution fusion | flops 4310694912 | bytes 6373376 | tf_op jit(solution)/shard_map/dot_general | solution.py:181
  177.9 0.6 log.3
  178.5 22.4 %all-gather.10.cloned.1.call-done = f32[4096,128]{1,0:T(8,128)} async-done(((f32[512,128]{1,0:T(8,128)}), f32[4096,128]{1,0:T(8,128)}) %all-gather.10.cloned.1.call-update) | async-done | bytes 2097168 | tf_op jit(solution)/shard_map/all_gather | solution.py:172
  200.9 1.6 copy-done
  202.5 2.4 %join.1 = f32[512,1024]{1,0:T(8,128)} custom-call(f32[8,512,128]{2,1,0:T(8,128)S(1)} %bitcast.41), custom_call_target="tpu_custom_call" | custom-call | tf_op jit(solution)/shard_map/join/pallas_call | solution.py:191
  (21 shorter events, 0.2 us)
Async XLA Ops:
  7.2 11.7 %copy-start.4 = (bf16[1024,1024]{1,0:T(8,128)(2,1)S(1)}, bf16[1024,1024]{1,0:T(8,128)(2,1)}, u32[]{:S(2)}) copy-start(bf16[1024,1024]{1,0:T(8,128)(2,1)} %param.6) | copy-start | bytes 6291460
  7.2 161.9 %all-gather.8.cloned.1.call-start = ((), (), s32[]{:S(2)}) async-start(), calls=%async_computation.3 | async-start | bytes 5242880 | tf_op jit(solution)/shard_map/all_gather | solution.py:151
  11.6 21.8 %all-to-all-start.1 = ((s16[8,256,128]{2,1,0:T(8,128)(2,1)}), s16[8,256,128]{2,1,0:T(8,128)(2,1)S(1)}, u32[]{:S(2)}, u32[]{:S(2)}) async-start(s16[8,256,128]{2,1,0:T(8,128)(2,1)} %bitcast_bitcast_fusion.1), calls=%async_computation.1 | async-start | bytes 1048576 | tf_op jit(solution)/shard_map/all_to_all | solution.py:123
  18.8 19.0 %copy-start.9 = (s32[256]{0:T(256)S(1)}, s32[256]{0:T(256)}, u32[]{:S(2)}) copy-start(s32[256]{0:T(256)} %param.10) | copy-start | bytes 3076
  18.9 19.0 %copy-start.8 = (s32[1024]{0:T(1024)S(1)}, s32[1024]{0:T(1024)}, u32[]{:S(2)}) copy-start(s32[1024]{0:T(1024)} %param.7) | copy-start | bytes 12292
  33.3 0.8 copy-start.1
  34.1 72.8 %all-to-all-start = ((bf16[8,1024,128]{2,1,0:T(8,128)(2,1)}), bf16[8,1024,128]{2,1,0:T(8,128)(2,1)S(1)}, u32[]{:S(2)}, u32[]{:S(2)}) async-start(bf16[8,1024,128]{2,1,0:T(8,128)(2,1)} %bitcast_bitcast_fusion), calls=%async_computation | async-start | bytes 4194304 | tf_op jit(solution)/shard_map/all_to_all | solution.py:123
  37.8 115.4 %copy-start.7 = (s32[8,8]{1,0:T(8,128)S(1)}, s32[8,8]{1,0:T(8,128)}, u32[]{:S(2)}) copy-start(s32[8,8]{1,0:T(8,128)} %param.8) | copy-start | bytes 772
  37.8 163.1 %all-gather.10.cloned.1.call-start = ((), (), s32[]{:S(2)}) async-start(), calls=%async_computation.4 | async-start | bytes 2359296 | tf_op jit(solution)/shard_map/all_gather | solution.py:172
  106.9 1.0 copy-start.2
  114.7 0.8 copy-start.3
  115.5 37.9 %copy-start.5 = (bf16[1024,1024]{1,0:T(8,128)(2,1)S(1)}, bf16[1024,1024]{1,0:T(8,128)(2,1)}, u32[]{:S(2)}) copy-start(bf16[1024,1024]{1,0:T(8,128)(2,1)} %param.6) | copy-start | bytes 6291460
  149.6 17.5 %all-to-all-start.2 = ((s16[8,256,128]{2,1,0:T(8,128)(2,1)}), s16[8,256,128]{2,1,0:T(8,128)(2,1)S(1)}, u32[]{:S(2)}, u32[]{:S(2)}) async-start(s16[8,256,128]{2,1,0:T(8,128)(2,1)} %bitcast.43), calls=%async_computation.2 | async-start | bytes 1048576 | tf_op jit(solution)/shard_map/all_to_all | solution.py:123
  169.1 3.5 %copy-start.6 = (bf16[2048,1024]{1,0:T(8,128)(2,1)S(1)}, bf16[2048,1024]{1,0:T(8,128)(2,1)}, u32[]{:S(2)}) copy-start(bf16[2048,1024]{1,0:T(8,128)(2,1)} %all-gather.8.cloned.1.call-done) | copy-start | bytes 12582916
  200.9 1.6 copy-start
Sparse Core Ops, SparseCore 0:
  9.6 37.1 all-gather.7
  149.7 51.1 all-gather.9

commit v2 on v0

v2 whole, which is shorter than its diff:
```python
import functools

import jax
import jax.numpy as jnp
from jax import lax
from jax.experimental import pallas as pl
from jax.experimental.pallas import tpu as pltpu
from jax.sharding import PartitionSpec as P

BLOCK = 128
EPSILON = 1e-06
SHARPNESS = 20.0
CODE = 32000.0
FLOOR = 1e-30
VMEM_LIMIT = 48 * 1024 * 1024
f32, bf16, i16, i32 = jnp.float32, jnp.bfloat16, jnp.int16, jnp.int32
shape = jax.ShapeDtypeStruct
VMEM = pl.BlockSpec(memory_space=pltpu.VMEM)
SMEM = pl.BlockSpec(memory_space=pltpu.SMEM)


def rms_norm(values):
    return values * lax.rsqrt(jnp.mean(values * values, axis=-1, keepdims=True) + EPSILON)


def split(values):
    high = values.astype(bf16)
    return high, (values - high.astype(f32)).astype(bf16)


def dot(a, b):
    return jnp.dot(a, b, preferred_element_type=f32)


def dot_lanes(a, b):
    return lax.dot_general(a, b, (((1,), (1,)), ((), ())), preferred_element_type=f32)


def to_lanes(column):
    rows = column.shape[0]
    pick = jnp.where(lax.broadcasted_iota(i32, (8, BLOCK), 1) == 0, 1.0, 0.0).astype(bf16)
    return dot_lanes(pick, jnp.broadcast_to(column, (rows, BLOCK)).astype(bf16))[0:1]


def to_column(lanes):
    k = lanes.shape[1]
    eye = lax.broadcasted_iota(i32, (k, k), 0) == lax.broadcasted_iota(i32, (k, k), 1)
    return jnp.sum(jnp.where(eye, lanes, 0.0), axis=1, keepdims=True)


def exponent_of(top):
    return jnp.clip(jnp.ceil(jnp.log2(jnp.maximum(top * 1.001, FLOOR))), -100.0, 100.0)


def head_rows(count, w):
    return -(-count // (16 * w)) * 16


def part(ref, s, w):
    return ref.at[s] if len(ref.shape) == 3 else ref.at[:, pl.ds(pl.multiple_of(s * w, w), w)]


def pack_kernel(me_ref, *refs):
    n = len(refs) // 2
    for m in range(n):
        refs[n + m][...] = refs[m][...].reshape(refs[n + m].shape)


def prev_kernel(w, me_ref, prev_ref, small_ref, *refs):
    outs, head = refs[:-1], refs[-1]
    n = len(outs)
    owned = outs[0].shape[0] - head.shape[0]
    me = me_ref[0]
    top = jnp.zeros((owned, 1), f32)
    for s in range(n):
        top = jnp.maximum(top, jnp.max(jnp.abs(part(prev_ref, s, w)[...]), axis=1, keepdims=True))
    exponent = exponent_of(top)
    factor = CODE * jnp.exp2(-exponent)
    head[...] = jnp.zeros_like(head)
    known = small_ref.shape[0]
    head[0:known, :] = small_ref[...]
    for j in range(owned // w):
        lanes = to_lanes(exponent[j * w : (j + 1) * w])
        head[known + j : known + j + 1, :] = lanes.astype(i32)
    for m in range(n):
        outs[m][0:owned, :] = jnp.round(part(prev_ref, me ^ m, w)[...] * factor).astype(i16)
        outs[m][owned:, :] = head[...].astype(i16)


def sums_kernel(n, me_ref, block_ref, ids_ref, scale_ref, *refs):
    points, prevs, (high_ref, low_ref, stat_ref), codes = refs[:n], refs[n : 2 * n], refs[2 * n : 2 * n + 3], refs[2 * n + 3 : 3 * n + 3]
    acc, count = refs[3 * n + 3 :]
    rows, w = acc.shape
    owned = codes[0].shape[0]
    blocks = ids_ref.shape[0] // n
    me = me_ref[0]
    acc[...] = jnp.zeros_like(acc)
    count[...] = jnp.zeros_like(count)
    centroid = lax.broadcasted_iota(i32, (BLOCK, BLOCK), 0)
    ones = jnp.ones((BLOCK, BLOCK), bf16)
    for m in range(n):

        def add(i, carry, m=m):
            at_block = m * blocks + i
            member = jnp.where(centroid == ids_ref[pl.ds(at_block, 1), :], 1.0, 0.0).astype(bf16)
            at = pl.ds(pl.multiple_of(block_ref[at_block] * BLOCK, BLOCK), BLOCK)
            acc[at, :] += dot(member, points[m][pl.ds(pl.multiple_of(i * BLOCK, BLOCK), BLOCK), :])
            count[at, :] += dot(member, ones)
            return carry

        lax.fori_loop(0, blocks, add, 0, unroll=4)
    unit = jnp.ones((8, w), bf16)
    for m in range(n):
        at = pl.ds(pl.multiple_of((me ^ m) * owned, owned), owned)
        prev = prevs[m][0:owned, :].astype(f32) * scale_ref[m * owned : (m + 1) * owned, :]
        x = acc[at, :] / jnp.maximum(count[at, :][:, :w], 1.0) + prev
        high, low = split(x)
        high_ref[at, :] = high
        low_ref[at, :] = low
        square_high, square_low = split(x * x)
        stat_ref[0:1, at] = (dot_lanes(unit, square_high) + dot_lanes(unit, square_low))[0:1]
        top = jnp.max(jnp.abs(x), axis=1, keepdims=True) * 1.01
        scale = jnp.maximum(top, FLOOR).astype(bf16).astype(f32)
        stat_ref[1:2, at] = to_lanes(scale)
        codes[m][...] = jnp.round(x * (CODE / scale)).astype(i16)


def upper_kernel(n, width, parent_ref, high_ref, low_ref, *refs):
    stats, code_ref, sums, head = refs[:n], refs[n], refs[n + 1], refs[n + 2]
    rows, w = sums.shape
    squares = stats[0][0:1, :]
    for m in range(1, n):
        squares += stats[m][0:1, :]
    factor = lax.rsqrt(squares / width + EPSILON)
    parent = parent_ref[...]
    at_row = lax.broadcasted_iota(i32, (BLOCK, parent.shape[1]), 0)

    def one(i, carry):
        weight_high, weight_low = split(jnp.where(at_row + i * BLOCK == parent, factor, 0.0))
        total = dot(weight_high, high_ref[...]) + dot(weight_high, low_ref[...])
        sums[pl.ds(pl.multiple_of(i * BLOCK, BLOCK), BLOCK), :] = total + dot(weight_low, high_ref[...])
        return carry

    lax.fori_loop(0, rows // BLOCK, one, 0)
    head[...] = jnp.zeros_like(head)
    for j in range(rows // w):
        at = slice(j * w, (j + 1) * w)
        total = sums[at, :]
        exponent = exponent_of(jnp.max(jnp.abs(total), axis=1, keepdims=True))
        code_ref[at, :] = jnp.round(total * (CODE * jnp.exp2(-exponent))).astype(i16)
        head[j : j + 1, :] = to_lanes(exponent).astype(i32)
    code_ref[rows:, :] = head[...].astype(i16)


def join_kernel(w, me_ref, *refs):
    parts, out_ref, values = refs[:-2], refs[-2], refs[-1]
    n = len(parts)
    rows = values.shape[1]
    me = me_ref[0]

    for j in range(rows // w):
        at = slice(j * w, (j + 1) * w)
        squares = jnp.zeros((w, 1), f32)
        for m in range(n):
            head = parts[m][rows : rows + 16, :].astype(i32).astype(f32)
            scale = jnp.exp2(to_column(head[j : j + 1, :])) / CODE
            value = parts[m][at, :].astype(f32) * scale
            values[m, at, :] = value
            squares += jnp.sum(value * value, axis=1, keepdims=True)
        factor = lax.rsqrt(squares / (n * w) + EPSILON)
        for m in range(n):
            part(out_ref, me ^ m, w)[at, :] = values[m, at, :] * factor


def decode_kernel(w, n, me_ref, *refs):
    codes, stats, out_ref, values = refs[:n], refs[n : 2 * n], refs[2 * n], refs[2 * n + 1]
    rows = codes[0].shape[0]
    me = me_ref[0]
    for j in range(rows // BLOCK):
        at = slice(j * BLOCK, (j + 1) * BLOCK)
        squares = jnp.zeros((BLOCK, 1), f32)
        for m in range(n):
            lanes = stats[m][1:2, pl.ds(pl.multiple_of(me * rows + j * BLOCK, BLOCK), BLOCK)]
            value = codes[m][at, :].astype(f32) * (to_column(lanes) / CODE)
            values[m, at, :] = value
            squares += jnp.sum(value * value, axis=1, keepdims=True)
        factor = lax.rsqrt(squares / (n * w) + EPSILON)
        for m in range(n):
            part(out_ref, me ^ m, w)[at, :] = values[m, at, :] * factor


def call(kernel, out_shape, **kw):
    params = pltpu.CompilerParams(vmem_limit_bytes=VMEM_LIMIT)
    return pl.pallas_call(kernel, out_shape=out_shape, compiler_params=params, **kw)


def columns(values, n):
    rows, width = values.shape
    return values.reshape(rows, n, width // n).transpose(1, 0, 2)


def shards(points, point_cluster, cand_blocks, cent1_prev, parent, cent2_prev):
    point_rows, width = points.shape
    block_count = point_rows // BLOCK
    owned = cent1_prev.shape[0]
    upper_rows = cent2_prev.shape[0]
    n = lax.axis_size("cent")
    dp = lax.axis_index("dp")
    me = lax.axis_index("cent").astype(i32).reshape(1)
    w = width // n
    rows = n * owned
    wide = w % BLOCK == 0
    far_first = range(n - 1, 0, -1)

    def swap(value, mask):
        return lax.ppermute(value, "cent", [(i, i ^ mask) for i in range(n)])

    def swap_all(values):
        arrived = {m: swap(values[m], m) for m in far_first}
        return [values[0]] + [arrived[m] for m in range(1, n)]

    tile = 2 * BLOCK
    if wide:
        source = points
        specs = [pl.BlockSpec((tile, w), lambda i, at, m=m: (i, at[0] ^ m)) for m in range(n)]
    else:
        source = columns(points, n)
        specs = [pl.BlockSpec((1, tile, w), lambda i, at, m=m: (at[0] ^ m, i, 0)) for m in range(n)]
    packed = call(
        pack_kernel,
        [shape((point_rows, w), bf16)] * n,
        grid_spec=pltpu.PrefetchScalarGridSpec(
            num_scalar_prefetch=1,
            grid=(point_rows // tile,),
            in_specs=specs,
            out_specs=[pl.BlockSpec((tile, w), lambda i, at: (i, 0))] * n,
        ),
        name="pack",
    )(me, *([source] * n))
    arrived = swap_all(packed)

    small = jnp.concatenate([point_cluster - dp * rows, parent - dp * upper_rows]).reshape(-1, w)
    head = head_rows(point_rows + 2 * owned, w)
    prev_codes = call(
        functools.partial(prev_kernel, w),
        [shape((owned + head, w), i16)] * n,
        in_specs=[SMEM, VMEM, VMEM],
        out_specs=[VMEM] * n,
        scratch_shapes=[pltpu.VMEM((head, w), i32)],
        name="prev",
    )(me, cent1_prev if wide else columns(cent1_prev, n), small)
    prevs = swap_all(prev_codes)
    heads = jnp.stack([p[owned:].astype(i32) for p in prevs]).reshape(n, head * w)
    ids = heads[:, :point_rows].reshape(n * block_count, BLOCK)
    origin = me ^ jnp.arange(n)
    parents = heads[origin, point_rows : point_rows + owned].reshape(1, rows)
    scales = jnp.exp2(heads[:, point_rows + owned : point_rows + 2 * owned].astype(f32)) / CODE

    table_rows = lax.all_gather(cent2_prev, "dp", axis=0, tiled=True)

    out = call(
        functools.partial(sums_kernel, n),
        [shape((rows, w), bf16)] * 2 + [shape((2, rows), f32)] + [shape((owned, w), i16)] * n,
        in_specs=[SMEM, SMEM] + [VMEM] * (2 * n + 2),
        out_specs=[VMEM] * (n + 3),
        scratch_shapes=[pltpu.VMEM((rows, w), f32), pltpu.VMEM((rows, BLOCK), f32)],
        name="sums",
    )(me, ids[:, 0] // BLOCK, ids % BLOCK, scales.reshape(rows, 1), *arrived, *prevs)
    high, low, stat = out[:3]
    stats = swap_all([stat] * n)
    back = swap_all(out[3:])

    upper_head = head_rows(upper_rows, w)
    code = call(
        functools.partial(upper_kernel, n, width),
        shape((upper_rows + upper_head, w), i16),
        in_specs=[VMEM] * (n + 3),
        out_specs=VMEM,
        scratch_shapes=[pltpu.VMEM((upper_rows, w), f32), pltpu.VMEM((upper_head, w), i32)],
        name="upper",
    )(parents, high, low, *stats)
    half = n // 2
    parts = {0: code, half: swap(code, half)}
    for m in range(half - 1, 0, -1):
        parts[m] = swap(code, m)
    for m in range(half - 1, 0, -1):
        parts[half + m] = swap(parts[half], m)

    def joined(kernel, values, out_rows, name, scratch_rows):
        result = call(
            kernel,
            shape((out_rows, width) if wide else (n, out_rows, w), f32),
            in_specs=[SMEM] + [VMEM] * len(values),
            out_specs=VMEM,
            scratch_shapes=[pltpu.VMEM((n, scratch_rows, w), f32)],
            name=name,
        )(me, *values)
        return result if wide else result.transpose(1, 0, 2).reshape(out_rows, width)

    cent1_new = joined(functools.partial(decode_kernel, w, n), back + stats, owned, "decode", owned)

    unit_points = rms_norm(points.astype(f32)).astype(bf16)
    table_units = rms_norm(table_rows.astype(f32)).astype(bf16)
    products = lax.dot_general(
        unit_points, table_units, (((1,), (1,)), ((), ())), preferred_element_type=f32
    )
    column_block = jnp.arange(table_rows.shape[0]) // BLOCK
    listed = jnp.any(cand_blocks[:, :, None] == column_block[None, None, :], axis=1)
    weights = jnp.exp(products * (SHARPNESS / width)).reshape(block_count, BLOCK, -1)
    running = jnp.sum(weights * listed[:, None, :].astype(f32), axis=2).reshape(point_rows)
    point_score = jnp.log(running)

    cent2_new = joined(functools.partial(join_kernel, w), [parts[m] for m in range(n)], upper_rows, "join", upper_rows)
    return (cent1_new, cent2_new, point_score)


def solution(mesh):
    placed = (
        P(("dp", "cent"), None),
        P(("dp", "cent")),
        P(("dp", "cent"), None),
        P(("dp", "cent"), None),
        P(("dp", "cent")),
        P("dp", None),
    )
    return jax.shard_map(
        shards,
        mesh=mesh,
        in_specs=placed,
        out_specs=(P(("dp", "cent"), None), P("dp", None), P(("dp", "cent"))),
        check_vma=False,
    )
```

time: 242 us -> 187 us (0.77)
  waiting for transfers between devices: 185 us -> 29.1 us
  starting transfers between devices: 11.9 us -> 60.9 us
  local copies, waits for them, and re-layouts: 6.64 us -> 45.7 us
  Pallas kernels: 0 us -> 21 us
  matrix products: 11.3 us -> 5.34 us
  other arithmetic: 11.2 us -> 8.7 us
    all_to_all x2 -> x0, waiting for transfers between devices: 93.2 us -> none  [the longest x1 91.2 us: shards(): lax.all_to_all(outgoing, 'cent', split_axis=0, concat_axis=0, tiled=True)]
    psum x1 -> x0, waiting for transfers between devices: 91.1 us -> none  [shards(): cent2_new = rms_norm(lax.psum(upper_part, 'cent'))]
    ppermute x0 -> x35, starting transfers between devices: none -> 60.9 us  [swap(): return lax.ppermute(value, 'cent', [(i, i ^ mask) for i in range(n)])]
    ppermute x0 -> x35, waiting for transfers between devices: none -> 28.4 us  [swap(): return lax.ppermute(value, 'cent', [(i, i ^ mask) for i in range(n)])]
    unnamed x12 -> x91, local copies, waits for them, and re-layouts: 0.21 us -> 23.3 us
    pallas_call x0 -> x6, Pallas kernels: none -> 21 us  [the longest x2 7.68 us: joined(): call(kernel, shape((out_rows, width) if wide else (n, out_rows, w), f32),...]
    gather x2 -> x32, local copies, waits for them, and re-layouts: 4.94 us -> 21.6 us  [the longest x1 4.38 us: shards(): outgoing = point_blocks[source]]
    all_to_all x2 -> x0, starting transfers between devices: 11.8 us -> none  [the longest x1 7.28 us: shards(): lax.all_to_all(outgoing_ids, 'cent', split_axis=0, concat_axis=0, tiled=T...]
  transfers between devices with their start and end apart: 4 -> 36, of which waited for: 3 -> 6; matrix products, arithmetic and copies ran while one was open for 9% -> 16% of each run, Pallas kernels for 0% -> 11%
where the time goes in v2:
time: 187 us; the launch traced here: 185 us
  starting transfers between devices  60.9 us (33%)
  local copies, waits for them, and re-layouts  45.7 us (24%)
  waiting for transfers between devices  29.1 us (16%)
  Pallas kernels  21 us (11%)
  between operations  14.4 us (8%)
  other arithmetic  8.7 us (5%)
  matrix products  5.34 us (3%)
    ppermute x35, starting transfers between devices, swap(): return lax.ppermute(value, 'cent', [(i, i ^ mask) for i in range(n)])  60.9 us
    ppermute x35, waiting for transfers between devices, swap(): return lax.ppermute(value, 'cent', [(i, i ^ mask) for i in range(n)])  28.4 us
    unnamed x91, local copies, waits for them, and re-layouts  23.3 us
    gather x32, local copies, waits for them, and re-layouts  21.6 us
    pallas_call x2, Pallas kernels, joined(): call(kernel, shape((out_rows, width) if wide else (n, out_rows, w), f32),...  7.68 us
    pallas_call x1, Pallas kernels, shards(): call(functools.partial(sums_kernel, n), [shape((rows, w), bf16)] * 2 + [s...  7.1 us
    reduce_sum x2, other arithmetic, rms_norm(): jnp.mean(values * values, axis=-1, keepdims=True) + EPSILON  5.57 us
    dot_general x1, matrix products, shards(): lax.dot_general(unit_points, table_units, (((1,), (1,)), ((), ())), prefe...  5.34 us
  transfers between devices with their start and end apart: 36, of which 6 were waited for; matrix products, arithmetic and copies ran while one was open for 16% of the time, Pallas kernels for 11%

profile of v2, /device:TPU:0, one launch (start us, length us, event | category | flops | bytes accessed | tf_op | source)
XLA Modules:
  0.0 185.2 jit_solution(3784148328819816063)
XLA Ops:
  9.3 1.2 copy-done.1
  11.1 3.0 %collective-permute-start = (s16[272,128]{1,0:T(8,128)(2,1)S(1)}, s16[272,128]{1,0:T(8,128)(2,1)S(1)}, u32[]{:S(2)}, u32[]{:S(2)}) collective-permute-start(s16[272,128]{1,0:T(8,128)(2,1)S(1)} %get-tuple-element.31), channel_id=1, source_target_pairs={{0,1},{1,0},{2,3},{3,2},{4,5},{5,4},{6,7},{7,6},{8,9},{9,8},{10,11... | collective-permute-start | bytes 208904 | tf_op jit(solution)/shard_map/ppermute | solution.py:216
  14.0 1.6 collective-permute-start.1
  15.6 3.0 %collective-permute-start.3 = (s16[272,128]{1,0:T(8,128)(2,1)S(1)}, s16[272,128]{1,0:T(8,128)(2,1)S(1)}, u32[]{:S(2)}, u32[]{:S(2)}) collective-permute-start(s16[272,128]{1,0:T(8,128)(2,1)S(1)} %get-tuple-element.34), channel_id=1, source_target_pairs={{0,4},{1,5},{2,6},{3,7},{4,0},{5,1},{6,2},{7,3},{8,12},{9,13},{10,... | collective-permute-start | bytes 208904 | tf_op jit(solution)/shard_map/ppermute | solution.py:216
  18.6 1.3 collective-permute-start.4
  19.9 2.3 %fusion.3 = f32[1024]{0:T(1024)S(1)} fusion(bf16[1024,1024]{1,0:T(8,128)(2,1)} %refs_7_.1), kind=kLoop, calls=%fused_computation.9 | loop fusion | flops 3144704 | bytes 2101248 | tf_op jit(solution)/shard_map/reduce_sum | solution.py:23
  22.3 2.2 %pack.1 = (bf16[1024,128]{1,0:T(8,128)(2,1)S(1)}, bf16[1024,128]{1,0:T(8,128)(2,1)}, bf16[1024,128]{1,0:T(8,128)(2,1)}, bf16[1024,128]{1,0:T(8,128)(2,1)}, bf16[...) custom-call(s32[1]{0:T(128)} %bitcast.me_ref, ...), custom_call_target="tpu_custom_call" | custom-call | tf_op jit(solution)/shard_map/pack/pallas_call | solution.py:229
  25.2 3.5 %collective-permute-start.5 = (s16[272,128]{1,0:T(8,128)(2,1)S(1)}, s16[272,128]{1,0:T(8,128)(2,1)S(1)}, u32[]{:S(2)}, u32[]{:S(2)}) collective-permute-start(s16[272,128]{1,0:T(8,128)(2,1)S(1)} %get-tuple-element.36), channel_id=1, source_target_pairs={{0,6},{1,7},{2,4},{3,5},{4,2},{5,3},{6,0},{7,1},{8,14},{9,15},{10,... | collective-permute-start | bytes 208904 | tf_op jit(solution)/shard_map/ppermute | solution.py:216
  29.4 1.7 collective-permute-start.7
  31.8 1.7 collective-permute-start.9
  33.6 2.4 %collective-permute-start.10 = (bf16[1024,128]{1,0:T(8,128)(2,1)}, bf16[1024,128]{1,0:T(8,128)(2,1)}, u32[]{:S(2)}, u32[]{:S(2)}) collective-permute-start(bf16[1024,128]{1,0:T(8,128)(2,1)} %get-tuple-element.42), channel_id=1, source_target_pairs={{0,4},{1,5},{2,6},{3,7},{4,0},{5,1},{6,2},{7,3},{8,12},{9,13},{10,... | collective-permute-start | bytes 786440 | tf_op jit(solution)/shard_map/ppermute | solution.py:216
  36.8 1.0 collective-permute-start.11
  38.9 3.5 %collective-permute-start.12 = (bf16[1024,128]{1,0:T(8,128)(2,1)}, bf16[1024,128]{1,0:T(8,128)(2,1)}, u32[]{:S(2)}, u32[]{:S(2)}) collective-permute-start(bf16[1024,128]{1,0:T(8,128)(2,1)} %copy-done.25), channel_id=1, source_target_pairs={{0,6},{1,7},{2,4},{3,5},{4,2},{5,3},{6,0},{7,1},{8,14},{9,15},{10,... | collective-permute-start | bytes 786440 | tf_op jit(solution)/shard_map/ppermute | solution.py:216
  42.4 7.9 %collective-permute-done.8.refs_2_ = bf16[1024,128]{1,0:T(8,128)(2,1)S(1)} collective-permute-done((bf16[1024,128]{1,0:T(8,128)(2,1)}, bf16[1024,128]{1,0:T(8,128)(2,1)S(1)}, u32[]{:S(2)}, u32[]{:S(2)}) %collective-permute-start.8) | collective-permute-done | bytes 262176 | tf_op jit(solution)/shard_map/ppermute | solution.py:216
  51.0 1.9 %collective-permute-start.13 = (bf16[1024,128]{1,0:T(8,128)(2,1)}, bf16[1024,128]{1,0:T(8,128)(2,1)}, u32[]{:S(2)}, u32[]{:S(2)}) collective-permute-start(bf16[1024,128]{1,0:T(8,128)(2,1)} %copy-done.24), channel_id=1, source_target_pairs={{0,7},{1,6},{2,5},{3,4},{4,3},{5,2},{6,1},{7,0},{8,15},{9,14},{10,... | collective-permute-start | bytes 786440 | tf_op jit(solution)/shard_map/ppermute | solution.py:216
  53.6 1.1 copy.20
  55.5 17.8 %collective-permute-done.11.refs_5_ = bf16[1024,128]{1,0:T(8,128)(2,1)} collective-permute-done((bf16[1024,128]{1,0:T(8,128)(2,1)}, bf16[1024,128]{1,0:T(8,128)(2,1)}, u32[]{:S(2)}, u32[]{:S(2)}) %collective-permute-start.11) | collective-permute-done | bytes 262176 | tf_op jit(solution)/shard_map/ppermute | solution.py:216
  74.2 0.9 copy-done.9
  80.5 7.1 %sums.1 = (bf16[2048,128]{1,0:T(8,128)(2,1)S(1)}, bf16[2048,128]{1,0:T(8,128)(2,1)S(1)}, f32[2,2048]{1,0:T(2,128)}, s16[256,128]{1,0:T(8,128)(2,1)S(1)}, s16[256...) custom-call(s32[1]{0:T(128)} %bitcast.me_ref, ...), custom_call_target="tpu_custom_call" | custom-call | tf_op jit(solution)/shard_map/sums/pallas_call | solution.py:261
  94.2 3.5 %collective-permute-start.27 = (f32[2,2048]{1,0:T(2,128)}, f32[2,2048]{1,0:T(2,128)S(1)}, u32[]{:S(2)}, u32[]{:S(2)}) collective-permute-start(f32[2,2048]{1,0:T(2,128)} %get-tuple-element.54.refs_8_.refs_0_), channel_id=1, source_target_pairs={{0,7},{1,6},{2,5},{3,4},{4,3},{5,2},{6,1},{7,0},{8,15},{9,14},{10,... | collective-permute-start | bytes 49160 | tf_op jit(solution)/shard_map/ppermute | solution.py:216
  97.8 9.2 %collective-permute-start.25 = (f32[2,2048]{1,0:T(2,128)}, f32[2,2048]{1,0:T(2,128)S(1)}, u32[]{:S(2)}, u32[]{:S(2)}) collective-permute-start(f32[2,2048]{1,0:T(2,128)} %get-tuple-element.54.refs_8_.refs_0_), channel_id=1, source_target_pairs={{0,5},{1,4},{2,7},{3,6},{4,1},{5,0},{6,3},{7,2},{8,13},{9,12},{10,... | collective-permute-start | bytes 49160 | tf_op jit(solution)/shard_map/ppermute | solution.py:216
  107.1 1.5 collective-permute-start.23
  109.1 1.5 collective-permute-start.21
  111.2 21.7 %while.1 = (s32[]{:T(128)}, s32[8,2048]{1,0:T(8,128)}, s32[8,2]{0,1:T(2,128)S(1)}, s32[8,256]{1,0:T(8,128)S(1)}, s32[]{:T(128)}, /*index=5*/s32[]{:T(128)}) while((s32[]{:T(128)}, s32[8,2048]{1,0:T(8,128)}, s32[8,2]{0,1:T(2,128)S(1)}, s32[8,256]{1,0:T(8,128)S(1)}, s32[]{:T(128)}, /*index=5*/s32[]{:T(128)}) %tuple.28), condition=%wide.while_cond, body=%wide.while_body.sunk | while | flops 2 | bytes 4217 | solution.py:256
  111.8 2.0 %dynamic-slice.7 = s32[1,256]{1,0:T(1,128)S(1)} dynamic-slice(s32[8,2048]{1,0:T(8,128)} %get-tuple-element.117, s32[]{:T(128)} %bitcast.67, s32[]{:T(128)} %bitcast.68), dynamic_slice_sizes={1,256} | dynamic-slice | bytes 2052 | tf_op jit(solution)/shard_map/gather
  114.5 2.0 %dynamic-slice.7 = s32[1,256]{1,0:T(1,128)S(1)} dynamic-slice(s32[8,2048]{1,0:T(8,128)} %get-tuple-element.117, s32[]{:T(128)} %bitcast.67, s32[]{:T(128)} %bitcast.68), dynamic_slice_sizes={1,256} | dynamic-slice | bytes 2052 | tf_op jit(solution)/shard_map/gather
  117.3 2.0 %dynamic-slice.7 = s32[1,256]{1,0:T(1,128)S(1)} dynamic-slice(s32[8,2048]{1,0:T(8,128)} %get-tuple-element.117, s32[]{:T(128)} %bitcast.67, s32[]{:T(128)} %bitcast.68), dynamic_slice_sizes={1,256} | dynamic-slice | bytes 2052 | tf_op jit(solution)/shard_map/gather
  120.0 2.0 %dynamic-slice.7 = s32[1,256]{1,0:T(1,128)S(1)} dynamic-slice(s32[8,2048]{1,0:T(8,128)} %get-tuple-element.117, s32[]{:T(128)} %bitcast.67, s32[]{:T(128)} %bitcast.68), dynamic_slice_sizes={1,256} | dynamic-slice | bytes 2052 | tf_op jit(solution)/shard_map/gather
  122.7 2.0 %dynamic-slice.7 = s32[1,256]{1,0:T(1,128)S(1)} dynamic-slice(s32[8,2048]{1,0:T(8,128)} %get-tuple-element.117, s32[]{:T(128)} %bitcast.67, s32[]{:T(128)} %bitcast.68), dynamic_slice_sizes={1,256} | dynamic-slice | bytes 2052 | tf_op jit(solution)/shard_map/gather
  125.4 2.0 %dynamic-slice.7 = s32[1,256]{1,0:T(1,128)S(1)} dynamic-slice(s32[8,2048]{1,0:T(8,128)} %get-tuple-element.117, s32[]{:T(128)} %bitcast.67, s32[]{:T(128)} %bitcast.68), dynamic_slice_sizes={1,256} | dynamic-slice | bytes 2052 | tf_op jit(solution)/shard_map/gather
  128.1 2.0 %dynamic-slice.7 = s32[1,256]{1,0:T(1,128)S(1)} dynamic-slice(s32[8,2048]{1,0:T(8,128)} %get-tuple-element.117, s32[]{:T(128)} %bitcast.67, s32[]{:T(128)} %bitcast.68), dynamic_slice_sizes={1,256} | dynamic-slice | bytes 2052 | tf_op jit(solution)/shard_map/gather
  130.8 2.0 %dynamic-slice.7 = s32[1,256]{1,0:T(1,128)S(1)} dynamic-slice(s32[8,2048]{1,0:T(8,128)} %get-tuple-element.117, s32[]{:T(128)} %bitcast.67, s32[]{:T(128)} %bitcast.68), dynamic_slice_sizes={1,256} | dynamic-slice | bytes 2052 | tf_op jit(solution)/shard_map/gather
  132.9 1.5 collective-permute-start.15
  134.4 1.5 collective-permute-start.16
  135.9 2.8 %collective-permute-start.17 = (s16[256,128]{1,0:T(8,128)(2,1)}, s16[256,128]{1,0:T(8,128)(2,1)S(1)}, u32[]{:S(2)}, u32[]{:S(2)}) collective-permute-start(s16[256,128]{1,0:T(8,128)(2,1)} %copy-done.29), channel_id=1, source_target_pairs={{0,4},{1,5},{2,6},{3,7},{4,0},{5,1},{6,2},{7,3},{8,12},{9,13},{10,... | collective-permute-start | bytes 196616 | tf_op jit(solution)/shard_map/ppermute | solution.py:216
  138.8 1.0 copy-done.3
  139.8 1.0 copy-done.5
  140.9 3.5 %upper.1.refs_0_ = s16[528,128]{1,0:T(8,128)(2,1)S(1)} custom-call(s32[1,2048]{1,0:T(1,128)S(1)} %bitcast.70, bf16[2048,128]{1,0:T(8,128)(2,1)S(1)} %copy-done.3, bf16[2048,128]{1,0:T(8,128)(2,1)S(1)} %copy-done.5, f32[2,2048]{1,0:T(2,128)} %get-tuple-element.54.refs_8_.refs_0_, f32[2,2048]{1,0:T(2,128)S(1)} %collective-permute-done.21.refs_9_.refs_1_, ...), custom_call_target="tpu_custom_call" | custom-call | tf_op jit(solution)/shard_map/upper/pallas_call | solution.py:274
  144.4 1.4 collective-permute-start.30
  145.8 2.4 %collective-permute-start.18 = (s16[256,128]{1,0:T(8,128)(2,1)}, s16[256,128]{1,0:T(8,128)(2,1)S(1)}, u32[]{:S(2)}, u32[]{:S(2)}) collective-permute-start(s16[256,128]{1,0:T(8,128)(2,1)} %copy-done.28), channel_id=1, source_target_pairs={{0,5},{1,4},{2,7},{3,6},{4,1},{5,0},{6,3},{7,2},{8,13},{9,12},{10,... | collective-permute-start | bytes 196616 | tf_op jit(solution)/shard_map/ppermute | solution.py:216
  148.3 1.5 collective-permute-start.19
  149.7 2.4 %collective-permute-start.20 = (s16[256,128]{1,0:T(8,128)(2,1)}, s16[256,128]{1,0:T(8,128)(2,1)S(1)}, u32[]{:S(2)}, u32[]{:S(2)}) collective-permute-start(s16[256,128]{1,0:T(8,128)(2,1)} %copy-done.26), channel_id=1, source_target_pairs={{0,7},{1,6},{2,5},{3,4},{4,3},{5,2},{6,1},{7,0},{8,15},{9,14},{10,... | collective-permute-start | bytes 196616 | tf_op jit(solution)/shard_map/ppermute | solution.py:216
  153.1 2.0 %collective-permute-start.29 = (s16[528,128]{1,0:T(8,128)(2,1)S(1)}, s16[528,128]{1,0:T(8,128)(2,1)S(1)}, u32[]{:S(2)}, u32[]{:S(2)}) collective-permute-start(s16[528,128]{1,0:T(8,128)(2,1)S(1)} %upper.1.refs_0_), channel_id=1, source_target_pairs={{0,2},{1,3},{2,0},{3,1},{4,6},{5,7},{6,4},{7,5},{8,10},{9,11},{10,... | collective-permute-start | bytes 405512 | tf_op jit(solution)/shard_map/ppermute | solution.py:216
  157.7 1.7 collective-permute-start.33
  161.0 3.1 %decode.1 = f32[256,1024]{1,0:T(8,128)} custom-call(s32[1]{0:T(128)} %bitcast.me_ref, s16[256,128]{1,0:T(8,128)(2,1)S(1)} %copy-done.23, s16[256,128]{1,0:T(8,128)(2,1)S(1)} %collective-permute-done.14.refs_1_, s16[256,128]{1,0:T(8,128)(2,1)S(1)} %collective-permute-done.15.refs_2_, s16[256,128]{1,0:T(8,128)(2,1)S(1)} %collective-permute-done.16.refs_3_, ...), custom_call_target="tpu_custom_call" | custom-call | tf_op jit(solution)/shard_map/decode/pallas_call | solution.py:290
  164.4 4.6 %join.1 = f32[512,1024]{1,0:T(8,128)} custom-call(s32[1]{0:T(128)} %bitcast.me_ref, s16[528,128]{1,0:T(8,128)(2,1)S(1)} %upper.1.refs_0_, s16[528,128]{1,0:T(8,128)(2,1)S(1)} %collective-permute-done.28.refs_1_, s16[528,128]{1,0:T(8,128)(2,1)S(1)} %collective-permute-done.29.refs_2_, s16[528,128]{1,0:T(8,128)(2,1)S(1)} %collective-permute-done.30.refs_3_, ...), custom_call_target="tpu_custom_call" | custom-call | tf_op jit(solution)/shard_map/join/pallas_call | solution.py:290
  169.0 3.2 %fusion = f32[2048]{0:T(1024)S(1)} fusion(bf16[2048,1024]{1,0:T(8,128)(2,1)} %all-gather.2.cloned.1.call-done), kind=kLoop, calls=%fused_computation.3 | loop fusion | flops 6289408 | bytes 4202496 | tf_op jit(solution)/shard_map/reduce_sum | solution.py:23
  172.4 5.3 %fusion.2 = f32[1024]{0:T(1024)S(1)} fusion(bf16[2048,1024]{1,0:T(8,128)(2,1)S(1)} %copy-done.33, f32[8,2048]{1,0:T(8,128)S(1)} %convert_element_type.36, f32[2048]{0:T(1024)S(1)} %add_rsqrt_fusion, bf16[1024,1024]{1,0:T(8,128)(2,1)S(1)} %copy-done, f32[1024]{0:T(1024)S(1)} %add_rsqrt_fusion.1), kind=kOutput, calls=%fused_computation.6 | convolution fusion | flops 4310694912 | bytes 6373376 | tf_op jit(solution)/shard_map/dot_general | solution.py:304
  (178 shorter events, 34.5 us)
Async XLA Ops:
  7.2 15.1 %copy-start = (bf16[1024,1024]{1,0:T(8,128)(2,1)S(1)}, bf16[1024,1024]{1,0:T(8,128)(2,1)}, u32[]{:S(2)}) copy-start(bf16[1024,1024]{1,0:T(8,128)(2,1)} %refs_7_.1) | copy-start | bytes 6291460
  7.2 161.8 %all-gather.2.cloned.1.call-start = ((), (), s32[]{:S(2)}) async-start(), calls=%async_computation | async-start | bytes 5242880 | tf_op jit(solution)/shard_map/all_gather | solution.py:259
  9.3 1.2 copy-start.1
  11.1 13.4 %collective-permute-start = (s16[272,128]{1,0:T(8,128)(2,1)S(1)}, s16[272,128]{1,0:T(8,128)(2,1)S(1)}, u32[]{:S(2)}, u32[]{:S(2)}) collective-permute-start(s16[272,128]{1,0:T(8,128)(2,1)S(1)} %get-tuple-element.31), channel_id=1, source_target_pairs={{0,1},{1,0},{2,3},{3,2},{4,5},{5,4},{6,7},{7,6},{8,9},{9,8},{10,11... | collective-permute-start | bytes 208904 | tf_op jit(solution)/shard_map/ppermute | solution.py:216
  14.0 14.7 %collective-permute-start.1 = (s16[272,128]{1,0:T(8,128)(2,1)S(1)}, s16[272,128]{1,0:T(8,128)(2,1)S(1)}, u32[]{:S(2)}, u32[]{:S(2)}) collective-permute-start(s16[272,128]{1,0:T(8,128)(2,1)S(1)} %get-tuple-element.32), channel_id=1, source_target_pairs={{0,2},{1,3},{2,0},{3,1},{4,6},{5,7},{6,4},{7,5},{8,10},{9,11},{10,... | collective-permute-start | bytes 208904 | tf_op jit(solution)/shard_map/ppermute | solution.py:216
  15.6 13.8 %collective-permute-start.2 = (s16[272,128]{1,0:T(8,128)(2,1)S(1)}, s16[272,128]{1,0:T(8,128)(2,1)S(1)}, u32[]{:S(2)}, u32[]{:S(2)}) collective-permute-start(s16[272,128]{1,0:T(8,128)(2,1)S(1)} %get-tuple-element.33), channel_id=1, source_target_pairs={{0,3},{1,2},{2,1},{3,0},{4,7},{5,6},{6,5},{7,4},{8,11},{9,10},{10,... | collective-permute-start | bytes 208904 | tf_op jit(solution)/shard_map/ppermute | solution.py:216
  15.6 16.2 %collective-permute-start.3 = (s16[272,128]{1,0:T(8,128)(2,1)S(1)}, s16[272,128]{1,0:T(8,128)(2,1)S(1)}, u32[]{:S(2)}, u32[]{:S(2)}) collective-permute-start(s16[272,128]{1,0:T(8,128)(2,1)S(1)} %get-tuple-element.34), channel_id=1, source_target_pairs={{0,4},{1,5},{2,6},{3,7},{4,0},{5,1},{6,2},{7,3},{8,12},{9,13},{10,... | collective-permute-start | bytes 208904 | tf_op jit(solution)/shard_map/ppermute | solution.py:216
  18.6 13.2 %collective-permute-start.4 = (s16[272,128]{1,0:T(8,128)(2,1)S(1)}, s16[272,128]{1,0:T(8,128)(2,1)S(1)}, u32[]{:S(2)}, u32[]{:S(2)}) collective-permute-start(s16[272,128]{1,0:T(8,128)(2,1)S(1)} %get-tuple-element.35), channel_id=1, source_target_pairs={{0,5},{1,4},{2,7},{3,6},{4,1},{5,0},{6,3},{7,2},{8,13},{9,12},{10,... | collective-permute-start | bytes 208904 | tf_op jit(solution)/shard_map/ppermute | solution.py:216
  24.5 12.3 %copy-start.25 = (bf16[1024,128]{1,0:T(8,128)(2,1)}, bf16[1024,128]{1,0:T(8,128)(2,1)S(1)}, u32[]{:S(2)}) copy-start(bf16[1024,128]{1,0:T(8,128)(2,1)S(1)} %get-tuple-element.44) | copy-start | bytes 786436
  25.2 8.3 %collective-permute-start.5 = (s16[272,128]{1,0:T(8,128)(2,1)S(1)}, s16[272,128]{1,0:T(8,128)(2,1)S(1)}, u32[]{:S(2)}, u32[]{:S(2)}) collective-permute-start(s16[272,128]{1,0:T(8,128)(2,1)S(1)} %get-tuple-element.36), channel_id=1, source_target_pairs={{0,6},{1,7},{2,4},{3,5},{4,2},{5,3},{6,0},{7,1},{8,14},{9,15},{10,... | collective-permute-start | bytes 208904 | tf_op jit(solution)/shard_map/ppermute | solution.py:216
  28.8 8.0 %collective-permute-start.6 = (s16[272,128]{1,0:T(8,128)(2,1)S(1)}, s16[272,128]{1,0:T(8,128)(2,1)S(1)}, u32[]{:S(2)}, u32[]{:S(2)}) collective-permute-start(s16[272,128]{1,0:T(8,128)(2,1)S(1)} %get-tuple-element.37), channel_id=1, source_target_pairs={{0,7},{1,6},{2,5},{3,4},{4,3},{5,2},{6,1},{7,0},{8,15},{9,14},{10,... | collective-permute-start | bytes 208904 | tf_op jit(solution)/shard_map/ppermute | solution.py:216
  29.4 8.7 %collective-permute-start.7 = (bf16[1024,128]{1,0:T(8,128)(2,1)}, bf16[1024,128]{1,0:T(8,128)(2,1)S(1)}, u32[]{:S(2)}, u32[]{:S(2)}) collective-permute-start(bf16[1024,128]{1,0:T(8,128)(2,1)} %get-tuple-element.39), channel_id=1, source_target_pairs={{0,1},{1,0},{2,3},{3,2},{4,5},{5,4},{6,7},{7,6},{8,9},{9,8},{10,11... | collective-permute-start | bytes 786440 | tf_op jit(solution)/shard_map/ppermute | solution.py:216
  31.8 21.8 %copy-start.14 = (s16[272,128]{1,0:T(8,128)(2,1)}, s16[272,128]{1,0:T(8,128)(2,1)S(1)}, u32[]{:S(2)}) copy-start(s16[272,128]{1,0:T(8,128)(2,1)S(1)} %collective-permute-done.3.refs_12_) | copy-start | bytes 208900
  31.8 18.6 %collective-permute-start.8 = (bf16[1024,128]{1,0:T(8,128)(2,1)}, bf16[1024,128]{1,0:T(8,128)(2,1)S(1)}, u32[]{:S(2)}, u32[]{:S(2)}) collective-permute-start(bf16[1024,128]{1,0:T(8,128)(2,1)} %get-tuple-element.40), channel_id=1, source_target_pairs={{0,2},{1,3},{2,0},{3,1},{4,6},{5,7},{6,4},{7,5},{8,10},{9,11},{10,... | collective-permute-start | bytes 786440 | tf_op jit(solution)/shard_map/ppermute | solution.py:216
  31.8 21.8 %copy-start.16 = (s16[272,128]{1,0:T(8,128)(2,1)}, s16[272,128]{1,0:T(8,128)(2,1)S(1)}, u32[]{:S(2)}) copy-start(s16[272,128]{1,0:T(8,128)(2,1)S(1)} %collective-permute-done.4.refs_13_) | copy-start | bytes 208900
  31.8 23.6 %collective-permute-start.9 = (bf16[1024,128]{1,0:T(8,128)(2,1)}, bf16[1024,128]{1,0:T(8,128)(2,1)}, u32[]{:S(2)}, u32[]{:S(2)}) collective-permute-start(bf16[1024,128]{1,0:T(8,128)(2,1)} %get-tuple-element.41), channel_id=1, source_target_pairs={{0,3},{1,2},{2,1},{3,0},{4,7},{5,6},{6,5},{7,4},{8,11},{9,10},{10,... | collective-permute-start | bytes 786440 | tf_op jit(solution)/shard_map/ppermute | solution.py:216
  33.6 20.0 %copy-start.18 = (s16[272,128]{1,0:T(8,128)(2,1)}, s16[272,128]{1,0:T(8,128)(2,1)S(1)}, u32[]{:S(2)}) copy-start(s16[272,128]{1,0:T(8,128)(2,1)S(1)} %collective-permute-done.5.refs_14_) | copy-start | bytes 208900
  33.6 21.9 %collective-permute-start.10 = (bf16[1024,128]{1,0:T(8,128)(2,1)}, bf16[1024,128]{1,0:T(8,128)(2,1)}, u32[]{:S(2)}, u32[]{:S(2)}) collective-permute-start(bf16[1024,128]{1,0:T(8,128)(2,1)} %get-tuple-element.42), channel_id=1, source_target_pairs={{0,4},{1,5},{2,6},{3,7},{4,0},{5,1},{6,2},{7,3},{8,12},{9,13},{10,... | collective-permute-start | bytes 786440 | tf_op jit(solution)/shard_map/ppermute | solution.py:216
  36.8 16.8 %copy-start.20 = (s16[272,128]{1,0:T(8,128)(2,1)}, s16[272,128]{1,0:T(8,128)(2,1)S(1)}, u32[]{:S(2)}) copy-start(s16[272,128]{1,0:T(8,128)(2,1)S(1)} %collective-permute-done.6.refs_15_) | copy-start | bytes 208900
  36.8 36.5 %collective-permute-start.11 = (bf16[1024,128]{1,0:T(8,128)(2,1)}, bf16[1024,128]{1,0:T(8,128)(2,1)}, u32[]{:S(2)}, u32[]{:S(2)}) collective-permute-start(bf16[1024,128]{1,0:T(8,128)(2,1)} %get-tuple-element.43), channel_id=1, source_target_pairs={{0,5},{1,4},{2,7},{3,6},{4,1},{5,0},{6,3},{7,2},{8,13},{9,12},{10,... | collective-permute-start | bytes 786440 | tf_op jit(solution)/shard_map/ppermute | solution.py:216
  38.0 15.6 %copy-start.35 = (s32[8,2048]{1,0:T(8,128)}, s32[8,2048]{1,0:T(8,128)S(1)}, u32[]{:S(2)}) copy-start(s32[8,2048]{1,0:T(8,128)S(1)} %stack.38) | copy-start | bytes 196612
  38.0 15.6 %copy-start.34 = (s32[64,128]{1,0:T(8,128)}, s32[64,128]{1,0:T(8,128)S(1)}, u32[]{:S(2)}) copy-start(s32[64,128]{1,0:T(8,128)S(1)} %reshape.104) | copy-start | bytes 98308
  38.9 34.4 %collective-permute-start.12 = (bf16[1024,128]{1,0:T(8,128)(2,1)}, bf16[1024,128]{1,0:T(8,128)(2,1)}, u32[]{:S(2)}, u32[]{:S(2)}) collective-permute-start(bf16[1024,128]{1,0:T(8,128)(2,1)} %copy-done.25), channel_id=1, source_target_pairs={{0,6},{1,7},{2,4},{3,5},{4,2},{5,3},{6,0},{7,1},{8,14},{9,15},{10,... | collective-permute-start | bytes 786440 | tf_op jit(solution)/shard_map/ppermute | solution.py:216
  51.0 22.2 %collective-permute-start.13 = (bf16[1024,128]{1,0:T(8,128)(2,1)}, bf16[1024,128]{1,0:T(8,128)(2,1)}, u32[]{:S(2)}, u32[]{:S(2)}) collective-permute-start(bf16[1024,128]{1,0:T(8,128)(2,1)} %copy-done.24), channel_id=1, source_target_pairs={{0,7},{1,6},{2,5},{3,4},{4,3},{5,2},{6,1},{7,0},{8,15},{9,14},{10,... | collective-permute-start | bytes 786440 | tf_op jit(solution)/shard_map/ppermute | solution.py:216
  94.2 14.4 %collective-permute-start.27 = (f32[2,2048]{1,0:T(2,128)}, f32[2,2048]{1,0:T(2,128)S(1)}, u32[]{:S(2)}, u32[]{:S(2)}) collective-permute-start(f32[2,2048]{1,0:T(2,128)} %get-tuple-element.54.refs_8_.refs_0_), channel_id=1, source_target_pairs={{0,7},{1,6},{2,5},{3,4},{4,3},{5,2},{6,1},{7,0},{8,15},{9,14},{10,... | collective-permute-start | bytes 49160 | tf_op jit(solution)/shard_map/ppermute | solution.py:216
  97.7 11.5 %collective-permute-start.26 = (f32[2,2048]{1,0:T(2,128)}, f32[2,2048]{1,0:T(2,128)S(1)}, u32[]{:S(2)}, u32[]{:S(2)}) collective-permute-start(f32[2,2048]{1,0:T(2,128)} %get-tuple-element.54.refs_8_.refs_0_), channel_id=1, source_target_pairs={{0,6},{1,7},{2,4},{3,5},{4,2},{5,3},{6,0},{7,1},{8,14},{9,15},{10,... | collective-permute-start | bytes 49160 | tf_op jit(solution)/shard_map/ppermute | solution.py:216
  97.8 12.9 %collective-permute-start.25 = (f32[2,2048]{1,0:T(2,128)}, f32[2,2048]{1,0:T(2,128)S(1)}, u32[]{:S(2)}, u32[]{:S(2)}) collective-permute-start(f32[2,2048]{1,0:T(2,128)} %get-tuple-element.54.refs_8_.refs_0_), channel_id=1, source_target_pairs={{0,5},{1,4},{2,7},{3,6},{4,1},{5,0},{6,3},{7,2},{8,13},{9,12},{10,... | collective-permute-start | bytes 49160 | tf_op jit(solution)/shard_map/ppermute | solution.py:216
  107.0 25.9 %collective-permute-start.24 = (f32[2,2048]{1,0:T(2,128)}, f32[2,2048]{1,0:T(2,128)S(1)}, u32[]{:S(2)}, u32[]{:S(2)}) collective-permute-start(f32[2,2048]{1,0:T(2,128)} %get-tuple-element.54.refs_8_.refs_0_), channel_id=1, source_target_pairs={{0,4},{1,5},{2,6},{3,7},{4,0},{5,1},{6,2},{7,3},{8,12},{9,13},{10,... | collective-permute-start | bytes 49160 | tf_op jit(solution)/shard_map/ppermute | solution.py:216
  107.1 27.3 %collective-permute-start.23 = (f32[2,2048]{1,0:T(2,128)}, f32[2,2048]{1,0:T(2,128)S(1)}, u32[]{:S(2)}, u32[]{:S(2)}) collective-permute-start(f32[2,2048]{1,0:T(2,128)} %get-tuple-element.54.refs_8_.refs_0_), channel_id=1, source_target_pairs={{0,3},{1,2},{2,1},{3,0},{4,7},{5,6},{6,5},{7,4},{8,11},{9,10},{10,... | collective-permute-start | bytes 49160 | tf_op jit(solution)/shard_map/ppermute | solution.py:216
  108.6 27.4 %collective-permute-start.22 = (f32[2,2048]{1,0:T(2,128)}, f32[2,2048]{1,0:T(2,128)S(1)}, u32[]{:S(2)}, u32[]{:S(2)}) collective-permute-start(f32[2,2048]{1,0:T(2,128)} %get-tuple-element.54.refs_8_.refs_0_), channel_id=1, source_target_pairs={{0,2},{1,3},{2,0},{3,1},{4,6},{5,7},{6,4},{7,5},{8,10},{9,11},{10,... | collective-permute-start | bytes 49160 | tf_op jit(solution)/shard_map/ppermute | solution.py:216
  109.1 29.6 %collective-permute-start.21 = (f32[2,2048]{1,0:T(2,128)}, f32[2,2048]{1,0:T(2,128)S(1)}, u32[]{:S(2)}, u32[]{:S(2)}) collective-permute-start(f32[2,2048]{1,0:T(2,128)} %get-tuple-element.54.refs_8_.refs_0_), channel_id=1, source_target_pairs={{0,1},{1,0},{2,3},{3,2},{4,5},{5,4},{6,7},{7,6},{8,9},{9,8},{10,11... | collective-permute-start | bytes 49160 | tf_op jit(solution)/shard_map/ppermute | solution.py:216
  110.7 33.8 %collective-permute-start.14 = (s16[256,128]{1,0:T(8,128)(2,1)}, s16[256,128]{1,0:T(8,128)(2,1)S(1)}, u32[]{:S(2)}, u32[]{:S(2)}) collective-permute-start(s16[256,128]{1,0:T(8,128)(2,1)} %copy-done.32), channel_id=1, source_target_pairs={{0,1},{1,0},{2,3},{3,2},{4,5},{5,4},{6,7},{7,6},{8,9},{9,8},{10,11... | collective-permute-start | bytes 196616 | tf_op jit(solution)/shard_map/ppermute | solution.py:216
  132.9 12.9 %collective-permute-start.15 = (s16[256,128]{1,0:T(8,128)(2,1)}, s16[256,128]{1,0:T(8,128)(2,1)S(1)}, u32[]{:S(2)}, u32[]{:S(2)}) collective-permute-start(s16[256,128]{1,0:T(8,128)(2,1)} %copy-done.31), channel_id=1, source_target_pairs={{0,2},{1,3},{2,0},{3,1},{4,6},{5,7},{6,4},{7,5},{8,10},{9,11},{10,... | collective-permute-start | bytes 196616 | tf_op jit(solution)/shard_map/ppermute | solution.py:216
  134.4 13.9 %collective-permute-start.16 = (s16[256,128]{1,0:T(8,128)(2,1)}, s16[256,128]{1,0:T(8,128)(2,1)S(1)}, u32[]{:S(2)}, u32[]{:S(2)}) collective-permute-start(s16[256,128]{1,0:T(8,128)(2,1)} %copy-done.30), channel_id=1, source_target_pairs={{0,3},{1,2},{2,1},{3,0},{4,7},{5,6},{6,5},{7,4},{8,11},{9,10},{10,... | collective-permute-start | bytes 196616 | tf_op jit(solution)/shard_map/ppermute | solution.py:216
  135.9 13.8 %collective-permute-start.17 = (s16[256,128]{1,0:T(8,128)(2,1)}, s16[256,128]{1,0:T(8,128)(2,1)S(1)}, u32[]{:S(2)}, u32[]{:S(2)}) collective-permute-start(s16[256,128]{1,0:T(8,128)(2,1)} %copy-done.29), channel_id=1, source_target_pairs={{0,4},{1,5},{2,6},{3,7},{4,0},{5,1},{6,2},{7,3},{8,12},{9,13},{10,... | collective-permute-start | bytes 196616 | tf_op jit(solution)/shard_map/ppermute | solution.py:216
  138.8 1.0 copy-start.3
  139.8 1.0 copy-start.5
  144.3 12.3 %collective-permute-start.31 = (s16[528,128]{1,0:T(8,128)(2,1)S(1)}, s16[528,128]{1,0:T(8,128)(2,1)S(1)}, u32[]{:S(2)}, u32[]{:S(2)}) collective-permute-start(s16[528,128]{1,0:T(8,128)(2,1)S(1)} %upper.1.refs_0_), channel_id=1, source_target_pairs={{0,4},{1,5},{2,6},{3,7},{4,0},{5,1},{6,2},{7,3},{8,12},{9,13},{10,... | collective-permute-start | bytes 405512 | tf_op jit(solution)/shard_map/ppermute | solution.py:216
  144.4 15.0 %collective-permute-start.30 = (s16[528,128]{1,0:T(8,128)(2,1)S(1)}, s16[528,128]{1,0:T(8,128)(2,1)S(1)}, u32[]{:S(2)}, u32[]{:S(2)}) collective-permute-start(s16[528,128]{1,0:T(8,128)(2,1)S(1)} %upper.1.refs_0_), channel_id=1, source_target_pairs={{0,3},{1,2},{2,1},{3,0},{4,7},{5,6},{6,5},{7,4},{8,11},{9,10},{10,... | collective-permute-start | bytes 405512 | tf_op jit(solution)/shard_map/ppermute | solution.py:216
  145.8 7.2 %collective-permute-start.18 = (s16[256,128]{1,0:T(8,128)(2,1)}, s16[256,128]{1,0:T(8,128)(2,1)S(1)}, u32[]{:S(2)}, u32[]{:S(2)}) collective-permute-start(s16[256,128]{1,0:T(8,128)(2,1)} %copy-done.28), channel_id=1, source_target_pairs={{0,5},{1,4},{2,7},{3,6},{4,1},{5,0},{6,3},{7,2},{8,13},{9,12},{10,... | collective-permute-start | bytes 196616 | tf_op jit(solution)/shard_map/ppermute | solution.py:216
  148.3 7.6 %collective-permute-start.19 = (s16[256,128]{1,0:T(8,128)(2,1)}, s16[256,128]{1,0:T(8,128)(2,1)S(1)}, u32[]{:S(2)}, u32[]{:S(2)}) collective-permute-start(s16[256,128]{1,0:T(8,128)(2,1)} %copy-done.27), channel_id=1, source_target_pairs={{0,6},{1,7},{2,4},{3,5},{4,2},{5,3},{6,0},{7,1},{8,14},{9,15},{10,... | collective-permute-start | bytes 196616 | tf_op jit(solution)/shard_map/ppermute | solution.py:216
  149.7 7.9 %collective-permute-start.20 = (s16[256,128]{1,0:T(8,128)(2,1)}, s16[256,128]{1,0:T(8,128)(2,1)S(1)}, u32[]{:S(2)}, u32[]{:S(2)}) collective-permute-start(s16[256,128]{1,0:T(8,128)(2,1)} %copy-done.26), channel_id=1, source_target_pairs={{0,7},{1,6},{2,5},{3,4},{4,3},{5,2},{6,1},{7,0},{8,15},{9,14},{10,... | collective-permute-start | bytes 196616 | tf_op jit(solution)/shard_map/ppermute | solution.py:216
  153.1 11.1 %collective-permute-start.29 = (s16[528,128]{1,0:T(8,128)(2,1)S(1)}, s16[528,128]{1,0:T(8,128)(2,1)S(1)}, u32[]{:S(2)}, u32[]{:S(2)}) collective-permute-start(s16[528,128]{1,0:T(8,128)(2,1)S(1)} %upper.1.refs_0_), channel_id=1, source_target_pairs={{0,2},{1,3},{2,0},{3,1},{4,6},{5,7},{6,4},{7,5},{8,10},{9,11},{10,... | collective-permute-start | bytes 405512 | tf_op jit(solution)/shard_map/ppermute | solution.py:216
  155.9 8.2 %collective-permute-start.28 = (s16[528,128]{1,0:T(8,128)(2,1)S(1)}, s16[528,128]{1,0:T(8,128)(2,1)S(1)}, u32[]{:S(2)}, u32[]{:S(2)}) collective-permute-start(s16[528,128]{1,0:T(8,128)(2,1)S(1)} %upper.1.refs_0_), channel_id=1, source_target_pairs={{0,1},{1,0},{2,3},{3,2},{4,5},{5,4},{6,7},{7,6},{8,9},{9,8},{10,11... | collective-permute-start | bytes 405512 | tf_op jit(solution)/shard_map/ppermute | solution.py:216
  156.7 7.5 %collective-permute-start.34 = (s16[528,128]{1,0:T(8,128)(2,1)S(1)}, s16[528,128]{1,0:T(8,128)(2,1)S(1)}, u32[]{:S(2)}, u32[]{:S(2)}) collective-permute-start(s16[528,128]{1,0:T(8,128)(2,1)S(1)} %collective-permute-done.31.refs_4_), channel_id=1, source_target_pairs={{0,3},{1,2},{2,1},{3,0},{4,7},{5,6},{6,5},{7,4},{8,11},{9,10},{10,... | collective-permute-start | bytes 405512 | tf_op jit(solution)/shard_map/ppermute | solution.py:216
  157.7 6.4 %collective-permute-start.33 = (s16[528,128]{1,0:T(8,128)(2,1)S(1)}, s16[528,128]{1,0:T(8,128)(2,1)S(1)}, u32[]{:S(2)}, u32[]{:S(2)}) collective-permute-start(s16[528,128]{1,0:T(8,128)(2,1)S(1)} %collective-permute-done.31.refs_4_), channel_id=1, source_target_pairs={{0,2},{1,3},{2,0},{3,1},{4,6},{5,7},{6,4},{7,5},{8,10},{9,11},{10,... | collective-permute-start | bytes 405512 | tf_op jit(solution)/shard_map/ppermute | solution.py:216
  159.4 5.0 %collective-permute-start.32 = (s16[528,128]{1,0:T(8,128)(2,1)S(1)}, s16[528,128]{1,0:T(8,128)(2,1)S(1)}, u32[]{:S(2)}, u32[]{:S(2)}) collective-permute-start(s16[528,128]{1,0:T(8,128)(2,1)S(1)} %collective-permute-done.31.refs_4_), channel_id=1, source_target_pairs={{0,1},{1,0},{2,3},{3,2},{4,5},{5,4},{6,7},{7,6},{8,9},{9,8},{10,11... | collective-permute-start | bytes 405512 | tf_op jit(solution)/shard_map/ppermute | solution.py:216
  169.0 3.4 %copy-start.33 = (bf16[2048,1024]{1,0:T(8,128)(2,1)S(1)}, bf16[2048,1024]{1,0:T(8,128)(2,1)}, u32[]{:S(2)}) copy-start(bf16[2048,1024]{1,0:T(8,128)(2,1)} %all-gather.2.cloned.1.call-done) | copy-start | bytes 12582916
  (24 other events, 18.0 us)
Sparse Core Ops, SparseCore 0:
  9.6 37.1 all-gather.1

commit v3 on v2

v3 whole, which is shorter than its diff:
```python
import functools

import jax
import jax.numpy as jnp
from jax import lax
from jax.experimental import pallas as pl
from jax.experimental.pallas import tpu as pltpu
from jax.sharding import PartitionSpec as P

BLOCK = 128
EPSILON = 1e-06
SHARPNESS = 20.0
CODE = 32000.0
FLOOR = 1e-30
VMEM_LIMIT = 48 * 1024 * 1024
f32, bf16, i16, i32 = jnp.float32, jnp.bfloat16, jnp.int16, jnp.int32
shape = jax.ShapeDtypeStruct
VMEM = pl.BlockSpec(memory_space=pltpu.VMEM)
SMEM = pl.BlockSpec(memory_space=pltpu.SMEM)


def rms_norm(values):
    return values * lax.rsqrt(jnp.mean(values * values, axis=-1, keepdims=True) + EPSILON)


def split(values):
    high = values.astype(bf16)
    return high, (values - high.astype(f32)).astype(bf16)


def dot(a, b):
    return jnp.dot(a, b, preferred_element_type=f32)


def dot_lanes(a, b):
    return lax.dot_general(a, b, (((1,), (1,)), ((), ())), preferred_element_type=f32)


def to_lanes(column):
    rows = column.shape[0]
    pick = jnp.where(lax.broadcasted_iota(i32, (8, BLOCK), 1) == 0, 1.0, 0.0).astype(bf16)
    return dot_lanes(pick, jnp.broadcast_to(column, (rows, BLOCK)).astype(bf16))[0:1]


def to_column(lanes):
    k = lanes.shape[1]
    eye = lax.broadcasted_iota(i32, (k, k), 0) == lax.broadcasted_iota(i32, (k, k), 1)
    return jnp.sum(jnp.where(eye, lanes, 0.0), axis=1, keepdims=True)


def exponent_of(top):
    return jnp.clip(jnp.ceil(jnp.log2(jnp.maximum(top * 1.001, FLOOR))), -100.0, 100.0)


def head_rows(count, w):
    return -(-count // (16 * w)) * 16


def part(ref, s, w):
    return ref.at[s] if len(ref.shape) == 3 else ref.at[:, pl.ds(pl.multiple_of(s * w, w), w)]


def chunk(index, size):
    return pl.ds(pl.multiple_of(index * size, size), size)


def pack_kernel(points_ref, out_ref):
    n, _, w = out_ref.shape
    for s in range(n):
        out_ref[s] = points_ref[:, s * w : (s + 1) * w]


def prev_kernel(w, me_ref, prev_ref, small_ref, *refs):
    outs, head = refs[:-1], refs[-1]
    n = len(outs)
    owned = outs[0].shape[0] - head.shape[0]
    me = me_ref[0]
    top = jnp.zeros((owned, 1), f32)
    for s in range(n):
        top = jnp.maximum(top, jnp.max(jnp.abs(part(prev_ref, s, w)[...]), axis=1, keepdims=True))
    exponent = exponent_of(top)
    factor = CODE * jnp.exp2(-exponent)
    head[...] = jnp.zeros_like(head)
    known = small_ref.shape[0]
    head[0:known, :] = small_ref[...]
    for j in range(owned // w):
        lanes = to_lanes(exponent[j * w : (j + 1) * w])
        head[known + j : known + j + 1, :] = lanes.astype(i32)
    for m in range(n):
        outs[m][0:owned, :] = jnp.round(part(prev_ref, me ^ m, w)[...] * factor).astype(i16)
        outs[m][owned:, :] = head[...].astype(i16)


def prepare_kernel(blocks, me_ref, *refs):
    arrived, (member_ref, block_ref, inverse_ref, prev_ref, upper_ref, count) = refs[:-6], refs[-6:]
    n = len(arrived)
    rows, w = prev_ref.shape
    owned = rows // n
    upper_rows = upper_ref.shape[-2]
    me = me_ref[0]
    lines = blocks * BLOCK // w
    count[...] = jnp.zeros_like(count)
    centroid = lax.broadcasted_iota(i32, (BLOCK, BLOCK), 0)
    ones = jnp.ones((BLOCK, BLOCK), bf16)
    parent_at = lax.broadcasted_iota(i32, (upper_rows, w), 0)
    for m in range(n):
        s = me ^ m
        head = arrived[m][owned:, :].astype(i32)
        for i in range(blocks):
            row = [head[(i * BLOCK + k) // w : (i * BLOCK + k) // w + 1, :] for k in range(0, BLOCK, w)]
            ids = jnp.concatenate(row, axis=1) if len(row) > 1 else row[0]
            number = jnp.max(ids.astype(f32)).astype(i32) // BLOCK
            block_ref[s * blocks + i] = number
            member = jnp.where(centroid == ids - number * BLOCK, 1.0, 0.0).astype(bf16)
            member_ref[chunk(s * blocks + i, BLOCK), :] = member
            count[chunk(number, BLOCK), :] += dot(member, ones)
        for j in range(owned // w):
            parents = head[lines + j : lines + j + 1, :]
            one_hot = jnp.where(parent_at == parents, 1.0, 0.0).astype(bf16)
            if len(upper_ref.shape) == 2:
                upper_ref[:, chunk(s * (owned // w) + j, w)] = one_hot
            else:
                upper_ref[s * (owned // w) + j] = one_hot
            scale = head[lines + owned // w + j : lines + owned // w + j + 1, :].astype(f32)
            values = arrived[m][j * w : (j + 1) * w, :].astype(f32)
            prev_ref[chunk(s * (owned // w) + j, w), :] = values * (jnp.exp2(to_column(scale)) / CODE)
    inverse_ref[...] = 1.0 / jnp.maximum(count[...][:, :w], 1.0)


def sums_kernel(block_ref, points_ref, member_ref, inverse_ref, prev_ref, x_ref, stat_ref, code_ref, acc):
    s = pl.program_id(0)
    rows, w = acc.shape
    n, owned, _ = code_ref.shape
    blocks = points_ref.shape[1] // BLOCK

    @pl.when(s == 0)
    def _():
        acc[...] = jnp.zeros_like(acc)

    for i in range(blocks):
        at = slice(i * BLOCK, (i + 1) * BLOCK)
        acc[chunk(block_ref[s * blocks + i], BLOCK), :] += dot(member_ref[at, :], points_ref[0, at, :])

    @pl.when(s == pl.num_programs(0) - 1)
    def _():
        unit = jnp.ones((8, w), bf16)
        for o in range(n):
            at = slice(o * owned, (o + 1) * owned)
            x = acc[at, :] * inverse_ref[at, :] + prev_ref[at, :]
            x_ref[at, :] = x
            square_high, square_low = split(x * x)
            squares = (dot_lanes(unit, square_high) + dot_lanes(unit, square_low))[0:1]
            top = jnp.max(jnp.abs(x), axis=1, keepdims=True) * 1.01
            scale = jnp.maximum(top, FLOOR).astype(bf16).astype(f32)
            scales = to_lanes(scale)
            for d in range(n):
                stat_ref[d, 0:1, at] = squares
                stat_ref[d, 1:2, at] = scales
            code_ref[o] = jnp.round(x * (CODE / scale)).astype(i16)


def upper_kernel(width, stat_ref, member_ref, x_ref, code_ref, high, low, sums, head):
    n = stat_ref.shape[0]
    rows, w = sums.shape
    squares = stat_ref[0, 0:1, :]
    for s in range(1, n):
        squares += stat_ref[s, 0:1, :]
    factor = lax.rsqrt(squares / width + EPSILON)
    for j in range(x_ref.shape[0] // BLOCK):
        at = slice(j * BLOCK, (j + 1) * BLOCK)
        high[at, :], low[at, :] = split(x_ref[at, :] * to_column(factor[:, at]))
    member = member_ref[...]
    sums[...] = dot(member, high[...]) + dot(member, low[...])
    head[...] = jnp.zeros_like(head)
    for j in range(rows // w):
        at = slice(j * w, (j + 1) * w)
        total = sums[at, :]
        exponent = exponent_of(jnp.max(jnp.abs(total), axis=1, keepdims=True))
        code_ref[at, :] = jnp.round(total * (CODE * jnp.exp2(-exponent))).astype(i16)
        head[j : j + 1, :] = to_lanes(exponent).astype(i32)
    code_ref[rows:, :] = head[...].astype(i16)


def join_kernel(w, me_ref, *refs):
    parts, out_ref, values = refs[:-2], refs[-2], refs[-1]
    n = len(parts)
    rows = values.shape[1]
    me = me_ref[0]
    for j in range(rows // w):
        at = slice(j * w, (j + 1) * w)
        squares = jnp.zeros((w, 1), f32)
        for m in range(n):
            head = parts[m][rows : rows + 16, :].astype(i32).astype(f32)
            scale = jnp.exp2(to_column(head[j : j + 1, :])) / CODE
            value = parts[m][at, :].astype(f32) * scale
            values[m, at, :] = value
            squares += jnp.sum(value * value, axis=1, keepdims=True)
        factor = lax.rsqrt(squares / (n * w) + EPSILON)
        for m in range(n):
            part(out_ref, me ^ m, w)[at, :] = values[m, at, :] * factor


def decode_kernel(me_ref, code_ref, stat_ref, out_ref):
    n, rows, w = code_ref.shape
    me = me_ref[0]
    for j in range(rows // BLOCK):
        at = slice(j * BLOCK, (j + 1) * BLOCK)
        squares = jnp.zeros((BLOCK, 1), f32)
        for s in range(n):
            lanes = stat_ref[s, 1:2, chunk(me * (rows // BLOCK) + j, BLOCK)]
            value = code_ref[s, at, :].astype(f32) * (to_column(lanes) / CODE)
            out_ref[at, s * w : (s + 1) * w] = value
            squares += jnp.sum(value * value, axis=1, keepdims=True)
        out_ref[at, :] *= lax.rsqrt(squares / (n * w) + EPSILON)


def call(kernel, out_shape, **kw):
    params = pltpu.CompilerParams(vmem_limit_bytes=VMEM_LIMIT)
    return pl.pallas_call(kernel, out_shape=out_shape, compiler_params=params, **kw)


def columns(values, n):
    rows, width = values.shape
    return values.reshape(rows, n, width // n).transpose(1, 0, 2)


def shards(points, point_cluster, cand_blocks, cent1_prev, parent, cent2_prev):
    point_rows, width = points.shape
    block_count = point_rows // BLOCK
    owned = cent1_prev.shape[0]
    upper_rows = cent2_prev.shape[0]
    n = lax.axis_size("cent")
    dp = lax.axis_index("dp")
    me = lax.axis_index("cent").astype(i32).reshape(1)
    w = width // n
    rows = n * owned
    wide = w % BLOCK == 0

    def swap(value, mask):
        return lax.ppermute(value, "cent", [(i, i ^ mask) for i in range(n)])

    def exchange(values):
        return lax.all_to_all(values, "cent", split_axis=0, concat_axis=0, tiled=True)

    table_rows = lax.all_gather(cent2_prev, "dp", axis=0, tiled=True)
    tile = 2 * BLOCK
    if wide:
        packed = call(
            pack_kernel,
            shape((n, point_rows, w), bf16),
            grid=(point_rows // tile,),
            in_specs=[pl.BlockSpec((tile, width), lambda i: (i, 0))],
            out_specs=pl.BlockSpec((n, tile, w), lambda i: (0, i, 0)),
            name="pack",
        )(points)
    else:
        packed = columns(points, n)
    packed, point_cluster, parent = lax.optimization_barrier((packed, point_cluster, parent))
    arrived = exchange(packed)

    small = jnp.concatenate([point_cluster - dp * rows, parent - dp * upper_rows]).reshape(-1, w)
    head = head_rows(point_rows + 2 * owned, w)
    prev_codes = call(
        functools.partial(prev_kernel, w),
        [shape((owned + head, w), i16)] * n,
        in_specs=[SMEM, VMEM, VMEM],
        out_specs=[VMEM] * n,
        scratch_shapes=[pltpu.VMEM((head, w), i32)],
        name="prev",
    )(me, cent1_prev if wide else columns(cent1_prev, n), small)
    prevs = {m: swap(prev_codes[m], m) for m in range(n - 1, 0, -1)}
    prevs = [prev_codes[0]] + [prevs[m] for m in range(1, n)]
    upper_shape = (upper_rows, rows) if wide else (rows // w, upper_rows, w)
    member, numbers, inverse, prev, upper_member = call(
        functools.partial(prepare_kernel, block_count),
        [
            shape((n * point_rows, BLOCK), bf16),
            shape((n * block_count,), i32),
            shape((rows, w), f32),
            shape((rows, w), f32),
            shape(upper_shape, bf16),
        ],
        in_specs=[SMEM] + [VMEM] * n,
        out_specs=[VMEM, SMEM, VMEM, VMEM, VMEM],
        scratch_shapes=[pltpu.VMEM((rows, BLOCK), f32)],
        name="prepare",
    )(me, *prevs)

    points, table_rows = lax.optimization_barrier((points, table_rows))
    unit_points = rms_norm(points.astype(f32)).astype(bf16)
    table_units = rms_norm(table_rows.astype(f32)).astype(bf16)
    products = lax.dot_general(
        unit_points, table_units, (((1,), (1,)), ((), ())), preferred_element_type=f32
    )
    column_block = jnp.arange(table_rows.shape[0]) // BLOCK
    listed = jnp.any(cand_blocks[:, :, None] == column_block[None, None, :], axis=1)
    weights = jnp.exp(products * (SHARPNESS / width)).reshape(block_count, BLOCK, -1)
    running = jnp.sum(weights * listed[:, None, :].astype(f32), axis=2).reshape(point_rows)
    point_score, numbers = lax.optimization_barrier((jnp.log(running), numbers))

    whole = lambda *dims: pl.BlockSpec(dims, lambda s, *_: (0,) * len(dims))
    x, stat, code = call(
        sums_kernel,
        [shape((rows, w), f32), shape((n, 2, rows), f32), shape((n, owned, w), i16)],
        grid_spec=pltpu.PrefetchScalarGridSpec(
            num_scalar_prefetch=1,
            grid=(n,),
            in_specs=[
                pl.BlockSpec((1, point_rows, w), lambda s, _: (s, 0, 0)),
                pl.BlockSpec((point_rows, BLOCK), lambda s, _: (s, 0)),
                whole(rows, w),
                whole(rows, w),
            ],
            out_specs=[whole(rows, w), whole(n, 2, rows), whole(n, owned, w)],
            scratch_shapes=[pltpu.VMEM((rows, w), f32)],
        ),
        name="sums",
    )(numbers, arrived, member, inverse, prev)
    stats = exchange(stat)
    back = exchange(code)

    upper_head = head_rows(upper_rows, w)
    code = call(
        functools.partial(upper_kernel, width),
        shape((upper_rows + upper_head, w), i16),
        in_specs=[VMEM] * 3,
        out_specs=VMEM,
        scratch_shapes=[
            pltpu.VMEM((rows, w), bf16),
            pltpu.VMEM((rows, w), bf16),
            pltpu.VMEM((upper_rows, w), f32),
            pltpu.VMEM((upper_head, w), i32),
        ],
        name="upper",
    )(stats, upper_member if wide else upper_member.transpose(1, 0, 2).reshape(upper_rows, rows), x)
    half = n // 2
    parts = {0: code, half: swap(code, half)}
    for m in range(half - 1, 0, -1):
        parts[m] = swap(code, m)
    for m in range(half - 1, 0, -1):
        parts[half + m] = swap(parts[half], m)

    cent1_new = call(
        decode_kernel,
        shape((owned, width), f32),
        in_specs=[SMEM, VMEM, VMEM],
        out_specs=VMEM,
        name="decode",
    )(me, back, stats)

    cent2_new = call(
        functools.partial(join_kernel, w),
        shape((upper_rows, width) if wide else (n, upper_rows, w), f32),
        in_specs=[SMEM] + [VMEM] * n,
        out_specs=VMEM,
        scratch_shapes=[pltpu.VMEM((n, upper_rows, w), f32)],
        name="join",
    )(me, *[parts[m] for m in range(n)])
    if not wide:
        cent2_new = cent2_new.transpose(1, 0, 2).reshape(upper_rows, width)
    return (cent1_new, cent2_new, point_score)


def solution(mesh):
    placed = (
        P(("dp", "cent"), None),
        P(("dp", "cent")),
        P(("dp", "cent"), None),
        P(("dp", "cent"), None),
        P(("dp", "cent")),
        P("dp", None),
    )
    return jax.shard_map(
        shards,
        mesh=mesh,
        in_specs=placed,
        out_specs=(P(("dp", "cent"), None), P("dp", None), P(("dp", "cent"))),
        check_vma=False,
    )
```

time: 187 us -> 162 us (0.87)
  local copies, waits for them, and re-layouts: 45.7 us -> 11.7 us
  waiting for transfers between devices: 29.1 us -> 57.5 us
  starting transfers between devices: 60.9 us -> 35 us
  blocking collectives: 0 us -> 11.7 us
  other arithmetic: 8.7 us -> 5.79 us
    ppermute x35 -> x14, starting transfers between devices: 60.9 us -> 24 us  [swap(): return lax.ppermute(value, 'cent', [(i, i ^ mask) for i in range(n)])]
    ppermute x35 -> x14, waiting for transfers between devices: 28.4 us -> 56.8 us  [swap(): return lax.ppermute(value, 'cent', [(i, i ^ mask) for i in range(n)])]
    gather x32 -> x0, local copies, waits for them, and re-layouts: 21.6 us -> none
    unnamed x91 -> x30, local copies, waits for them, and re-layouts: 23.3 us -> 11.1 us
    all_to_all x0 -> x1, blocking collectives: none -> 11.7 us  [exchange(): lax.all_to_all(values, 'cent', split_axis=0, concat_axis=0, tiled=True)]
    all_to_all x0 -> x2, starting transfers between devices: none -> 11 us  [exchange(): lax.all_to_all(values, 'cent', split_axis=0, concat_axis=0, tiled=True)]
    pallas_call x5 -> x6, Pallas kernels: 20.5 us -> 19.5 us  [the longest x1 6.44 us: shards(): call(sums_kernel, [shape((rows, w), f32), shape((n, 2, rows), f32), shape...]
  transfers between devices with their start and end apart: 36 -> 17, of which waited for: 6 -> 8; matrix products, arithmetic and copies ran while one was open for 16% -> 7% of each run, Pallas kernels for 11% -> 7%
where the time goes in v3:
time: 162 us; the launch traced here: 161 us
  waiting for transfers between devices  57.5 us (35%)
  starting transfers between devices  35 us (22%)
  Pallas kernels  20 us (12%)
  between operations  14.2 us (9%)
  local copies, waits for them, and re-layouts  11.7 us (7%)
  blocking collectives  11.7 us (7%)
  other arithmetic  5.79 us (4%)
  matrix products  5.39 us (3%)
    ppermute x14, waiting for transfers between devices, swap(): return lax.ppermute(value, 'cent', [(i, i ^ mask) for i in range(n)])  56.8 us
    ppermute x14, starting transfers between devices, swap(): return lax.ppermute(value, 'cent', [(i, i ^ mask) for i in range(n)])  24 us
    all_to_all x1, blocking collectives, exchange(): lax.all_to_all(values, 'cent', split_axis=0, concat_axis=0, tiled=True)  11.7 us
    unnamed x30, local copies, waits for them, and re-layouts  11.1 us
    all_to_all x2, starting transfers between devices, exchange(): lax.all_to_all(values, 'cent', split_axis=0, concat_axis=0, tiled=True)  11 us
    pallas_call x1, Pallas kernels, shards(): call(sums_kernel, [shape((rows, w), f32), shape((n, 2, rows), f32), shape...  6.44 us
    reduce_sum x2, other arithmetic, rms_norm(): jnp.mean(values * values, axis=-1, keepdims=True) + EPSILON  5.52 us
    dot_general x1, matrix products, shards(): lax.dot_general(unit_points, table_units, (((1,), (1,)), ((), ())), prefe...  5.39 us
  transfers between devices with their start and end apart: 17, of which 8 were waited for; matrix products, arithmetic and copies ran while one was open for 7% of the time, Pallas kernels for 7%

profile of v3, /device:TPU:0, one launch (start us, length us, event | category | flops | bytes accessed | tf_op | source)
XLA Modules:
  0.0 161.3 jit_solution(17504800853763195437)
XLA Ops:
  7.2 0.0 all-gather.2.cloned.1.call-start
  7.2 0.7 all-gather.2.cloned.1.call-update
  7.9 0.0 copy-start
  7.9 1.6 copy-done
  9.5 0.6 pack.1
  10.1 1.3 copy-done.2
  11.4 7.3 %all-to-all-start = ((bf16[8,1024,128]{2,1,0:T(8,128)(2,1)}), bf16[8,1024,128]{2,1,0:T(8,128)(2,1)S(1)}, u32[]{:S(2)}, u32[]{:S(2)}) async-start(bf16[8,1024,128]{2,1,0:T(8,128)(2,1)} %copy-done.2), calls=%async_computation | async-start | bytes 4194304 | tf_op jit(solution)/shard_map/all_to_all | solution.py:243
  18.8 0.5 prev.1
  19.3 2.0 %collective-permute-start = (s16[272,128]{1,0:T(8,128)(2,1)S(1)}, s16[272,128]{1,0:T(8,128)(2,1)S(1)}, u32[]{:S(2)}, u32[]{:S(2)}) collective-permute-start(s16[272,128]{1,0:T(8,128)(2,1)S(1)} %get-tuple-element.31), channel_id=1, source_target_pairs={{0,1},{1,0},{2,3},{3,2},{4,5},{5,4},{6,7},{7,6},{8,9},{9,8},{10,11... | collective-permute-start | bytes 208904 | tf_op jit(solution)/shard_map/ppermute | solution.py:240
  21.3 1.5 collective-permute-start.1
  22.8 0.1 collective-permute-start.2
  22.9 2.8 %collective-permute-start.3 = (s16[272,128]{1,0:T(8,128)(2,1)S(1)}, s16[272,128]{1,0:T(8,128)(2,1)S(1)}, u32[]{:S(2)}, u32[]{:S(2)}) collective-permute-start(s16[272,128]{1,0:T(8,128)(2,1)S(1)} %get-tuple-element.34), channel_id=1, source_target_pairs={{0,4},{1,5},{2,6},{3,7},{4,0},{5,1},{6,2},{7,3},{8,12},{9,13},{10,... | collective-permute-start | bytes 208904 | tf_op jit(solution)/shard_map/ppermute | solution.py:240
  25.7 1.5 collective-permute-start.4
  27.2 10.6 %collective-permute-done.refs_1_ = s16[272,128]{1,0:T(8,128)(2,1)S(1)} collective-permute-done((s16[272,128]{1,0:T(8,128)(2,1)S(1)}, s16[272,128]{1,0:T(8,128)(2,1)S(1)}, u32[]{:S(2)}, u32[]{:S(2)}) %collective-permute-start) | collective-permute-done | bytes 69664 | tf_op jit(solution)/shard_map/ppermute | solution.py:240
  37.8 2.7 %collective-permute-start.5 = (s16[272,128]{1,0:T(8,128)(2,1)S(1)}, s16[272,128]{1,0:T(8,128)(2,1)S(1)}, u32[]{:S(2)}, u32[]{:S(2)}) collective-permute-start(s16[272,128]{1,0:T(8,128)(2,1)S(1)} %get-tuple-element.36), channel_id=1, source_target_pairs={{0,6},{1,7},{2,4},{3,5},{4,2},{5,3},{6,0},{7,1},{8,14},{9,15},{10,... | collective-permute-start | bytes 208904 | tf_op jit(solution)/shard_map/ppermute | solution.py:240
  40.5 15.8 %collective-permute-done.1.refs_2_ = s16[272,128]{1,0:T(8,128)(2,1)S(1)} collective-permute-done((s16[272,128]{1,0:T(8,128)(2,1)S(1)}, s16[272,128]{1,0:T(8,128)(2,1)S(1)}, u32[]{:S(2)}, u32[]{:S(2)}) %collective-permute-start.1) | collective-permute-done | bytes 69664 | tf_op jit(solution)/shard_map/ppermute | solution.py:240
  56.3 3.7 %collective-permute-start.6 = (s16[272,128]{1,0:T(8,128)(2,1)S(1)}, s16[272,128]{1,0:T(8,128)(2,1)S(1)}, u32[]{:S(2)}, u32[]{:S(2)}) collective-permute-start(s16[272,128]{1,0:T(8,128)(2,1)S(1)} %get-tuple-element.37), channel_id=1, source_target_pairs={{0,7},{1,6},{2,5},{3,4},{4,3},{5,2},{6,1},{7,0},{8,15},{9,14},{10,... | collective-permute-start | bytes 208904 | tf_op jit(solution)/shard_map/ppermute | solution.py:240
  60.1 0.2 compare_reduce_fusion
  60.3 15.5 %collective-permute-done.3.refs_4_ = s16[272,128]{1,0:T(8,128)(2,1)S(1)} collective-permute-done((s16[272,128]{1,0:T(8,128)(2,1)S(1)}, s16[272,128]{1,0:T(8,128)(2,1)S(1)}, u32[]{:S(2)}, u32[]{:S(2)}) %collective-permute-start.3) | collective-permute-done | bytes 69664 | tf_op jit(solution)/shard_map/ppermute | solution.py:240
  75.8 2.0 %collective-permute-done.4.refs_5_ = s16[272,128]{1,0:T(8,128)(2,1)S(1)} collective-permute-done((s16[272,128]{1,0:T(8,128)(2,1)S(1)}, s16[272,128]{1,0:T(8,128)(2,1)S(1)}, u32[]{:S(2)}, u32[]{:S(2)}) %collective-permute-start.4) | collective-permute-done | bytes 69664 | tf_op jit(solution)/shard_map/ppermute | solution.py:240
  77.9 3.9 %prepare.1 = (bf16[8192,128]{1,0:T(8,128)(2,1)S(1)}, s32[64]{0:T(128)S(1)}, f32[2048,128]{1,0:T(8,128)S(1)}, f32[2048,128]{1,0:T(8,128)S(1)}, bf16[512,2048]{1,0:T(8,128)(2,1)}) custom-call(s32[1]{0:T(128)} %bitcast.me_ref, s16[272,128]{1,0:T(8,128)(2,1)S(1)} %get-tuple-element.30.refs_0_, s16[272,128]{1,0:T(8,128)(2,1)S(1)} %collective-permute-done.refs_1_, ...), custom_call_target="tpu_custom_call" | custom-call | tf_op jit(solution)/shard_map/prepare/pallas_call | solution.py:274
  81.8 1.4 copy-done.3
  83.2 1.0 copy-done.5
  84.1 2.2 %fusion.3 = f32[1024]{0:T(1024)S(1)} fusion(bf16[1024,1024]{1,0:T(8,128)(2,1)} %points_ref.1), kind=kLoop, calls=%fused_computation.8 | loop fusion | flops 3144704 | bytes 2101248 | tf_op jit(solution)/shard_map/reduce_sum | solution.py:23
  86.4 3.3 %fusion = f32[2048]{0:T(1024)S(1)} fusion(bf16[2048,1024]{1,0:T(8,128)(2,1)} %all-gather.2.cloned.1.call-done), kind=kLoop, calls=%fused_computation.2 | loop fusion | flops 6289408 | bytes 4202496 | tf_op jit(solution)/shard_map/reduce_sum | solution.py:23
  89.7 5.4 %fusion.2 = f32[1024]{0:T(1024)S(1)} fusion(bf16[2048,1024]{1,0:T(8,128)(2,1)S(1)} %copy-done.11, f32[8,2048]{1,0:T(8,128)S(1)} %convert_element_type.24, f32[2048]{0:T(1024)S(1)} %add_rsqrt_fusion, bf16[1024,1024]{1,0:T(8,128)(2,1)S(1)} %copy-done.1, f32[1024]{0:T(1024)S(1)} %add_rsqrt_fusion.1), kind=kOutput, calls=%fused_computation.5 | convolution fusion | flops 4310694912 | bytes 6373376 | tf_op jit(solution)/shard_map/dot_general | solution.py:292
  95.1 0.6 log.3
  95.7 1.2 copy-done.6
  96.9 6.4 %sums.1 = (f32[2048,128]{1,0:T(8,128)S(1)}, f32[8,2,2048]{2,1,0:T(2,128)S(1)}, s16[8,256,128]{2,1,0:T(8,128)(2,1)S(1)}) custom-call(s32[64]{0:T(128)S(1)} %get-tuple-element.39.block_ref, bf16[8,1024,128]{2,1,0:T(8,128)(2,1)S(1)} %all-to-all-done.points_ref, bf16[8192,128]{1,0:T(8,128)(2,1)} %copy-done.3, f32[2048,128]{1,0:T(8,128)S(1)} %get-tuple-element.42.inverse_ref, ...), custom_call_target="tpu_custom_call" | custom-call | tf_op jit(solution)/shard_map/sums/pallas_call | solution.py:302
  103.4 1.0 copy-done.8
  104.4 0.8 copy-done.10
  105.2 11.7 %all_to_all.15.stat_ref = f32[8,2,2048]{2,1,0:T(2,128)S(1)} all-to-all(f32[8,2,2048]{2,1,0:T(2,128)S(1)} %get-tuple-element.45), channel_id=1, replica_groups=mesh['dp'=4,'cent'=8] {'cent'}, dimensions={0} | all-to-all | bytes 262144 | tf_op jit(solution)/shard_map/all_to_all | solution.py:243
  116.9 3.7 %all-to-all-start.1 = ((s16[8,256,128]{2,1,0:T(8,128)(2,1)}), s16[8,256,128]{2,1,0:T(8,128)(2,1)S(1)}, u32[]{:S(2)}, u32[]{:S(2)}) async-start(s16[8,256,128]{2,1,0:T(8,128)(2,1)} %copy-done.10), calls=%async_computation.1 | async-start | bytes 1048576 | tf_op jit(solution)/shard_map/all_to_all | solution.py:243
  120.6 1.6 copy-done.4
  122.2 1.2 copy-done.9
  123.4 1.7 %upper.1.refs_0_ = s16[528,128]{1,0:T(8,128)(2,1)S(1)} custom-call(f32[8,2,2048]{2,1,0:T(2,128)S(1)} %all_to_all.15.stat_ref, bf16[512,2048]{1,0:T(8,128)(2,1)S(1)} %copy-done.4, f32[2048,128]{1,0:T(8,128)S(1)} %copy-done.9), custom_call_target="tpu_custom_call" | custom-call | tf_op jit(solution)/shard_map/upper/pallas_call | solution.py:323
  125.1 2.7 %collective-permute-start.10 = (s16[528,128]{1,0:T(8,128)(2,1)S(1)}, s16[528,128]{1,0:T(8,128)(2,1)S(1)}, u32[]{:S(2)}, u32[]{:S(2)}) collective-permute-start(s16[528,128]{1,0:T(8,128)(2,1)S(1)} %upper.1.refs_0_), channel_id=1, source_target_pairs={{0,4},{1,5},{2,6},{3,7},{4,0},{5,1},{6,2},{7,3},{8,12},{9,13},{10,... | collective-permute-start | bytes 405512 | tf_op jit(solution)/shard_map/ppermute | solution.py:240
  127.8 2.4 %collective-permute-start.9 = (s16[528,128]{1,0:T(8,128)(2,1)S(1)}, s16[528,128]{1,0:T(8,128)(2,1)S(1)}, u32[]{:S(2)}, u32[]{:S(2)}) collective-permute-start(s16[528,128]{1,0:T(8,128)(2,1)S(1)} %upper.1.refs_0_), channel_id=1, source_target_pairs={{0,3},{1,2},{2,1},{3,0},{4,7},{5,6},{6,5},{7,4},{8,11},{9,10},{10,... | collective-permute-start | bytes 405512 | tf_op jit(solution)/shard_map/ppermute | solution.py:240
  130.2 0.5 collective-permute-start.8
  130.7 0.6 collective-permute-start.7
  131.3 8.5 %collective-permute-done.10.refs_4_ = s16[528,128]{1,0:T(8,128)(2,1)S(1)} collective-permute-done((s16[528,128]{1,0:T(8,128)(2,1)S(1)}, s16[528,128]{1,0:T(8,128)(2,1)S(1)}, u32[]{:S(2)}, u32[]{:S(2)}) %collective-permute-start.10) | collective-permute-done | bytes 135200 | tf_op jit(solution)/shard_map/ppermute | solution.py:240
  139.7 2.9 %collective-permute-start.12 = (s16[528,128]{1,0:T(8,128)(2,1)S(1)}, s16[528,128]{1,0:T(8,128)(2,1)S(1)}, u32[]{:S(2)}, u32[]{:S(2)}) collective-permute-start(s16[528,128]{1,0:T(8,128)(2,1)S(1)} %collective-permute-done.10.refs_4_), channel_id=1, source_target_pairs={{0,2},{1,3},{2,0},{3,1},{4,6},{5,7},{6,4},{7,5},{8,10},{9,11},{10,... | collective-permute-start | bytes 405512 | tf_op jit(solution)/shard_map/ppermute | solution.py:240
  142.6 0.6 collective-permute-start.11
  143.2 2.6 %collective-permute-done.13.refs_7_ = s16[528,128]{1,0:T(8,128)(2,1)S(1)} collective-permute-done((s16[528,128]{1,0:T(8,128)(2,1)S(1)}, s16[528,128]{1,0:T(8,128)(2,1)S(1)}, u32[]{:S(2)}, u32[]{:S(2)}) %collective-permute-start.13) | collective-permute-done | bytes 135200 | tf_op jit(solution)/shard_map/ppermute | solution.py:240
  145.9 1.4 collective-permute-done.12.refs_6_
  147.3 0.3 collective-permute-done.11.refs_5_
  147.6 4.6 %join.1 = f32[512,1024]{1,0:T(8,128)} custom-call(s32[1]{0:T(128)} %bitcast.me_ref, s16[528,128]{1,0:T(8,128)(2,1)S(1)} %upper.1.refs_0_, s16[528,128]{1,0:T(8,128)(2,1)S(1)} %collective-permute-done.7.refs_1_, s16[528,128]{1,0:T(8,128)(2,1)S(1)} %collective-permute-done.8.refs_2_, s16[528,128]{1,0:T(8,128)(2,1)S(1)} %collective-permute-done.9.refs_3_, ...), custom_call_target="tpu_custom_call" | custom-call | tf_op jit(solution)/shard_map/join/pallas_call | solution.py:351
  152.2 2.3 %decode.1 = f32[256,1024]{1,0:T(8,128)} custom-call(s32[1]{0:T(128)} %bitcast.me_ref, s16[8,256,128]{2,1,0:T(8,128)(2,1)S(1)} %all-to-all-done.1.code_ref, f32[8,2,2048]{2,1,0:T(2,128)S(1)} %all_to_all.15.stat_ref), custom_call_target="tpu_custom_call" | custom-call | tf_op jit(solution)/shard_map/decode/pallas_call | solution.py:343
  (37 shorter events, 0.1 us)
Async XLA Ops:
  7.2 77.0 %all-gather.2.cloned.1.call-start = ((), (), s32[]{:S(2)}) async-start(), calls=%async_computation.3 | async-start | bytes 5242880 | tf_op jit(solution)/shard_map/all_gather | solution.py:245
  7.9 1.6 copy-start
  9.5 9.2 %copy-start.14 = (s32[256]{0:T(256)S(1)}, s32[256]{0:T(256)}, u32[]{:S(2)}) copy-start(s32[256]{0:T(256)} %param.10) | copy-start | bytes 3076
  9.5 9.2 %copy-start.13 = (s32[1024]{0:T(1024)S(1)}, s32[1024]{0:T(1024)}, u32[]{:S(2)}) copy-start(s32[1024]{0:T(1024)} %param.7) | copy-start | bytes 12292
  9.5 9.3 %copy-start.7 = (f32[256,1024]{1,0:T(8,128)S(1)}, f32[256,1024]{1,0:T(8,128)}, u32[]{:S(2)}) copy-start(f32[256,1024]{1,0:T(8,128)} %prev_ref.1) | copy-start | bytes 3145732
  9.5 50.6 %copy-start.12 = (s32[8,8]{1,0:T(8,128)S(1)}, s32[8,8]{1,0:T(8,128)}, u32[]{:S(2)}) copy-start(s32[8,8]{1,0:T(8,128)} %param.8) | copy-start | bytes 772
  10.1 1.4 copy-start.2
  11.4 84.3 %all-to-all-start = ((bf16[8,1024,128]{2,1,0:T(8,128)(2,1)}), bf16[8,1024,128]{2,1,0:T(8,128)(2,1)S(1)}, u32[]{:S(2)}, u32[]{:S(2)}) async-start(bf16[8,1024,128]{2,1,0:T(8,128)(2,1)} %copy-done.2), calls=%async_computation | async-start | bytes 4194304 | tf_op jit(solution)/shard_map/all_to_all | solution.py:243
  19.3 18.4 %collective-permute-start = (s16[272,128]{1,0:T(8,128)(2,1)S(1)}, s16[272,128]{1,0:T(8,128)(2,1)S(1)}, u32[]{:S(2)}, u32[]{:S(2)}) collective-permute-start(s16[272,128]{1,0:T(8,128)(2,1)S(1)} %get-tuple-element.31), channel_id=1, source_target_pairs={{0,1},{1,0},{2,3},{3,2},{4,5},{5,4},{6,7},{7,6},{8,9},{9,8},{10,11... | collective-permute-start | bytes 208904 | tf_op jit(solution)/shard_map/ppermute | solution.py:240
  21.3 35.0 %collective-permute-start.1 = (s16[272,128]{1,0:T(8,128)(2,1)S(1)}, s16[272,128]{1,0:T(8,128)(2,1)S(1)}, u32[]{:S(2)}, u32[]{:S(2)}) collective-permute-start(s16[272,128]{1,0:T(8,128)(2,1)S(1)} %get-tuple-element.32), channel_id=1, source_target_pairs={{0,2},{1,3},{2,0},{3,1},{4,6},{5,7},{6,4},{7,5},{8,10},{9,11},{10,... | collective-permute-start | bytes 208904 | tf_op jit(solution)/shard_map/ppermute | solution.py:240
  22.8 37.5 %collective-permute-start.2 = (s16[272,128]{1,0:T(8,128)(2,1)S(1)}, s16[272,128]{1,0:T(8,128)(2,1)S(1)}, u32[]{:S(2)}, u32[]{:S(2)}) collective-permute-start(s16[272,128]{1,0:T(8,128)(2,1)S(1)} %get-tuple-element.33), channel_id=1, source_target_pairs={{0,3},{1,2},{2,1},{3,0},{4,7},{5,6},{6,5},{7,4},{8,11},{9,10},{10,... | collective-permute-start | bytes 208904 | tf_op jit(solution)/shard_map/ppermute | solution.py:240
  22.9 53.0 %collective-permute-start.3 = (s16[272,128]{1,0:T(8,128)(2,1)S(1)}, s16[272,128]{1,0:T(8,128)(2,1)S(1)}, u32[]{:S(2)}, u32[]{:S(2)}) collective-permute-start(s16[272,128]{1,0:T(8,128)(2,1)S(1)} %get-tuple-element.34), channel_id=1, source_target_pairs={{0,4},{1,5},{2,6},{3,7},{4,0},{5,1},{6,2},{7,3},{8,12},{9,13},{10,... | collective-permute-start | bytes 208904 | tf_op jit(solution)/shard_map/ppermute | solution.py:240
  25.7 52.1 %collective-permute-start.4 = (s16[272,128]{1,0:T(8,128)(2,1)S(1)}, s16[272,128]{1,0:T(8,128)(2,1)S(1)}, u32[]{:S(2)}, u32[]{:S(2)}) collective-permute-start(s16[272,128]{1,0:T(8,128)(2,1)S(1)} %get-tuple-element.35), channel_id=1, source_target_pairs={{0,5},{1,4},{2,7},{3,6},{4,1},{5,0},{6,3},{7,2},{8,13},{9,12},{10,... | collective-permute-start | bytes 208904 | tf_op jit(solution)/shard_map/ppermute | solution.py:240
  37.8 40.1 %collective-permute-start.5 = (s16[272,128]{1,0:T(8,128)(2,1)S(1)}, s16[272,128]{1,0:T(8,128)(2,1)S(1)}, u32[]{:S(2)}, u32[]{:S(2)}) collective-permute-start(s16[272,128]{1,0:T(8,128)(2,1)S(1)} %get-tuple-element.36), channel_id=1, source_target_pairs={{0,6},{1,7},{2,4},{3,5},{4,2},{5,3},{6,0},{7,1},{8,14},{9,15},{10,... | collective-permute-start | bytes 208904 | tf_op jit(solution)/shard_map/ppermute | solution.py:240
  56.3 21.5 %collective-permute-start.6 = (s16[272,128]{1,0:T(8,128)(2,1)S(1)}, s16[272,128]{1,0:T(8,128)(2,1)S(1)}, u32[]{:S(2)}, u32[]{:S(2)}) collective-permute-start(s16[272,128]{1,0:T(8,128)(2,1)S(1)} %get-tuple-element.37), channel_id=1, source_target_pairs={{0,7},{1,6},{2,5},{3,4},{4,3},{5,2},{6,1},{7,0},{8,15},{9,14},{10,... | collective-permute-start | bytes 208904 | tf_op jit(solution)/shard_map/ppermute | solution.py:240
  81.8 1.4 copy-start.3
  83.2 1.0 copy-start.5
  84.1 5.6 %copy-start.1 = (bf16[1024,1024]{1,0:T(8,128)(2,1)S(1)}, bf16[1024,1024]{1,0:T(8,128)(2,1)}, u32[]{:S(2)}) copy-start(bf16[1024,1024]{1,0:T(8,128)(2,1)} %points_ref.1) | copy-start | bytes 6291460
  84.1 5.6 %copy-start.11 = (bf16[2048,1024]{1,0:T(8,128)(2,1)S(1)}, bf16[2048,1024]{1,0:T(8,128)(2,1)}, u32[]{:S(2)}) copy-start(bf16[2048,1024]{1,0:T(8,128)(2,1)} %all-gather.2.cloned.1.call-done) | copy-start | bytes 12582916
  95.7 1.2 copy-start.6
  103.4 1.0 copy-start.8
  104.4 0.8 copy-start.10
  116.9 35.3 %all-to-all-start.1 = ((s16[8,256,128]{2,1,0:T(8,128)(2,1)}), s16[8,256,128]{2,1,0:T(8,128)(2,1)S(1)}, u32[]{:S(2)}, u32[]{:S(2)}) async-start(s16[8,256,128]{2,1,0:T(8,128)(2,1)} %copy-done.10), calls=%async_computation.1 | async-start | bytes 1048576 | tf_op jit(solution)/shard_map/all_to_all | solution.py:243
  120.6 1.6 copy-start.4
  122.2 1.2 copy-start.9
  125.1 14.6 %collective-permute-start.10 = (s16[528,128]{1,0:T(8,128)(2,1)S(1)}, s16[528,128]{1,0:T(8,128)(2,1)S(1)}, u32[]{:S(2)}, u32[]{:S(2)}) collective-permute-start(s16[528,128]{1,0:T(8,128)(2,1)S(1)} %upper.1.refs_0_), channel_id=1, source_target_pairs={{0,4},{1,5},{2,6},{3,7},{4,0},{5,1},{6,2},{7,3},{8,12},{9,13},{10,... | collective-permute-start | bytes 405512 | tf_op jit(solution)/shard_map/ppermute | solution.py:240
  127.8 14.8 %collective-permute-start.9 = (s16[528,128]{1,0:T(8,128)(2,1)S(1)}, s16[528,128]{1,0:T(8,128)(2,1)S(1)}, u32[]{:S(2)}, u32[]{:S(2)}) collective-permute-start(s16[528,128]{1,0:T(8,128)(2,1)S(1)} %upper.1.refs_0_), channel_id=1, source_target_pairs={{0,3},{1,2},{2,1},{3,0},{4,7},{5,6},{6,5},{7,4},{8,11},{9,10},{10,... | collective-permute-start | bytes 405512 | tf_op jit(solution)/shard_map/ppermute | solution.py:240
  130.2 13.1 %collective-permute-start.8 = (s16[528,128]{1,0:T(8,128)(2,1)S(1)}, s16[528,128]{1,0:T(8,128)(2,1)S(1)}, u32[]{:S(2)}, u32[]{:S(2)}) collective-permute-start(s16[528,128]{1,0:T(8,128)(2,1)S(1)} %upper.1.refs_0_), channel_id=1, source_target_pairs={{0,2},{1,3},{2,0},{3,1},{4,6},{5,7},{6,4},{7,5},{8,10},{9,11},{10,... | collective-permute-start | bytes 405512 | tf_op jit(solution)/shard_map/ppermute | solution.py:240
  130.7 12.5 %collective-permute-start.7 = (s16[528,128]{1,0:T(8,128)(2,1)S(1)}, s16[528,128]{1,0:T(8,128)(2,1)S(1)}, u32[]{:S(2)}, u32[]{:S(2)}) collective-permute-start(s16[528,128]{1,0:T(8,128)(2,1)S(1)} %upper.1.refs_0_), channel_id=1, source_target_pairs={{0,1},{1,0},{2,3},{3,2},{4,5},{5,4},{6,7},{7,6},{8,9},{9,8},{10,11... | collective-permute-start | bytes 405512 | tf_op jit(solution)/shard_map/ppermute | solution.py:240
  139.7 6.1 %collective-permute-start.13 = (s16[528,128]{1,0:T(8,128)(2,1)S(1)}, s16[528,128]{1,0:T(8,128)(2,1)S(1)}, u32[]{:S(2)}, u32[]{:S(2)}) collective-permute-start(s16[528,128]{1,0:T(8,128)(2,1)S(1)} %collective-permute-done.10.refs_4_), channel_id=1, source_target_pairs={{0,3},{1,2},{2,1},{3,0},{4,7},{5,6},{6,5},{7,4},{8,11},{9,10},{10,... | collective-permute-start | bytes 405512 | tf_op jit(solution)/shard_map/ppermute | solution.py:240
  139.7 7.6 %collective-permute-start.12 = (s16[528,128]{1,0:T(8,128)(2,1)S(1)}, s16[528,128]{1,0:T(8,128)(2,1)S(1)}, u32[]{:S(2)}, u32[]{:S(2)}) collective-permute-start(s16[528,128]{1,0:T(8,128)(2,1)S(1)} %collective-permute-done.10.refs_4_), channel_id=1, source_target_pairs={{0,2},{1,3},{2,0},{3,1},{4,6},{5,7},{6,4},{7,5},{8,10},{9,11},{10,... | collective-permute-start | bytes 405512 | tf_op jit(solution)/shard_map/ppermute | solution.py:240
  142.6 5.0 %collective-permute-start.11 = (s16[528,128]{1,0:T(8,128)(2,1)S(1)}, s16[528,128]{1,0:T(8,128)(2,1)S(1)}, u32[]{:S(2)}, u32[]{:S(2)}) collective-permute-start(s16[528,128]{1,0:T(8,128)(2,1)S(1)} %collective-permute-done.10.refs_4_), channel_id=1, source_target_pairs={{0,1},{1,0},{2,3},{3,2},{4,5},{5,4},{6,7},{7,6},{8,9},{9,8},{10,11... | collective-permute-start | bytes 405512 | tf_op jit(solution)/shard_map/ppermute | solution.py:240
Sparse Core Ops, SparseCore 0:
  9.6 37.1 all-gather.1

commit v4 on v0

v4 whole, which is shorter than its diff:
```python
import functools

import jax
import jax.numpy as jnp
from jax import lax
from jax.experimental import pallas as pl
from jax.experimental.pallas import tpu as pltpu
from jax.sharding import PartitionSpec as P

BLOCK = 128
EPSILON = 1e-06
SHARPNESS = 20.0
CODE = 32000.0
FLOOR = 1e-30
VMEM_LIMIT = 48 * 1024 * 1024
f32, bf16, i16, i32 = jnp.float32, jnp.bfloat16, jnp.int16, jnp.int32
shape = jax.ShapeDtypeStruct
VMEM = pl.BlockSpec(memory_space=pltpu.VMEM)
SMEM = pl.BlockSpec(memory_space=pltpu.SMEM)
HBM = pl.BlockSpec(memory_space=pltpu.HBM)


def rms_norm(values):
    return values * lax.rsqrt(jnp.mean(values * values, axis=-1, keepdims=True) + EPSILON)


def split(values):
    high = values.astype(bf16)
    return high, (values - high.astype(f32)).astype(bf16)


def dot(a, b):
    return jnp.dot(a, b, preferred_element_type=f32)


def dot_lanes(a, b):
    return lax.dot_general(a, b, (((1,), (1,)), ((), ())), preferred_element_type=f32)


def to_lanes(column):
    rows = column.shape[0]
    pick = jnp.where(lax.broadcasted_iota(i32, (8, BLOCK), 1) == 0, 1.0, 0.0).astype(bf16)
    return dot_lanes(pick, jnp.broadcast_to(column, (rows, BLOCK)).astype(bf16))[0:1]


def to_column(lanes):
    k = lanes.shape[1]
    eye = lax.broadcasted_iota(i32, (k, k), 0) == lax.broadcasted_iota(i32, (k, k), 1)
    return jnp.sum(jnp.where(eye, lanes, 0.0), axis=1, keepdims=True)


def exponent_of(top):
    return jnp.clip(jnp.ceil(jnp.log2(jnp.maximum(top * 1.001, FLOOR))), -100.0, 100.0)


def encode(values, exponent):
    return jnp.round(values * (CODE * jnp.exp2(-exponent))).astype(i16)


def decode(codes, exponent):
    return codes.astype(f32) * (jnp.exp2(exponent) * (1.0 / CODE))


def head_rows(count, w):
    return -(-count // (16 * w)) * 16


def chunk(index, size):
    return pl.ds(pl.multiple_of(index * size, size), size)


def start(source, target, sem):
    copy = pltpu.make_async_copy(source, target, sem)
    copy.start()
    return copy


def start_all(sources, targets, sems):
    return [start(a, b, sems.at[k]) for k, (a, b) in enumerate(zip(sources, targets))]


def wait_all(copies):
    for copy in copies:
        copy.wait()


def pack_kernel(chunks, q_ref, points_ref, *refs):
    outs, sems = refs[:-1], refs[-1]
    sources = [
        points_ref.at[:, chunk((q_ref[0] ^ (k // chunks)) * chunks + k % chunks, BLOCK)] for k in range(len(outs))
    ]
    wait_all(start_all(sources, outs, sems))


def prev_kernel(q_ref, prev_ref, small_ref, *refs):
    h = (len(refs) - 4) // 2
    outs, (prev, head, sem, sems), held = refs[:h], refs[h : h + 4], refs[h + 4 :]
    owned, width = prev.shape
    w = width // h
    copy = start(prev_ref, prev, sem)
    known = small_ref.shape[0]
    head[...] = jnp.zeros_like(head)
    head[0:known, :] = small_ref[...]
    copy.wait()
    exponent = exponent_of(jnp.max(jnp.abs(prev[...]), axis=1, keepdims=True))
    for j in range(owned // w):
        lanes = to_lanes(exponent[j * w : (j + 1) * w])
        head[known + j : known + j + 1, :] = lanes.astype(i32)
    copies = []
    for m in range(h):
        held[m][0:owned, :] = encode(prev[:, chunk(q_ref[0] ^ m, w)], exponent)
        held[m][owned:, :] = head[...].astype(i16)
        copies.append(start(held[m], outs[m], sems.at[m]))
    wait_all(copies)


def prepare_kernel(blocks, n, me_ref, *refs):
    arrived, (member_ref, place_ref, near_ref, far_ref, prev_ref, upper_ref, count) = refs[:-7], refs[-7:]
    h = len(arrived)
    rows, w = prev_ref.shape
    owned = rows // h
    upper_rows = upper_ref.shape[0]
    me = me_ref[0]
    lines, each = blocks * BLOCK // w, owned // w
    count[...] = jnp.zeros_like(count)
    centroid = lax.broadcasted_iota(i32, (BLOCK, BLOCK), 0)
    ones = jnp.ones((BLOCK, BLOCK), bf16)
    parent_at = lax.broadcasted_iota(i32, (upper_rows, w), 0)
    for m in range(h):
        head = arrived[m][owned:, :].astype(i32)
        for i in range(blocks):
            row, lane = i * BLOCK // w, i * BLOCK % w
            ids = head[row : row + 1, lane : lane + BLOCK]
            number = jnp.max(ids.astype(f32)).astype(i32) // BLOCK
            place = number ^ (me * (owned // BLOCK))
            place_ref[m * blocks + i] = place
            member = jnp.where(centroid == ids - number * BLOCK, 1.0, 0.0).astype(bf16)
            at = (m * blocks + i) * BLOCK
            member_ref[at : at + BLOCK, :] = member
            count[chunk(place, BLOCK), :] += dot(member, ones)
        for j in range(each):
            at = slice(m * owned + j * w, m * owned + (j + 1) * w)
            parents = head[lines + j : lines + j + 1, :]
            upper_ref[:, at] = jnp.where(parent_at == parents, 1.0, 0.0).astype(bf16)
            exponent = to_column(head[lines + each + j : lines + each + j + 1, :].astype(f32))
            prev_ref[at, :] = decode(arrived[m][j * w : (j + 1) * w, :], exponent)
    near_ref[...] = count[0:rows, :]
    for j in range(rows // BLOCK):
        far = count[rows + j * BLOCK : rows + (j + 1) * BLOCK, 0:1]
        high = jnp.floor(far / 64.0)
        far_ref[j : j + 1, :] = (to_lanes(high) * 64.0 + to_lanes(far - high * 64.0)).astype(i32)


def sums_kernel(place_ref, member_ref, far_count_ref, *refs):
    h = (len(refs) - 5) // 2
    points, (acc_ref, code_ref), (code, head, sem), held = (
        refs[:h],
        refs[h : h + 2],
        refs[h + 2 : h + 5],
        refs[h + 5 :],
    )
    rows = acc_ref.shape[0] // 2
    blocks = held[0].shape[0] // BLOCK
    copies = start_all(points, held, sem)
    acc_ref[...] = jnp.zeros_like(acc_ref)
    for m in range(h):
        copies[m].wait()
        for i in range(blocks):
            at, here = (m * blocks + i) * BLOCK, slice(i * BLOCK, (i + 1) * BLOCK)
            acc_ref[chunk(place_ref[m * blocks + i], BLOCK), :] += dot(member_ref[at : at + BLOCK, :], held[m][here, :])
    copies = []
    lines = rows // BLOCK
    step = 2 * BLOCK
    for j in range(rows // step):
        at = slice(j * step, (j + 1) * step)
        value = acc_ref[rows + j * step : rows + (j + 1) * step, :]
        exponent = exponent_of(jnp.max(jnp.abs(value), axis=1, keepdims=True))
        code[at, :] = encode(value, exponent)
        lanes = to_lanes(exponent).astype(i32)
        for k in range(step // BLOCK):
            row = j * (step // BLOCK) + k
            head[row : row + 1, :] = lanes[:, k * BLOCK : (k + 1) * BLOCK]
    head[lines:, :] = far_count_ref[...]
    code[rows:, :] = head[...].astype(i16)
    start(code, code_ref, sem.at[h]).wait()


def refresh_kernel(chunks, h, near_ref, prev_ref, *refs):
    accs, crossed, (x_ref, stat_ref), outs = (
        refs[:chunks],
        refs[chunks : 2 * chunks],
        refs[2 * chunks : 2 * chunks + 2],
        refs[2 * chunks + 2 : 2 * chunks + 2 + h],
    )
    codes, stat, sem, held = refs[2 * chunks + 2 + h :][:h], *refs[2 * chunks + 2 + 2 * h :][:2], refs[2 * chunks + 4 + 2 * h :]
    rows, w = x_ref.shape
    owned = rows // h
    lines = rows // BLOCK
    wait_all(start_all(crossed, held, sem))
    heads = [held[c][rows:, :].astype(i32).astype(f32) for c in range(chunks)]
    unit = jnp.ones((8, BLOCK), bf16)
    copies = []
    for j in range(lines):
        at = slice(j * BLOCK, (j + 1) * BLOCK)
        count = near_ref[at, :] + to_column(heads[0][lines + j : lines + j + 1, :])
        inverse = 1.0 / jnp.maximum(count, 1.0)
        square, top = None, None
        for c in range(chunks):
            lanes = slice(c * BLOCK, (c + 1) * BLOCK)
            far = decode(held[c][at, :], to_column(heads[c][j : j + 1, :]))
            x = (accs[c][at, :] + far) * inverse + prev_ref[at, lanes]
            x_ref[at, lanes] = x
            square = x * x if c == 0 else square + x * x
            top = jnp.abs(x) if c == 0 else jnp.maximum(top, jnp.abs(x))
        square_high, square_low = split(square)
        stat[0:1, at] = (dot_lanes(unit, square_high) + dot_lanes(unit, square_low))[0:1]
        exponent = exponent_of(jnp.max(top, axis=1, keepdims=True))
        stat[1:2, at] = to_lanes(exponent)
        m, here = j * BLOCK // owned, slice(j * BLOCK % owned, j * BLOCK % owned + BLOCK)
        codes[m][here, :] = encode(x_ref[at, :], exponent)
        if (j + 1) * BLOCK % owned == 0:
            copies.append(start(codes[m], outs[m], sem.at[chunks + m]))
    copies.append(start(stat, stat_ref, sem.at[chunks + h]))
    wait_all(copies)


def put_codes(values, code, head):
    rows, w = values.shape
    head[...] = jnp.zeros_like(head)
    for j in range(rows // w):
        at = slice(j * w, (j + 1) * w)
        exponent = exponent_of(jnp.max(jnp.abs(values[at, :]), axis=1, keepdims=True))
        code[at, :] = encode(values[at, :], exponent)
        head[j : j + 1, :] = to_lanes(exponent).astype(i32)
    code[rows:, :] = head[...].astype(i16)


def get_codes(code, j, rows, size):
    w = code.shape[1]
    row, lane = j * size // w, j * size % w
    lanes = code[rows : rows + 16, :].astype(i32).astype(f32)[row : row + 1, lane : lane + size]
    return decode(code[j * size : (j + 1) * size, :], to_column(lanes))


def upper_kernel(width, member_ref, x_ref, *refs):
    stats, code_ref, (high, low, sums, code, head, sem) = refs[:-7], refs[-7], refs[-6:]
    h = len(stats)
    owned = x_ref.shape[0] // h
    for p in range(h):
        squares = stats[0][0:1, p * owned : (p + 1) * owned]
        for m in range(1, h):
            squares += stats[m][0:1, (p ^ m) * owned : ((p ^ m) + 1) * owned]
        factor = lax.rsqrt(squares / width + EPSILON)
        for j in range(0, owned, BLOCK):
            at = slice(p * owned + j, p * owned + j + BLOCK)
            high[at, :], low[at, :] = split(x_ref[at, :] * to_column(factor[:, j : j + BLOCK]))
    sums[...] = dot(member_ref[...], high[...]) + dot(member_ref[...], low[...])
    put_codes(sums, code, head)
    start(code, code_ref, sem).wait()


def both_kernel(own_ref, far_ref, code_ref, own, far, sums, code, head, sems):
    wait_all(start_all([own_ref, far_ref], [own, far], sems))
    rows = sums.shape[0]
    for j in range(rows // BLOCK):
        sums[j * BLOCK : (j + 1) * BLOCK, :] = get_codes(own, j, rows, BLOCK) + get_codes(far, j, rows, BLOCK)
    put_codes(sums, code, head)
    start(code, code_ref, sems.at[0]).wait()


def join_kernel(q_ref, *refs):
    h = (len(refs) - 4) // 2
    parts, (out_ref, out, sems, out_sems), held = refs[:h], refs[h : h + 4], refs[h + 4 :]
    rows, width = out.shape
    w = width // h
    wait_all(start_all(parts, held, sems))
    copies = []
    for j in range(rows // BLOCK):
        at = slice(j * BLOCK, (j + 1) * BLOCK)
        values = [get_codes(held[m], j, rows, BLOCK) for m in range(h)]
        square = sum(v * v for v in values)
        factor = lax.rsqrt(jnp.sum(square, axis=1, keepdims=True) / width + EPSILON)
        for m in range(h):
            out[at, chunk(q_ref[0] ^ m, w)] = values[m] * factor
        copies.append(start(out.at[at, :], out_ref.at[at, :], out_sems.at[j]))
    wait_all(copies)


def decode_kernel(q_ref, *refs):
    h = (len(refs) - 1) // 2
    codes, stats, out_ref = refs[:h], refs[h : 2 * h], refs[2 * h]
    rows, w = codes[0].shape
    width = h * w
    for j in range(rows // BLOCK):
        at = slice(j * BLOCK, (j + 1) * BLOCK)
        values = []
        for m in range(h):
            lanes = stats[m][1:2, m * rows + j * BLOCK : m * rows + (j + 1) * BLOCK]
            values.append(decode(codes[m][at, :], to_column(lanes)))
        square = sum(v * v for v in values)
        factor = lax.rsqrt(jnp.sum(square, axis=1, keepdims=True) / width + EPSILON)
        for m in range(h):
            out_ref[at, chunk(q_ref[0] ^ m, w)] = values[m] * factor


def call(kernel, out_shape, **kw):
    params = pltpu.CompilerParams(vmem_limit_bytes=VMEM_LIMIT)
    return pl.pallas_call(kernel, out_shape=out_shape, compiler_params=params, **kw)


def dma(*dims):
    return pltpu.SemaphoreType.DMA(dims) if dims else pltpu.SemaphoreType.DMA


def shards(points, point_cluster, cand_blocks, cent1_prev, parent, cent2_prev):
    point_rows, width = points.shape
    blocks = point_rows // BLOCK
    owned = cent1_prev.shape[0]
    upper_rows = cent2_prev.shape[0]
    n = lax.axis_size("cent")
    h = n // 2
    dp = lax.axis_index("dp")
    me = lax.axis_index("cent").astype(i32).reshape(1)
    q = me % h
    w = width // h
    chunks = w // BLOCK
    rows = h * owned

    def swap(value, mask):
        return lax.ppermute(value, "cent", [(i, i ^ mask) for i in range(n)])

    def swap_half(values):
        arrived = {m: swap(values[m], m) for m in range(h - 1, 0, -1)}
        return [values[0]] + [arrived[m] for m in range(1, h)]

    table = rms_norm(cent2_prev.astype(f32)).astype(bf16)
    table_units = lax.all_gather(table, "dp", axis=0, tiled=True)

    small = jnp.concatenate([point_cluster - dp * (n * owned), parent - dp * upper_rows]).reshape(-1, w)
    head = head_rows(point_rows + 2 * owned, w)
    prevs = call(
        prev_kernel,
        [shape((owned + head, w), i16)] * h,
        in_specs=[SMEM, HBM, VMEM],
        out_specs=[HBM] * h,
        scratch_shapes=[pltpu.VMEM((owned, width), f32), pltpu.VMEM((head, w), i32), dma(), dma(h)]
        + [pltpu.VMEM((owned + head, w), i16)] * h,
        name="prev",
    )(q, cent1_prev, small)
    prevs = swap_half(prevs)
    packed = call(
        functools.partial(pack_kernel, chunks),
        [shape((point_rows, BLOCK), bf16)] * (h * chunks),
        in_specs=[SMEM, HBM],
        out_specs=[HBM] * (h * chunks),
        scratch_shapes=[dma(h * chunks)],
        name="pack",
    )(q, points)
    arrived = [swap_half(packed[c::chunks]) for c in range(chunks)]

    member, place, near, far_count, prev, upper_member = call(
        functools.partial(prepare_kernel, blocks, n),
        [
            shape((h * point_rows, BLOCK), bf16),
            shape((h * blocks,), i32),
            shape((rows, BLOCK), f32),
            shape((rows // BLOCK, BLOCK), i32),
            shape((rows, w), f32),
            shape((upper_rows, rows), bf16),
        ],
        in_specs=[SMEM] + [VMEM] * h,
        out_specs=[VMEM, SMEM] + [VMEM] * 4,
        scratch_shapes=[pltpu.VMEM((2 * rows, BLOCK), f32)],
        name="prepare",
    )(me, *prevs)

    lines = rows + 2 * rows // BLOCK
    accs, crossed = [], []
    for c in range(chunks):
        acc, code = call(
            sums_kernel,
            [shape((2 * rows, BLOCK), f32), shape((lines, BLOCK), i16)],
            in_specs=[SMEM, VMEM, VMEM] + [HBM] * h,
            out_specs=[VMEM, HBM],
            scratch_shapes=[
                pltpu.VMEM((lines, BLOCK), i16),
                pltpu.VMEM((2 * rows // BLOCK, BLOCK), i32),
                dma(h + 1),
            ]
            + [pltpu.VMEM((point_rows, BLOCK), bf16)] * h,
            name=f"sums{c}",
        )(place, member, far_count, *arrived[c])
        accs.append(acc)
        crossed.append(swap(code, h))

    points, table_units = lax.optimization_barrier((points, table_units))
    unit_points = rms_norm(points.astype(f32)).astype(bf16)
    products = lax.dot_general(
        unit_points, table_units, (((1,), (1,)), ((), ())), preferred_element_type=f32
    )
    column_block = jnp.arange(table_units.shape[0]) // BLOCK
    listed = jnp.any(cand_blocks[:, :, None] == column_block[None, None, :], axis=1)
    weights = jnp.exp(products * (SHARPNESS / width)).reshape(blocks, BLOCK, -1)
    running = jnp.sum(weights * listed[:, None, :].astype(f32), axis=2).reshape(point_rows)
    point_score, near = lax.optimization_barrier((jnp.log(running), near))

    out = call(
        functools.partial(refresh_kernel, chunks, h),
        [shape((rows, w), f32), shape((2, rows), f32)] + [shape((owned, w), i16)] * h,
        in_specs=[VMEM] * (2 + chunks) + [HBM] * chunks,
        out_specs=[VMEM] + [HBM] * (h + 1),
        scratch_shapes=[pltpu.VMEM((owned, w), i16)] * h
        + [pltpu.VMEM((2, rows), f32), dma(chunks + h + 1)]
        + [pltpu.VMEM((lines, BLOCK), i16)] * chunks,
        name="refresh",
    )(near, prev, *accs, *crossed)
    x, stat = out[:2]
    stats = swap_half([stat] * h)
    back = swap_half(out[2:])

    upper_shape = shape((upper_rows + head_rows(upper_rows, w), w), i16)
    held_code = pltpu.VMEM(upper_shape.shape, i16)
    put = [pltpu.VMEM((upper_rows, w), f32), held_code, pltpu.VMEM((upper_shape.shape[0] - upper_rows, w), i32)]
    code = call(
        functools.partial(upper_kernel, width),
        upper_shape,
        in_specs=[VMEM] * (h + 2),
        out_specs=HBM,
        scratch_shapes=[pltpu.VMEM((rows, w), bf16), pltpu.VMEM((rows, w), bf16)] + put + [dma()],
        name="upper",
    )(upper_member, x, *stats)
    code = call(
        both_kernel,
        upper_shape,
        in_specs=[HBM, HBM],
        out_specs=HBM,
        scratch_shapes=[held_code, held_code] + put + [dma(2)],
        name="both",
    )(code, swap(code, h))
    parts = swap_half([code] * h)

    cent1_new = call(
        decode_kernel,
        shape((owned, width), f32),
        in_specs=[SMEM] + [VMEM] * (2 * h),
        out_specs=VMEM,
        name="decode",
    )(q, *back, *stats)
    q, cent1_new = lax.optimization_barrier((q, cent1_new))
    cent2_new = call(
        join_kernel,
        shape((upper_rows, width), f32),
        in_specs=[SMEM] + [HBM] * h,
        out_specs=HBM,
        scratch_shapes=[pltpu.VMEM((upper_rows, width), f32), dma(h), dma(upper_rows // BLOCK)] + [held_code] * h,
        name="join",
    )(q, *parts)
    return (cent1_new, cent2_new, point_score)


def solution(mesh):
    placed = (
        P(("dp", "cent"), None),
        P(("dp", "cent")),
        P(("dp", "cent"), None),
        P(("dp", "cent"), None),
        P(("dp", "cent")),
        P("dp", None),
    )
    return jax.shard_map(
        shards,
        mesh=mesh,
        in_specs=placed,
        out_specs=(P(("dp", "cent"), None), P("dp", None), P(("dp", "cent"))),
        check_vma=False,
    )
```

time: 242 us -> 135 us (0.56)
  waiting for transfers between devices: 185 us -> 54.6 us
  Pallas kernels: 0 us -> 18.8 us
  starting transfers between devices: 11.9 us -> 26.7 us
  other arithmetic: 11.2 us -> 4.89 us
  matrix products: 11.3 us -> 7.72 us
    all_to_all x2 -> x0, waiting for transfers between devices: 93.2 us -> none  [the longest x1 91.2 us: shards(): lax.all_to_all(outgoing, 'cent', split_axis=0, concat_axis=0, tiled=True)]
    psum x1 -> x0, waiting for transfers between devices: 91.1 us -> none  [shards(): cent2_new = rms_norm(lax.psum(upper_part, 'cent'))]
    ppermute x0 -> x21, waiting for transfers between devices: none -> 54.5 us  [swap(): return lax.ppermute(value, 'cent', [(i, i ^ mask) for i in range(n)])]
    ppermute x0 -> x21, starting transfers between devices: none -> 26.6 us  [swap(): return lax.ppermute(value, 'cent', [(i, i ^ mask) for i in range(n)])]
    pallas_call x0 -> x10, Pallas kernels: none -> 18.8 us  [the longest x2 6.22 us: shards(): call(sums_kernel, [shape((2 * rows, BLOCK), f32), shape((lines, BLOCK), i...]
    all_to_all x2 -> x0, starting transfers between devices: 11.8 us -> none  [the longest x1 7.28 us: shards(): lax.all_to_all(outgoing_ids, 'cent', split_axis=0, concat_axis=0, tiled=T...]
    unnamed x12 -> x40, local copies, waits for them, and re-layouts: 0.21 us -> 6.75 us
    dot_general x2 -> x0, matrix products: 5.94 us -> none  [the longest x1 3.55 us: shards(): jnp.einsum('spc,spd->cd', member, arrived, preferred_element_type=jnp.flo...]
  transfers between devices with their start and end apart: 4 -> 22, of which waited for: 3 -> 10; matrix products, arithmetic and copies ran while one was open for 9% -> 7% of each run, Pallas kernels for 0% -> 9%
where the time goes in v4:
time: 135 us; the launch traced here: 134 us
  waiting for transfers between devices  54.6 us (40%)
  starting transfers between devices  26.7 us (20%)
  Pallas kernels  18.8 us (14%)
  between operations  14.4 us (11%)
  matrix products  7.72 us (6%)
  local copies, waits for them, and re-layouts  7.35 us (5%)
  other arithmetic  4.89 us (4%)
    ppermute x21, waiting for transfers between devices, swap(): return lax.ppermute(value, 'cent', [(i, i ^ mask) for i in range(n)])  54.5 us
    ppermute x21, starting transfers between devices, swap(): return lax.ppermute(value, 'cent', [(i, i ^ mask) for i in range(n)])  26.6 us
    dot_general x1, matrix products, shards(): lax.dot_general(unit_points, table_units, (((1,), (1,)), ((), ())), prefe...  7.72 us
    unnamed x40, local copies, waits for them, and re-layouts  6.75 us
    pallas_call x2, Pallas kernels, shards(): call(sums_kernel, [shape((2 * rows, BLOCK), f32), shape((lines, BLOCK), i...  6.22 us
    pallas_call x1, Pallas kernels, shards(): call(functools.partial(refresh_kernel, chunks, h), [shape((rows, w), f32)...  3.42 us
  transfers between devices with their start and end apart: 22, of which 10 were waited for; matrix products, arithmetic and copies ran while one was open for 7% of the time, Pallas kernels for 9%

profile of v4, /device:TPU:0, one launch (start us, length us, event | category | flops | bytes accessed | tf_op | source)
XLA Modules:
  0.0 134.3 jit_solution(18167140003506273300)
XLA Ops:
  7.3 1.7 %fusion.3 = f32[512]{0:T(512)S(1)} fusion(bf16[512,1024]{1,0:T(8,128)(2,1)} %param.11), kind=kLoop, calls=%fused_computation.8 | loop fusion | flops 1572352 | bytes 1050624 | tf_op jit(solution)/shard_map/reduce_sum | solution.py:24
  8.9 2.5 %fusion.4 = bf16[512,1024]{1,0:T(8,128)(2,1)} fusion(bf16[512,1024]{1,0:T(8,128)(2,1)} %param.11, f32[512]{0:T(512)S(1)} %add_rsqrt_fusion.1), kind=kLoop, calls=%fused_computation.9 | loop fusion | flops 1572864 | bytes 2099200 | tf_op jit(solution)/shard_map/convert_element_type | solution.py:336
  11.5 1.0 pack.1
  12.5 0.7 copy-done.10
  13.2 0.7 copy-done.12
  13.9 0.7 copy-done.16
  14.6 0.7 copy-done.13
  15.5 3.0 %collective-permute-start.6 = (bf16[1024,128]{1,0:T(8,128)(2,1)}, bf16[1024,128]{1,0:T(8,128)(2,1)}, u32[]{:S(2)}, u32[]{:S(2)}) collective-permute-start(bf16[1024,128]{1,0:T(8,128)(2,1)} %get-tuple-element.55), channel_id=1, source_target_pairs={{0,1},{1,0},{2,3},{3,2},{4,5},{5,4},{6,7},{7,6},{8,9},{9,8},{10,11... | collective-permute-start | bytes 786440 | tf_op jit(solution)/shard_map/ppermute | solution.py:330
  18.5 1.3 prev.1
  19.9 2.1 %collective-permute-start.1 = (s16[272,256]{1,0:T(8,128)(2,1)S(1)}, s16[272,256]{1,0:T(8,128)(2,1)S(1)}, u32[]{:S(2)}, u32[]{:S(2)}) collective-permute-start(s16[272,256]{1,0:T(8,128)(2,1)S(1)} %get-tuple-element.41), channel_id=1, source_target_pairs={{0,2},{1,3},{2,0},{3,1},{4,6},{5,7},{6,4},{7,5},{8,10},{9,11},{10,... | collective-permute-start | bytes 417800 | tf_op jit(solution)/shard_map/ppermute | solution.py:330
  22.0 1.4 %collective-permute-start.2 = (s16[272,256]{1,0:T(8,128)(2,1)S(1)}, s16[272,256]{1,0:T(8,128)(2,1)S(1)}, u32[]{:S(2)}, u32[]{:S(2)}) collective-permute-start(s16[272,256]{1,0:T(8,128)(2,1)S(1)} %get-tuple-element.42), channel_id=1, source_target_pairs={{0,3},{1,2},{2,1},{3,0},{4,7},{5,6},{6,5},{7,4},{8,11},{9,10},{10,... | collective-permute-start | bytes 417800 | tf_op jit(solution)/shard_map/ppermute | solution.py:330
  23.4 1.6 %collective-permute-start.7 = (bf16[1024,128]{1,0:T(8,128)(2,1)}, bf16[1024,128]{1,0:T(8,128)(2,1)S(1)}, u32[]{:S(2)}, u32[]{:S(2)}) collective-permute-start(bf16[1024,128]{1,0:T(8,128)(2,1)} %copy-done.16), channel_id=1, source_target_pairs={{0,2},{1,3},{2,0},{3,1},{4,6},{5,7},{6,4},{7,5},{8,10},{9,11},{10,... | collective-permute-start | bytes 786440 | tf_op jit(solution)/shard_map/ppermute | solution.py:330
  24.9 6.0 %collective-permute-done.refs_1_ = s16[272,256]{1,0:T(8,128)(2,1)S(1)} collective-permute-done((s16[272,256]{1,0:T(8,128)(2,1)S(1)}, s16[272,256]{1,0:T(8,128)(2,1)S(1)}, u32[]{:S(2)}, u32[]{:S(2)}) %collective-permute-start) | collective-permute-done | bytes 139296 | tf_op jit(solution)/shard_map/ppermute | solution.py:330
  30.9 2.8 %collective-permute-start.8 = (bf16[1024,128]{1,0:T(8,128)(2,1)}, bf16[1024,128]{1,0:T(8,128)(2,1)S(1)}, u32[]{:S(2)}, u32[]{:S(2)}) collective-permute-start(bf16[1024,128]{1,0:T(8,128)(2,1)} %copy-done.15), channel_id=1, source_target_pairs={{0,3},{1,2},{2,1},{3,0},{4,7},{5,6},{6,5},{7,4},{8,11},{9,10},{10,... | collective-permute-start | bytes 786440 | tf_op jit(solution)/shard_map/ppermute | solution.py:330
  33.7 0.5 collective-permute-start.3
  34.4 2.8 %collective-permute-start.5 = (bf16[1024,128]{1,0:T(8,128)(2,1)}, bf16[1024,128]{1,0:T(8,128)(2,1)S(1)}, u32[]{:S(2)}, u32[]{:S(2)}) collective-permute-start(bf16[1024,128]{1,0:T(8,128)(2,1)} %copy-done.12), channel_id=1, source_target_pairs={{0,3},{1,2},{2,1},{3,0},{4,7},{5,6},{6,5},{7,4},{8,11},{9,10},{10,... | collective-permute-start | bytes 786440 | tf_op jit(solution)/shard_map/ppermute | solution.py:330
  37.5 1.7 %prepare.1 = (bf16[4096,128]{1,0:T(8,128)(2,1)S(1)}, s32[32]{0:T(128)S(1)}, f32[1024,128]{1,0:T(8,128)S(1)}, s32[8,128]{1,0:T(8,128)S(1)}, f32[1024,256]{1,0:T(8,128)S(1)}, /*index=5*/bf16[512,1024]{1,0:T(8,128)(2,1)S(1)}) custom-call(s32[1]{0:T(128)} %bitcast.me_ref, s16[272,256]{1,0:T(8,128)(2,1)S(1)} %get-tuple-element.39.refs_0_, ...), custom_call_target="tpu_custom_call" | custom-call | tf_op jit(solution)/shard_map/prepare/pallas_call | solution.py:361
  39.2 1.0 copy-done.2
  40.1 0.8 copy-done.8
  41.0 0.4 collective-permute-done.8.refs_3_
  41.4 3.4 %sums1.1 = (f32[2048,128]{1,0:T(8,128)S(1)}, s16[1040,128]{1,0:T(8,128)(2,1)}) custom-call(s32[32]{0:T(128)S(1)} %get-tuple-element.46.place_ref, bf16[4096,128]{1,0:T(8,128)(2,1)S(1)} %get-tuple-element.47.member_ref, s32[8,128]{1,0:T(8,128)S(1)} %get-tuple-element.48.far_count_ref, bf16[1024,128]{1,0:T(8,128)(2,1)S(1)} %get-tuple-element.54.refs_0_, ...), custom_call_target="tpu_custom_call" | custom-call | tf_op jit(solution)/shard_map/sums1/pallas_call | solution.py:380
  44.8 2.9 %collective-permute-start.10 = (s16[1040,128]{1,0:T(8,128)(2,1)}, s16[1040,128]{1,0:T(8,128)(2,1)S(1)}, u32[]{:S(2)}, u32[]{:S(2)}) collective-permute-start(s16[1040,128]{1,0:T(8,128)(2,1)} %get-tuple-element.60), channel_id=1, source_target_pairs={{0,4},{1,5},{2,6},{3,7},{4,0},{5,1},{6,2},{7,3},{8,12},{9,13},{10,... | collective-permute-start | bytes 798728 | tf_op jit(solution)/shard_map/ppermute | solution.py:330
  47.7 4.0 %collective-permute-done.4.refs_2_ = bf16[1024,128]{1,0:T(8,128)(2,1)S(1)} collective-permute-done((bf16[1024,128]{1,0:T(8,128)(2,1)}, bf16[1024,128]{1,0:T(8,128)(2,1)S(1)}, u32[]{:S(2)}, u32[]{:S(2)}) %collective-permute-start.4) | collective-permute-done | bytes 262176 | tf_op jit(solution)/shard_map/ppermute | solution.py:330
  51.7 5.7 %collective-permute-done.5.refs_3_ = bf16[1024,128]{1,0:T(8,128)(2,1)S(1)} collective-permute-done((bf16[1024,128]{1,0:T(8,128)(2,1)}, bf16[1024,128]{1,0:T(8,128)(2,1)S(1)}, u32[]{:S(2)}, u32[]{:S(2)}) %collective-permute-start.5) | collective-permute-done | bytes 262176 | tf_op jit(solution)/shard_map/ppermute | solution.py:330
  57.4 0.9 copy-done.11
  58.4 2.8 %sums0.1 = (f32[2048,128]{1,0:T(8,128)S(1)}, s16[1040,128]{1,0:T(8,128)(2,1)}) custom-call(s32[32]{0:T(128)S(1)} %get-tuple-element.46.place_ref, bf16[4096,128]{1,0:T(8,128)(2,1)S(1)} %get-tuple-element.47.member_ref, s32[8,128]{1,0:T(8,128)S(1)} %get-tuple-element.48.far_count_ref, bf16[1024,128]{1,0:T(8,128)(2,1)S(1)} %copy-done.11, ...), custom_call_target="tpu_custom_call" | custom-call | tf_op jit(solution)/shard_map/sums0/pallas_call | solution.py:380
  61.2 1.0 copy-done.6
  62.2 0.5 fusion.1
  62.7 7.7 %fusion = f32[1024]{0:T(1024)S(1)} fusion(bf16[2048,1024]{1,0:T(8,128)(2,1)} %all-gather.2.cloned.1.call-done, f32[8,2048]{1,0:T(8,128)S(1)} %convert_element_type.24, bf16[1024,1024]{1,0:T(8,128)(2,1)S(1)} %copy-done, f32[1024]{0:T(1024)S(1)} %add_rsqrt_fusion), kind=kOutput, calls=%fused_computation.1 | convolution fusion | flops 4304403456 | bytes 6365184 | tf_op jit(solution)/shard_map/dot_general | solution.py:398
  70.4 0.6 log.3
  71.0 4.2 %collective-permute-done.9.refs_2_ = s16[1040,128]{1,0:T(8,128)(2,1)} collective-permute-done((s16[1040,128]{1,0:T(8,128)(2,1)}, s16[1040,128]{1,0:T(8,128)(2,1)}, u32[]{:S(2)}, u32[]{:S(2)}) %collective-permute-start.9) | collective-permute-done | bytes 266272 | tf_op jit(solution)/shard_map/ppermute | solution.py:330
  75.2 3.4 %refresh.1 = (f32[1024,256]{1,0:T(8,128)S(1)}, f32[2,1024]{1,0:T(2,128)S(1)}, s16[256,256]{1,0:T(8,128)(2,1)S(1)}, s16[256,256]{1,0:T(8,128)(2,1)S(1)}, s16[256,...) custom-call(f32[1024,128]{1,0:T(8,128)S(1)} %copy-done.9, f32[1024,256]{1,0:T(8,128)S(1)} %copy-done.3, ...), custom_call_target="tpu_custom_call" | custom-call | tf_op jit(solution)/shard_map/refresh/pallas_call | solution.py:407
  78.7 2.4 %collective-permute-start.15 = (f32[2,1024]{1,0:T(2,128)S(1)}, f32[2,1024]{1,0:T(2,128)S(1)}, u32[]{:S(2)}, u32[]{:S(2)}) collective-permute-start(f32[2,1024]{1,0:T(2,128)S(1)} %get-tuple-element.65.refs_4_.refs_0_), channel_id=1, source_target_pairs={{0,2},{1,3},{2,0},{3,1},{4,6},{5,7},{6,4},{7,5},{8,10},{9,11},{10,... | collective-permute-start | bytes 24584 | tf_op jit(solution)/shard_map/ppermute | solution.py:330
  81.2 1.0 collective-permute-start.14
  82.2 1.1 collective-permute-done.16.refs_7_.refs_3_
  83.3 1.6 %collective-permute-done.14.refs_5_.refs_1_ = f32[2,1024]{1,0:T(2,128)S(1)} collective-permute-done((f32[2,1024]{1,0:T(2,128)S(1)}, f32[2,1024]{1,0:T(2,128)S(1)}, u32[]{:S(2)}, u32[]{:S(2)}) %collective-permute-start.14) | collective-permute-done | bytes 8224 | tf_op jit(solution)/shard_map/ppermute | solution.py:330
  84.8 1.2 upper.1.own_ref
  86.1 0.8 collective-permute-start.17
  86.9 12.3 %collective-permute-done.17.far_ref = s16[528,256]{1,0:T(8,128)(2,1)S(1)} collective-permute-done((s16[528,256]{1,0:T(8,128)(2,1)S(1)}, s16[528,256]{1,0:T(8,128)(2,1)S(1)}, u32[]{:S(2)}, u32[]{:S(2)}) %collective-permute-start.17) | collective-permute-done | bytes 270368 | tf_op jit(solution)/shard_map/ppermute | solution.py:330
  99.2 0.7 both.1.refs_0_
  99.9 0.3 collective-permute-start.20
  100.2 2.5 %collective-permute-start.19 = (s16[528,256]{1,0:T(8,128)(2,1)S(1)}, s16[528,256]{1,0:T(8,128)(2,1)S(1)}, u32[]{:S(2)}, u32[]{:S(2)}) collective-permute-start(s16[528,256]{1,0:T(8,128)(2,1)S(1)} %both.1.refs_0_), channel_id=1, source_target_pairs={{0,2},{1,3},{2,0},{3,1},{4,6},{5,7},{6,4},{7,5},{8,10},{9,11},{10,... | collective-permute-start | bytes 811016 | tf_op jit(solution)/shard_map/ppermute | solution.py:330
  102.7 0.8 collective-permute-start.18
  103.5 1.2 collective-permute-start.11
  104.7 13.2 %collective-permute-done.11.refs_1_ = s16[256,256]{1,0:T(8,128)(2,1)S(1)} collective-permute-done((s16[256,256]{1,0:T(8,128)(2,1)S(1)}, s16[256,256]{1,0:T(8,128)(2,1)S(1)}, u32[]{:S(2)}, u32[]{:S(2)}) %collective-permute-start.11) | collective-permute-done | bytes 131104 | tf_op jit(solution)/shard_map/ppermute | solution.py:330
  118.2 6.0 %collective-permute-done.13.refs_3_ = s16[256,256]{1,0:T(8,128)(2,1)S(1)} collective-permute-done((s16[256,256]{1,0:T(8,128)(2,1)S(1)}, s16[256,256]{1,0:T(8,128)(2,1)S(1)}, u32[]{:S(2)}, u32[]{:S(2)}) %collective-permute-start.13) | collective-permute-done | bytes 131104 | tf_op jit(solution)/shard_map/ppermute | solution.py:330
  124.2 1.4 %decode.1 = f32[256,1024]{1,0:T(8,128)} custom-call(s32[1]{0:T(128)S(6)} %select_n.16.q_ref, s16[256,256]{1,0:T(8,128)(2,1)S(1)} %get-tuple-element.61.refs_0_, s16[256,256]{1,0:T(8,128)(2,1)S(1)} %collective-permute-done.11.refs_1_, s16[256,256]{1,0:T(8,128)(2,1)S(1)} %collective-permute-done.12.refs_2_, ...), custom_call_target="tpu_custom_call" | custom-call | tf_op jit(solution)/shard_map/decode/pallas_call | solution.py:442
  125.6 1.9 %join.1 = f32[512,1024]{1,0:T(8,128)} custom-call(s32[1]{0:T(128)S(6)} %select_n.16.q_ref, s16[528,256]{1,0:T(8,128)(2,1)S(1)} %both.1.refs_0_, s16[528,256]{1,0:T(8,128)(2,1)S(1)} %collective-permute-done.18.refs_1_, s16[528,256]{1,0:T(8,128)(2,1)S(1)} %collective-permute-done.19.refs_2_, s16[528,256]{1,0:T(8,128)(2,1)S(1)} %collective-permute-done.20.refs_3_), custom_call_target="tpu_custom_call" | custom-call | tf_op jit(solution)/shard_map/join/pallas_call | solution.py:450
  (61 shorter events, 1.3 us)
Async XLA Ops:
  7.2 4.3 %copy-start = (bf16[1024,1024]{1,0:T(8,128)(2,1)S(1)}, bf16[1024,1024]{1,0:T(8,128)(2,1)}, u32[]{:S(2)}) copy-start(bf16[1024,1024]{1,0:T(8,128)(2,1)} %points_ref.1) | copy-start | bytes 6291460
  7.2 11.3 %copy-start.18 = (s32[1024]{0:T(1024)S(1)}, s32[1024]{0:T(1024)}, u32[]{:S(2)}) copy-start(s32[1024]{0:T(1024)} %param.7) | copy-start | bytes 12292
  7.2 11.3 %copy-start.19 = (s32[256]{0:T(256)S(1)}, s32[256]{0:T(256)}, u32[]{:S(2)}) copy-start(s32[256]{0:T(256)} %param.10) | copy-start | bytes 3076
  7.2 11.3 %copy-start.1 = (f32[256,1024]{1,0:T(8,128)S(1)}, f32[256,1024]{1,0:T(8,128)}, u32[]{:S(2)}) copy-start(f32[256,1024]{1,0:T(8,128)} %prev_ref.1) | copy-start | bytes 3145732
  7.2 30.0 %copy-start.17 = (s32[8,8]{1,0:T(8,128)S(1)}, s32[8,8]{1,0:T(8,128)}, u32[]{:S(2)}) copy-start(s32[8,8]{1,0:T(8,128)} %param.8) | copy-start | bytes 772
  7.2 54.9 %all-gather.2.cloned.1.call-start = ((), (), s32[]{:S(2)}) async-start(), calls=%async_computation | async-start | bytes 5242880 | tf_op jit(solution)/shard_map/all_gather | solution.py:337
  12.5 0.7 copy-start.10
  13.2 0.7 copy-start.12
  13.9 0.7 copy-start.16
  14.6 0.7 copy-start.13
  14.6 0.8 copy-start.14
  14.6 0.9 copy-start.15
  15.5 18.9 %collective-permute-start.6 = (bf16[1024,128]{1,0:T(8,128)(2,1)}, bf16[1024,128]{1,0:T(8,128)(2,1)}, u32[]{:S(2)}, u32[]{:S(2)}) collective-permute-start(bf16[1024,128]{1,0:T(8,128)(2,1)} %get-tuple-element.55), channel_id=1, source_target_pairs={{0,1},{1,0},{2,3},{3,2},{4,5},{5,4},{6,7},{7,6},{8,9},{9,8},{10,11... | collective-permute-start | bytes 786440 | tf_op jit(solution)/shard_map/ppermute | solution.py:330
  19.8 11.1 %collective-permute-start = (s16[272,256]{1,0:T(8,128)(2,1)S(1)}, s16[272,256]{1,0:T(8,128)(2,1)S(1)}, u32[]{:S(2)}, u32[]{:S(2)}) collective-permute-start(s16[272,256]{1,0:T(8,128)(2,1)S(1)} %get-tuple-element.40), channel_id=1, source_target_pairs={{0,1},{1,0},{2,3},{3,2},{4,5},{5,4},{6,7},{7,6},{8,9},{9,8},{10,11... | collective-permute-start | bytes 417800 | tf_op jit(solution)/shard_map/ppermute | solution.py:330
  19.9 13.8 %collective-permute-start.1 = (s16[272,256]{1,0:T(8,128)(2,1)S(1)}, s16[272,256]{1,0:T(8,128)(2,1)S(1)}, u32[]{:S(2)}, u32[]{:S(2)}) collective-permute-start(s16[272,256]{1,0:T(8,128)(2,1)S(1)} %get-tuple-element.41), channel_id=1, source_target_pairs={{0,2},{1,3},{2,0},{3,1},{4,6},{5,7},{6,4},{7,5},{8,10},{9,11},{10,... | collective-permute-start | bytes 417800 | tf_op jit(solution)/shard_map/ppermute | solution.py:330
  22.0 12.3 %collective-permute-start.2 = (s16[272,256]{1,0:T(8,128)(2,1)S(1)}, s16[272,256]{1,0:T(8,128)(2,1)S(1)}, u32[]{:S(2)}, u32[]{:S(2)}) collective-permute-start(s16[272,256]{1,0:T(8,128)(2,1)S(1)} %get-tuple-element.42), channel_id=1, source_target_pairs={{0,3},{1,2},{2,1},{3,0},{4,7},{5,6},{6,5},{7,4},{8,11},{9,10},{10,... | collective-permute-start | bytes 417800 | tf_op jit(solution)/shard_map/ppermute | solution.py:330
  23.4 17.6 %collective-permute-start.7 = (bf16[1024,128]{1,0:T(8,128)(2,1)}, bf16[1024,128]{1,0:T(8,128)(2,1)S(1)}, u32[]{:S(2)}, u32[]{:S(2)}) collective-permute-start(bf16[1024,128]{1,0:T(8,128)(2,1)} %copy-done.16), channel_id=1, source_target_pairs={{0,2},{1,3},{2,0},{3,1},{4,6},{5,7},{6,4},{7,5},{8,10},{9,11},{10,... | collective-permute-start | bytes 786440 | tf_op jit(solution)/shard_map/ppermute | solution.py:330
  30.9 10.4 %collective-permute-start.8 = (bf16[1024,128]{1,0:T(8,128)(2,1)}, bf16[1024,128]{1,0:T(8,128)(2,1)S(1)}, u32[]{:S(2)}, u32[]{:S(2)}) collective-permute-start(bf16[1024,128]{1,0:T(8,128)(2,1)} %copy-done.15), channel_id=1, source_target_pairs={{0,3},{1,2},{2,1},{3,0},{4,7},{5,6},{6,5},{7,4},{8,11},{9,10},{10,... | collective-permute-start | bytes 786440 | tf_op jit(solution)/shard_map/ppermute | solution.py:330
  33.7 14.0 %collective-permute-start.3 = (bf16[1024,128]{1,0:T(8,128)(2,1)}, bf16[1024,128]{1,0:T(8,128)(2,1)S(1)}, u32[]{:S(2)}, u32[]{:S(2)}) collective-permute-start(bf16[1024,128]{1,0:T(8,128)(2,1)} %copy-done.14), channel_id=1, source_target_pairs={{0,1},{1,0},{2,3},{3,2},{4,5},{5,4},{6,7},{7,6},{8,9},{9,8},{10,11... | collective-permute-start | bytes 786440 | tf_op jit(solution)/shard_map/ppermute | solution.py:330
  34.2 17.5 %collective-permute-start.4 = (bf16[1024,128]{1,0:T(8,128)(2,1)}, bf16[1024,128]{1,0:T(8,128)(2,1)S(1)}, u32[]{:S(2)}, u32[]{:S(2)}) collective-permute-start(bf16[1024,128]{1,0:T(8,128)(2,1)} %copy-done.13), channel_id=1, source_target_pairs={{0,2},{1,3},{2,0},{3,1},{4,6},{5,7},{6,4},{7,5},{8,10},{9,11},{10,... | collective-permute-start | bytes 786440 | tf_op jit(solution)/shard_map/ppermute | solution.py:330
  34.4 23.0 %collective-permute-start.5 = (bf16[1024,128]{1,0:T(8,128)(2,1)}, bf16[1024,128]{1,0:T(8,128)(2,1)S(1)}, u32[]{:S(2)}, u32[]{:S(2)}) collective-permute-start(bf16[1024,128]{1,0:T(8,128)(2,1)} %copy-done.12), channel_id=1, source_target_pairs={{0,3},{1,2},{2,1},{3,0},{4,7},{5,6},{6,5},{7,4},{8,11},{9,10},{10,... | collective-permute-start | bytes 786440 | tf_op jit(solution)/shard_map/ppermute | solution.py:330
  39.2 1.0 copy-start.2
  40.1 0.8 copy-start.8
  44.8 16.4 %copy-start.4 = (f32[2048,128]{1,0:T(8,128)}, f32[2048,128]{1,0:T(8,128)S(1)}, u32[]{:S(2)}) copy-start(f32[2048,128]{1,0:T(8,128)S(1)} %get-tuple-element.58.refs_1_) | copy-start | bytes 3145732
  44.8 26.2 %collective-permute-start.10 = (s16[1040,128]{1,0:T(8,128)(2,1)}, s16[1040,128]{1,0:T(8,128)(2,1)S(1)}, u32[]{:S(2)}, u32[]{:S(2)}) collective-permute-start(s16[1040,128]{1,0:T(8,128)(2,1)} %get-tuple-element.60), channel_id=1, source_target_pairs={{0,4},{1,5},{2,6},{3,7},{4,0},{5,1},{6,2},{7,3},{8,12},{9,13},{10,... | collective-permute-start | bytes 798728 | tf_op jit(solution)/shard_map/ppermute | solution.py:330
  57.4 1.0 copy-start.11
  61.2 1.0 copy-start.6
  62.2 13.1 %collective-permute-start.9 = (s16[1040,128]{1,0:T(8,128)(2,1)}, s16[1040,128]{1,0:T(8,128)(2,1)}, u32[]{:S(2)}, u32[]{:S(2)}) collective-permute-start(s16[1040,128]{1,0:T(8,128)(2,1)} %get-tuple-element.59), channel_id=1, source_target_pairs={{0,4},{1,5},{2,6},{3,7},{4,0},{5,1},{6,2},{7,3},{8,12},{9,13},{10,... | collective-permute-start | bytes 798728 | tf_op jit(solution)/shard_map/ppermute | solution.py:330
  62.7 12.6 %copy-start.3 = (f32[1024,256]{1,0:T(8,128)S(1)}, f32[1024,256]{1,0:T(8,128)}, u32[]{:S(2)}) copy-start(f32[1024,256]{1,0:T(8,128)} %copy-done.2) | copy-start | bytes 3145732
  62.7 12.5 %copy-start.5 = (f32[2048,128]{1,0:T(8,128)S(1)}, f32[2048,128]{1,0:T(8,128)}, u32[]{:S(2)}) copy-start(f32[2048,128]{1,0:T(8,128)} %copy-done.4) | copy-start | bytes 3145732
  62.7 12.5 %copy-start.7 = (f32[2048,128]{1,0:T(8,128)S(1)}, f32[2048,128]{1,0:T(8,128)}, u32[]{:S(2)}) copy-start(f32[2048,128]{1,0:T(8,128)} %copy-done.6) | copy-start | bytes 3145732
  62.7 12.5 %copy-start.9 = (f32[1024,128]{1,0:T(8,128)S(1)}, f32[1024,128]{1,0:T(8,128)}, u32[]{:S(2)}) copy-start(f32[1024,128]{1,0:T(8,128)} %copy-done.8) | copy-start | bytes 1572868
  78.7 4.6 %collective-permute-start.16 = (f32[2,1024]{1,0:T(2,128)S(1)}, f32[2,1024]{1,0:T(2,128)S(1)}, u32[]{:S(2)}, u32[]{:S(2)}) collective-permute-start(f32[2,1024]{1,0:T(2,128)S(1)} %get-tuple-element.65.refs_4_.refs_0_), channel_id=1, source_target_pairs={{0,3},{1,2},{2,1},{3,0},{4,7},{5,6},{6,5},{7,4},{8,11},{9,10},{10,... | collective-permute-start | bytes 24584 | tf_op jit(solution)/shard_map/ppermute | solution.py:330
  78.7 4.5 %collective-permute-start.15 = (f32[2,1024]{1,0:T(2,128)S(1)}, f32[2,1024]{1,0:T(2,128)S(1)}, u32[]{:S(2)}, u32[]{:S(2)}) collective-permute-start(f32[2,1024]{1,0:T(2,128)S(1)} %get-tuple-element.65.refs_4_.refs_0_), channel_id=1, source_target_pairs={{0,2},{1,3},{2,0},{3,1},{4,6},{5,7},{6,4},{7,5},{8,10},{9,11},{10,... | collective-permute-start | bytes 24584 | tf_op jit(solution)/shard_map/ppermute | solution.py:330
  81.2 3.7 %collective-permute-start.14 = (f32[2,1024]{1,0:T(2,128)S(1)}, f32[2,1024]{1,0:T(2,128)S(1)}, u32[]{:S(2)}, u32[]{:S(2)}) collective-permute-start(f32[2,1024]{1,0:T(2,128)S(1)} %get-tuple-element.65.refs_4_.refs_0_), channel_id=1, source_target_pairs={{0,1},{1,0},{2,3},{3,2},{4,5},{5,4},{6,7},{7,6},{8,9},{9,8},{10,11... | collective-permute-start | bytes 24584 | tf_op jit(solution)/shard_map/ppermute | solution.py:330
  86.1 13.1 %collective-permute-start.17 = (s16[528,256]{1,0:T(8,128)(2,1)S(1)}, s16[528,256]{1,0:T(8,128)(2,1)S(1)}, u32[]{:S(2)}, u32[]{:S(2)}) collective-permute-start(s16[528,256]{1,0:T(8,128)(2,1)S(1)} %upper.1.own_ref), channel_id=1, source_target_pairs={{0,4},{1,5},{2,6},{3,7},{4,0},{5,1},{6,2},{7,3},{8,12},{9,13},{10,... | collective-permute-start | bytes 811016 | tf_op jit(solution)/shard_map/ppermute | solution.py:330
  99.9 25.7 %collective-permute-start.20 = (s16[528,256]{1,0:T(8,128)(2,1)S(1)}, s16[528,256]{1,0:T(8,128)(2,1)S(1)}, u32[]{:S(2)}, u32[]{:S(2)}) collective-permute-start(s16[528,256]{1,0:T(8,128)(2,1)S(1)} %both.1.refs_0_), channel_id=1, source_target_pairs={{0,3},{1,2},{2,1},{3,0},{4,7},{5,6},{6,5},{7,4},{8,11},{9,10},{10,... | collective-permute-start | bytes 811016 | tf_op jit(solution)/shard_map/ppermute | solution.py:330
  100.2 25.4 %collective-permute-start.19 = (s16[528,256]{1,0:T(8,128)(2,1)S(1)}, s16[528,256]{1,0:T(8,128)(2,1)S(1)}, u32[]{:S(2)}, u32[]{:S(2)}) collective-permute-start(s16[528,256]{1,0:T(8,128)(2,1)S(1)} %both.1.refs_0_), channel_id=1, source_target_pairs={{0,2},{1,3},{2,0},{3,1},{4,6},{5,7},{6,4},{7,5},{8,10},{9,11},{10,... | collective-permute-start | bytes 811016 | tf_op jit(solution)/shard_map/ppermute | solution.py:330
  102.7 22.9 %collective-permute-start.18 = (s16[528,256]{1,0:T(8,128)(2,1)S(1)}, s16[528,256]{1,0:T(8,128)(2,1)S(1)}, u32[]{:S(2)}, u32[]{:S(2)}) collective-permute-start(s16[528,256]{1,0:T(8,128)(2,1)S(1)} %both.1.refs_0_), channel_id=1, source_target_pairs={{0,1},{1,0},{2,3},{3,2},{4,5},{5,4},{6,7},{7,6},{8,9},{9,8},{10,11... | collective-permute-start | bytes 811016 | tf_op jit(solution)/shard_map/ppermute | solution.py:330
  103.5 14.4 %collective-permute-start.11 = (s16[256,256]{1,0:T(8,128)(2,1)S(1)}, s16[256,256]{1,0:T(8,128)(2,1)S(1)}, u32[]{:S(2)}, u32[]{:S(2)}) collective-permute-start(s16[256,256]{1,0:T(8,128)(2,1)S(1)} %get-tuple-element.62), channel_id=1, source_target_pairs={{0,1},{1,0},{2,3},{3,2},{4,5},{5,4},{6,7},{7,6},{8,9},{9,8},{10,11... | collective-permute-start | bytes 393224 | tf_op jit(solution)/shard_map/ppermute | solution.py:330
  104.7 13.5 %collective-permute-start.12 = (s16[256,256]{1,0:T(8,128)(2,1)S(1)}, s16[256,256]{1,0:T(8,128)(2,1)S(1)}, u32[]{:S(2)}, u32[]{:S(2)}) collective-permute-start(s16[256,256]{1,0:T(8,128)(2,1)S(1)} %get-tuple-element.63), channel_id=1, source_target_pairs={{0,2},{1,3},{2,0},{3,1},{4,6},{5,7},{6,4},{7,5},{8,10},{9,11},{10,... | collective-permute-start | bytes 393224 | tf_op jit(solution)/shard_map/ppermute | solution.py:330
  117.9 6.3 %collective-permute-start.13 = (s16[256,256]{1,0:T(8,128)(2,1)S(1)}, s16[256,256]{1,0:T(8,128)(2,1)S(1)}, u32[]{:S(2)}, u32[]{:S(2)}) collective-permute-start(s16[256,256]{1,0:T(8,128)(2,1)S(1)} %get-tuple-element.64), channel_id=1, source_target_pairs={{0,3},{1,2},{2,1},{3,0},{4,7},{5,6},{6,5},{7,4},{8,11},{9,10},{10,... | collective-permute-start | bytes 393224 | tf_op jit(solution)/shard_map/ppermute | solution.py:330
Sparse Core Ops, SparseCore 0:
  11.6 37.1 all-gather.1

commit v5 on v4

--- a/solution.py
+++ b/solution.py
@@ -12,7 +12,7 @@
 SHARPNESS = 20.0
 CODE = 32000.0
 FLOOR = 1e-30
-VMEM_LIMIT = 48 * 1024 * 1024
+VMEM_LIMIT = 16 * 1024 * 1024
 f32, bf16, i16, i32 = jnp.float32, jnp.bfloat16, jnp.int16, jnp.int32
 shape = jax.ShapeDtypeStruct
 VMEM = pl.BlockSpec(memory_space=pltpu.VMEM)
@@ -93,8 +93,9 @@
 
 
 def prev_kernel(q_ref, prev_ref, small_ref, *refs):
-    h = (len(refs) - 4) // 2
-    outs, (prev, head, sem, sems), held = refs[:h], refs[h : h + 4], refs[h + 4 :]
+    h = (len(refs) - 5) // 2
+    outs, (next_ref, prev, head, sem, sems), held = refs[:h], refs[h : h + 5], refs[h + 5 :]
+    next_ref[0] = q_ref[0]
     owned, width = prev.shape
     w = width // h
     copy = start(prev_ref, prev, sem)
@@ -321,7 +322,7 @@
     h = n // 2
     dp = lax.axis_index("dp")
     me = lax.axis_index("cent").astype(i32).reshape(1)
-    q = me % h
+    q = me & (h - 1)
     w = width // h
     chunks = w // BLOCK
     rows = h * owned
@@ -333,21 +334,20 @@
         arrived = {m: swap(values[m], m) for m in range(h - 1, 0, -1)}
         return [values[0]] + [arrived[m] for m in range(1, h)]
 
-    table = rms_norm(cent2_prev.astype(f32)).astype(bf16)
-    table_units = lax.all_gather(table, "dp", axis=0, tiled=True)
+    table_rows = lax.all_gather(cent2_prev, "dp", axis=0, tiled=True)
 
     small = jnp.concatenate([point_cluster - dp * (n * owned), parent - dp * upper_rows]).reshape(-1, w)
     head = head_rows(point_rows + 2 * owned, w)
     prevs = call(
         prev_kernel,
-        [shape((owned + head, w), i16)] * h,
+        [shape((owned + head, w), i16)] * h + [shape((1,), i32)],
         in_specs=[SMEM, HBM, VMEM],
-        out_specs=[HBM] * h,
+        out_specs=[HBM] * h + [SMEM],
         scratch_shapes=[pltpu.VMEM((owned, width), f32), pltpu.VMEM((head, w), i32), dma(), dma(h)]
         + [pltpu.VMEM((owned + head, w), i16)] * h,
         name="prev",
     )(q, cent1_prev, small)
-    prevs = swap_half(prevs)
+    prevs, after_prev = swap_half(prevs[:h]), prevs[h]
     packed = call(
         functools.partial(pack_kernel, chunks),
         [shape((point_rows, BLOCK), bf16)] * (h * chunks),
@@ -355,7 +355,7 @@
         out_specs=[HBM] * (h * chunks),
         scratch_shapes=[dma(h * chunks)],
         name="pack",
-    )(q, points)
+    )(after_prev, points)
     arrived = [swap_half(packed[c::chunks]) for c in range(chunks)]
 
     member, place, near, far_count, prev, upper_member = call(
@@ -393,12 +393,13 @@
         accs.append(acc)
         crossed.append(swap(code, h))
 
-    points, table_units = lax.optimization_barrier((points, table_units))
+    points, table_rows = lax.optimization_barrier((points, table_rows))
     unit_points = rms_norm(points.astype(f32)).astype(bf16)
+    table_units = rms_norm(table_rows.astype(f32)).astype(bf16)
     products = lax.dot_general(
         unit_points, table_units, (((1,), (1,)), ((), ())), preferred_element_type=f32
     )
-    column_block = jnp.arange(table_units.shape[0]) // BLOCK
+    column_block = jnp.arange(table_rows.shape[0]) // BLOCK
     listed = jnp.any(cand_blocks[:, :, None] == column_block[None, None, :], axis=1)
     weights = jnp.exp(products * (SHARPNESS / width)).reshape(blocks, BLOCK, -1)
     running = jnp.sum(weights * listed[:, None, :].astype(f32), axis=2).reshape(point_rows)
@@ -429,6 +430,8 @@
         scratch_shapes=[pltpu.VMEM((rows, w), bf16), pltpu.VMEM((rows, w), bf16)] + put + [dma()],
         name="upper",
     )(upper_member, x, *stats)
+    far_code = swap(code, h)
+    code, back = lax.optimization_barrier((code, back))
     code = call(
         both_kernel,
         upper_shape,
@@ -436,7 +439,7 @@
         out_specs=HBM,
         scratch_shapes=[held_code, held_code] + put + [dma(2)],
         name="both",
-    )(code, swap(code, h))
+    )(code, far_code)
     parts = swap_half([code] * h)
 
     cent1_new = call(

time: 135 us -> 123 us (0.911)
  waiting for transfers between devices: 54.6 us -> 42.9 us
  matrix products: 7.72 us -> 5.37 us
  starting transfers between devices: 26.7 us -> 28.4 us
    ppermute x21, waiting for transfers between devices: 54.5 us -> 42.2 us  [swap(): return lax.ppermute(value, 'cent', [(i, i ^ mask) for i in range(n)])]
    convert_element_type x1 -> x0, other arithmetic: 2.49 us -> none  [shards(): table = rms_norm(cent2_prev.astype(f32)).astype(bf16)]
    dot_general x1, matrix products: 7.72 us -> 5.37 us  [shards(): lax.dot_general(unit_points, table_units, (((1,), (1,)), ((), ())), prefe...]
    ppermute x21, starting transfers between devices: 26.6 us -> 28.3 us  [swap(): return lax.ppermute(value, 'cent', [(i, i ^ mask) for i in range(n)])]
    reduce_sum x2, other arithmetic: 2.13 us -> 3.79 us  [rms_norm(): jnp.mean(values * values, axis=-1, keepdims=True) + EPSILON]
    unnamed x40 -> x24, local copies, waits for them, and re-layouts: 6.75 us -> 5.57 us
  transfers between devices with their start and end apart: 22 -> 22, of which waited for: 10 -> 13; matrix products, arithmetic and copies ran while one was open for 7% -> 10% of each run, Pallas kernels for 9% -> 10%
where the time goes in v5:
time: 123 us; the launch traced here: 122 us
  waiting for transfers between devices  42.9 us (35%)
  starting transfers between devices  28.4 us (23%)
  Pallas kernels  19.2 us (16%)
  between operations  14.3 us (12%)
  local copies, waits for them, and re-layouts  6.18 us (5%)
  other arithmetic  6.11 us (5%)
  matrix products  5.37 us (4%)
    ppermute x21, waiting for transfers between devices, swap(): return lax.ppermute(value, 'cent', [(i, i ^ mask) for i in range(n)])  42.2 us
    ppermute x21, starting transfers between devices, swap(): return lax.ppermute(value, 'cent', [(i, i ^ mask) for i in range(n)])  28.3 us
    pallas_call x2, Pallas kernels, shards(): call(sums_kernel, [shape((2 * rows, BLOCK), f32), shape((lines, BLOCK), i...  5.68 us
    unnamed x24, local copies, waits for them, and re-layouts  5.57 us
    dot_general x1, matrix products, shards(): lax.dot_general(unit_points, table_units, (((1,), (1,)), ((), ())), prefe...  5.37 us
    reduce_sum x2, other arithmetic, rms_norm(): jnp.mean(values * values, axis=-1, keepdims=True) + EPSILON  3.79 us
    pallas_call x1, Pallas kernels, shards(): call(functools.partial(refresh_kernel, chunks, h), [shape((rows, w), f32)...  3.42 us
  transfers between devices with their start and end apart: 22, of which 13 were waited for; matrix products, arithmetic and copies ran while one was open for 10% of the time, Pallas kernels for 10%

profile of v5, /device:TPU:0, one launch (start us, length us, event | category | flops | bytes accessed | tf_op | source)
XLA Modules:
  0.0 122.5 jit_solution(7125343399818908643)
XLA Ops:
  7.2 0.7 all-gather.2.cloned.1.call-update
  7.9 0.7 broadcast_subtract_fusion.1
  8.6 0.7 broadcast_subtract_fusion
  9.3 1.2 copy-done.2
  10.5 1.8 %prev.1 = (s16[272,256]{1,0:T(8,128)(2,1)S(1)}, s16[272,256]{1,0:T(8,128)(2,1)S(1)}, s16[272,256]{1,0:T(8,128)(2,1)S(1)}, s16[272,256]{1,0:T(8,128)(2,1)S(1)}, s32[1]{0:T(128)}) custom-call(s32[1]{0:T(128)S(6)} %and.18.q_ref, f32[256,1024]{1,0:T(8,128)S(1)} %copy-done.2, s32[5,256]{1,0:T(8,128)S(1)} %reshape.52.small_ref), custom_call_target="tpu_custom_call" | custom-call | tf_op jit(solution)/shard_map/prev/pallas_call | solution.py:341
  12.3 1.6 %copy-done = bf16[1024,1024]{1,0:T(8,128)(2,1)S(1)} copy-done((bf16[1024,1024]{1,0:T(8,128)(2,1)S(1)}, bf16[1024,1024]{1,0:T(8,128)(2,1)}, u32[]{:S(2)}) %copy-start) | copy-done | bytes 2097176
  13.9 1.3 %pack.1 = (bf16[1024,128]{1,0:T(8,128)(2,1)S(1)}, bf16[1024,128]{1,0:T(8,128)(2,1)S(1)}, bf16[1024,128]{1,0:T(8,128)(2,1)S(1)}, bf16[1024,128]{1,0:T(8,128)(2,1)...) custom-call(s32[1]{0:T(128)} %get-tuple-element.56.q_ref, ...), custom_call_target="tpu_custom_call" | custom-call | tf_op jit(solution)/shard_map/pack/pallas_call | solution.py:351
  15.2 3.0 %collective-permute-start.6 = (bf16[1024,128]{1,0:T(8,128)(2,1)S(1)}, bf16[1024,128]{1,0:T(8,128)(2,1)S(1)}, u32[]{:S(2)}, u32[]{:S(2)}) collective-permute-start(bf16[1024,128]{1,0:T(8,128)(2,1)S(1)} %get-tuple-element.63), channel_id=1, source_target_pairs={{0,1},{1,0},{2,3},{3,2},{4,5},{5,4},{6,7},{7,6},{8,9},{9,8},{10,11... | collective-permute-start | bytes 786440 | tf_op jit(solution)/shard_map/ppermute | solution.py:331
  18.3 2.0 %collective-permute-start.1 = (s16[272,256]{1,0:T(8,128)(2,1)S(1)}, s16[272,256]{1,0:T(8,128)(2,1)S(1)}, u32[]{:S(2)}, u32[]{:S(2)}) collective-permute-start(s16[272,256]{1,0:T(8,128)(2,1)S(1)} %get-tuple-element.45), channel_id=1, source_target_pairs={{0,2},{1,3},{2,0},{3,1},{4,6},{5,7},{6,4},{7,5},{8,10},{9,11},{10,... | collective-permute-start | bytes 417800 | tf_op jit(solution)/shard_map/ppermute | solution.py:331
  20.3 1.4 %collective-permute-start.2 = (s16[272,256]{1,0:T(8,128)(2,1)S(1)}, s16[272,256]{1,0:T(8,128)(2,1)S(1)}, u32[]{:S(2)}, u32[]{:S(2)}) collective-permute-start(s16[272,256]{1,0:T(8,128)(2,1)S(1)} %get-tuple-element.46), channel_id=1, source_target_pairs={{0,3},{1,2},{2,1},{3,0},{4,7},{5,6},{6,5},{7,4},{8,11},{9,10},{10,... | collective-permute-start | bytes 417800 | tf_op jit(solution)/shard_map/ppermute | solution.py:331
  21.7 1.6 %collective-permute-start.7 = (bf16[1024,128]{1,0:T(8,128)(2,1)S(1)}, bf16[1024,128]{1,0:T(8,128)(2,1)S(1)}, u32[]{:S(2)}, u32[]{:S(2)}) collective-permute-start(bf16[1024,128]{1,0:T(8,128)(2,1)S(1)} %get-tuple-element.64), channel_id=1, source_target_pairs={{0,2},{1,3},{2,0},{3,1},{4,6},{5,7},{6,4},{7,5},{8,10},{9,11},{10,... | collective-permute-start | bytes 786440 | tf_op jit(solution)/shard_map/ppermute | solution.py:331
  23.3 7.2 %collective-permute-done.refs_1_ = s16[272,256]{1,0:T(8,128)(2,1)S(1)} collective-permute-done((s16[272,256]{1,0:T(8,128)(2,1)S(1)}, s16[272,256]{1,0:T(8,128)(2,1)S(1)}, u32[]{:S(2)}, u32[]{:S(2)}) %collective-permute-start) | collective-permute-done | bytes 139296 | tf_op jit(solution)/shard_map/ppermute | solution.py:331
  30.5 2.8 %collective-permute-start.8 = (bf16[1024,128]{1,0:T(8,128)(2,1)S(1)}, bf16[1024,128]{1,0:T(8,128)(2,1)S(1)}, u32[]{:S(2)}, u32[]{:S(2)}) collective-permute-start(bf16[1024,128]{1,0:T(8,128)(2,1)S(1)} %get-tuple-element.65), channel_id=1, source_target_pairs={{0,3},{1,2},{2,1},{3,0},{4,7},{5,6},{6,5},{7,4},{8,11},{9,10},{10,... | collective-permute-start | bytes 786440 | tf_op jit(solution)/shard_map/ppermute | solution.py:331
  34.0 2.8 %collective-permute-start.5 = (bf16[1024,128]{1,0:T(8,128)(2,1)S(1)}, bf16[1024,128]{1,0:T(8,128)(2,1)S(1)}, u32[]{:S(2)}, u32[]{:S(2)}) collective-permute-start(bf16[1024,128]{1,0:T(8,128)(2,1)S(1)} %get-tuple-element.60), channel_id=1, source_target_pairs={{0,3},{1,2},{2,1},{3,0},{4,7},{5,6},{6,5},{7,4},{8,11},{9,10},{10,... | collective-permute-start | bytes 786440 | tf_op jit(solution)/shard_map/ppermute | solution.py:331
  36.8 0.9 compare_reduce_fusion
  37.7 1.7 %prepare.1 = (bf16[4096,128]{1,0:T(8,128)(2,1)S(1)}, s32[32]{0:T(128)S(1)}, f32[1024,128]{1,0:T(8,128)S(1)}, s32[8,128]{1,0:T(8,128)S(1)}, f32[1024,256]{1,0:T(8,128)S(1)}, /*index=5*/bf16[512,1024]{1,0:T(8,128)(2,1)S(1)}) custom-call(s32[1]{0:T(128)} %bitcast.me_ref, s16[272,256]{1,0:T(8,128)(2,1)S(1)} %get-tuple-element.43.refs_0_, ...), custom_call_target="tpu_custom_call" | custom-call | tf_op jit(solution)/shard_map/prepare/pallas_call | solution.py:361
  39.4 1.0 copy-done.3
  40.4 0.8 copy-done.9
  41.2 2.8 %sums1.1 = (f32[2048,128]{1,0:T(8,128)S(1)}, s16[1040,128]{1,0:T(8,128)(2,1)}) custom-call(s32[32]{0:T(128)S(1)} %get-tuple-element.53.place_ref, bf16[4096,128]{1,0:T(8,128)(2,1)S(1)} %get-tuple-element.54.member_ref, s32[8,128]{1,0:T(8,128)S(1)} %get-tuple-element.55.far_count_ref, bf16[1024,128]{1,0:T(8,128)(2,1)S(1)} %get-tuple-element.62.refs_0_, ...), custom_call_target="tpu_custom_call" | custom-call | tf_op jit(solution)/shard_map/sums1/pallas_call | solution.py:380
  44.1 2.7 %collective-permute-start.10 = (s16[1040,128]{1,0:T(8,128)(2,1)}, s16[1040,128]{1,0:T(8,128)(2,1)S(1)}, u32[]{:S(2)}, u32[]{:S(2)}) collective-permute-start(s16[1040,128]{1,0:T(8,128)(2,1)} %get-tuple-element.68), channel_id=1, source_target_pairs={{0,4},{1,5},{2,6},{3,7},{4,0},{5,1},{6,2},{7,3},{8,12},{9,13},{10,... | collective-permute-start | bytes 798728 | tf_op jit(solution)/shard_map/ppermute | solution.py:331
  46.7 4.9 %collective-permute-done.4.refs_2_ = bf16[1024,128]{1,0:T(8,128)(2,1)S(1)} collective-permute-done((bf16[1024,128]{1,0:T(8,128)(2,1)S(1)}, bf16[1024,128]{1,0:T(8,128)(2,1)S(1)}, u32[]{:S(2)}, u32[]{:S(2)}) %collective-permute-start.4) | collective-permute-done | bytes 262176 | tf_op jit(solution)/shard_map/ppermute | solution.py:331
  51.6 4.4 %collective-permute-done.5.refs_3_ = bf16[1024,128]{1,0:T(8,128)(2,1)S(1)} collective-permute-done((bf16[1024,128]{1,0:T(8,128)(2,1)S(1)}, bf16[1024,128]{1,0:T(8,128)(2,1)S(1)}, u32[]{:S(2)}, u32[]{:S(2)}) %collective-permute-start.5) | collective-permute-done | bytes 262176 | tf_op jit(solution)/shard_map/ppermute | solution.py:331
  56.0 2.9 %sums0.1 = (f32[2048,128]{1,0:T(8,128)S(1)}, s16[1040,128]{1,0:T(8,128)(2,1)}) custom-call(s32[32]{0:T(128)S(1)} %get-tuple-element.53.place_ref, bf16[4096,128]{1,0:T(8,128)(2,1)S(1)} %get-tuple-element.54.member_ref, s32[8,128]{1,0:T(8,128)S(1)} %get-tuple-element.55.far_count_ref, bf16[1024,128]{1,0:T(8,128)(2,1)S(1)} %get-tuple-element.57.refs_0_, ...), custom_call_target="tpu_custom_call" | custom-call | tf_op jit(solution)/shard_map/sums0/pallas_call | solution.py:380
  58.9 1.0 copy-done.7
  61.0 3.3 %fusion = f32[2048]{0:T(1024)S(1)} fusion(bf16[2048,1024]{1,0:T(8,128)(2,1)} %all-gather.2.cloned.1.call-done), kind=kLoop, calls=%fused_computation.2 | loop fusion | flops 6289408 | bytes 4202496 | tf_op jit(solution)/shard_map/reduce_sum | solution.py:24
  64.3 5.4 %fusion.2 = f32[1024]{0:T(1024)S(1)} fusion(bf16[2048,1024]{1,0:T(8,128)(2,1)S(1)} %copy-done.11, f32[8,2048]{1,0:T(8,128)S(1)} %convert_element_type.24, f32[2048]{0:T(1024)S(1)} %add_rsqrt_fusion, bf16[1024,1024]{1,0:T(8,128)(2,1)S(1)} %copy-done.1, f32[1024]{0:T(1024)S(1)} %add_rsqrt_fusion.1), kind=kOutput, calls=%fused_computation.5 | convolution fusion | flops 4310694912 | bytes 6373376 | tf_op jit(solution)/shard_map/dot_general | solution.py:399
  70.3 2.3 %collective-permute-done.9.refs_2_ = s16[1040,128]{1,0:T(8,128)(2,1)} collective-permute-done((s16[1040,128]{1,0:T(8,128)(2,1)}, s16[1040,128]{1,0:T(8,128)(2,1)}, u32[]{:S(2)}, u32[]{:S(2)}) %collective-permute-start.9) | collective-permute-done | bytes 266272 | tf_op jit(solution)/shard_map/ppermute | solution.py:331
  72.6 3.4 %refresh.1 = (f32[1024,256]{1,0:T(8,128)S(1)}, f32[2,1024]{1,0:T(2,128)S(1)}, s16[256,256]{1,0:T(8,128)(2,1)S(1)}, s16[256,256]{1,0:T(8,128)(2,1)S(1)}, s16[256,...) custom-call(f32[1024,128]{1,0:T(8,128)S(1)} %copy-done.10, f32[1024,256]{1,0:T(8,128)S(1)} %copy-done.4, ...), custom_call_target="tpu_custom_call" | custom-call | tf_op jit(solution)/shard_map/refresh/pallas_call | solution.py:408
  76.0 1.2 collective-permute-start.13
  77.3 2.3 %collective-permute-start.12 = (f32[2,1024]{1,0:T(2,128)S(1)}, f32[2,1024]{1,0:T(2,128)S(1)}, u32[]{:S(2)}, u32[]{:S(2)}) collective-permute-start(f32[2,1024]{1,0:T(2,128)S(1)} %get-tuple-element.70.refs_0_.refs_4_), channel_id=1, source_target_pairs={{0,2},{1,3},{2,0},{3,1},{4,6},{5,7},{6,4},{7,5},{8,10},{9,11},{10,... | collective-permute-start | bytes 24584 | tf_op jit(solution)/shard_map/ppermute | solution.py:331
  79.6 1.1 collective-permute-done.13.refs_3_.refs_7_
  80.7 0.7 collective-permute-done.12.refs_2_.refs_6_
  81.3 1.9 %collective-permute-done.11.refs_1_.refs_5_ = f32[2,1024]{1,0:T(2,128)S(1)} collective-permute-done((f32[2,1024]{1,0:T(2,128)S(1)}, f32[2,1024]{1,0:T(2,128)S(1)}, u32[]{:S(2)}, u32[]{:S(2)}) %collective-permute-start.11) | collective-permute-done | bytes 8224 | tf_op jit(solution)/shard_map/ppermute | solution.py:331
  83.2 1.4 %upper.1.own_ref = s16[528,256]{1,0:T(8,128)(2,1)S(1)} custom-call(bf16[512,1024]{1,0:T(8,128)(2,1)S(1)} %get-tuple-element.47.member_ref, f32[1024,256]{1,0:T(8,128)S(1)} %get-tuple-element.69.x_ref, f32[2,1024]{1,0:T(2,128)S(1)} %get-tuple-element.70.refs_0_.refs_4_, f32[2,1024]{1,0:T(2,128)S(1)} %collective-permute-done.11.refs_1_.refs_5_, ...), custom_call_target="tpu_custom_call" | custom-call | tf_op jit(solution)/shard_map/upper/pallas_call | solution.py:425
  84.8 0.7 collective-permute-start.14
  85.5 2.0 %collective-permute-start.15 = (s16[256,256]{1,0:T(8,128)(2,1)S(1)}, s16[256,256]{1,0:T(8,128)(2,1)S(1)}, u32[]{:S(2)}, u32[]{:S(2)}) collective-permute-start(s16[256,256]{1,0:T(8,128)(2,1)S(1)} %get-tuple-element.73), channel_id=1, source_target_pairs={{0,2},{1,3},{2,0},{3,1},{4,6},{5,7},{6,4},{7,5},{8,10},{9,11},{10,... | collective-permute-start | bytes 393224 | tf_op jit(solution)/shard_map/ppermute | solution.py:331
  87.5 0.8 collective-permute-start.16
  88.3 2.9 %collective-permute-done.14.refs_1_ = s16[256,256]{1,0:T(8,128)(2,1)S(1)} collective-permute-done((s16[256,256]{1,0:T(8,128)(2,1)S(1)}, s16[256,256]{1,0:T(8,128)(2,1)S(1)}, u32[]{:S(2)}, u32[]{:S(2)}) %collective-permute-start.14) | collective-permute-done | bytes 131104 | tf_op jit(solution)/shard_map/ppermute | solution.py:331
  91.2 2.3 %collective-permute-done.15.refs_2_ = s16[256,256]{1,0:T(8,128)(2,1)S(1)} collective-permute-done((s16[256,256]{1,0:T(8,128)(2,1)S(1)}, s16[256,256]{1,0:T(8,128)(2,1)S(1)}, u32[]{:S(2)}, u32[]{:S(2)}) %collective-permute-start.15) | collective-permute-done | bytes 131104 | tf_op jit(solution)/shard_map/ppermute | solution.py:331
  93.5 5.2 %collective-permute-done.16.refs_3_ = s16[256,256]{1,0:T(8,128)(2,1)S(1)} collective-permute-done((s16[256,256]{1,0:T(8,128)(2,1)S(1)}, s16[256,256]{1,0:T(8,128)(2,1)S(1)}, u32[]{:S(2)}, u32[]{:S(2)}) %collective-permute-start.16) | collective-permute-done | bytes 131104 | tf_op jit(solution)/shard_map/ppermute | solution.py:331
  98.7 0.7 both.1.refs_0_
  99.4 2.4 %collective-permute-start.19 = (s16[528,256]{1,0:T(8,128)(2,1)S(1)}, s16[528,256]{1,0:T(8,128)(2,1)S(1)}, u32[]{:S(2)}, u32[]{:S(2)}) collective-permute-start(s16[528,256]{1,0:T(8,128)(2,1)S(1)} %both.1.refs_0_), channel_id=1, source_target_pairs={{0,2},{1,3},{2,0},{3,1},{4,6},{5,7},{6,4},{7,5},{8,10},{9,11},{10,... | collective-permute-start | bytes 811016 | tf_op jit(solution)/shard_map/ppermute | solution.py:331
  101.8 1.1 collective-permute-start.18
  102.9 1.4 %decode.1 = f32[256,1024]{1,0:T(8,128)} custom-call(s32[1]{0:T(128)S(6)} %and.18.q_ref, s16[256,256]{1,0:T(8,128)(2,1)S(1)} %get-tuple-element.75.refs_0_, s16[256,256]{1,0:T(8,128)(2,1)S(1)} %collective-permute-done.14.refs_1_, s16[256,256]{1,0:T(8,128)(2,1)S(1)} %collective-permute-done.15.refs_2_, s16[256,256]{1,0:T(8,128)(2,1)S(1)} %collective-permute-done.16.refs_3_, ...), custom_call_target="tpu_custom_call" | custom-call | tf_op jit(solution)/shard_map/decode/pallas_call | solution.py:445
  104.3 5.5 %collective-permute-done.20.refs_3_ = s16[528,256]{1,0:T(8,128)(2,1)S(1)} collective-permute-done((s16[528,256]{1,0:T(8,128)(2,1)S(1)}, s16[528,256]{1,0:T(8,128)(2,1)S(1)}, u32[]{:S(2)}, u32[]{:S(2)}) %collective-permute-start.20) | collective-permute-done | bytes 270368 | tf_op jit(solution)/shard_map/ppermute | solution.py:331
  109.8 3.2 %collective-permute-done.19.refs_2_ = s16[528,256]{1,0:T(8,128)(2,1)S(1)} collective-permute-done((s16[528,256]{1,0:T(8,128)(2,1)S(1)}, s16[528,256]{1,0:T(8,128)(2,1)S(1)}, u32[]{:S(2)}, u32[]{:S(2)}) %collective-permute-start.19) | collective-permute-done | bytes 270368 | tf_op jit(solution)/shard_map/ppermute | solution.py:331
  112.9 0.8 collective-permute-done.18.refs_1_
  113.7 1.9 %join.1 = f32[512,1024]{1,0:T(8,128)} custom-call(s32[1]{0:T(128)S(6)} %and.18.q_ref, s16[528,256]{1,0:T(8,128)(2,1)S(1)} %both.1.refs_0_, s16[528,256]{1,0:T(8,128)(2,1)S(1)} %collective-permute-done.18.refs_1_, s16[528,256]{1,0:T(8,128)(2,1)S(1)} %collective-permute-done.19.refs_2_, s16[528,256]{1,0:T(8,128)(2,1)S(1)} %collective-permute-done.20.refs_3_), custom_call_target="tpu_custom_call" | custom-call | tf_op jit(solution)/shard_map/join/pallas_call | solution.py:453
  (44 shorter events, 2.8 us)
Async XLA Ops:
  7.2 53.3 %all-gather.2.cloned.1.call-start = ((), (), s32[]{:S(2)}) async-start(), calls=%async_computation | async-start | bytes 5242880 | tf_op jit(solution)/shard_map/all_gather | solution.py:337
  7.2 53.3 %copy-start.1 = (bf16[1024,1024]{1,0:T(8,128)(2,1)S(1)}, bf16[1024,1024]{1,0:T(8,128)(2,1)}, u32[]{:S(2)}) copy-start(bf16[1024,1024]{1,0:T(8,128)(2,1)} %points_ref.1) | copy-start | bytes 6291460
  9.3 1.2 %copy-start.2 = (f32[256,1024]{1,0:T(8,128)S(1)}, f32[256,1024]{1,0:T(8,128)}, u32[]{:S(2)}) copy-start(f32[256,1024]{1,0:T(8,128)} %prev_ref.1) | copy-start | bytes 3145732
  12.3 1.6 %copy-start = (bf16[1024,1024]{1,0:T(8,128)(2,1)S(1)}, bf16[1024,1024]{1,0:T(8,128)(2,1)}, u32[]{:S(2)}) copy-start(bf16[1024,1024]{1,0:T(8,128)(2,1)} %points_ref.1) | copy-start | bytes 6291460
  15.2 18.8 %collective-permute-start.6 = (bf16[1024,128]{1,0:T(8,128)(2,1)S(1)}, bf16[1024,128]{1,0:T(8,128)(2,1)S(1)}, u32[]{:S(2)}, u32[]{:S(2)}) collective-permute-start(bf16[1024,128]{1,0:T(8,128)(2,1)S(1)} %get-tuple-element.63), channel_id=1, source_target_pairs={{0,1},{1,0},{2,3},{3,2},{4,5},{5,4},{6,7},{7,6},{8,9},{9,8},{10,11... | collective-permute-start | bytes 786440 | tf_op jit(solution)/shard_map/ppermute | solution.py:331
  18.3 12.3 %collective-permute-start = (s16[272,256]{1,0:T(8,128)(2,1)S(1)}, s16[272,256]{1,0:T(8,128)(2,1)S(1)}, u32[]{:S(2)}, u32[]{:S(2)}) collective-permute-start(s16[272,256]{1,0:T(8,128)(2,1)S(1)} %get-tuple-element.44), channel_id=1, source_target_pairs={{0,1},{1,0},{2,3},{3,2},{4,5},{5,4},{6,7},{7,6},{8,9},{9,8},{10,11... | collective-permute-start | bytes 417800 | tf_op jit(solution)/shard_map/ppermute | solution.py:331
  18.3 15.0 %collective-permute-start.1 = (s16[272,256]{1,0:T(8,128)(2,1)S(1)}, s16[272,256]{1,0:T(8,128)(2,1)S(1)}, u32[]{:S(2)}, u32[]{:S(2)}) collective-permute-start(s16[272,256]{1,0:T(8,128)(2,1)S(1)} %get-tuple-element.45), channel_id=1, source_target_pairs={{0,2},{1,3},{2,0},{3,1},{4,6},{5,7},{6,4},{7,5},{8,10},{9,11},{10,... | collective-permute-start | bytes 417800 | tf_op jit(solution)/shard_map/ppermute | solution.py:331
  20.3 13.5 %collective-permute-start.2 = (s16[272,256]{1,0:T(8,128)(2,1)S(1)}, s16[272,256]{1,0:T(8,128)(2,1)S(1)}, u32[]{:S(2)}, u32[]{:S(2)}) collective-permute-start(s16[272,256]{1,0:T(8,128)(2,1)S(1)} %get-tuple-element.46), channel_id=1, source_target_pairs={{0,3},{1,2},{2,1},{3,0},{4,7},{5,6},{6,5},{7,4},{8,11},{9,10},{10,... | collective-permute-start | bytes 417800 | tf_op jit(solution)/shard_map/ppermute | solution.py:331
  21.7 19.5 %collective-permute-start.7 = (bf16[1024,128]{1,0:T(8,128)(2,1)S(1)}, bf16[1024,128]{1,0:T(8,128)(2,1)S(1)}, u32[]{:S(2)}, u32[]{:S(2)}) collective-permute-start(bf16[1024,128]{1,0:T(8,128)(2,1)S(1)} %get-tuple-element.64), channel_id=1, source_target_pairs={{0,2},{1,3},{2,0},{3,1},{4,6},{5,7},{6,4},{7,5},{8,10},{9,11},{10,... | collective-permute-start | bytes 786440 | tf_op jit(solution)/shard_map/ppermute | solution.py:331
  30.5 10.7 %collective-permute-start.8 = (bf16[1024,128]{1,0:T(8,128)(2,1)S(1)}, bf16[1024,128]{1,0:T(8,128)(2,1)S(1)}, u32[]{:S(2)}, u32[]{:S(2)}) collective-permute-start(bf16[1024,128]{1,0:T(8,128)(2,1)S(1)} %get-tuple-element.65), channel_id=1, source_target_pairs={{0,3},{1,2},{2,1},{3,0},{4,7},{5,6},{6,5},{7,4},{8,11},{9,10},{10,... | collective-permute-start | bytes 786440 | tf_op jit(solution)/shard_map/ppermute | solution.py:331
  33.3 13.4 %collective-permute-start.3 = (bf16[1024,128]{1,0:T(8,128)(2,1)S(1)}, bf16[1024,128]{1,0:T(8,128)(2,1)S(1)}, u32[]{:S(2)}, u32[]{:S(2)}) collective-permute-start(bf16[1024,128]{1,0:T(8,128)(2,1)S(1)} %get-tuple-element.58), channel_id=1, source_target_pairs={{0,1},{1,0},{2,3},{3,2},{4,5},{5,4},{6,7},{7,6},{8,9},{9,8},{10,11... | collective-permute-start | bytes 786440 | tf_op jit(solution)/shard_map/ppermute | solution.py:331
  33.8 17.8 %collective-permute-start.4 = (bf16[1024,128]{1,0:T(8,128)(2,1)S(1)}, bf16[1024,128]{1,0:T(8,128)(2,1)S(1)}, u32[]{:S(2)}, u32[]{:S(2)}) collective-permute-start(bf16[1024,128]{1,0:T(8,128)(2,1)S(1)} %get-tuple-element.59), channel_id=1, source_target_pairs={{0,2},{1,3},{2,0},{3,1},{4,6},{5,7},{6,4},{7,5},{8,10},{9,11},{10,... | collective-permute-start | bytes 786440 | tf_op jit(solution)/shard_map/ppermute | solution.py:331
  34.0 22.0 %collective-permute-start.5 = (bf16[1024,128]{1,0:T(8,128)(2,1)S(1)}, bf16[1024,128]{1,0:T(8,128)(2,1)S(1)}, u32[]{:S(2)}, u32[]{:S(2)}) collective-permute-start(bf16[1024,128]{1,0:T(8,128)(2,1)S(1)} %get-tuple-element.60), channel_id=1, source_target_pairs={{0,3},{1,2},{2,1},{3,0},{4,7},{5,6},{6,5},{7,4},{8,11},{9,10},{10,... | collective-permute-start | bytes 786440 | tf_op jit(solution)/shard_map/ppermute | solution.py:331
  39.4 1.0 copy-start.3
  40.4 0.8 copy-start.9
  44.1 14.8 %copy-start.5 = (f32[2048,128]{1,0:T(8,128)}, f32[2048,128]{1,0:T(8,128)S(1)}, u32[]{:S(2)}) copy-start(f32[2048,128]{1,0:T(8,128)S(1)} %get-tuple-element.66.refs_1_) | copy-start | bytes 3145732
  44.1 26.3 %collective-permute-start.10 = (s16[1040,128]{1,0:T(8,128)(2,1)}, s16[1040,128]{1,0:T(8,128)(2,1)S(1)}, u32[]{:S(2)}, u32[]{:S(2)}) collective-permute-start(s16[1040,128]{1,0:T(8,128)(2,1)} %get-tuple-element.68), channel_id=1, source_target_pairs={{0,4},{1,5},{2,6},{3,7},{4,0},{5,1},{6,2},{7,3},{8,12},{9,13},{10,... | collective-permute-start | bytes 798728 | tf_op jit(solution)/shard_map/ppermute | solution.py:331
  58.9 1.0 copy-start.7
  59.9 12.7 %collective-permute-start.9 = (s16[1040,128]{1,0:T(8,128)(2,1)}, s16[1040,128]{1,0:T(8,128)(2,1)}, u32[]{:S(2)}, u32[]{:S(2)}) collective-permute-start(s16[1040,128]{1,0:T(8,128)(2,1)} %get-tuple-element.67), channel_id=1, source_target_pairs={{0,4},{1,5},{2,6},{3,7},{4,0},{5,1},{6,2},{7,3},{8,12},{9,13},{10,... | collective-permute-start | bytes 798728 | tf_op jit(solution)/shard_map/ppermute | solution.py:331
  60.5 3.8 %copy-start.11 = (bf16[2048,1024]{1,0:T(8,128)(2,1)S(1)}, bf16[2048,1024]{1,0:T(8,128)(2,1)}, u32[]{:S(2)}) copy-start(bf16[2048,1024]{1,0:T(8,128)(2,1)} %all-gather.2.cloned.1.call-done) | copy-start | bytes 12582916
  64.3 8.3 %copy-start.4 = (f32[1024,256]{1,0:T(8,128)S(1)}, f32[1024,256]{1,0:T(8,128)}, u32[]{:S(2)}) copy-start(f32[1024,256]{1,0:T(8,128)} %copy-done.3) | copy-start | bytes 3145732
  64.3 8.3 %copy-start.6 = (f32[2048,128]{1,0:T(8,128)S(1)}, f32[2048,128]{1,0:T(8,128)}, u32[]{:S(2)}) copy-start(f32[2048,128]{1,0:T(8,128)} %copy-done.5) | copy-start | bytes 3145732
  64.3 8.3 %copy-start.8 = (f32[2048,128]{1,0:T(8,128)S(1)}, f32[2048,128]{1,0:T(8,128)}, u32[]{:S(2)}) copy-start(f32[2048,128]{1,0:T(8,128)} %copy-done.7) | copy-start | bytes 3145732
  64.3 8.3 %copy-start.10 = (f32[1024,128]{1,0:T(8,128)S(1)}, f32[1024,128]{1,0:T(8,128)}, u32[]{:S(2)}) copy-start(f32[1024,128]{1,0:T(8,128)} %copy-done.9) | copy-start | bytes 1572868
  76.0 4.6 %collective-permute-start.13 = (f32[2,1024]{1,0:T(2,128)S(1)}, f32[2,1024]{1,0:T(2,128)S(1)}, u32[]{:S(2)}, u32[]{:S(2)}) collective-permute-start(f32[2,1024]{1,0:T(2,128)S(1)} %get-tuple-element.70.refs_0_.refs_4_), channel_id=1, source_target_pairs={{0,3},{1,2},{2,1},{3,0},{4,7},{5,6},{6,5},{7,4},{8,11},{9,10},{10,... | collective-permute-start | bytes 24584 | tf_op jit(solution)/shard_map/ppermute | solution.py:331
  77.3 4.1 %collective-permute-start.12 = (f32[2,1024]{1,0:T(2,128)S(1)}, f32[2,1024]{1,0:T(2,128)S(1)}, u32[]{:S(2)}, u32[]{:S(2)}) collective-permute-start(f32[2,1024]{1,0:T(2,128)S(1)} %get-tuple-element.70.refs_0_.refs_4_), channel_id=1, source_target_pairs={{0,2},{1,3},{2,0},{3,1},{4,6},{5,7},{6,4},{7,5},{8,10},{9,11},{10,... | collective-permute-start | bytes 24584 | tf_op jit(solution)/shard_map/ppermute | solution.py:331
  79.6 3.7 %collective-permute-start.11 = (f32[2,1024]{1,0:T(2,128)S(1)}, f32[2,1024]{1,0:T(2,128)S(1)}, u32[]{:S(2)}, u32[]{:S(2)}) collective-permute-start(f32[2,1024]{1,0:T(2,128)S(1)} %get-tuple-element.70.refs_0_.refs_4_), channel_id=1, source_target_pairs={{0,1},{1,0},{2,3},{3,2},{4,5},{5,4},{6,7},{7,6},{8,9},{9,8},{10,11... | collective-permute-start | bytes 24584 | tf_op jit(solution)/shard_map/ppermute | solution.py:331
  84.7 14.0 %collective-permute-start.17 = (s16[528,256]{1,0:T(8,128)(2,1)S(1)}, s16[528,256]{1,0:T(8,128)(2,1)S(1)}, u32[]{:S(2)}, u32[]{:S(2)}) collective-permute-start(s16[528,256]{1,0:T(8,128)(2,1)S(1)} %upper.1.own_ref), channel_id=1, source_target_pairs={{0,4},{1,5},{2,6},{3,7},{4,0},{5,1},{6,2},{7,3},{8,12},{9,13},{10,... | collective-permute-start | bytes 811016 | tf_op jit(solution)/shard_map/ppermute | solution.py:331
  84.8 6.4 %collective-permute-start.14 = (s16[256,256]{1,0:T(8,128)(2,1)S(1)}, s16[256,256]{1,0:T(8,128)(2,1)S(1)}, u32[]{:S(2)}, u32[]{:S(2)}) collective-permute-start(s16[256,256]{1,0:T(8,128)(2,1)S(1)} %get-tuple-element.72), channel_id=1, source_target_pairs={{0,1},{1,0},{2,3},{3,2},{4,5},{5,4},{6,7},{7,6},{8,9},{9,8},{10,11... | collective-permute-start | bytes 393224 | tf_op jit(solution)/shard_map/ppermute | solution.py:331
  85.5 8.0 %collective-permute-start.15 = (s16[256,256]{1,0:T(8,128)(2,1)S(1)}, s16[256,256]{1,0:T(8,128)(2,1)S(1)}, u32[]{:S(2)}, u32[]{:S(2)}) collective-permute-start(s16[256,256]{1,0:T(8,128)(2,1)S(1)} %get-tuple-element.73), channel_id=1, source_target_pairs={{0,2},{1,3},{2,0},{3,1},{4,6},{5,7},{6,4},{7,5},{8,10},{9,11},{10,... | collective-permute-start | bytes 393224 | tf_op jit(solution)/shard_map/ppermute | solution.py:331
  87.5 11.2 %collective-permute-start.16 = (s16[256,256]{1,0:T(8,128)(2,1)S(1)}, s16[256,256]{1,0:T(8,128)(2,1)S(1)}, u32[]{:S(2)}, u32[]{:S(2)}) collective-permute-start(s16[256,256]{1,0:T(8,128)(2,1)S(1)} %get-tuple-element.74), channel_id=1, source_target_pairs={{0,3},{1,2},{2,1},{3,0},{4,7},{5,6},{6,5},{7,4},{8,11},{9,10},{10,... | collective-permute-start | bytes 393224 | tf_op jit(solution)/shard_map/ppermute | solution.py:331
  99.3 10.4 %collective-permute-start.20 = (s16[528,256]{1,0:T(8,128)(2,1)S(1)}, s16[528,256]{1,0:T(8,128)(2,1)S(1)}, u32[]{:S(2)}, u32[]{:S(2)}) collective-permute-start(s16[528,256]{1,0:T(8,128)(2,1)S(1)} %both.1.refs_0_), channel_id=1, source_target_pairs={{0,3},{1,2},{2,1},{3,0},{4,7},{5,6},{6,5},{7,4},{8,11},{9,10},{10,... | collective-permute-start | bytes 811016 | tf_op jit(solution)/shard_map/ppermute | solution.py:331
  99.4 13.5 %collective-permute-start.19 = (s16[528,256]{1,0:T(8,128)(2,1)S(1)}, s16[528,256]{1,0:T(8,128)(2,1)S(1)}, u32[]{:S(2)}, u32[]{:S(2)}) collective-permute-start(s16[528,256]{1,0:T(8,128)(2,1)S(1)} %both.1.refs_0_), channel_id=1, source_target_pairs={{0,2},{1,3},{2,0},{3,1},{4,6},{5,7},{6,4},{7,5},{8,10},{9,11},{10,... | collective-permute-start | bytes 811016 | tf_op jit(solution)/shard_map/ppermute | solution.py:331
  101.8 11.9 %collective-permute-start.18 = (s16[528,256]{1,0:T(8,128)(2,1)S(1)}, s16[528,256]{1,0:T(8,128)(2,1)S(1)}, u32[]{:S(2)}, u32[]{:S(2)}) collective-permute-start(s16[528,256]{1,0:T(8,128)(2,1)S(1)} %both.1.refs_0_), channel_id=1, source_target_pairs={{0,1},{1,0},{2,3},{3,2},{4,5},{5,4},{6,7},{7,6},{8,9},{9,8},{10,11... | collective-permute-start | bytes 811016 | tf_op jit(solution)/shard_map/ppermute | solution.py:331
Sparse Core Ops, SparseCore 0:
  9.6 37.1 all-gather.1

commit v6 on v5

--- a/solution.py
+++ b/solution.py
@@ -13,6 +13,7 @@
 CODE = 32000.0
 FLOOR = 1e-30
 VMEM_LIMIT = 16 * 1024 * 1024
+PACK_LIMIT = 56 * 1024 * 1024
 f32, bf16, i16, i32 = jnp.float32, jnp.bfloat16, jnp.int16, jnp.int32
 shape = jax.ShapeDtypeStruct
 VMEM = pl.BlockSpec(memory_space=pltpu.VMEM)
@@ -84,24 +85,29 @@
         copy.wait()
 
 
-def pack_kernel(chunks, q_ref, points_ref, *refs):
-    outs, sems = refs[:-1], refs[-1]
-    sources = [
-        points_ref.at[:, chunk((q_ref[0] ^ (k // chunks)) * chunks + k % chunks, BLOCK)] for k in range(len(outs))
-    ]
-    wait_all(start_all(sources, outs, sems))
-
-
-def prev_kernel(q_ref, prev_ref, small_ref, *refs):
-    h = (len(refs) - 5) // 2
-    outs, (next_ref, prev, head, sem, sems), held = refs[:h], refs[h : h + 5], refs[h + 5 :]
-    next_ref[0] = q_ref[0]
+def pack_kernel(chunks, me_ref, points_ref, cluster_ref, *refs):
+    outs, (head, sems, head_sems) = refs[:-3], refs[-3:]
+    rows = points_ref.shape[0]
+    h = len(outs) // chunks
+    q = me_ref[0] & (h - 1)
+    sources = [points_ref.at[:, chunk((q ^ (k // chunks)) * chunks + k % chunks, BLOCK)] for k in range(len(outs))]
+    copies = start_all(sources, [out.at[0:rows, :] for out in outs], sems)
+    cluster = cluster_ref[...]
+    head[...] = jnp.concatenate([cluster & (BLOCK - 1), (cluster - me_ref[1]) // BLOCK]).astype(f32).astype(bf16)
+    copies += start_all([head] * h, [out.at[rows:, :] for out in outs[::chunks]], head_sems)
+    wait_all(copies)
+
+
+def prev_kernel(me_ref, after_ref, prev_ref, parent_ref, *refs):
+    h = (len(refs) - 4) // 2
+    outs, (prev, head, sem, sems), held = refs[:h], refs[h : h + 4], refs[h + 4 :]
+    q = me_ref[0] & (h - 1)
     owned, width = prev.shape
     w = width // h
     copy = start(prev_ref, prev, sem)
-    known = small_ref.shape[0]
+    known = parent_ref.shape[0]
     head[...] = jnp.zeros_like(head)
-    head[0:known, :] = small_ref[...]
+    head[0:known, :] = parent_ref[...] - me_ref[2]
     copy.wait()
     exponent = exponent_of(jnp.max(jnp.abs(prev[...]), axis=1, keepdims=True))
     for j in range(owned // w):
@@ -109,42 +115,32 @@
         head[known + j : known + j + 1, :] = lanes.astype(i32)
     copies = []
     for m in range(h):
-        held[m][0:owned, :] = encode(prev[:, chunk(q_ref[0] ^ m, w)], exponent)
+        held[m][0:owned, :] = encode(prev[:, chunk(q ^ m, w)], exponent)
         held[m][owned:, :] = head[...].astype(i16)
         copies.append(start(held[m], outs[m], sems.at[m]))
     wait_all(copies)
 
 
-def prepare_kernel(blocks, n, me_ref, *refs):
-    arrived, (member_ref, place_ref, near_ref, far_ref, prev_ref, upper_ref, count) = refs[:-7], refs[-7:]
+def prepare_kernel(per, me_ref, *refs):
+    arrived, (member_ref, place_ref, near_ref, far_ref, count, heads, sems) = refs[:-7], refs[-7:]
     h = len(arrived)
-    rows, w = prev_ref.shape
-    owned = rows // h
-    upper_rows = upper_ref.shape[0]
-    me = me_ref[0]
-    lines, each = blocks * BLOCK // w, owned // w
+    rows = near_ref.shape[0]
+    blocks = place_ref.shape[0] // h
+    copies = start_all([a.at[blocks * BLOCK :, :] for a in arrived], [heads.at[m] for m in range(h)], sems)
     count[...] = jnp.zeros_like(count)
     centroid = lax.broadcasted_iota(i32, (BLOCK, BLOCK), 0)
     ones = jnp.ones((BLOCK, BLOCK), bf16)
-    parent_at = lax.broadcasted_iota(i32, (upper_rows, w), 0)
     for m in range(h):
-        head = arrived[m][owned:, :].astype(i32)
+        copies[m].wait()
+        head = heads[m].astype(f32)
         for i in range(blocks):
-            row, lane = i * BLOCK // w, i * BLOCK % w
-            ids = head[row : row + 1, lane : lane + BLOCK]
-            number = jnp.max(ids.astype(f32)).astype(i32) // BLOCK
-            place = number ^ (me * (owned // BLOCK))
+            number = jnp.max(head[blocks + i : blocks + i + 1, :]).astype(i32)
+            place = number ^ (me_ref[0] * per)
             place_ref[m * blocks + i] = place
-            member = jnp.where(centroid == ids - number * BLOCK, 1.0, 0.0).astype(bf16)
+            member = jnp.where(centroid == head[i : i + 1, :].astype(i32), 1.0, 0.0).astype(bf16)
             at = (m * blocks + i) * BLOCK
             member_ref[at : at + BLOCK, :] = member
             count[chunk(place, BLOCK), :] += dot(member, ones)
-        for j in range(each):
-            at = slice(m * owned + j * w, m * owned + (j + 1) * w)
-            parents = head[lines + j : lines + j + 1, :]
-            upper_ref[:, at] = jnp.where(parent_at == parents, 1.0, 0.0).astype(bf16)
-            exponent = to_column(head[lines + each + j : lines + each + j + 1, :].astype(f32))
-            prev_ref[at, :] = decode(arrived[m][j * w : (j + 1) * w, :], exponent)
     near_ref[...] = count[0:rows, :]
     for j in range(rows // BLOCK):
         far = count[rows + j * BLOCK : rows + (j + 1) * BLOCK, 0:1]
@@ -152,17 +148,34 @@
         far_ref[j : j + 1, :] = (to_lanes(high) * 64.0 + to_lanes(far - high * 64.0)).astype(i32)
 
 
+def previous_kernel(*refs):
+    arrived, (prev_ref, upper_ref) = refs[:-2], refs[-2:]
+    h = len(arrived)
+    rows, w = prev_ref.shape
+    owned = rows // h
+    each = owned // w
+    parent_at = lax.broadcasted_iota(i32, (upper_ref.shape[0], w), 0)
+    for m in range(h):
+        head = arrived[m][owned:, :].astype(i32)
+        for j in range(each):
+            at = slice(m * owned + j * w, m * owned + (j + 1) * w)
+            upper_ref[:, at] = jnp.where(parent_at == head[j : j + 1, :], 1.0, 0.0).astype(bf16)
+            exponent = to_column(head[each + j : each + j + 1, :].astype(f32))
+            prev_ref[at, :] = decode(arrived[m][j * w : (j + 1) * w, :], exponent)
+
+
 def sums_kernel(place_ref, member_ref, far_count_ref, *refs):
-    h = (len(refs) - 5) // 2
-    points, (acc_ref, code_ref), (code, head, sem), held = (
+    h = (len(refs) - 6) // 2
+    points, (acc_ref, code_ref, after_ref), (code, head, sem), held = (
         refs[:h],
-        refs[h : h + 2],
-        refs[h + 2 : h + 5],
-        refs[h + 5 :],
+        refs[h : h + 3],
+        refs[h + 3 : h + 6],
+        refs[h + 6 :],
     )
+    after_ref[0] = place_ref[0]
     rows = acc_ref.shape[0] // 2
     blocks = held[0].shape[0] // BLOCK
-    copies = start_all(points, held, sem)
+    copies = start_all([p.at[0 : blocks * BLOCK, :] for p in points], held, sem)
     acc_ref[...] = jnp.zeros_like(acc_ref)
     for m in range(h):
         copies[m].wait()
@@ -227,24 +240,25 @@
 
 def put_codes(values, code, head):
     rows, w = values.shape
+    size = min(rows, w)
     head[...] = jnp.zeros_like(head)
-    for j in range(rows // w):
-        at = slice(j * w, (j + 1) * w)
+    for j in range(rows // size):
+        at = slice(j * size, (j + 1) * size)
         exponent = exponent_of(jnp.max(jnp.abs(values[at, :]), axis=1, keepdims=True))
         code[at, :] = encode(values[at, :], exponent)
-        head[j : j + 1, :] = to_lanes(exponent).astype(i32)
+        head[j : j + 1, 0:size] = to_lanes(exponent).astype(i32)
     code[rows:, :] = head[...].astype(i16)
 
 
 def get_codes(code, j, rows, size):
     w = code.shape[1]
-    row, lane = j * size // w, j * size % w
+    row, lane = j * size // min(rows, w), j * size % min(rows, w)
     lanes = code[rows : rows + 16, :].astype(i32).astype(f32)[row : row + 1, lane : lane + size]
     return decode(code[j * size : (j + 1) * size, :], to_column(lanes))
 
 
 def upper_kernel(width, member_ref, x_ref, *refs):
-    stats, code_ref, (high, low, sums, code, head, sem) = refs[:-7], refs[-7], refs[-6:]
+    stats, outs, (high, low, sums, sems), held = refs[:-10], refs[-10:-8], refs[-8:-4], refs[-4:]
     h = len(stats)
     owned = x_ref.shape[0] // h
     for p in range(h):
@@ -255,9 +269,14 @@
         for j in range(0, owned, BLOCK):
             at = slice(p * owned + j, p * owned + j + BLOCK)
             high[at, :], low[at, :] = split(x_ref[at, :] * to_column(factor[:, j : j + BLOCK]))
-    sums[...] = dot(member_ref[...], high[...]) + dot(member_ref[...], low[...])
-    put_codes(sums, code, head)
-    start(code, code_ref, sem).wait()
+    rows = sums.shape[0]
+    copies = []
+    for k in range(2):
+        member = member_ref[k * rows : (k + 1) * rows, :]
+        sums[...] = dot(member, high[...]) + dot(member, low[...])
+        put_codes(sums, held[k], held[2 + k])
+        copies.append(start(held[k], outs[k], sems.at[k]))
+    wait_all(copies)
 
 
 def both_kernel(own_ref, far_ref, code_ref, own, far, sums, code, head, sems):
@@ -269,9 +288,10 @@
     start(code, code_ref, sems.at[0]).wait()
 
 
-def join_kernel(q_ref, *refs):
+def join_kernel(first, me_ref, *refs):
     h = (len(refs) - 4) // 2
-    parts, (out_ref, out, sems, out_sems), held = refs[:h], refs[h : h + 4], refs[h + 4 :]
+    parts, (out_ref, out, sems, out_sems), held = refs[:h], refs[-4 - h : -h], refs[-h:]
+    q = me_ref[0] & (h - 1)
     rows, width = out.shape
     w = width // h
     wait_all(start_all(parts, held, sems))
@@ -282,13 +302,15 @@
         square = sum(v * v for v in values)
         factor = lax.rsqrt(jnp.sum(square, axis=1, keepdims=True) / width + EPSILON)
         for m in range(h):
-            out[at, chunk(q_ref[0] ^ m, w)] = values[m] * factor
-        copies.append(start(out.at[at, :], out_ref.at[at, :], out_sems.at[j]))
+            out[at, chunk(q ^ m, w)] = values[m] * factor
+        there = out_ref.at[first + j * BLOCK : first + (j + 1) * BLOCK, :]
+        copies.append(start(out.at[at, :], there, out_sems.at[j]))
     wait_all(copies)
 
 
-def decode_kernel(q_ref, *refs):
+def decode_kernel(me_ref, *refs):
     h = (len(refs) - 1) // 2
+    q = me_ref[0] & (h - 1)
     codes, stats, out_ref = refs[:h], refs[h : 2 * h], refs[2 * h]
     rows, w = codes[0].shape
     width = h * w
@@ -301,11 +323,11 @@
         square = sum(v * v for v in values)
         factor = lax.rsqrt(jnp.sum(square, axis=1, keepdims=True) / width + EPSILON)
         for m in range(h):
-            out_ref[at, chunk(q_ref[0] ^ m, w)] = values[m] * factor
-
-
-def call(kernel, out_shape, **kw):
-    params = pltpu.CompilerParams(vmem_limit_bytes=VMEM_LIMIT)
+            out_ref[at, chunk(q ^ m, w)] = values[m] * factor
+
+
+def call(kernel, out_shape, limit=VMEM_LIMIT, **kw):
+    params = pltpu.CompilerParams(vmem_limit_bytes=limit)
     return pl.pallas_call(kernel, out_shape=out_shape, compiler_params=params, **kw)
 
 
@@ -321,11 +343,10 @@
     n = lax.axis_size("cent")
     h = n // 2
     dp = lax.axis_index("dp")
-    me = lax.axis_index("cent").astype(i32).reshape(1)
-    q = me & (h - 1)
     w = width // h
     chunks = w // BLOCK
     rows = h * owned
+    me = jnp.stack([lax.axis_index("cent").astype(i32), dp * (n * owned), dp * upper_rows])
 
     def swap(value, mask):
         return lax.ppermute(value, "cent", [(i, i ^ mask) for i in range(n)])
@@ -336,52 +357,40 @@
 
     table_rows = lax.all_gather(cent2_prev, "dp", axis=0, tiled=True)
 
-    small = jnp.concatenate([point_cluster - dp * (n * owned), parent - dp * upper_rows]).reshape(-1, w)
-    head = head_rows(point_rows + 2 * owned, w)
-    prevs = call(
-        prev_kernel,
-        [shape((owned + head, w), i16)] * h + [shape((1,), i32)],
-        in_specs=[SMEM, HBM, VMEM],
-        out_specs=[HBM] * h + [SMEM],
-        scratch_shapes=[pltpu.VMEM((owned, width), f32), pltpu.VMEM((head, w), i32), dma(), dma(h)]
-        + [pltpu.VMEM((owned + head, w), i16)] * h,
-        name="prev",
-    )(q, cent1_prev, small)
-    prevs, after_prev = swap_half(prevs[:h]), prevs[h]
+    first_shape = shape((point_rows + 2 * blocks, BLOCK), bf16)
     packed = call(
         functools.partial(pack_kernel, chunks),
-        [shape((point_rows, BLOCK), bf16)] * (h * chunks),
-        in_specs=[SMEM, HBM],
+        ([first_shape] + [shape((point_rows, BLOCK), bf16)] * (chunks - 1)) * h,
+        limit=PACK_LIMIT,
+        in_specs=[SMEM, HBM, VMEM],
         out_specs=[HBM] * (h * chunks),
-        scratch_shapes=[dma(h * chunks)],
+        scratch_shapes=[pltpu.VMEM((2 * blocks, BLOCK), bf16), dma(h * chunks), dma(h)],
         name="pack",
-    )(after_prev, points)
+    )(me, points, point_cluster.reshape(blocks, BLOCK))
     arrived = [swap_half(packed[c::chunks]) for c in range(chunks)]
 
-    member, place, near, far_count, prev, upper_member = call(
-        functools.partial(prepare_kernel, blocks, n),
+    member, place, near, far_count = call(
+        functools.partial(prepare_kernel, owned // BLOCK),
         [
             shape((h * point_rows, BLOCK), bf16),
             shape((h * blocks,), i32),
             shape((rows, BLOCK), f32),
             shape((rows // BLOCK, BLOCK), i32),
-            shape((rows, w), f32),
-            shape((upper_rows, rows), bf16),
         ],
-        in_specs=[SMEM] + [VMEM] * h,
-        out_specs=[VMEM, SMEM] + [VMEM] * 4,
-        scratch_shapes=[pltpu.VMEM((2 * rows, BLOCK), f32)],
+        in_specs=[SMEM] + [HBM] * h,
+        out_specs=[VMEM, SMEM] + [VMEM] * 2,
+        scratch_shapes=[pltpu.VMEM((2 * rows, BLOCK), f32), pltpu.VMEM((h, 2 * blocks, BLOCK), bf16), dma(h)],
         name="prepare",
-    )(me, *prevs)
+    )(me, *arrived[0])
 
     lines = rows + 2 * rows // BLOCK
-    accs, crossed = [], []
+    accs, crossed, after = [], [], None
     for c in range(chunks):
-        acc, code = call(
+        acc, code, ended = call(
             sums_kernel,
-            [shape((2 * rows, BLOCK), f32), shape((lines, BLOCK), i16)],
+            [shape((2 * rows, BLOCK), f32), shape((lines, BLOCK), i16), shape((1,), i32)],
             in_specs=[SMEM, VMEM, VMEM] + [HBM] * h,
-            out_specs=[VMEM, HBM],
+            out_specs=[VMEM, HBM, SMEM],
             scratch_shapes=[
                 pltpu.VMEM((lines, BLOCK), i16),
                 pltpu.VMEM((2 * rows // BLOCK, BLOCK), i32),
@@ -392,6 +401,25 @@
         )(place, member, far_count, *arrived[c])
         accs.append(acc)
         crossed.append(swap(code, h))
+        after = ended
+
+    head = head_rows(2 * owned, w)
+    prevs = call(
+        prev_kernel,
+        [shape((owned + head, w), i16)] * h,
+        in_specs=[SMEM, SMEM, HBM, VMEM],
+        out_specs=[HBM] * h,
+        scratch_shapes=[pltpu.VMEM((owned, width), f32), pltpu.VMEM((head, w), i32), dma(), dma(h)]
+        + [pltpu.VMEM((owned + head, w), i16)] * h,
+        name="prev",
+    )(me, after, cent1_prev, parent.reshape(owned // w, w))
+    prev, upper_member = call(
+        previous_kernel,
+        [shape((rows, w), f32), shape((upper_rows, rows), bf16)],
+        in_specs=[VMEM] * h,
+        out_specs=[VMEM] * 2,
+        name="previous",
+    )(*swap_half(prevs))
 
     points, table_rows = lax.optimization_barrier((points, table_rows))
     unit_points = rms_norm(points.astype(f32)).astype(bf16)
@@ -419,28 +447,35 @@
     stats = swap_half([stat] * h)
     back = swap_half(out[2:])
 
-    upper_shape = shape((upper_rows + head_rows(upper_rows, w), w), i16)
-    held_code = pltpu.VMEM(upper_shape.shape, i16)
-    put = [pltpu.VMEM((upper_rows, w), f32), held_code, pltpu.VMEM((upper_shape.shape[0] - upper_rows, w), i32)]
-    code = call(
+    part = upper_rows // 2
+    tail = head_rows(part, w)
+    code_shape = shape((part + tail, w), i16)
+    held_code, held_head = pltpu.VMEM(code_shape.shape, i16), pltpu.VMEM((tail, w), i32)
+    codes = call(
         functools.partial(upper_kernel, width),
-        upper_shape,
+        [code_shape] * 2,
         in_specs=[VMEM] * (h + 2),
-        out_specs=HBM,
-        scratch_shapes=[pltpu.VMEM((rows, w), bf16), pltpu.VMEM((rows, w), bf16)] + put + [dma()],
+        out_specs=[HBM] * 2,
+        scratch_shapes=[pltpu.VMEM((rows, w), bf16), pltpu.VMEM((rows, w), bf16), pltpu.VMEM((part, w), f32), dma(2)]
+        + [held_code] * 2
+        + [held_head] * 2,
         name="upper",
     )(upper_member, x, *stats)
-    far_code = swap(code, h)
-    code, back = lax.optimization_barrier((code, back))
-    code = call(
-        both_kernel,
-        upper_shape,
-        in_specs=[HBM, HBM],
-        out_specs=HBM,
-        scratch_shapes=[held_code, held_code] + put + [dma(2)],
-        name="both",
-    )(code, far_code)
-    parts = swap_half([code] * h)
+    far_codes = [swap(code, h) for code in codes]
+    parts = []
+    for k in range(2):
+        code = codes[k]
+        if k == 0:
+            code, back = lax.optimization_barrier((code, back))
+        code = call(
+            both_kernel,
+            code_shape,
+            in_specs=[HBM, HBM],
+            out_specs=HBM,
+            scratch_shapes=[held_code, held_code, pltpu.VMEM((part, w), f32), held_code, held_head, dma(2)],
+            name=f"both{k}",
+        )(code, far_codes[k])
+        parts.append(swap_half([code] * h))
 
     cent1_new = call(
         decode_kernel,
@@ -448,17 +483,24 @@
         in_specs=[SMEM] + [VMEM] * (2 * h),
         out_specs=VMEM,
         name="decode",
-    )(q, *back, *stats)
-    q, cent1_new = lax.optimization_barrier((q, cent1_new))
-    cent2_new = call(
-        join_kernel,
-        shape((upper_rows, width), f32),
-        in_specs=[SMEM] + [HBM] * h,
-        out_specs=HBM,
-        scratch_shapes=[pltpu.VMEM((upper_rows, width), f32), dma(h), dma(upper_rows // BLOCK)] + [held_code] * h,
-        name="join",
-    )(q, *parts)
-    return (cent1_new, cent2_new, point_score)
+    )(me, *back, *stats)
+    cent2_new = []
+    for k in range(2):
+        last = me
+        if k == 1:
+            last, cent1_new = lax.optimization_barrier((me, cent1_new))
+        cent2_new = [
+            call(
+                functools.partial(join_kernel, k * part),
+                shape((upper_rows, width), f32),
+                in_specs=[SMEM] + [HBM] * (h + k),
+                out_specs=HBM,
+                scratch_shapes=[pltpu.VMEM((part, width), f32), dma(h), dma(part // BLOCK)] + [held_code] * h,
+                input_output_aliases={h + 1: 0} if k else {},
+                name=f"join{k}",
+            )(last, *parts[k], *cent2_new)
+        ]
+    return (cent1_new, cent2_new[0], point_score)
 
 
 def solution(mesh):

time: 123 us -> 192 us (1.56)
  Pallas kernels: 19.2 us -> 92.2 us
  waiting for transfers between devices: 42.9 us -> 34.1 us
  starting transfers between devices: 28.4 us -> 35.3 us
  local copies, waits for them, and re-layouts: 6.18 us -> 4.12 us
    pallas_call x6 -> x9, Pallas kernels: 8.78 us -> 80.1 us  [the longest x1 65.4 us: shards(): call(functools.partial(pack_kernel, chunks), ([first_shape] + [shape((poi...]
    ppermute x21 -> x25, waiting for transfers between devices: 42.2 us -> 33.4 us  [swap(): return lax.ppermute(value, 'cent', [(i, i ^ mask) for i in range(n)])]
    ppermute x21 -> x25, starting transfers between devices: 28.3 us -> 35.3 us  [swap(): return lax.ppermute(value, 'cent', [(i, i ^ mask) for i in range(n)])]
    unnamed x24 -> x28, local copies, waits for them, and re-layouts: 5.57 us -> 3.52 us
  transfers between devices with their start and end apart: 22 -> 26, of which waited for: 13 -> 14; matrix products, arithmetic and copies ran while one was open for 10% -> 6% of each run, Pallas kernels for 10% -> 44%
where the time goes in v6:
time: 192 us
  Pallas kernels  92.2 us (48%)
  starting transfers between devices  35.3 us (18%)
  waiting for transfers between devices  34.1 us (18%)
  between operations  14.4 us (8%)
  other arithmetic  6.39 us (3%)
  matrix products  5.39 us (3%)
  local copies, waits for them, and re-layouts  4.12 us (2%)
    pallas_call x1, Pallas kernels, shards(): call(functools.partial(pack_kernel, chunks), ([first_shape] + [shape((poi...  65.4 us
    ppermute x25, starting transfers between devices, swap(): return lax.ppermute(value, 'cent', [(i, i ^ mask) for i in range(n)])  35.3 us
    ppermute x25, waiting for transfers between devices, swap(): return lax.ppermute(value, 'cent', [(i, i ^ mask) for i in range(n)])  33.4 us
    pallas_call x2, Pallas kernels, shards(): call(sums_kernel, [shape((2 * rows, BLOCK), f32), shape((lines, BLOCK), i...  6.75 us
    reduce_sum x2, other arithmetic, rms_norm(): jnp.mean(values * values, axis=-1, keepdims=True) + EPSILON  5.54 us
    dot_general x1, matrix products, shards(): lax.dot_general(unit_points, table_units, (((1,), (1,)), ((), ())), prefe...  5.39 us
    pallas_call x2, Pallas kernels, shards(): call(functools.partial(join_kernel, k * part), shape((upper_rows, width),...  5.23 us
  transfers between devices with their start and end apart: 26, of which 14 were waited for; matrix products, arithmetic and copies ran while one was open for 6% of the time, Pallas kernels for 44%

profile of v6, /device:TPU:0, one launch (start us, length us, event | category | flops | bytes accessed | tf_op | source)
XLA Modules:
  0.0 191.8 jit_solution(2629621125133498944)
XLA Ops:
  7.2 0.7 all-gather.2.cloned.1.call-update
  8.5 65.4 %pack.1 = (bf16[1040,128]{1,0:T(8,128)(2,1)}, bf16[1024,128]{1,0:T(8,128)(2,1)}, bf16[1040,128]{1,0:T(8,128)(2,1)}, bf16[1024,128]{1,0:T(8,128)(2,1)}, bf16[1040...) custom-call(s32[3]{0:T(128)} %pad_add_fusion.me_ref, ...), custom_call_target="tpu_custom_call" | custom-call | tf_op jit(solution)/shard_map/pack/pallas_call | solution.py:361
  74.0 3.0 %collective-permute-start = (bf16[1040,128]{1,0:T(8,128)(2,1)}, bf16[1040,128]{1,0:T(8,128)(2,1)S(1)}, u32[]{:S(2)}, u32[]{:S(2)}) collective-permute-start(bf16[1040,128]{1,0:T(8,128)(2,1)} %get-tuple-element.46), channel_id=1, source_target_pairs={{0,1},{1,0},{2,3},{3,2},{4,5},{5,4},{6,7},{7,6},{8,9},{9,8},{10,11... | collective-permute-start | bytes 798728 | tf_op jit(solution)/shard_map/ppermute | solution.py:352
  77.0 1.6 collective-permute-start.1
  78.6 1.9 collective-permute-start.3
  80.5 1.6 collective-permute-start.4
  82.1 3.1 %collective-permute-done.refs_1_ = bf16[1040,128]{1,0:T(8,128)(2,1)S(1)} collective-permute-done((bf16[1040,128]{1,0:T(8,128)(2,1)}, bf16[1040,128]{1,0:T(8,128)(2,1)S(1)}, u32[]{:S(2)}, u32[]{:S(2)}) %collective-permute-start) | collective-permute-done | bytes 266272 | tf_op jit(solution)/shard_map/ppermute | solution.py:352
  85.2 3.8 %collective-permute-start.5 = (bf16[1024,128]{1,0:T(8,128)(2,1)}, bf16[1024,128]{1,0:T(8,128)(2,1)S(1)}, u32[]{:S(2)}, u32[]{:S(2)}) collective-permute-start(bf16[1024,128]{1,0:T(8,128)(2,1)} %get-tuple-element.55), channel_id=1, source_target_pairs={{0,3},{1,2},{2,1},{3,0},{4,7},{5,6},{6,5},{7,4},{8,11},{9,10},{10,... | collective-permute-start | bytes 786440 | tf_op jit(solution)/shard_map/ppermute | solution.py:352
  88.9 2.8 %collective-permute-done.2.refs_3_ = bf16[1040,128]{1,0:T(8,128)(2,1)S(1)} collective-permute-done((bf16[1040,128]{1,0:T(8,128)(2,1)}, bf16[1040,128]{1,0:T(8,128)(2,1)S(1)}, u32[]{:S(2)}, u32[]{:S(2)}) %collective-permute-start.2) | collective-permute-done | bytes 266272 | tf_op jit(solution)/shard_map/ppermute | solution.py:352
  91.8 0.9 copy-done
  93.3 2.3 %prepare.1 = (bf16[4096,128]{1,0:T(8,128)(2,1)S(1)}, s32[32]{0:T(128)S(1)}, f32[1024,128]{1,0:T(8,128)S(1)}, s32[8,128]{1,0:T(8,128)S(1)}) custom-call(s32[3]{0:T(128)S(1)} %copy-done.8, bf16[1040,128]{1,0:T(8,128)(2,1)S(1)} %copy-done, bf16[1040,128]{1,0:T(8,128)(2,1)S(1)} %collective-permute-done.refs_1_, ...), custom_call_target="tpu_custom_call" | custom-call | tf_op jit(solution)/shard_map/prepare/pallas_call | solution.py:372
  95.6 2.3 %collective-permute-done.4.refs_2_ = bf16[1024,128]{1,0:T(8,128)(2,1)S(1)} collective-permute-done((bf16[1024,128]{1,0:T(8,128)(2,1)}, bf16[1024,128]{1,0:T(8,128)(2,1)S(1)}, u32[]{:S(2)}, u32[]{:S(2)}) %collective-permute-start.4) | collective-permute-done | bytes 262176 | tf_op jit(solution)/shard_map/ppermute | solution.py:352
  97.9 3.9 %collective-permute-done.5.refs_3_ = bf16[1024,128]{1,0:T(8,128)(2,1)S(1)} collective-permute-done((bf16[1024,128]{1,0:T(8,128)(2,1)}, bf16[1024,128]{1,0:T(8,128)(2,1)S(1)}, u32[]{:S(2)}, u32[]{:S(2)}) %collective-permute-start.5) | collective-permute-done | bytes 262176 | tf_op jit(solution)/shard_map/ppermute | solution.py:352
  101.9 0.9 copy-done.7
  102.8 3.4 %sums1.1 = (f32[2048,128]{1,0:T(8,128)S(1)}, s16[1040,128]{1,0:T(8,128)(2,1)}, s32[1]{0:T(128)}) custom-call(s32[32]{0:T(128)S(1)} %get-tuple-element.49.place_ref, bf16[4096,128]{1,0:T(8,128)(2,1)S(1)} %get-tuple-element.50.member_ref, s32[8,128]{1,0:T(8,128)S(1)} %get-tuple-element.51.far_count_ref, bf16[1024,128]{1,0:T(8,128)(2,1)S(1)} %copy-done.7, ...), custom_call_target="tpu_custom_call" | custom-call | tf_op jit(solution)/shard_map/sums1/pallas_call | solution.py:389
  106.2 2.5 %prev.1 = (s16[272,256]{1,0:T(8,128)(2,1)S(1)}, s16[272,256]{1,0:T(8,128)(2,1)S(1)}, s16[272,256]{1,0:T(8,128)(2,1)S(1)}, s16[272,256]{1,0:T(8,128)(2,1)S(1)}) custom-call(s32[3]{0:T(128)S(1)} %copy-done.8, s32[1]{0:T(128)} %get-tuple-element.56.after_ref, f32[256,1024]{1,0:T(8,128)S(1)} %copy-done.2, s32[1,256]{1,0:T(1,128)S(1)} %bitcast.9), custom_call_target="tpu_custom_call" | custom-call | tf_op jit(solution)/shard_map/prev/pallas_call | solution.py:407
  108.7 1.7 collective-permute-start.6
  110.4 1.6 collective-permute-start.7
  112.5 3.4 %sums0.1 = (f32[2048,128]{1,0:T(8,128)S(1)}, s16[1040,128]{1,0:T(8,128)(2,1)}, s32[1]{0:T(128)}) custom-call(s32[32]{0:T(128)S(1)} %get-tuple-element.49.place_ref, bf16[4096,128]{1,0:T(8,128)(2,1)S(1)} %get-tuple-element.50.member_ref, s32[8,128]{1,0:T(8,128)S(1)} %get-tuple-element.51.far_count_ref, bf16[1040,128]{1,0:T(8,128)(2,1)S(1)} %copy-done.1, ...), custom_call_target="tpu_custom_call" | custom-call | tf_op jit(solution)/shard_map/sums0/pallas_call | solution.py:389
  115.9 2.8 %collective-permute-start.9 = (s16[1040,128]{1,0:T(8,128)(2,1)}, s16[1040,128]{1,0:T(8,128)(2,1)S(1)}, u32[]{:S(2)}, u32[]{:S(2)}) collective-permute-start(s16[1040,128]{1,0:T(8,128)(2,1)} %get-tuple-element.69), channel_id=1, source_target_pairs={{0,4},{1,5},{2,6},{3,7},{4,0},{5,1},{6,2},{7,3},{8,12},{9,13},{10,... | collective-permute-start | bytes 798728 | tf_op jit(solution)/shard_map/ppermute | solution.py:352
  119.4 1.0 copy-done.3
  120.4 2.2 %fusion.3 = f32[1024]{0:T(1024)S(1)} fusion(bf16[1024,1024]{1,0:T(8,128)(2,1)} %points_ref.1), kind=kLoop, calls=%fused_computation.8 | loop fusion | flops 3144704 | bytes 2101248 | tf_op jit(solution)/shard_map/reduce_sum | solution.py:25
  122.6 3.3 %fusion = f32[2048]{0:T(1024)S(1)} fusion(bf16[2048,1024]{1,0:T(8,128)(2,1)} %all-gather.2.cloned.1.call-done), kind=kLoop, calls=%fused_computation.2 | loop fusion | flops 6289408 | bytes 4202496 | tf_op jit(solution)/shard_map/reduce_sum | solution.py:25
  126.0 5.4 %fusion.2 = f32[1024]{0:T(1024)S(1)} fusion(bf16[2048,1024]{1,0:T(8,128)(2,1)S(1)} %copy-done.12, f32[8,2048]{1,0:T(8,128)S(1)} %convert_element_type.24, f32[2048]{0:T(1024)S(1)} %add_rsqrt_fusion, bf16[1024,1024]{1,0:T(8,128)(2,1)S(1)} %copy-done.11, f32[1024]{0:T(1024)S(1)} %add_rsqrt_fusion.1), kind=kOutput, calls=%fused_computation.5 | convolution fusion | flops 4310694912 | bytes 6373376 | tf_op jit(solution)/shard_map/dot_general | solution.py:427
  132.0 4.7 %collective-permute-done.9.refs_2_ = s16[1040,128]{1,0:T(8,128)(2,1)S(1)} collective-permute-done((s16[1040,128]{1,0:T(8,128)(2,1)}, s16[1040,128]{1,0:T(8,128)(2,1)S(1)}, u32[]{:S(2)}, u32[]{:S(2)}) %collective-permute-start.9) | collective-permute-done | bytes 266272 | tf_op jit(solution)/shard_map/ppermute | solution.py:352
  136.7 4.0 %collective-permute-done.10.refs_3_ = s16[1040,128]{1,0:T(8,128)(2,1)} collective-permute-done((s16[1040,128]{1,0:T(8,128)(2,1)}, s16[1040,128]{1,0:T(8,128)(2,1)}, u32[]{:S(2)}, u32[]{:S(2)}) %collective-permute-start.10) | collective-permute-done | bytes 266272 | tf_op jit(solution)/shard_map/ppermute | solution.py:352
  140.7 3.4 %refresh.1 = (f32[1024,256]{1,0:T(8,128)S(1)}, f32[2,1024]{1,0:T(2,128)S(1)}, s16[256,256]{1,0:T(8,128)(2,1)S(1)}, s16[256,256]{1,0:T(8,128)(2,1)S(1)}, s16[256,...) custom-call(f32[1024,128]{1,0:T(8,128)S(1)} %copy-done.6, f32[1024,256]{1,0:T(8,128)S(1)} %copy-done.4, ...), custom_call_target="tpu_custom_call" | custom-call | tf_op jit(solution)/shard_map/refresh/pallas_call | solution.py:436
  144.1 1.5 collective-permute-start.13
  145.7 1.4 collective-permute-start.12
  147.7 1.1 collective-permute-done.13.refs_3_.refs_7_
  149.3 1.4 collective-permute-done.11.refs_1_.refs_5_
  150.7 2.3 %upper.1 = (s16[272,256]{1,0:T(8,128)(2,1)S(1)}, s16[272,256]{1,0:T(8,128)(2,1)S(1)}) custom-call(bf16[512,1024]{1,0:T(8,128)(2,1)S(1)} %get-tuple-element.61.member_ref, f32[1024,256]{1,0:T(8,128)S(1)} %get-tuple-element.71.x_ref, f32[2,1024]{1,0:T(2,128)S(1)} %get-tuple-element.72.refs_0_.refs_4_, f32[2,1024]{1,0:T(2,128)S(1)} %collective-permute-done.11.refs_1_.refs_5_, ...), custom_call_target="tpu_custom_call" | custom-call | tf_op jit(solution)/shard_map/upper/pallas_call | solution.py:454
  153.0 2.1 %collective-permute-start.21 = (s16[272,256]{1,0:T(8,128)(2,1)S(1)}, s16[272,256]{1,0:T(8,128)(2,1)S(1)}, u32[]{:S(2)}, u32[]{:S(2)}) collective-permute-start(s16[272,256]{1,0:T(8,128)(2,1)S(1)} %get-tuple-element.85.own_ref), channel_id=1, source_target_pairs={{0,4},{1,5},{2,6},{3,7},{4,0},{5,1},{6,2},{7,3},{8,12},{9,13},{10,... | collective-permute-start | bytes 417800 | tf_op jit(solution)/shard_map/ppermute | solution.py:352
  155.8 1.9 collective-permute-start.15
  157.6 1.0 collective-permute-start.16
  158.6 0.9 collective-permute-start.17
  160.1 4.7 %collective-permute-done.15.refs_2_ = s16[256,256]{1,0:T(8,128)(2,1)S(1)} collective-permute-done((s16[256,256]{1,0:T(8,128)(2,1)S(1)}, s16[256,256]{1,0:T(8,128)(2,1)S(1)}, u32[]{:S(2)}, u32[]{:S(2)}) %collective-permute-start.15) | collective-permute-done | bytes 131104 | tf_op jit(solution)/shard_map/ppermute | solution.py:352
  164.8 2.5 %collective-permute-done.16.refs_3_ = s16[256,256]{1,0:T(8,128)(2,1)S(1)} collective-permute-done((s16[256,256]{1,0:T(8,128)(2,1)S(1)}, s16[256,256]{1,0:T(8,128)(2,1)S(1)}, u32[]{:S(2)}, u32[]{:S(2)}) %collective-permute-start.16) | collective-permute-done | bytes 131104 | tf_op jit(solution)/shard_map/ppermute | solution.py:352
  167.4 0.9 both0.1.refs_0_
  168.8 2.0 %collective-permute-start.23 = (s16[272,256]{1,0:T(8,128)(2,1)S(1)}, s16[272,256]{1,0:T(8,128)(2,1)S(1)}, u32[]{:S(2)}, u32[]{:S(2)}) collective-permute-start(s16[272,256]{1,0:T(8,128)(2,1)S(1)} %both0.1.refs_0_), channel_id=1, source_target_pairs={{0,2},{1,3},{2,0},{3,1},{4,6},{5,7},{6,4},{7,5},{8,10},{9,11},{10,... | collective-permute-start | bytes 417800 | tf_op jit(solution)/shard_map/ppermute | solution.py:352
  170.8 1.1 collective-permute-start.22
  171.8 0.9 both1.1.refs_0_
  173.3 2.0 %collective-permute-start.19 = (s16[272,256]{1,0:T(8,128)(2,1)S(1)}, s16[272,256]{1,0:T(8,128)(2,1)S(1)}, u32[]{:S(2)}, u32[]{:S(2)}) collective-permute-start(s16[272,256]{1,0:T(8,128)(2,1)S(1)} %both1.1.refs_0_), channel_id=1, source_target_pairs={{0,2},{1,3},{2,0},{3,1},{4,6},{5,7},{6,4},{7,5},{8,10},{9,11},{10,... | collective-permute-start | bytes 417800 | tf_op jit(solution)/shard_map/ppermute | solution.py:352
  175.5 0.8 collective-permute-start.18
  176.3 1.9 decode.1
  178.2 1.5 collective-permute-done.22.refs_1_
  179.7 2.6 %join0.1.refs_4_ = f32[512,1024]{1,0:T(8,128)} custom-call(s32[3]{0:T(128)S(1)} %copy-done.9, s16[272,256]{1,0:T(8,128)(2,1)S(1)} %both0.1.refs_0_, s16[272,256]{1,0:T(8,128)(2,1)S(1)} %collective-permute-done.22.refs_1_, s16[272,256]{1,0:T(8,128)(2,1)S(1)} %collective-permute-done.23.refs_2_, s16[272,256]{1,0:T(8,128)(2,1)S(1)} %collective-permute-done.24.refs_3_), custom_call_target="tpu_custom_call" | custom-call | tf_op jit(solution)/shard_map/join0/pallas_call | solution.py:493
  182.3 2.6 %join1.1 = f32[512,1024]{1,0:T(8,128)} custom-call(s32[3]{0:T(128)S(1)} %copy-done.9, s16[272,256]{1,0:T(8,128)(2,1)S(1)} %both1.1.refs_0_, s16[272,256]{1,0:T(8,128)(2,1)S(1)} %collective-permute-done.18.refs_1_, s16[272,256]{1,0:T(8,128)(2,1)S(1)} %collective-permute-done.19.refs_2_, ...), custom_call_target="tpu_custom_call", output_to_operand_aliasing={{}: (5, {})} | custom-call | tf_op jit(solution)/shard_map/join1/pallas_call | solution.py:493
  (56 shorter events, 6.9 us)
Async XLA Ops:
  7.2 99.0 %copy-start.10 = (s32[256]{0:T(256)S(1)}, s32[256]{0:T(256)}, u32[]{:S(2)}) copy-start(s32[256]{0:T(256)} %param.10) | copy-start | bytes 3076
  7.2 99.0 %copy-start.2 = (f32[256,1024]{1,0:T(8,128)S(1)}, f32[256,1024]{1,0:T(8,128)}, u32[]{:S(2)}) copy-start(f32[256,1024]{1,0:T(8,128)} %prev_ref.1) | copy-start | bytes 3145732
  7.2 105.1 %copy-start.13 = (s32[8,8]{1,0:T(8,128)S(1)}, s32[8,8]{1,0:T(8,128)}, u32[]{:S(2)}) copy-start(s32[8,8]{1,0:T(8,128)} %param.8) | copy-start | bytes 772
  7.2 113.2 %all-gather.2.cloned.1.call-start = ((), (), s32[]{:S(2)}) async-start(), calls=%async_computation | async-start | bytes 5242880 | tf_op jit(solution)/shard_map/all_gather | solution.py:358
  74.0 11.2 %collective-permute-start = (bf16[1040,128]{1,0:T(8,128)(2,1)}, bf16[1040,128]{1,0:T(8,128)(2,1)S(1)}, u32[]{:S(2)}, u32[]{:S(2)}) collective-permute-start(bf16[1040,128]{1,0:T(8,128)(2,1)} %get-tuple-element.46), channel_id=1, source_target_pairs={{0,1},{1,0},{2,3},{3,2},{4,5},{5,4},{6,7},{7,6},{8,9},{9,8},{10,11... | collective-permute-start | bytes 798728 | tf_op jit(solution)/shard_map/ppermute | solution.py:352
  77.0 11.9 %collective-permute-start.1 = (bf16[1040,128]{1,0:T(8,128)(2,1)}, bf16[1040,128]{1,0:T(8,128)(2,1)S(1)}, u32[]{:S(2)}, u32[]{:S(2)}) collective-permute-start(bf16[1040,128]{1,0:T(8,128)(2,1)} %get-tuple-element.47), channel_id=1, source_target_pairs={{0,2},{1,3},{2,0},{3,1},{4,6},{5,7},{6,4},{7,5},{8,10},{9,11},{10,... | collective-permute-start | bytes 798728 | tf_op jit(solution)/shard_map/ppermute | solution.py:352
  78.6 13.2 %collective-permute-start.2 = (bf16[1040,128]{1,0:T(8,128)(2,1)}, bf16[1040,128]{1,0:T(8,128)(2,1)S(1)}, u32[]{:S(2)}, u32[]{:S(2)}) collective-permute-start(bf16[1040,128]{1,0:T(8,128)(2,1)} %get-tuple-element.48), channel_id=1, source_target_pairs={{0,3},{1,2},{2,1},{3,0},{4,7},{5,6},{6,5},{7,4},{8,11},{9,10},{10,... | collective-permute-start | bytes 798728 | tf_op jit(solution)/shard_map/ppermute | solution.py:352
  78.6 17.0 %collective-permute-start.3 = (bf16[1024,128]{1,0:T(8,128)(2,1)}, bf16[1024,128]{1,0:T(8,128)(2,1)S(1)}, u32[]{:S(2)}, u32[]{:S(2)}) collective-permute-start(bf16[1024,128]{1,0:T(8,128)(2,1)} %get-tuple-element.53), channel_id=1, source_target_pairs={{0,1},{1,0},{2,3},{3,2},{4,5},{5,4},{6,7},{7,6},{8,9},{9,8},{10,11... | collective-permute-start | bytes 786440 | tf_op jit(solution)/shard_map/ppermute | solution.py:352
  80.5 17.4 %collective-permute-start.4 = (bf16[1024,128]{1,0:T(8,128)(2,1)}, bf16[1024,128]{1,0:T(8,128)(2,1)S(1)}, u32[]{:S(2)}, u32[]{:S(2)}) collective-permute-start(bf16[1024,128]{1,0:T(8,128)(2,1)} %get-tuple-element.54), channel_id=1, source_target_pairs={{0,2},{1,3},{2,0},{3,1},{4,6},{5,7},{6,4},{7,5},{8,10},{9,11},{10,... | collective-permute-start | bytes 786440 | tf_op jit(solution)/shard_map/ppermute | solution.py:352
  85.2 16.7 %collective-permute-start.5 = (bf16[1024,128]{1,0:T(8,128)(2,1)}, bf16[1024,128]{1,0:T(8,128)(2,1)S(1)}, u32[]{:S(2)}, u32[]{:S(2)}) collective-permute-start(bf16[1024,128]{1,0:T(8,128)(2,1)} %get-tuple-element.55), channel_id=1, source_target_pairs={{0,3},{1,2},{2,1},{3,0},{4,7},{5,6},{6,5},{7,4},{8,11},{9,10},{10,... | collective-permute-start | bytes 786440 | tf_op jit(solution)/shard_map/ppermute | solution.py:352
  91.8 1.0 copy-start
  92.7 0.6 copy-start.8
  93.3 19.2 %copy-start.1 = (bf16[1040,128]{1,0:T(8,128)(2,1)S(1)}, bf16[1040,128]{1,0:T(8,128)(2,1)}, u32[]{:S(2)}) copy-start(bf16[1040,128]{1,0:T(8,128)(2,1)} %get-tuple-element.45.refs_0_) | copy-start | bytes 798724
  95.6 23.3 %copy-start.5 = (f32[1024,128]{1,0:T(8,128)}, f32[1024,128]{1,0:T(8,128)S(1)}, u32[]{:S(2)}) copy-start(f32[1024,128]{1,0:T(8,128)S(1)} %get-tuple-element.65.near_ref) | copy-start | bytes 1572868
  101.9 1.0 copy-start.7
  108.7 10.2 %collective-permute-start.6 = (s16[272,256]{1,0:T(8,128)(2,1)S(1)}, s16[272,256]{1,0:T(8,128)(2,1)S(1)}, u32[]{:S(2)}, u32[]{:S(2)}) collective-permute-start(s16[272,256]{1,0:T(8,128)(2,1)S(1)} %get-tuple-element.58), channel_id=1, source_target_pairs={{0,1},{1,0},{2,3},{3,2},{4,5},{5,4},{6,7},{7,6},{8,9},{9,8},{10,11... | collective-permute-start | bytes 417800 | tf_op jit(solution)/shard_map/ppermute | solution.py:352
  110.4 8.5 %collective-permute-start.7 = (s16[272,256]{1,0:T(8,128)(2,1)S(1)}, s16[272,256]{1,0:T(8,128)(2,1)S(1)}, u32[]{:S(2)}, u32[]{:S(2)}) collective-permute-start(s16[272,256]{1,0:T(8,128)(2,1)S(1)} %get-tuple-element.59), channel_id=1, source_target_pairs={{0,2},{1,3},{2,0},{3,1},{4,6},{5,7},{6,4},{7,5},{8,10},{9,11},{10,... | collective-permute-start | bytes 417800 | tf_op jit(solution)/shard_map/ppermute | solution.py:352
  112.0 6.9 %collective-permute-start.8 = (s16[272,256]{1,0:T(8,128)(2,1)S(1)}, s16[272,256]{1,0:T(8,128)(2,1)S(1)}, u32[]{:S(2)}, u32[]{:S(2)}) collective-permute-start(s16[272,256]{1,0:T(8,128)(2,1)S(1)} %get-tuple-element.60), channel_id=1, source_target_pairs={{0,3},{1,2},{2,1},{3,0},{4,7},{5,6},{6,5},{7,4},{8,11},{9,10},{10,... | collective-permute-start | bytes 417800 | tf_op jit(solution)/shard_map/ppermute | solution.py:352
  115.9 20.8 %collective-permute-start.9 = (s16[1040,128]{1,0:T(8,128)(2,1)}, s16[1040,128]{1,0:T(8,128)(2,1)S(1)}, u32[]{:S(2)}, u32[]{:S(2)}) collective-permute-start(s16[1040,128]{1,0:T(8,128)(2,1)} %get-tuple-element.69), channel_id=1, source_target_pairs={{0,4},{1,5},{2,6},{3,7},{4,0},{5,1},{6,2},{7,3},{8,12},{9,13},{10,... | collective-permute-start | bytes 798728 | tf_op jit(solution)/shard_map/ppermute | solution.py:352
  118.7 22.0 %collective-permute-start.10 = (s16[1040,128]{1,0:T(8,128)(2,1)}, s16[1040,128]{1,0:T(8,128)(2,1)}, u32[]{:S(2)}, u32[]{:S(2)}) collective-permute-start(s16[1040,128]{1,0:T(8,128)(2,1)} %get-tuple-element.70), channel_id=1, source_target_pairs={{0,4},{1,5},{2,6},{3,7},{4,0},{5,1},{6,2},{7,3},{8,12},{9,13},{10,... | collective-permute-start | bytes 798728 | tf_op jit(solution)/shard_map/ppermute | solution.py:352
  119.4 1.0 copy-start.3
  120.4 5.6 %copy-start.11 = (bf16[1024,1024]{1,0:T(8,128)(2,1)S(1)}, bf16[1024,1024]{1,0:T(8,128)(2,1)}, u32[]{:S(2)}) copy-start(bf16[1024,1024]{1,0:T(8,128)(2,1)} %points_ref.1) | copy-start | bytes 6291460
  120.4 5.6 %copy-start.12 = (bf16[2048,1024]{1,0:T(8,128)(2,1)S(1)}, bf16[2048,1024]{1,0:T(8,128)(2,1)}, u32[]{:S(2)}) copy-start(bf16[2048,1024]{1,0:T(8,128)(2,1)} %all-gather.2.cloned.1.call-done) | copy-start | bytes 12582916
  126.0 14.7 %copy-start.4 = (f32[1024,256]{1,0:T(8,128)S(1)}, f32[1024,256]{1,0:T(8,128)}, u32[]{:S(2)}) copy-start(f32[1024,256]{1,0:T(8,128)} %copy-done.3) | copy-start | bytes 3145732
  126.0 14.7 %copy-start.6 = (f32[1024,128]{1,0:T(8,128)S(1)}, f32[1024,128]{1,0:T(8,128)}, u32[]{:S(2)}) copy-start(f32[1024,128]{1,0:T(8,128)} %copy-done.5) | copy-start | bytes 1572868
  131.4 44.9 %copy-start.9 = (s32[3]{0:T(128)S(1)}, s32[3]{0:T(128)}, u32[]{:S(2)}) copy-start(s32[3]{0:T(128)} %pad_add_fusion.me_ref) | copy-start | bytes 40
  144.1 4.6 %collective-permute-start.13 = (f32[2,1024]{1,0:T(2,128)S(1)}, f32[2,1024]{1,0:T(2,128)S(1)}, u32[]{:S(2)}, u32[]{:S(2)}) collective-permute-start(f32[2,1024]{1,0:T(2,128)S(1)} %get-tuple-element.72.refs_0_.refs_4_), channel_id=1, source_target_pairs={{0,3},{1,2},{2,1},{3,0},{4,7},{5,6},{6,5},{7,4},{8,11},{9,10},{10,... | collective-permute-start | bytes 24584 | tf_op jit(solution)/shard_map/ppermute | solution.py:352
  145.7 3.7 %collective-permute-start.12 = (f32[2,1024]{1,0:T(2,128)S(1)}, f32[2,1024]{1,0:T(2,128)S(1)}, u32[]{:S(2)}, u32[]{:S(2)}) collective-permute-start(f32[2,1024]{1,0:T(2,128)S(1)} %get-tuple-element.72.refs_0_.refs_4_), channel_id=1, source_target_pairs={{0,2},{1,3},{2,0},{3,1},{4,6},{5,7},{6,4},{7,5},{8,10},{9,11},{10,... | collective-permute-start | bytes 24584 | tf_op jit(solution)/shard_map/ppermute | solution.py:352
  147.0 3.7 %collective-permute-start.11 = (f32[2,1024]{1,0:T(2,128)S(1)}, f32[2,1024]{1,0:T(2,128)S(1)}, u32[]{:S(2)}, u32[]{:S(2)}) collective-permute-start(f32[2,1024]{1,0:T(2,128)S(1)} %get-tuple-element.72.refs_0_.refs_4_), channel_id=1, source_target_pairs={{0,1},{1,0},{2,3},{3,2},{4,5},{5,4},{6,7},{7,6},{8,9},{9,8},{10,11... | collective-permute-start | bytes 24584 | tf_op jit(solution)/shard_map/ppermute | solution.py:352
  153.0 14.3 %collective-permute-start.21 = (s16[272,256]{1,0:T(8,128)(2,1)S(1)}, s16[272,256]{1,0:T(8,128)(2,1)S(1)}, u32[]{:S(2)}, u32[]{:S(2)}) collective-permute-start(s16[272,256]{1,0:T(8,128)(2,1)S(1)} %get-tuple-element.85.own_ref), channel_id=1, source_target_pairs={{0,4},{1,5},{2,6},{3,7},{4,0},{5,1},{6,2},{7,3},{8,12},{9,13},{10,... | collective-permute-start | bytes 417800 | tf_op jit(solution)/shard_map/ppermute | solution.py:352
  155.1 5.0 %collective-permute-start.14 = (s16[256,256]{1,0:T(8,128)(2,1)S(1)}, s16[256,256]{1,0:T(8,128)(2,1)S(1)}, u32[]{:S(2)}, u32[]{:S(2)}) collective-permute-start(s16[256,256]{1,0:T(8,128)(2,1)S(1)} %get-tuple-element.75), channel_id=1, source_target_pairs={{0,1},{1,0},{2,3},{3,2},{4,5},{5,4},{6,7},{7,6},{8,9},{9,8},{10,11... | collective-permute-start | bytes 393224 | tf_op jit(solution)/shard_map/ppermute | solution.py:352
  155.8 9.1 %collective-permute-start.15 = (s16[256,256]{1,0:T(8,128)(2,1)S(1)}, s16[256,256]{1,0:T(8,128)(2,1)S(1)}, u32[]{:S(2)}, u32[]{:S(2)}) collective-permute-start(s16[256,256]{1,0:T(8,128)(2,1)S(1)} %get-tuple-element.76), channel_id=1, source_target_pairs={{0,2},{1,3},{2,0},{3,1},{4,6},{5,7},{6,4},{7,5},{8,10},{9,11},{10,... | collective-permute-start | bytes 393224 | tf_op jit(solution)/shard_map/ppermute | solution.py:352
  157.6 9.7 %collective-permute-start.16 = (s16[256,256]{1,0:T(8,128)(2,1)S(1)}, s16[256,256]{1,0:T(8,128)(2,1)S(1)}, u32[]{:S(2)}, u32[]{:S(2)}) collective-permute-start(s16[256,256]{1,0:T(8,128)(2,1)S(1)} %get-tuple-element.77), channel_id=1, source_target_pairs={{0,3},{1,2},{2,1},{3,0},{4,7},{5,6},{6,5},{7,4},{8,11},{9,10},{10,... | collective-permute-start | bytes 393224 | tf_op jit(solution)/shard_map/ppermute | solution.py:352
  158.6 13.2 %collective-permute-start.17 = (s16[272,256]{1,0:T(8,128)(2,1)S(1)}, s16[272,256]{1,0:T(8,128)(2,1)S(1)}, u32[]{:S(2)}, u32[]{:S(2)}) collective-permute-start(s16[272,256]{1,0:T(8,128)(2,1)S(1)} %get-tuple-element.84.own_ref), channel_id=1, source_target_pairs={{0,4},{1,5},{2,6},{3,7},{4,0},{5,1},{6,2},{7,3},{8,12},{9,13},{10,... | collective-permute-start | bytes 417800 | tf_op jit(solution)/shard_map/ppermute | solution.py:352
  168.3 7.2 %collective-permute-start.24 = (s16[272,256]{1,0:T(8,128)(2,1)S(1)}, s16[272,256]{1,0:T(8,128)(2,1)S(1)}, u32[]{:S(2)}, u32[]{:S(2)}) collective-permute-start(s16[272,256]{1,0:T(8,128)(2,1)S(1)} %both0.1.refs_0_), channel_id=1, source_target_pairs={{0,3},{1,2},{2,1},{3,0},{4,7},{5,6},{6,5},{7,4},{8,11},{9,10},{10,... | collective-permute-start | bytes 417800 | tf_op jit(solution)/shard_map/ppermute | solution.py:352
  168.8 9.5 %collective-permute-start.23 = (s16[272,256]{1,0:T(8,128)(2,1)S(1)}, s16[272,256]{1,0:T(8,128)(2,1)S(1)}, u32[]{:S(2)}, u32[]{:S(2)}) collective-permute-start(s16[272,256]{1,0:T(8,128)(2,1)S(1)} %both0.1.refs_0_), channel_id=1, source_target_pairs={{0,2},{1,3},{2,0},{3,1},{4,6},{5,7},{6,4},{7,5},{8,10},{9,11},{10,... | collective-permute-start | bytes 417800 | tf_op jit(solution)/shard_map/ppermute | solution.py:352
  170.8 8.9 %collective-permute-start.22 = (s16[272,256]{1,0:T(8,128)(2,1)S(1)}, s16[272,256]{1,0:T(8,128)(2,1)S(1)}, u32[]{:S(2)}, u32[]{:S(2)}) collective-permute-start(s16[272,256]{1,0:T(8,128)(2,1)S(1)} %both0.1.refs_0_), channel_id=1, source_target_pairs={{0,1},{1,0},{2,3},{3,2},{4,5},{5,4},{6,7},{7,6},{8,9},{9,8},{10,11... | collective-permute-start | bytes 417800 | tf_op jit(solution)/shard_map/ppermute | solution.py:352
  172.8 9.5 %collective-permute-start.20 = (s16[272,256]{1,0:T(8,128)(2,1)S(1)}, s16[272,256]{1,0:T(8,128)(2,1)S(1)}, u32[]{:S(2)}, u32[]{:S(2)}) collective-permute-start(s16[272,256]{1,0:T(8,128)(2,1)S(1)} %both1.1.refs_0_), channel_id=1, source_target_pairs={{0,3},{1,2},{2,1},{3,0},{4,7},{5,6},{6,5},{7,4},{8,11},{9,10},{10,... | collective-permute-start | bytes 417800 | tf_op jit(solution)/shard_map/ppermute | solution.py:352
  173.3 9.1 %collective-permute-start.19 = (s16[272,256]{1,0:T(8,128)(2,1)S(1)}, s16[272,256]{1,0:T(8,128)(2,1)S(1)}, u32[]{:S(2)}, u32[]{:S(2)}) collective-permute-start(s16[272,256]{1,0:T(8,128)(2,1)S(1)} %both1.1.refs_0_), channel_id=1, source_target_pairs={{0,2},{1,3},{2,0},{3,1},{4,6},{5,7},{6,4},{7,5},{8,10},{9,11},{10,... | collective-permute-start | bytes 417800 | tf_op jit(solution)/shard_map/ppermute | solution.py:352
  175.5 6.8 %collective-permute-start.18 = (s16[272,256]{1,0:T(8,128)(2,1)S(1)}, s16[272,256]{1,0:T(8,128)(2,1)S(1)}, u32[]{:S(2)}, u32[]{:S(2)}) collective-permute-start(s16[272,256]{1,0:T(8,128)(2,1)S(1)} %both1.1.refs_0_), channel_id=1, source_target_pairs={{0,1},{1,0},{2,3},{3,2},{4,5},{5,4},{6,7},{7,6},{8,9},{9,8},{10,11... | collective-permute-start | bytes 417800 | tf_op jit(solution)/shard_map/ppermute | solution.py:352
Sparse Core Ops, SparseCore 0:
  9.6 37.1 all-gather.1

commit v7 on v6

--- a/solution.py
+++ b/solution.py
@@ -13,7 +13,6 @@
 CODE = 32000.0
 FLOOR = 1e-30
 VMEM_LIMIT = 16 * 1024 * 1024
-PACK_LIMIT = 56 * 1024 * 1024
 f32, bf16, i16, i32 = jnp.float32, jnp.bfloat16, jnp.int16, jnp.int32
 shape = jax.ShapeDtypeStruct
 VMEM = pl.BlockSpec(memory_space=pltpu.VMEM)
@@ -86,7 +85,8 @@
 
 
 def pack_kernel(chunks, me_ref, points_ref, cluster_ref, *refs):
-    outs, (head, sems, head_sems) = refs[:-3], refs[-3:]
+    outs, (after_ref, head, sems, head_sems) = refs[:-4], refs[-4:]
+    after_ref[0] = me_ref[0]
     rows = points_ref.shape[0]
     h = len(outs) // chunks
     q = me_ref[0] & (h - 1)
@@ -164,15 +164,10 @@
             prev_ref[at, :] = decode(arrived[m][j * w : (j + 1) * w, :], exponent)
 
 
-def sums_kernel(place_ref, member_ref, far_count_ref, *refs):
-    h = (len(refs) - 6) // 2
-    points, (acc_ref, code_ref, after_ref), (code, head, sem), held = (
-        refs[:h],
-        refs[h : h + 3],
-        refs[h + 3 : h + 6],
-        refs[h + 6 :],
-    )
-    after_ref[0] = place_ref[0]
+def sums_kernel(place_ref, before_ref, member_ref, far_count_ref, *refs):
+    h = (len(refs) - 5) // 2
+    points, (acc_ref, code, after_ref, head, sem), held = refs[:h], refs[h : h + 5], refs[h + 5 :]
+    after_ref[0] = before_ref[0]
     rows = acc_ref.shape[0] // 2
     blocks = held[0].shape[0] // BLOCK
     copies = start_all([p.at[0 : blocks * BLOCK, :] for p in points], held, sem)
@@ -182,7 +177,6 @@
         for i in range(blocks):
             at, here = (m * blocks + i) * BLOCK, slice(i * BLOCK, (i + 1) * BLOCK)
             acc_ref[chunk(place_ref[m * blocks + i], BLOCK), :] += dot(member_ref[at : at + BLOCK, :], held[m][here, :])
-    copies = []
     lines = rows // BLOCK
     step = 2 * BLOCK
     for j in range(rows // step):
@@ -196,24 +190,20 @@
             head[row : row + 1, :] = lanes[:, k * BLOCK : (k + 1) * BLOCK]
     head[lines:, :] = far_count_ref[...]
     code[rows:, :] = head[...].astype(i16)
-    start(code, code_ref, sem.at[h]).wait()
-
-
-def refresh_kernel(chunks, h, near_ref, prev_ref, *refs):
-    accs, crossed, (x_ref, stat_ref), outs = (
-        refs[:chunks],
-        refs[chunks : 2 * chunks],
-        refs[2 * chunks : 2 * chunks + 2],
-        refs[2 * chunks + 2 : 2 * chunks + 2 + h],
-    )
-    codes, stat, sem, held = refs[2 * chunks + 2 + h :][:h], *refs[2 * chunks + 2 + 2 * h :][:2], refs[2 * chunks + 4 + 2 * h :]
+
+
+def spot(index, w):
+    return slice(index * BLOCK // w, index * BLOCK // w + 1), slice(index * BLOCK % w, index * BLOCK % w + BLOCK)
+
+
+def refresh_kernel(chunks, near_ref, prev_ref, *refs):
+    accs, crossed, x_ref, outs, tail = refs[:chunks], refs[chunks : 2 * chunks], refs[2 * chunks], refs[2 * chunks + 1 : -1], refs[-1]
+    h = len(outs)
     rows, w = x_ref.shape
     owned = rows // h
     lines = rows // BLOCK
-    wait_all(start_all(crossed, held, sem))
-    heads = [held[c][rows:, :].astype(i32).astype(f32) for c in range(chunks)]
+    heads = [crossed[c][rows:, :].astype(i32).astype(f32) for c in range(chunks)]
     unit = jnp.ones((8, BLOCK), bf16)
-    copies = []
     for j in range(lines):
         at = slice(j * BLOCK, (j + 1) * BLOCK)
         count = near_ref[at, :] + to_column(heads[0][lines + j : lines + j + 1, :])
@@ -221,21 +211,23 @@
         square, top = None, None
         for c in range(chunks):
             lanes = slice(c * BLOCK, (c + 1) * BLOCK)
-            far = decode(held[c][at, :], to_column(heads[c][j : j + 1, :]))
+            far = decode(crossed[c][at, :], to_column(heads[c][j : j + 1, :]))
             x = (accs[c][at, :] + far) * inverse + prev_ref[at, lanes]
             x_ref[at, lanes] = x
             square = x * x if c == 0 else square + x * x
             top = jnp.abs(x) if c == 0 else jnp.maximum(top, jnp.abs(x))
         square_high, square_low = split(square)
-        stat[0:1, at] = (dot_lanes(unit, square_high) + dot_lanes(unit, square_low))[0:1]
+        sums = (dot_lanes(unit, square_high) + dot_lanes(unit, square_low))[0:1]
+        sums_exponent = exponent_of(sums)
+        scaled = sums * (16384.0 * jnp.exp2(-sums_exponent))
+        whole = jnp.floor(scaled)
         exponent = exponent_of(jnp.max(top, axis=1, keepdims=True))
-        stat[1:2, at] = to_lanes(exponent)
-        m, here = j * BLOCK // owned, slice(j * BLOCK % owned, j * BLOCK % owned + BLOCK)
-        codes[m][here, :] = encode(x_ref[at, :], exponent)
-        if (j + 1) * BLOCK % owned == 0:
-            copies.append(start(codes[m], outs[m], sem.at[chunks + m]))
-    copies.append(start(stat, stat_ref, sem.at[chunks + h]))
-    wait_all(copies)
+        for k, value in enumerate((sums_exponent, whole, jnp.floor((scaled - whole) * 16384.0), to_lanes(exponent))):
+            tail[spot(k * lines + j, w)] = value.astype(i32)
+        here = slice(j * BLOCK % owned, j * BLOCK % owned + BLOCK)
+        outs[j * BLOCK // owned][here, :] = encode(x_ref[at, :], exponent)
+    for out in outs:
+        out[owned:, :] = tail[...].astype(i16)
 
 
 def put_codes(values, code, head):
@@ -258,76 +250,78 @@
 
 
 def upper_kernel(width, member_ref, x_ref, *refs):
-    stats, outs, (high, low, sums, sems), held = refs[:-10], refs[-10:-8], refs[-8:-4], refs[-4:]
-    h = len(stats)
-    owned = x_ref.shape[0] // h
+    backs, outs, (high, low, sums), heads = refs[:-7], refs[-7:-5], refs[-5:-2], refs[-2:]
+    h = len(backs)
+    total, w = x_ref.shape
+    owned = total // h
+    lines, per = total // BLOCK, owned // BLOCK
+    tails = [back[owned:, :].astype(i32).astype(f32) for back in backs]
     for p in range(h):
-        squares = stats[0][0:1, p * owned : (p + 1) * owned]
-        for m in range(1, h):
-            squares += stats[m][0:1, (p ^ m) * owned : ((p ^ m) + 1) * owned]
-        factor = lax.rsqrt(squares / width + EPSILON)
-        for j in range(0, owned, BLOCK):
-            at = slice(p * owned + j, p * owned + j + BLOCK)
-            high[at, :], low[at, :] = split(x_ref[at, :] * to_column(factor[:, j : j + BLOCK]))
+        for j in range(per):
+            squares = None
+            for m in range(h):
+                index = (p ^ m) * per + j
+                exponent, whole, rest = (tails[m][spot(k * lines + index, w)] for k in range(3))
+                value = (whole + rest * (1.0 / 16384.0)) * (jnp.exp2(exponent) * (1.0 / 16384.0))
+                squares = value if m == 0 else squares + value
+            factor = lax.rsqrt(squares / width + EPSILON)
+            at = slice(p * owned + j * BLOCK, p * owned + (j + 1) * BLOCK)
+            high[at, :], low[at, :] = split(x_ref[at, :] * to_column(factor))
     rows = sums.shape[0]
-    copies = []
     for k in range(2):
         member = member_ref[k * rows : (k + 1) * rows, :]
         sums[...] = dot(member, high[...]) + dot(member, low[...])
-        put_codes(sums, held[k], held[2 + k])
-        copies.append(start(held[k], outs[k], sems.at[k]))
-    wait_all(copies)
-
-
-def both_kernel(own_ref, far_ref, code_ref, own, far, sums, code, head, sems):
-    wait_all(start_all([own_ref, far_ref], [own, far], sems))
+        put_codes(sums, outs[k], heads[k])
+
+
+def both_kernel(own, far, code_ref, sums, head):
     rows = sums.shape[0]
     for j in range(rows // BLOCK):
         sums[j * BLOCK : (j + 1) * BLOCK, :] = get_codes(own, j, rows, BLOCK) + get_codes(far, j, rows, BLOCK)
-    put_codes(sums, code, head)
-    start(code, code_ref, sems.at[0]).wait()
-
-
-def join_kernel(first, me_ref, *refs):
-    h = (len(refs) - 4) // 2
-    parts, (out_ref, out, sems, out_sems), held = refs[:h], refs[-4 - h : -h], refs[-h:]
+    put_codes(sums, code_ref, head)
+
+
+def join_kernel(me_ref, *refs):
+    parts, (out_ref, out, out_sems) = refs[:-3], refs[-3:]
+    h = len(parts) // 2
     q = me_ref[0] & (h - 1)
-    rows, width = out.shape
+    total, width = out.shape
+    rows = total // 2
     w = width // h
-    wait_all(start_all(parts, held, sems))
     copies = []
-    for j in range(rows // BLOCK):
-        at = slice(j * BLOCK, (j + 1) * BLOCK)
-        values = [get_codes(held[m], j, rows, BLOCK) for m in range(h)]
+    for j in range(total // BLOCK):
+        at, k = slice(j * BLOCK, (j + 1) * BLOCK), j * BLOCK // rows
+        values = [get_codes(parts[k * h + m], j - k * (rows // BLOCK), rows, BLOCK) for m in range(h)]
         square = sum(v * v for v in values)
         factor = lax.rsqrt(jnp.sum(square, axis=1, keepdims=True) / width + EPSILON)
         for m in range(h):
             out[at, chunk(q ^ m, w)] = values[m] * factor
-        there = out_ref.at[first + j * BLOCK : first + (j + 1) * BLOCK, :]
-        copies.append(start(out.at[at, :], there, out_sems.at[j]))
+        copies.append(start(out.at[at, :], out_ref.at[at, :], out_sems.at[j]))
     wait_all(copies)
 
 
 def decode_kernel(me_ref, *refs):
-    h = (len(refs) - 1) // 2
+    codes, out_ref = refs[:-1], refs[-1]
+    h = len(codes)
     q = me_ref[0] & (h - 1)
-    codes, stats, out_ref = refs[:h], refs[h : 2 * h], refs[2 * h]
-    rows, w = codes[0].shape
-    width = h * w
-    for j in range(rows // BLOCK):
+    rows, width = out_ref.shape
+    w = width // h
+    lines, per = h * rows // BLOCK, rows // BLOCK
+    tails = [code[rows:, :].astype(i32).astype(f32) for code in codes]
+    for j in range(per):
         at = slice(j * BLOCK, (j + 1) * BLOCK)
         values = []
         for m in range(h):
-            lanes = stats[m][1:2, m * rows + j * BLOCK : m * rows + (j + 1) * BLOCK]
-            values.append(decode(codes[m][at, :], to_column(lanes)))
+            exponent = tails[m][spot(3 * lines + m * per + j, w)]
+            values.append(decode(codes[m][at, :], to_column(exponent)))
         square = sum(v * v for v in values)
         factor = lax.rsqrt(jnp.sum(square, axis=1, keepdims=True) / width + EPSILON)
         for m in range(h):
             out_ref[at, chunk(q ^ m, w)] = values[m] * factor
 
 
-def call(kernel, out_shape, limit=VMEM_LIMIT, **kw):
-    params = pltpu.CompilerParams(vmem_limit_bytes=limit)
+def call(kernel, out_shape, **kw):
+    params = pltpu.CompilerParams(vmem_limit_bytes=VMEM_LIMIT)
     return pl.pallas_call(kernel, out_shape=out_shape, compiler_params=params, **kw)
 
 
@@ -358,12 +352,11 @@
     table_rows = lax.all_gather(cent2_prev, "dp", axis=0, tiled=True)
 
     first_shape = shape((point_rows + 2 * blocks, BLOCK), bf16)
-    packed = call(
+    *packed, after_pack = call(
         functools.partial(pack_kernel, chunks),
-        ([first_shape] + [shape((point_rows, BLOCK), bf16)] * (chunks - 1)) * h,
-        limit=PACK_LIMIT,
+        ([first_shape] + [shape((point_rows, BLOCK), bf16)] * (chunks - 1)) * h + [shape((1,), i32)],
         in_specs=[SMEM, HBM, VMEM],
-        out_specs=[HBM] * (h * chunks),
+        out_specs=[HBM] * (h * chunks) + [SMEM],
         scratch_shapes=[pltpu.VMEM((2 * blocks, BLOCK), bf16), dma(h * chunks), dma(h)],
         name="pack",
     )(me, points, point_cluster.reshape(blocks, BLOCK))
@@ -384,21 +377,17 @@
     )(me, *arrived[0])
 
     lines = rows + 2 * rows // BLOCK
-    accs, crossed, after = [], [], None
+    accs, crossed, after = [], [], place
     for c in range(chunks):
         acc, code, ended = call(
             sums_kernel,
             [shape((2 * rows, BLOCK), f32), shape((lines, BLOCK), i16), shape((1,), i32)],
-            in_specs=[SMEM, VMEM, VMEM] + [HBM] * h,
-            out_specs=[VMEM, HBM, SMEM],
-            scratch_shapes=[
-                pltpu.VMEM((lines, BLOCK), i16),
-                pltpu.VMEM((2 * rows // BLOCK, BLOCK), i32),
-                dma(h + 1),
-            ]
+            in_specs=[SMEM, SMEM, VMEM, VMEM] + [HBM] * h,
+            out_specs=[VMEM, VMEM, SMEM],
+            scratch_shapes=[pltpu.VMEM((2 * rows // BLOCK, BLOCK), i32), dma(h)]
             + [pltpu.VMEM((point_rows, BLOCK), bf16)] * h,
             name=f"sums{c}",
-        )(place, member, far_count, *arrived[c])
+        )(place, after, member, far_count, *arrived[c])
         accs.append(acc)
         crossed.append(swap(code, h))
         after = ended
@@ -412,7 +401,7 @@
         scratch_shapes=[pltpu.VMEM((owned, width), f32), pltpu.VMEM((head, w), i32), dma(), dma(h)]
         + [pltpu.VMEM((owned + head, w), i16)] * h,
         name="prev",
-    )(me, after, cent1_prev, parent.reshape(owned // w, w))
+    )(me, after_pack, cent1_prev, parent.reshape(owned // w, w))
     prev, upper_member = call(
         previous_kernel,
         [shape((rows, w), f32), shape((upper_rows, rows), bf16)],
@@ -423,7 +412,9 @@
 
     points, table_rows = lax.optimization_barrier((points, table_rows))
     unit_points = rms_norm(points.astype(f32)).astype(bf16)
-    table_units = rms_norm(table_rows.astype(f32)).astype(bf16)
+    table_scale = lax.rsqrt(jnp.mean(jnp.square(table_rows.astype(f32)), axis=-1) + EPSILON)
+    table_scale, near = lax.optimization_barrier((table_scale, near))
+    table_units = (table_rows.astype(f32) * table_scale[:, None]).astype(bf16)
     products = lax.dot_general(
         unit_points, table_units, (((1,), (1,)), ((), ())), preferred_element_type=f32
     )
@@ -431,76 +422,65 @@
     listed = jnp.any(cand_blocks[:, :, None] == column_block[None, None, :], axis=1)
     weights = jnp.exp(products * (SHARPNESS / width)).reshape(blocks, BLOCK, -1)
     running = jnp.sum(weights * listed[:, None, :].astype(f32), axis=2).reshape(point_rows)
-    point_score, near = lax.optimization_barrier((jnp.log(running), near))
-
-    out = call(
-        functools.partial(refresh_kernel, chunks, h),
-        [shape((rows, w), f32), shape((2, rows), f32)] + [shape((owned, w), i16)] * h,
-        in_specs=[VMEM] * (2 + chunks) + [HBM] * chunks,
-        out_specs=[VMEM] + [HBM] * (h + 1),
-        scratch_shapes=[pltpu.VMEM((owned, w), i16)] * h
-        + [pltpu.VMEM((2, rows), f32), dma(chunks + h + 1)]
-        + [pltpu.VMEM((lines, BLOCK), i16)] * chunks,
+    point_score = jnp.log(running)
+
+    tail = 4 * rows // w
+    x, *backs = call(
+        functools.partial(refresh_kernel, chunks),
+        [shape((rows, w), f32)] + [shape((owned + tail, w), i16)] * h,
+        in_specs=[VMEM] * (2 + 2 * chunks),
+        out_specs=[VMEM] * (h + 1),
+        scratch_shapes=[pltpu.VMEM((tail, w), i32)],
         name="refresh",
     )(near, prev, *accs, *crossed)
-    x, stat = out[:2]
-    stats = swap_half([stat] * h)
-    back = swap_half(out[2:])
+    backs = swap_half(backs)
 
     part = upper_rows // 2
     tail = head_rows(part, w)
     code_shape = shape((part + tail, w), i16)
-    held_code, held_head = pltpu.VMEM(code_shape.shape, i16), pltpu.VMEM((tail, w), i32)
+    held_head = pltpu.VMEM((tail, w), i32)
     codes = call(
         functools.partial(upper_kernel, width),
         [code_shape] * 2,
         in_specs=[VMEM] * (h + 2),
-        out_specs=[HBM] * 2,
-        scratch_shapes=[pltpu.VMEM((rows, w), bf16), pltpu.VMEM((rows, w), bf16), pltpu.VMEM((part, w), f32), dma(2)]
-        + [held_code] * 2
+        out_specs=[VMEM] * 2,
+        scratch_shapes=[pltpu.VMEM((rows, w), bf16), pltpu.VMEM((rows, w), bf16), pltpu.VMEM((part, w), f32)]
         + [held_head] * 2,
         name="upper",
-    )(upper_member, x, *stats)
+    )(upper_member, x, *backs)
     far_codes = [swap(code, h) for code in codes]
     parts = []
     for k in range(2):
         code = codes[k]
         if k == 0:
-            code, back = lax.optimization_barrier((code, back))
+            code, point_score = lax.optimization_barrier((code, point_score))
         code = call(
             both_kernel,
             code_shape,
-            in_specs=[HBM, HBM],
-            out_specs=HBM,
-            scratch_shapes=[held_code, held_code, pltpu.VMEM((part, w), f32), held_code, held_head, dma(2)],
+            in_specs=[VMEM, VMEM],
+            out_specs=VMEM,
+            scratch_shapes=[pltpu.VMEM((part, w), f32), held_head],
             name=f"both{k}",
         )(code, far_codes[k])
-        parts.append(swap_half([code] * h))
+        parts += swap_half([code] * h)
 
     cent1_new = call(
         decode_kernel,
         shape((owned, width), f32),
-        in_specs=[SMEM] + [VMEM] * (2 * h),
+        in_specs=[SMEM] + [VMEM] * h,
         out_specs=VMEM,
         name="decode",
-    )(me, *back, *stats)
-    cent2_new = []
-    for k in range(2):
-        last = me
-        if k == 1:
-            last, cent1_new = lax.optimization_barrier((me, cent1_new))
-        cent2_new = [
-            call(
-                functools.partial(join_kernel, k * part),
-                shape((upper_rows, width), f32),
-                in_specs=[SMEM] + [HBM] * (h + k),
-                out_specs=HBM,
-                scratch_shapes=[pltpu.VMEM((part, width), f32), dma(h), dma(part // BLOCK)] + [held_code] * h,
-                input_output_aliases={h + 1: 0} if k else {},
-                name=f"join{k}",
-            )(last, *parts[k], *cent2_new)
-        ]
-    return (cent1_new, cent2_new[0], point_score)
+    )(me, *backs)
+    last, cent1_new = lax.optimization_barrier((me, cent1_new))
+    cent2_new = call(
+        join_kernel,
+        shape((upper_rows, width), f32),
+        in_specs=[SMEM] + [VMEM] * (2 * h),
+        out_specs=HBM,
+        scratch_shapes=[pltpu.VMEM((upper_rows, width), f32), dma(upper_rows // BLOCK)],
+        name="join",
+    )(last, *parts)
+    return (cent1_new, cent2_new, point_score)
 
 
 def solution(mesh):

time: 192 us -> 121 us (0.63)
  Pallas kernels: 92.2 us -> 22.4 us
  local copies, waits for them, and re-layouts: 4.12 us -> 9.86 us
  starting transfers between devices: 35.3 us -> 31.5 us
  other arithmetic: 6.39 us -> 4.03 us
    pallas_call x1, Pallas kernels: 65.4 us -> 1.78 us  [shards(): call(functools.partial(pack_kernel, chunks), ([first_shape] + [shape((poi...]
    unnamed x28 -> x30, local copies, waits for them, and re-layouts: 3.52 us -> 9.25 us
    pallas_call x5 -> x4, Pallas kernels: 10.5 us -> 5.28 us  [the longest x1 2.27 us: shards(): call(join_kernel, shape((upper_rows, width), f32), in_specs=[SMEM] + [VME...]
    reduce_sum x2 -> x1, other arithmetic: 5.54 us -> 0.48 us  [rms_norm(): jnp.mean(values * values, axis=-1, keepdims=True) + EPSILON]
    ppermute x25 -> x22, starting transfers between devices: 35.3 us -> 31.5 us  [swap(): return lax.ppermute(value, 'cent', [(i, i ^ mask) for i in range(n)])]
    reduce_sum x0 -> x1, other arithmetic: none -> 3.22 us  [shards(): jnp.mean(jnp.square(table_rows.astype(f32)), axis=-1) + EPSILON]
    ppermute x25 -> x22, waiting for transfers between devices: 33.4 us -> 32.5 us  [swap(): return lax.ppermute(value, 'cent', [(i, i ^ mask) for i in range(n)])]
  transfers between devices with their start and end apart: 26 -> 23, of which waited for: 14 -> 13; matrix products, arithmetic and copies ran while one was open for 6% -> 8% of each run, Pallas kernels for 44% -> 13%
where the time goes in v7:
time: 121 us
  waiting for transfers between devices  33.2 us (27%)
  starting transfers between devices  31.5 us (26%)
  Pallas kernels  22.4 us (19%)
  between operations  14.2 us (12%)
  local copies, waits for them, and re-layouts  9.86 us (8%)
  matrix products  5.37 us (4%)
  other arithmetic  4.03 us (3%)
    ppermute x22, waiting for transfers between devices, swap(): return lax.ppermute(value, 'cent', [(i, i ^ mask) for i in range(n)])  32.5 us
    ppermute x22, starting transfers between devices, swap(): return lax.ppermute(value, 'cent', [(i, i ^ mask) for i in range(n)])  31.5 us
    unnamed x30, local copies, waits for them, and re-layouts  9.25 us
    pallas_call x2, Pallas kernels, shards(): call(sums_kernel, [shape((2 * rows, BLOCK), f32), shape((lines, BLOCK), i...  6.35 us
    dot_general x1, matrix products, shards(): lax.dot_general(unit_points, table_units, (((1,), (1,)), ((), ())), prefe...  5.37 us
    reduce_sum x1, other arithmetic, shards(): jnp.mean(jnp.square(table_rows.astype(f32)), axis=-1) + EPSILON  3.22 us
    pallas_call x1, Pallas kernels, shards(): call(prev_kernel, [shape((owned + head, w), i16)] * h, in_specs=[SMEM, SM...  2.46 us
  transfers between devices with their start and end apart: 23, of which 13 were waited for; matrix products, arithmetic and copies ran while one was open for 8% of the time, Pallas kernels for 13%

profile of v7, /device:TPU:0, one launch (start us, length us, event | category | flops | bytes accessed | tf_op | source)
XLA Modules:
  0.0 120.6 jit_solution(16786261042631645077)
XLA Ops:
  7.2 0.7 all-gather.2.cloned.1.call-update
  8.0 1.6 %copy-done = bf16[1024,1024]{1,0:T(8,128)(2,1)S(1)} copy-done((bf16[1024,1024]{1,0:T(8,128)(2,1)S(1)}, bf16[1024,1024]{1,0:T(8,128)(2,1)}, u32[]{:S(2)}) %copy-start) | copy-done | bytes 2097176
  9.6 0.7 copy-done.11
  10.3 1.8 %pack.1 = (bf16[1040,128]{1,0:T(8,128)(2,1)S(1)}, bf16[1024,128]{1,0:T(8,128)(2,1)S(1)}, bf16[1040,128]{1,0:T(8,128)(2,1)S(1)}, bf16[1024,128]{1,0:T(8,128)(2,1)...) custom-call(s32[3]{0:T(128)S(1)} %pad_add_fusion.me_ref, ...), custom_call_target="tpu_custom_call" | custom-call | tf_op jit(solution)/shard_map/pack/pallas_call | solution.py:355
  12.1 3.0 %collective-permute-start = (bf16[1040,128]{1,0:T(8,128)(2,1)S(1)}, bf16[1040,128]{1,0:T(8,128)(2,1)S(1)}, u32[]{:S(2)}, u32[]{:S(2)}) collective-permute-start(bf16[1040,128]{1,0:T(8,128)(2,1)S(1)} %get-tuple-element.44), channel_id=1, source_target_pairs={{0,1},{1,0},{2,3},{3,2},{4,5},{5,4},{6,7},{7,6},{8,9},{9,8},{10,11... | collective-permute-start | bytes 798728 | tf_op jit(solution)/shard_map/ppermute | solution.py:346
  15.1 1.2 %copy-done.2 = f32[256,1024]{1,0:T(8,128)S(1)} copy-done((f32[256,1024]{1,0:T(8,128)S(1)}, f32[256,1024]{1,0:T(8,128)}, u32[]{:S(2)}) %copy-start.2) | copy-done | bytes 1048600
  17.0 2.5 %prev.1 = (s16[272,256]{1,0:T(8,128)(2,1)S(1)}, s16[272,256]{1,0:T(8,128)(2,1)S(1)}, s16[272,256]{1,0:T(8,128)(2,1)S(1)}, s16[272,256]{1,0:T(8,128)(2,1)S(1)}) custom-call(s32[3]{0:T(128)S(1)} %pad_add_fusion.me_ref, s32[1]{0:T(128)} %get-tuple-element.49.after_ref, f32[256,1024]{1,0:T(8,128)S(1)} %copy-done.2, s32[1,256]{1,0:T(1,128)S(1)} %bitcast.10), custom_call_target="tpu_custom_call" | custom-call | tf_op jit(solution)/shard_map/prev/pallas_call | solution.py:396
  19.5 2.1 %collective-permute-start.4 = (s16[272,256]{1,0:T(8,128)(2,1)S(1)}, s16[272,256]{1,0:T(8,128)(2,1)S(1)}, u32[]{:S(2)}, u32[]{:S(2)}) collective-permute-start(s16[272,256]{1,0:T(8,128)(2,1)S(1)} %get-tuple-element.52), channel_id=1, source_target_pairs={{0,2},{1,3},{2,0},{3,1},{4,6},{5,7},{6,4},{7,5},{8,10},{9,11},{10,... | collective-permute-start | bytes 417800 | tf_op jit(solution)/shard_map/ppermute | solution.py:346
  21.6 1.4 %collective-permute-start.5 = (s16[272,256]{1,0:T(8,128)(2,1)S(1)}, s16[272,256]{1,0:T(8,128)(2,1)S(1)}, u32[]{:S(2)}, u32[]{:S(2)}) collective-permute-start(s16[272,256]{1,0:T(8,128)(2,1)S(1)} %get-tuple-element.53), channel_id=1, source_target_pairs={{0,3},{1,2},{2,1},{3,0},{4,7},{5,6},{6,5},{7,4},{8,11},{9,10},{10,... | collective-permute-start | bytes 417800 | tf_op jit(solution)/shard_map/ppermute | solution.py:346
  23.0 1.6 %collective-permute-start.1 = (bf16[1040,128]{1,0:T(8,128)(2,1)S(1)}, bf16[1040,128]{1,0:T(8,128)(2,1)S(1)}, u32[]{:S(2)}, u32[]{:S(2)}) collective-permute-start(bf16[1040,128]{1,0:T(8,128)(2,1)S(1)} %get-tuple-element.45), channel_id=1, source_target_pairs={{0,2},{1,3},{2,0},{3,1},{4,6},{5,7},{6,4},{7,5},{8,10},{9,11},{10,... | collective-permute-start | bytes 798728 | tf_op jit(solution)/shard_map/ppermute | solution.py:346
  25.2 3.5 %collective-permute-start.2 = (bf16[1040,128]{1,0:T(8,128)(2,1)S(1)}, bf16[1040,128]{1,0:T(8,128)(2,1)S(1)}, u32[]{:S(2)}, u32[]{:S(2)}) collective-permute-start(bf16[1040,128]{1,0:T(8,128)(2,1)S(1)} %get-tuple-element.46), channel_id=1, source_target_pairs={{0,3},{1,2},{2,1},{3,0},{4,7},{5,6},{6,5},{7,4},{8,11},{9,10},{10,... | collective-permute-start | bytes 798728 | tf_op jit(solution)/shard_map/ppermute | solution.py:346
  28.7 1.9 %collective-permute-done.5.refs_3_ = s16[272,256]{1,0:T(8,128)(2,1)S(1)} collective-permute-done((s16[272,256]{1,0:T(8,128)(2,1)S(1)}, s16[272,256]{1,0:T(8,128)(2,1)S(1)}, u32[]{:S(2)}, u32[]{:S(2)}) %collective-permute-start.5) | collective-permute-done | bytes 139296 | tf_op jit(solution)/shard_map/ppermute | solution.py:346
  30.6 1.6 %collective-permute-start.7 = (bf16[1024,128]{1,0:T(8,128)(2,1)S(1)}, bf16[1024,128]{1,0:T(8,128)(2,1)S(1)}, u32[]{:S(2)}, u32[]{:S(2)}) collective-permute-start(bf16[1024,128]{1,0:T(8,128)(2,1)S(1)} %get-tuple-element.62), channel_id=1, source_target_pairs={{0,2},{1,3},{2,0},{3,1},{4,6},{5,7},{6,4},{7,5},{8,10},{9,11},{10,... | collective-permute-start | bytes 786440 | tf_op jit(solution)/shard_map/ppermute | solution.py:346
  33.0 1.9 %collective-permute-done.1.refs_2_ = bf16[1040,128]{1,0:T(8,128)(2,1)S(1)} collective-permute-done((bf16[1040,128]{1,0:T(8,128)(2,1)S(1)}, bf16[1040,128]{1,0:T(8,128)(2,1)S(1)}, u32[]{:S(2)}, u32[]{:S(2)}) %collective-permute-start.1) | collective-permute-done | bytes 266272 | tf_op jit(solution)/shard_map/ppermute | solution.py:346
  34.9 7.2 %collective-permute-done.2.refs_3_ = bf16[1040,128]{1,0:T(8,128)(2,1)S(1)} collective-permute-done((bf16[1040,128]{1,0:T(8,128)(2,1)S(1)}, bf16[1040,128]{1,0:T(8,128)(2,1)S(1)}, u32[]{:S(2)}, u32[]{:S(2)}) %collective-permute-start.2) | collective-permute-done | bytes 266272 | tf_op jit(solution)/shard_map/ppermute | solution.py:346
  42.0 2.3 %prepare.1 = (bf16[4096,128]{1,0:T(8,128)(2,1)S(1)}, s32[32]{0:T(128)S(1)}, f32[1024,128]{1,0:T(8,128)S(1)}, s32[8,128]{1,0:T(8,128)S(1)}) custom-call(s32[3]{0:T(128)S(1)} %pad_add_fusion.me_ref, bf16[1040,128]{1,0:T(8,128)(2,1)S(1)} %get-tuple-element.43.refs_0_, bf16[1040,128]{1,0:T(8,128)(2,1)S(1)} %collective-permute-done.refs_1_, ...), custom_call_target="tpu_custom_call" | custom-call | tf_op jit(solution)/shard_map/prepare/pallas_call | solution.py:365
  44.3 0.8 copy-done.9
  45.1 2.9 %sums0.1 = (f32[2048,128]{1,0:T(8,128)S(1)}, s16[1040,128]{1,0:T(8,128)(2,1)}, s32[1]{0:T(128)}) custom-call(s32[32]{0:T(128)S(1)} %get-tuple-element.55.place_ref.before_ref, s32[32]{0:T(128)S(1)} %get-tuple-element.55.place_ref.before_ref, bf16[4096,128]{1,0:T(8,128)(2,1)S(1)} %get-tuple-element.56.member_ref, ...), custom_call_target="tpu_custom_call" | custom-call | tf_op jit(solution)/shard_map/sums0/pallas_call | solution.py:382
  48.0 1.0 copy-done.5
  49.0 2.6 %collective-permute-start.9 = (s16[1040,128]{1,0:T(8,128)(2,1)}, s16[1040,128]{1,0:T(8,128)(2,1)S(1)}, u32[]{:S(2)}, u32[]{:S(2)}) collective-permute-start(s16[1040,128]{1,0:T(8,128)(2,1)} %get-tuple-element.65), channel_id=1, source_target_pairs={{0,4},{1,5},{2,6},{3,7},{4,0},{5,1},{6,2},{7,3},{8,12},{9,13},{10,... | collective-permute-start | bytes 798728 | tf_op jit(solution)/shard_map/ppermute | solution.py:346
  51.6 3.1 %collective-permute-done.8.refs_3_ = bf16[1024,128]{1,0:T(8,128)(2,1)S(1)} collective-permute-done((bf16[1024,128]{1,0:T(8,128)(2,1)S(1)}, bf16[1024,128]{1,0:T(8,128)(2,1)S(1)}, u32[]{:S(2)}, u32[]{:S(2)}) %collective-permute-start.8) | collective-permute-done | bytes 262176 | tf_op jit(solution)/shard_map/ppermute | solution.py:346
  54.7 3.5 %sums1.1 = (f32[2048,128]{1,0:T(8,128)S(1)}, s16[1040,128]{1,0:T(8,128)(2,1)}, s32[1]{0:T(128)}) custom-call(s32[32]{0:T(128)S(1)} %get-tuple-element.55.place_ref.before_ref, s32[1]{0:T(128)} %get-tuple-element.59.before_ref, bf16[4096,128]{1,0:T(8,128)(2,1)S(1)} %get-tuple-element.56.member_ref, s32[8,128]{1,0:T(8,128)S(1)} %get-tuple-element.57.far_count_ref, ...), custom_call_target="tpu_custom_call" | custom-call | tf_op jit(solution)/shard_map/sums1/pallas_call | solution.py:382
  58.2 1.0 copy-done.7
  59.2 1.2 collective-permute-start.10
  60.4 3.2 %fusion = f32[2048]{0:T(1024)S(1)} fusion(bf16[2048,1024]{1,0:T(8,128)(2,1)} %all-gather.2.cloned.1.call-done), kind=kLoop, calls=%fused_computation.2 | loop fusion | flops 6289408 | bytes 4202496 | tf_op jit(solution)/shard_map/reduce_sum | solution.py:415
  63.7 5.9 %collective-permute-done.9.refs_2_ = s16[1040,128]{1,0:T(8,128)(2,1)S(1)} collective-permute-done((s16[1040,128]{1,0:T(8,128)(2,1)}, s16[1040,128]{1,0:T(8,128)(2,1)S(1)}, u32[]{:S(2)}, u32[]{:S(2)}) %collective-permute-start.9) | collective-permute-done | bytes 266272 | tf_op jit(solution)/shard_map/ppermute | solution.py:346
  69.6 3.2 %collective-permute-done.10.refs_3_ = s16[1040,128]{1,0:T(8,128)(2,1)} collective-permute-done((s16[1040,128]{1,0:T(8,128)(2,1)}, s16[1040,128]{1,0:T(8,128)(2,1)}, u32[]{:S(2)}, u32[]{:S(2)}) %collective-permute-start.10) | collective-permute-done | bytes 266272 | tf_op jit(solution)/shard_map/ppermute | solution.py:346
  72.7 1.2 %copy-done.8 = f32[2048,128]{1,0:T(8,128)S(1)} copy-done((f32[2048,128]{1,0:T(8,128)S(1)}, f32[2048,128]{1,0:T(8,128)}, u32[]{:S(2)}) %copy-start.8) | copy-done | bytes 1048600
  74.0 1.0 copy-done.10
  75.0 2.2 %refresh.1 = (f32[1024,256]{1,0:T(8,128)S(1)}, s16[272,256]{1,0:T(8,128)(2,1)S(1)}, s16[272,256]{1,0:T(8,128)(2,1)S(1)}, s16[272,256]{1,0:T(8,128)(2,1)S(1)}, s16[272,256]{1,0:T(8,128)(2,1)S(1)}) custom-call(f32[1024,128]{1,0:T(8,128)S(1)} %copy-done.10, f32[1024,256]{1,0:T(8,128)S(1)} %copy-done.4, f32[2048,128]{1,0:T(8,128)S(1)} %copy-done.6, ...), custom_call_target="tpu_custom_call" | custom-call | tf_op jit(solution)/shard_map/refresh/pallas_call | solution.py:428
  77.2 0.9 collective-permute-start.11
  78.1 2.7 %collective-permute-start.13 = (s16[272,256]{1,0:T(8,128)(2,1)S(1)}, s16[272,256]{1,0:T(8,128)(2,1)S(1)}, u32[]{:S(2)}, u32[]{:S(2)}) collective-permute-start(s16[272,256]{1,0:T(8,128)(2,1)S(1)} %get-tuple-element.70), channel_id=1, source_target_pairs={{0,3},{1,2},{2,1},{3,0},{4,7},{5,6},{6,5},{7,4},{8,11},{9,10},{10,... | collective-permute-start | bytes 417800 | tf_op jit(solution)/shard_map/ppermute | solution.py:346
  81.3 1.8 %collective-permute-done.11.refs_1_ = s16[272,256]{1,0:T(8,128)(2,1)S(1)} collective-permute-done((s16[272,256]{1,0:T(8,128)(2,1)S(1)}, s16[272,256]{1,0:T(8,128)(2,1)S(1)}, u32[]{:S(2)}, u32[]{:S(2)}) %collective-permute-start.11) | collective-permute-done | bytes 139296 | tf_op jit(solution)/shard_map/ppermute | solution.py:346
  83.1 2.1 %collective-permute-done.13.refs_3_ = s16[272,256]{1,0:T(8,128)(2,1)S(1)} collective-permute-done((s16[272,256]{1,0:T(8,128)(2,1)S(1)}, s16[272,256]{1,0:T(8,128)(2,1)S(1)}, u32[]{:S(2)}, u32[]{:S(2)}) %collective-permute-start.13) | collective-permute-done | bytes 139296 | tf_op jit(solution)/shard_map/ppermute | solution.py:346
  85.3 1.9 %upper.1 = (s16[272,256]{1,0:T(8,128)(2,1)S(1)}, s16[272,256]{1,0:T(8,128)(2,1)S(1)}) custom-call(bf16[512,1024]{1,0:T(8,128)(2,1)S(1)} %get-tuple-element.73.member_ref, f32[1024,256]{1,0:T(8,128)S(1)} %get-tuple-element.74.x_ref, s16[272,256]{1,0:T(8,128)(2,1)S(1)} %get-tuple-element.67.refs_0_, s16[272,256]{1,0:T(8,128)(2,1)S(1)} %collective-permute-done.11.refs_1_, ...), custom_call_target="tpu_custom_call" | custom-call | tf_op jit(solution)/shard_map/upper/pallas_call | solution.py:442
  87.2 2.2 %collective-permute-start.14 = (s16[272,256]{1,0:T(8,128)(2,1)S(1)}, s16[272,256]{1,0:T(8,128)(2,1)S(1)}, u32[]{:S(2)}, u32[]{:S(2)}) collective-permute-start(s16[272,256]{1,0:T(8,128)(2,1)S(1)} %get-tuple-element.78.own), channel_id=1, source_target_pairs={{0,4},{1,5},{2,6},{3,7},{4,0},{5,1},{6,2},{7,3},{8,12},{9,13},{10,... | collective-permute-start | bytes 417800 | tf_op jit(solution)/shard_map/ppermute | solution.py:346
  89.4 5.4 %fusion.2 = f32[1024]{0:T(1024)S(1)} fusion(bf16[2048,1024]{1,0:T(8,128)(2,1)S(1)} %copy-done.13, f32[8,2048]{1,0:T(8,128)S(1)} %convert_element_type.25, f32[2048]{0:T(1024)S(1)} %add_rsqrt_fusion, bf16[1024,1024]{1,0:T(8,128)(2,1)S(1)} %copy-done.1, f32[1024]{0:T(1024)S(1)} %add_rsqrt_fusion.1), kind=kOutput, calls=%fused_computation.5 | convolution fusion | flops 4310694912 | bytes 6373376 | tf_op jit(solution)/shard_map/dot_general | solution.py:418
  95.3 0.7 collective-permute-start.18
  96.5 1.4 %collective-permute-start.17 = (s16[272,256]{1,0:T(8,128)(2,1)S(1)}, s16[272,256]{1,0:T(8,128)(2,1)S(1)}, u32[]{:S(2)}, u32[]{:S(2)}) collective-permute-start(s16[272,256]{1,0:T(8,128)(2,1)S(1)} %both0.1.refs_0_), channel_id=1, source_target_pairs={{0,3},{1,2},{2,1},{3,0},{4,7},{5,6},{6,5},{7,4},{8,11},{9,10},{10,... | collective-permute-start | bytes 417800 | tf_op jit(solution)/shard_map/ppermute | solution.py:346
  97.9 0.8 collective-permute-start.16
  98.8 1.2 %collective-permute-start.15 = (s16[272,256]{1,0:T(8,128)(2,1)S(1)}, s16[272,256]{1,0:T(8,128)(2,1)S(1)}, u32[]{:S(2)}, u32[]{:S(2)}) collective-permute-start(s16[272,256]{1,0:T(8,128)(2,1)S(1)} %both0.1.refs_0_), channel_id=1, source_target_pairs={{0,1},{1,0},{2,3},{3,2},{4,5},{5,4},{6,7},{7,6},{8,9},{9,8},{10,11... | collective-permute-start | bytes 417800 | tf_op jit(solution)/shard_map/ppermute | solution.py:346
  100.0 1.6 %collective-permute-done.18.far = s16[272,256]{1,0:T(8,128)(2,1)S(1)} collective-permute-done((s16[272,256]{1,0:T(8,128)(2,1)S(1)}, s16[272,256]{1,0:T(8,128)(2,1)S(1)}, u32[]{:S(2)}, u32[]{:S(2)}) %collective-permute-start.18) | collective-permute-done | bytes 139296 | tf_op jit(solution)/shard_map/ppermute | solution.py:346
  102.0 2.3 %collective-permute-start.21 = (s16[272,256]{1,0:T(8,128)(2,1)S(1)}, s16[272,256]{1,0:T(8,128)(2,1)S(1)}, u32[]{:S(2)}, u32[]{:S(2)}) collective-permute-start(s16[272,256]{1,0:T(8,128)(2,1)S(1)} %both1.1.refs_4_), channel_id=1, source_target_pairs={{0,3},{1,2},{2,1},{3,0},{4,7},{5,6},{6,5},{7,4},{8,11},{9,10},{10,... | collective-permute-start | bytes 417800 | tf_op jit(solution)/shard_map/ppermute | solution.py:346
  104.3 1.9 %collective-permute-start.20 = (s16[272,256]{1,0:T(8,128)(2,1)S(1)}, s16[272,256]{1,0:T(8,128)(2,1)S(1)}, u32[]{:S(2)}, u32[]{:S(2)}) collective-permute-start(s16[272,256]{1,0:T(8,128)(2,1)S(1)} %both1.1.refs_4_), channel_id=1, source_target_pairs={{0,2},{1,3},{2,0},{3,1},{4,6},{5,7},{6,4},{7,5},{8,10},{9,11},{10,... | collective-permute-start | bytes 417800 | tf_op jit(solution)/shard_map/ppermute | solution.py:346
  106.5 1.9 %decode.1 = f32[256,1024]{1,0:T(8,128)} custom-call(s32[3]{0:T(128)S(1)} %pad_add_fusion.me_ref, s16[272,256]{1,0:T(8,128)(2,1)S(1)} %get-tuple-element.67.refs_0_, s16[272,256]{1,0:T(8,128)(2,1)S(1)} %collective-permute-done.11.refs_1_, s16[272,256]{1,0:T(8,128)(2,1)S(1)} %collective-permute-done.12.refs_2_, s16[272,256]{1,0:T(8,128)(2,1)S(1)} %collective-permute-done.13.refs_3_), custom_call_target="tpu_custom_call" | custom-call | tf_op jit(solution)/shard_map/decode/pallas_call | solution.py:467
  108.4 1.4 %collective-permute-done.21.refs_7_ = s16[272,256]{1,0:T(8,128)(2,1)S(1)} collective-permute-done((s16[272,256]{1,0:T(8,128)(2,1)S(1)}, s16[272,256]{1,0:T(8,128)(2,1)S(1)}, u32[]{:S(2)}, u32[]{:S(2)}) %collective-permute-start.21) | collective-permute-done | bytes 139296 | tf_op jit(solution)/shard_map/ppermute | solution.py:346
  109.8 1.7 %collective-permute-done.20.refs_6_ = s16[272,256]{1,0:T(8,128)(2,1)S(1)} collective-permute-done((s16[272,256]{1,0:T(8,128)(2,1)S(1)}, s16[272,256]{1,0:T(8,128)(2,1)S(1)}, u32[]{:S(2)}, u32[]{:S(2)}) %collective-permute-start.20) | collective-permute-done | bytes 139296 | tf_op jit(solution)/shard_map/ppermute | solution.py:346
  111.5 2.3 %join.1 = f32[512,1024]{1,0:T(8,128)} custom-call(s32[3]{0:T(128)S(1)} %pad_add_fusion.me_ref, s16[272,256]{1,0:T(8,128)(2,1)S(1)} %both0.1.refs_0_, s16[272,256]{1,0:T(8,128)(2,1)S(1)} %collective-permute-done.15.refs_1_, s16[272,256]{1,0:T(8,128)(2,1)S(1)} %collective-permute-done.16.refs_2_, s16[272,256]{1,0:T(8,128)(2,1)S(1)} %collective-permute-done.17.refs_3_, ...), custom_call_target="tpu_custom_call" | custom-call | tf_op jit(solution)/shard_map/join/pallas_call | solution.py:475
  (51 shorter events, 4.7 us)
Async XLA Ops:
  7.2 25.1 %copy-start.14 = (s32[8,8]{1,0:T(8,128)S(1)}, s32[8,8]{1,0:T(8,128)}, u32[]{:S(2)}) copy-start(s32[8,8]{1,0:T(8,128)} %param.8) | copy-start | bytes 772
  7.2 53.2 %all-gather.2.cloned.1.call-start = ((), (), s32[]{:S(2)}) async-start(), calls=%async_computation | async-start | bytes 5242880 | tf_op jit(solution)/shard_map/all_gather | solution.py:352
  8.0 1.6 %copy-start = (bf16[1024,1024]{1,0:T(8,128)(2,1)S(1)}, bf16[1024,1024]{1,0:T(8,128)(2,1)}, u32[]{:S(2)}) copy-start(bf16[1024,1024]{1,0:T(8,128)(2,1)} %points_ref.1) | copy-start | bytes 6291460
  9.6 0.7 copy-start.11
  12.1 20.1 %collective-permute-start = (bf16[1040,128]{1,0:T(8,128)(2,1)S(1)}, bf16[1040,128]{1,0:T(8,128)(2,1)S(1)}, u32[]{:S(2)}, u32[]{:S(2)}) collective-permute-start(bf16[1040,128]{1,0:T(8,128)(2,1)S(1)} %get-tuple-element.44), channel_id=1, source_target_pairs={{0,1},{1,0},{2,3},{3,2},{4,5},{5,4},{6,7},{7,6},{8,9},{9,8},{10,11... | collective-permute-start | bytes 798728 | tf_op jit(solution)/shard_map/ppermute | solution.py:346
  15.1 1.2 %copy-start.2 = (f32[256,1024]{1,0:T(8,128)S(1)}, f32[256,1024]{1,0:T(8,128)}, u32[]{:S(2)}) copy-start(f32[256,1024]{1,0:T(8,128)} %prev_ref.1) | copy-start | bytes 3145732
  16.3 0.7 copy-start.12
  19.5 5.8 %collective-permute-start.3 = (s16[272,256]{1,0:T(8,128)(2,1)S(1)}, s16[272,256]{1,0:T(8,128)(2,1)S(1)}, u32[]{:S(2)}, u32[]{:S(2)}) collective-permute-start(s16[272,256]{1,0:T(8,128)(2,1)S(1)} %get-tuple-element.51), channel_id=1, source_target_pairs={{0,1},{1,0},{2,3},{3,2},{4,5},{5,4},{6,7},{7,6},{8,9},{9,8},{10,11... | collective-permute-start | bytes 417800 | tf_op jit(solution)/shard_map/ppermute | solution.py:346
  19.5 9.2 %collective-permute-start.4 = (s16[272,256]{1,0:T(8,128)(2,1)S(1)}, s16[272,256]{1,0:T(8,128)(2,1)S(1)}, u32[]{:S(2)}, u32[]{:S(2)}) collective-permute-start(s16[272,256]{1,0:T(8,128)(2,1)S(1)} %get-tuple-element.52), channel_id=1, source_target_pairs={{0,2},{1,3},{2,0},{3,1},{4,6},{5,7},{6,4},{7,5},{8,10},{9,11},{10,... | collective-permute-start | bytes 417800 | tf_op jit(solution)/shard_map/ppermute | solution.py:346
  21.6 9.0 %collective-permute-start.5 = (s16[272,256]{1,0:T(8,128)(2,1)S(1)}, s16[272,256]{1,0:T(8,128)(2,1)S(1)}, u32[]{:S(2)}, u32[]{:S(2)}) collective-permute-start(s16[272,256]{1,0:T(8,128)(2,1)S(1)} %get-tuple-element.53), channel_id=1, source_target_pairs={{0,3},{1,2},{2,1},{3,0},{4,7},{5,6},{6,5},{7,4},{8,11},{9,10},{10,... | collective-permute-start | bytes 417800 | tf_op jit(solution)/shard_map/ppermute | solution.py:346
  23.0 11.9 %collective-permute-start.1 = (bf16[1040,128]{1,0:T(8,128)(2,1)S(1)}, bf16[1040,128]{1,0:T(8,128)(2,1)S(1)}, u32[]{:S(2)}, u32[]{:S(2)}) collective-permute-start(bf16[1040,128]{1,0:T(8,128)(2,1)S(1)} %get-tuple-element.45), channel_id=1, source_target_pairs={{0,2},{1,3},{2,0},{3,1},{4,6},{5,7},{6,4},{7,5},{8,10},{9,11},{10,... | collective-permute-start | bytes 798728 | tf_op jit(solution)/shard_map/ppermute | solution.py:346
  25.2 16.8 %collective-permute-start.2 = (bf16[1040,128]{1,0:T(8,128)(2,1)S(1)}, bf16[1040,128]{1,0:T(8,128)(2,1)S(1)}, u32[]{:S(2)}, u32[]{:S(2)}) collective-permute-start(bf16[1040,128]{1,0:T(8,128)(2,1)S(1)} %get-tuple-element.46), channel_id=1, source_target_pairs={{0,3},{1,2},{2,1},{3,0},{4,7},{5,6},{6,5},{7,4},{8,11},{9,10},{10,... | collective-permute-start | bytes 798728 | tf_op jit(solution)/shard_map/ppermute | solution.py:346
  28.7 22.9 %collective-permute-start.6 = (bf16[1024,128]{1,0:T(8,128)(2,1)S(1)}, bf16[1024,128]{1,0:T(8,128)(2,1)S(1)}, u32[]{:S(2)}, u32[]{:S(2)}) collective-permute-start(bf16[1024,128]{1,0:T(8,128)(2,1)S(1)} %get-tuple-element.61), channel_id=1, source_target_pairs={{0,1},{1,0},{2,3},{3,2},{4,5},{5,4},{6,7},{7,6},{8,9},{9,8},{10,11... | collective-permute-start | bytes 786440 | tf_op jit(solution)/shard_map/ppermute | solution.py:346
  30.6 21.0 %collective-permute-start.7 = (bf16[1024,128]{1,0:T(8,128)(2,1)S(1)}, bf16[1024,128]{1,0:T(8,128)(2,1)S(1)}, u32[]{:S(2)}, u32[]{:S(2)}) collective-permute-start(bf16[1024,128]{1,0:T(8,128)(2,1)S(1)} %get-tuple-element.62), channel_id=1, source_target_pairs={{0,2},{1,3},{2,0},{3,1},{4,6},{5,7},{6,4},{7,5},{8,10},{9,11},{10,... | collective-permute-start | bytes 786440 | tf_op jit(solution)/shard_map/ppermute | solution.py:346
  32.2 22.5 %collective-permute-start.8 = (bf16[1024,128]{1,0:T(8,128)(2,1)S(1)}, bf16[1024,128]{1,0:T(8,128)(2,1)S(1)}, u32[]{:S(2)}, u32[]{:S(2)}) collective-permute-start(bf16[1024,128]{1,0:T(8,128)(2,1)S(1)} %get-tuple-element.63), channel_id=1, source_target_pairs={{0,3},{1,2},{2,1},{3,0},{4,7},{5,6},{6,5},{7,4},{8,11},{9,10},{10,... | collective-permute-start | bytes 786440 | tf_op jit(solution)/shard_map/ppermute | solution.py:346
  33.0 15.0 %copy-start.3 = (f32[1024,256]{1,0:T(8,128)}, f32[1024,256]{1,0:T(8,128)S(1)}, u32[]{:S(2)}) copy-start(f32[1024,256]{1,0:T(8,128)S(1)} %get-tuple-element.54.prev_ref) | copy-start | bytes 3145732
  44.3 0.8 copy-start.9
  48.0 1.0 copy-start.5
  49.0 20.6 %collective-permute-start.9 = (s16[1040,128]{1,0:T(8,128)(2,1)}, s16[1040,128]{1,0:T(8,128)(2,1)S(1)}, u32[]{:S(2)}, u32[]{:S(2)}) collective-permute-start(s16[1040,128]{1,0:T(8,128)(2,1)} %get-tuple-element.65), channel_id=1, source_target_pairs={{0,4},{1,5},{2,6},{3,7},{4,0},{5,1},{6,2},{7,3},{8,12},{9,13},{10,... | collective-permute-start | bytes 798728 | tf_op jit(solution)/shard_map/ppermute | solution.py:346
  58.2 1.0 copy-start.7
  59.2 21.5 %copy-start.1 = (bf16[1024,1024]{1,0:T(8,128)(2,1)S(1)}, bf16[1024,1024]{1,0:T(8,128)(2,1)}, u32[]{:S(2)}) copy-start(bf16[1024,1024]{1,0:T(8,128)(2,1)} %points_ref.1) | copy-start | bytes 6291460
  59.2 13.5 %collective-permute-start.10 = (s16[1040,128]{1,0:T(8,128)(2,1)}, s16[1040,128]{1,0:T(8,128)(2,1)}, u32[]{:S(2)}, u32[]{:S(2)}) collective-permute-start(s16[1040,128]{1,0:T(8,128)(2,1)} %get-tuple-element.66), channel_id=1, source_target_pairs={{0,4},{1,5},{2,6},{3,7},{4,0},{5,1},{6,2},{7,3},{8,12},{9,13},{10,... | collective-permute-start | bytes 798728 | tf_op jit(solution)/shard_map/ppermute | solution.py:346
  60.4 12.3 %copy-start.4 = (f32[1024,256]{1,0:T(8,128)S(1)}, f32[1024,256]{1,0:T(8,128)}, u32[]{:S(2)}) copy-start(f32[1024,256]{1,0:T(8,128)} %copy-done.3) | copy-start | bytes 3145732
  60.4 12.3 %copy-start.6 = (f32[2048,128]{1,0:T(8,128)S(1)}, f32[2048,128]{1,0:T(8,128)}, u32[]{:S(2)}) copy-start(f32[2048,128]{1,0:T(8,128)} %copy-done.5) | copy-start | bytes 3145732
  72.7 1.2 %copy-start.8 = (f32[2048,128]{1,0:T(8,128)S(1)}, f32[2048,128]{1,0:T(8,128)}, u32[]{:S(2)}) copy-start(f32[2048,128]{1,0:T(8,128)} %copy-done.7) | copy-start | bytes 3145732
  74.0 1.0 copy-start.10
  75.0 14.4 %copy-start.13 = (bf16[2048,1024]{1,0:T(8,128)(2,1)S(1)}, bf16[2048,1024]{1,0:T(8,128)(2,1)}, u32[]{:S(2)}) copy-start(bf16[2048,1024]{1,0:T(8,128)(2,1)} %all-gather.2.cloned.1.call-done) | copy-start | bytes 12582916
  77.2 5.8 %collective-permute-start.11 = (s16[272,256]{1,0:T(8,128)(2,1)S(1)}, s16[272,256]{1,0:T(8,128)(2,1)S(1)}, u32[]{:S(2)}, u32[]{:S(2)}) collective-permute-start(s16[272,256]{1,0:T(8,128)(2,1)S(1)} %get-tuple-element.68), channel_id=1, source_target_pairs={{0,1},{1,0},{2,3},{3,2},{4,5},{5,4},{6,7},{7,6},{8,9},{9,8},{10,11... | collective-permute-start | bytes 417800 | tf_op jit(solution)/shard_map/ppermute | solution.py:346
  78.1 5.1 %collective-permute-start.12 = (s16[272,256]{1,0:T(8,128)(2,1)S(1)}, s16[272,256]{1,0:T(8,128)(2,1)S(1)}, u32[]{:S(2)}, u32[]{:S(2)}) collective-permute-start(s16[272,256]{1,0:T(8,128)(2,1)S(1)} %get-tuple-element.69), channel_id=1, source_target_pairs={{0,2},{1,3},{2,0},{3,1},{4,6},{5,7},{6,4},{7,5},{8,10},{9,11},{10,... | collective-permute-start | bytes 417800 | tf_op jit(solution)/shard_map/ppermute | solution.py:346
  78.1 7.2 %collective-permute-start.13 = (s16[272,256]{1,0:T(8,128)(2,1)S(1)}, s16[272,256]{1,0:T(8,128)(2,1)S(1)}, u32[]{:S(2)}, u32[]{:S(2)}) collective-permute-start(s16[272,256]{1,0:T(8,128)(2,1)S(1)} %get-tuple-element.70), channel_id=1, source_target_pairs={{0,3},{1,2},{2,1},{3,0},{4,7},{5,6},{6,5},{7,4},{8,11},{9,10},{10,... | collective-permute-start | bytes 417800 | tf_op jit(solution)/shard_map/ppermute | solution.py:346
  87.2 8.9 %collective-permute-start.14 = (s16[272,256]{1,0:T(8,128)(2,1)S(1)}, s16[272,256]{1,0:T(8,128)(2,1)S(1)}, u32[]{:S(2)}, u32[]{:S(2)}) collective-permute-start(s16[272,256]{1,0:T(8,128)(2,1)S(1)} %get-tuple-element.78.own), channel_id=1, source_target_pairs={{0,4},{1,5},{2,6},{3,7},{4,0},{5,1},{6,2},{7,3},{8,12},{9,13},{10,... | collective-permute-start | bytes 417800 | tf_op jit(solution)/shard_map/ppermute | solution.py:346
  95.3 6.3 %collective-permute-start.18 = (s16[272,256]{1,0:T(8,128)(2,1)S(1)}, s16[272,256]{1,0:T(8,128)(2,1)S(1)}, u32[]{:S(2)}, u32[]{:S(2)}) collective-permute-start(s16[272,256]{1,0:T(8,128)(2,1)S(1)} %get-tuple-element.79.own), channel_id=1, source_target_pairs={{0,4},{1,5},{2,6},{3,7},{4,0},{5,1},{6,2},{7,3},{8,12},{9,13},{10,... | collective-permute-start | bytes 417800 | tf_op jit(solution)/shard_map/ppermute | solution.py:346
  96.5 9.7 %collective-permute-start.17 = (s16[272,256]{1,0:T(8,128)(2,1)S(1)}, s16[272,256]{1,0:T(8,128)(2,1)S(1)}, u32[]{:S(2)}, u32[]{:S(2)}) collective-permute-start(s16[272,256]{1,0:T(8,128)(2,1)S(1)} %both0.1.refs_0_), channel_id=1, source_target_pairs={{0,3},{1,2},{2,1},{3,0},{4,7},{5,6},{6,5},{7,4},{8,11},{9,10},{10,... | collective-permute-start | bytes 417800 | tf_op jit(solution)/shard_map/ppermute | solution.py:346
  97.9 10.5 %collective-permute-start.16 = (s16[272,256]{1,0:T(8,128)(2,1)S(1)}, s16[272,256]{1,0:T(8,128)(2,1)S(1)}, u32[]{:S(2)}, u32[]{:S(2)}) collective-permute-start(s16[272,256]{1,0:T(8,128)(2,1)S(1)} %both0.1.refs_0_), channel_id=1, source_target_pairs={{0,2},{1,3},{2,0},{3,1},{4,6},{5,7},{6,4},{7,5},{8,10},{9,11},{10,... | collective-permute-start | bytes 417800 | tf_op jit(solution)/shard_map/ppermute | solution.py:346
  98.8 9.6 %collective-permute-start.15 = (s16[272,256]{1,0:T(8,128)(2,1)S(1)}, s16[272,256]{1,0:T(8,128)(2,1)S(1)}, u32[]{:S(2)}, u32[]{:S(2)}) collective-permute-start(s16[272,256]{1,0:T(8,128)(2,1)S(1)} %both0.1.refs_0_), channel_id=1, source_target_pairs={{0,1},{1,0},{2,3},{3,2},{4,5},{5,4},{6,7},{7,6},{8,9},{9,8},{10,11... | collective-permute-start | bytes 417800 | tf_op jit(solution)/shard_map/ppermute | solution.py:346
  102.0 7.8 %collective-permute-start.21 = (s16[272,256]{1,0:T(8,128)(2,1)S(1)}, s16[272,256]{1,0:T(8,128)(2,1)S(1)}, u32[]{:S(2)}, u32[]{:S(2)}) collective-permute-start(s16[272,256]{1,0:T(8,128)(2,1)S(1)} %both1.1.refs_4_), channel_id=1, source_target_pairs={{0,3},{1,2},{2,1},{3,0},{4,7},{5,6},{6,5},{7,4},{8,11},{9,10},{10,... | collective-permute-start | bytes 417800 | tf_op jit(solution)/shard_map/ppermute | solution.py:346
  104.3 7.1 %collective-permute-start.20 = (s16[272,256]{1,0:T(8,128)(2,1)S(1)}, s16[272,256]{1,0:T(8,128)(2,1)S(1)}, u32[]{:S(2)}, u32[]{:S(2)}) collective-permute-start(s16[272,256]{1,0:T(8,128)(2,1)S(1)} %both1.1.refs_4_), channel_id=1, source_target_pairs={{0,2},{1,3},{2,0},{3,1},{4,6},{5,7},{6,4},{7,5},{8,10},{9,11},{10,... | collective-permute-start | bytes 417800 | tf_op jit(solution)/shard_map/ppermute | solution.py:346
  106.2 5.3 %collective-permute-start.19 = (s16[272,256]{1,0:T(8,128)(2,1)S(1)}, s16[272,256]{1,0:T(8,128)(2,1)S(1)}, u32[]{:S(2)}, u32[]{:S(2)}) collective-permute-start(s16[272,256]{1,0:T(8,128)(2,1)S(1)} %both1.1.refs_4_), channel_id=1, source_target_pairs={{0,1},{1,0},{2,3},{3,2},{4,5},{5,4},{6,7},{7,6},{8,9},{9,8},{10,11... | collective-permute-start | bytes 417800 | tf_op jit(solution)/shard_map/ppermute | solution.py:346
Sparse Core Ops, SparseCore 0:
  9.6 37.1 all-gather.1

commit v8 on v7

--- a/solution.py
+++ b/solution.py
@@ -85,8 +85,7 @@
 
 
 def pack_kernel(chunks, me_ref, points_ref, cluster_ref, *refs):
-    outs, (after_ref, head, sems, head_sems) = refs[:-4], refs[-4:]
-    after_ref[0] = me_ref[0]
+    outs, (head, sems, head_sems) = refs[:-3], refs[-3:]
     rows = points_ref.shape[0]
     h = len(outs) // chunks
     q = me_ref[0] & (h - 1)
@@ -98,10 +97,8 @@
     wait_all(copies)
 
 
-def prev_kernel(me_ref, after_ref, prev_ref, parent_ref, *refs):
-    h = (len(refs) - 4) // 2
-    outs, (prev, head, sem, sems), held = refs[:h], refs[h : h + 4], refs[h + 4 :]
-    q = me_ref[0] & (h - 1)
+def prev_kernel(after_ref, me_ref, prev_ref, parent_ref, out_ref, prev, head, sem):
+    h = out_ref.shape[0]
     owned, width = prev.shape
     w = width // h
     copy = start(prev_ref, prev, sem)
@@ -113,12 +110,9 @@
     for j in range(owned // w):
         lanes = to_lanes(exponent[j * w : (j + 1) * w])
         head[known + j : known + j + 1, :] = lanes.astype(i32)
-    copies = []
-    for m in range(h):
-        held[m][0:owned, :] = encode(prev[:, chunk(q ^ m, w)], exponent)
-        held[m][owned:, :] = head[...].astype(i16)
-        copies.append(start(held[m], outs[m], sems.at[m]))
-    wait_all(copies)
+    for d in range(h):
+        out_ref[d, 0:owned, :] = encode(prev[:, d * w : (d + 1) * w], exponent)
+        out_ref[d, owned:, :] = head[...].astype(i16)
 
 
 def prepare_kernel(per, me_ref, *refs):
@@ -148,20 +142,21 @@
         far_ref[j : j + 1, :] = (to_lanes(high) * 64.0 + to_lanes(far - high * 64.0)).astype(i32)
 
 
-def previous_kernel(*refs):
-    arrived, (prev_ref, upper_ref) = refs[:-2], refs[-2:]
-    h = len(arrived)
+def previous_kernel(me_ref, arrived_ref, prev_ref, upper_ref):
+    h = arrived_ref.shape[0]
+    q = me_ref[0] & (h - 1)
     rows, w = prev_ref.shape
     owned = rows // h
     each = owned // w
     parent_at = lax.broadcasted_iota(i32, (upper_ref.shape[0], w), 0)
     for m in range(h):
-        head = arrived[m][owned:, :].astype(i32)
+        arrived = arrived_ref.at[q ^ m]
+        head = arrived[owned:, :].astype(i32)
         for j in range(each):
             at = slice(m * owned + j * w, m * owned + (j + 1) * w)
             upper_ref[:, at] = jnp.where(parent_at == head[j : j + 1, :], 1.0, 0.0).astype(bf16)
             exponent = to_column(head[each + j : each + j + 1, :].astype(f32))
-            prev_ref[at, :] = decode(arrived[m][j * w : (j + 1) * w, :], exponent)
+            prev_ref[at, :] = decode(arrived[j * w : (j + 1) * w, :], exponent)
 
 
 def sums_kernel(place_ref, before_ref, member_ref, far_count_ref, *refs):
@@ -352,11 +347,11 @@
     table_rows = lax.all_gather(cent2_prev, "dp", axis=0, tiled=True)
 
     first_shape = shape((point_rows + 2 * blocks, BLOCK), bf16)
-    *packed, after_pack = call(
+    packed = call(
         functools.partial(pack_kernel, chunks),
-        ([first_shape] + [shape((point_rows, BLOCK), bf16)] * (chunks - 1)) * h + [shape((1,), i32)],
+        ([first_shape] + [shape((point_rows, BLOCK), bf16)] * (chunks - 1)) * h,
         in_specs=[SMEM, HBM, VMEM],
-        out_specs=[HBM] * (h * chunks) + [SMEM],
+        out_specs=[HBM] * (h * chunks),
         scratch_shapes=[pltpu.VMEM((2 * blocks, BLOCK), bf16), dma(h * chunks), dma(h)],
         name="pack",
     )(me, points, point_cluster.reshape(blocks, BLOCK))
@@ -377,7 +372,7 @@
     )(me, *arrived[0])
 
     lines = rows + 2 * rows // BLOCK
-    accs, crossed, after = [], [], place
+    accs, crossed, after, first = [], [], place, None
     for c in range(chunks):
         acc, code, ended = call(
             sums_kernel,
@@ -391,29 +386,30 @@
         accs.append(acc)
         crossed.append(swap(code, h))
         after = ended
+        first = first if c else ended
 
     head = head_rows(2 * owned, w)
     prevs = call(
         prev_kernel,
-        [shape((owned + head, w), i16)] * h,
+        shape((h, owned + head, w), i16),
         in_specs=[SMEM, SMEM, HBM, VMEM],
-        out_specs=[HBM] * h,
-        scratch_shapes=[pltpu.VMEM((owned, width), f32), pltpu.VMEM((head, w), i32), dma(), dma(h)]
-        + [pltpu.VMEM((owned + head, w), i16)] * h,
+        out_specs=VMEM,
+        scratch_shapes=[pltpu.VMEM((owned, width), f32), pltpu.VMEM((head, w), i32), dma()],
         name="prev",
-    )(me, after_pack, cent1_prev, parent.reshape(owned // w, w))
+    )(first, me, cent1_prev, parent.reshape(owned // w, w))
+    halves = [list(range(k * h, (k + 1) * h)) for k in range(2)]
+    prevs = lax.all_to_all(prevs, "cent", split_axis=0, concat_axis=0, axis_index_groups=halves, tiled=True)
     prev, upper_member = call(
         previous_kernel,
         [shape((rows, w), f32), shape((upper_rows, rows), bf16)],
-        in_specs=[VMEM] * h,
+        in_specs=[SMEM, VMEM],
         out_specs=[VMEM] * 2,
         name="previous",
-    )(*swap_half(prevs))
+    )(me, prevs)
 
     points, table_rows = lax.optimization_barrier((points, table_rows))
     unit_points = rms_norm(points.astype(f32)).astype(bf16)
     table_scale = lax.rsqrt(jnp.mean(jnp.square(table_rows.astype(f32)), axis=-1) + EPSILON)
-    table_scale, near = lax.optimization_barrier((table_scale, near))
     table_units = (table_rows.astype(f32) * table_scale[:, None]).astype(bf16)
     products = lax.dot_general(
         unit_points, table_units, (((1,), (1,)), ((), ())), preferred_element_type=f32
@@ -422,7 +418,7 @@
     listed = jnp.any(cand_blocks[:, :, None] == column_block[None, None, :], axis=1)
     weights = jnp.exp(products * (SHARPNESS / width)).reshape(blocks, BLOCK, -1)
     running = jnp.sum(weights * listed[:, None, :].astype(f32), axis=2).reshape(point_rows)
-    point_score = jnp.log(running)
+    point_score, near = lax.optimization_barrier((jnp.log(running), near))
 
     tail = 4 * rows // w
     x, *backs = call(
@@ -452,8 +448,6 @@
     parts = []
     for k in range(2):
         code = codes[k]
-        if k == 0:
-            code, point_score = lax.optimization_barrier((code, point_score))
         code = call(
             both_kernel,
             code_shape,

time: 121 us -> 134 us (1.11)
  waiting for transfers between devices: 33.2 us -> 50.3 us
  starting transfers between devices: 31.5 us -> 28.7 us
    ppermute x22 -> x19, waiting for transfers between devices: 32.5 us -> 49.6 us  [swap(): return lax.ppermute(value, 'cent', [(i, i ^ mask) for i in range(n)])]
    ppermute x22 -> x19, starting transfers between devices: 31.5 us -> 24.3 us  [swap(): return lax.ppermute(value, 'cent', [(i, i ^ mask) for i in range(n)])]
    all_to_all x0 -> x1, starting transfers between devices: none -> 4.34 us  [shards(): lax.all_to_all(prevs, 'cent', split_axis=0, concat_axis=0, axis_index_gro...]
    unnamed x30 -> x38, local copies, waits for them, and re-layouts: 9.25 us -> 8.52 us
  transfers between devices with their start and end apart: 23 -> 21, of which waited for: 13 -> 16; matrix products, arithmetic and copies ran while one was open for 8% -> 8% of each run, Pallas kernels for 13% -> 12%
where the time goes in v8:
time: 134 us
  waiting for transfers between devices  50.3 us (38%)
  starting transfers between devices  28.7 us (21%)
  Pallas kernels  22 us (16%)
  between operations  14.3 us (11%)
  local copies, waits for them, and re-layouts  9.13 us (7%)
  matrix products  5.38 us (4%)
  other arithmetic  4.12 us (3%)
    ppermute x19, waiting for transfers between devices, swap(): return lax.ppermute(value, 'cent', [(i, i ^ mask) for i in range(n)])  49.6 us
    ppermute x19, starting transfers between devices, swap(): return lax.ppermute(value, 'cent', [(i, i ^ mask) for i in range(n)])  24.3 us
    unnamed x38, local copies, waits for them, and re-layouts  8.52 us
    pallas_call x2, Pallas kernels, shards(): call(sums_kernel, [shape((2 * rows, BLOCK), f32), shape((lines, BLOCK), i...  5.73 us
    dot_general x1, matrix products, shards(): lax.dot_general(unit_points, table_units, (((1,), (1,)), ((), ())), prefe...  5.38 us
    all_to_all x1, starting transfers between devices, shards(): lax.all_to_all(prevs, 'cent', split_axis=0, concat_axis=0, axis_index_gro...  4.34 us
    reduce_sum x1, other arithmetic, shards(): jnp.mean(jnp.square(table_rows.astype(f32)), axis=-1) + EPSILON  3.31 us
  transfers between devices with their start and end apart: 21, of which 16 were waited for; matrix products, arithmetic and copies ran while one was open for 8% of the time, Pallas kernels for 12%

profile of v8, /device:TPU:0, one launch (start us, length us, event | category | flops | bytes accessed | tf_op | source)
XLA Modules:
  0.0 133.9 jit_solution(7062569465647091749)
XLA Ops:
  8.0 1.6 %copy-done = bf16[1024,1024]{1,0:T(8,128)(2,1)S(1)} copy-done((bf16[1024,1024]{1,0:T(8,128)(2,1)S(1)}, bf16[1024,1024]{1,0:T(8,128)(2,1)}, u32[]{:S(2)}) %copy-start) | copy-done | bytes 2097176
  10.3 1.8 %pack.1 = (bf16[1040,128]{1,0:T(8,128)(2,1)S(1)}, bf16[1024,128]{1,0:T(8,128)(2,1)S(1)}, bf16[1040,128]{1,0:T(8,128)(2,1)S(1)}, bf16[1024,128]{1,0:T(8,128)(2,1)...) custom-call(s32[3]{0:T(128)S(1)} %pad_add_fusion.me_ref, ...), custom_call_target="tpu_custom_call" | custom-call | tf_op jit(solution)/shard_map/pack/pallas_call | solution.py:350
  12.1 3.0 %collective-permute-start = (bf16[1040,128]{1,0:T(8,128)(2,1)S(1)}, bf16[1040,128]{1,0:T(8,128)(2,1)S(1)}, u32[]{:S(2)}, u32[]{:S(2)}) collective-permute-start(bf16[1040,128]{1,0:T(8,128)(2,1)S(1)} %get-tuple-element.38), channel_id=1, source_target_pairs={{0,1},{1,0},{2,3},{3,2},{4,5},{5,4},{6,7},{7,6},{8,9},{9,8},{10,11... | collective-permute-start | bytes 798728 | tf_op jit(solution)/shard_map/ppermute | solution.py:341
  15.1 1.6 %collective-permute-start.1 = (bf16[1040,128]{1,0:T(8,128)(2,1)S(1)}, bf16[1040,128]{1,0:T(8,128)(2,1)S(1)}, u32[]{:S(2)}, u32[]{:S(2)}) collective-permute-start(bf16[1040,128]{1,0:T(8,128)(2,1)S(1)} %get-tuple-element.39), channel_id=1, source_target_pairs={{0,2},{1,3},{2,0},{3,1},{4,6},{5,7},{6,4},{7,5},{8,10},{9,11},{10,... | collective-permute-start | bytes 798728 | tf_op jit(solution)/shard_map/ppermute | solution.py:341
  16.7 4.8 %collective-permute-done.refs_1_ = bf16[1040,128]{1,0:T(8,128)(2,1)S(1)} collective-permute-done((bf16[1040,128]{1,0:T(8,128)(2,1)S(1)}, bf16[1040,128]{1,0:T(8,128)(2,1)S(1)}, u32[]{:S(2)}, u32[]{:S(2)}) %collective-permute-start) | collective-permute-done | bytes 266272 | tf_op jit(solution)/shard_map/ppermute | solution.py:341
  21.5 2.9 %collective-permute-done.1.refs_2_ = bf16[1040,128]{1,0:T(8,128)(2,1)S(1)} collective-permute-done((bf16[1040,128]{1,0:T(8,128)(2,1)S(1)}, bf16[1040,128]{1,0:T(8,128)(2,1)S(1)}, u32[]{:S(2)}, u32[]{:S(2)}) %collective-permute-start.1) | collective-permute-done | bytes 266272 | tf_op jit(solution)/shard_map/ppermute | solution.py:341
  24.4 4.0 %collective-permute-done.2.refs_3_ = bf16[1040,128]{1,0:T(8,128)(2,1)S(1)} collective-permute-done((bf16[1040,128]{1,0:T(8,128)(2,1)S(1)}, bf16[1040,128]{1,0:T(8,128)(2,1)S(1)}, u32[]{:S(2)}, u32[]{:S(2)}) %collective-permute-start.2) | collective-permute-done | bytes 266272 | tf_op jit(solution)/shard_map/ppermute | solution.py:341
  28.5 2.3 %prepare.1 = (bf16[4096,128]{1,0:T(8,128)(2,1)S(1)}, s32[32]{0:T(128)S(1)}, f32[1024,128]{1,0:T(8,128)S(1)}, s32[8,128]{1,0:T(8,128)S(1)}) custom-call(s32[3]{0:T(128)S(1)} %pad_add_fusion.me_ref, bf16[1040,128]{1,0:T(8,128)(2,1)S(1)} %get-tuple-element.37.refs_0_, bf16[1040,128]{1,0:T(8,128)(2,1)S(1)} %collective-permute-done.refs_1_, ...), custom_call_target="tpu_custom_call" | custom-call | tf_op jit(solution)/shard_map/prepare/pallas_call | solution.py:360
  30.8 0.8 copy-done.10
  31.6 2.2 %sums0.1 = (f32[2048,128]{1,0:T(8,128)S(1)}, s16[1040,128]{1,0:T(8,128)(2,1)S(1)}, s32[1]{0:T(128)}) custom-call(s32[32]{0:T(128)S(1)} %get-tuple-element.43.place_ref.before_ref, s32[32]{0:T(128)S(1)} %get-tuple-element.43.place_ref.before_ref, bf16[4096,128]{1,0:T(8,128)(2,1)S(1)} %get-tuple-element.44.member_ref, ...), custom_call_target="tpu_custom_call" | custom-call | tf_op jit(solution)/shard_map/sums0/pallas_call | solution.py:377
  33.8 1.0 copy-done.4
  34.8 0.7 copy-done.16
  35.5 1.7 %prev.1 = s16[4,272,256]{2,1,0:T(8,128)(2,1)S(1)} custom-call(s32[1]{0:T(128)} %get-tuple-element.46.after_ref.before_ref, s32[3]{0:T(128)S(1)} %pad_add_fusion.me_ref, f32[256,1024]{1,0:T(8,128)S(1)} %copy-done.3, s32[1,256]{1,0:T(1,128)S(1)} %bitcast.10), custom_call_target="tpu_custom_call" | custom-call | tf_op jit(solution)/shard_map/prev/pallas_call | solution.py:392
  37.2 0.8 copy-done.2
  38.0 4.3 %all-to-all-start = ((s16[4,272,256]{2,1,0:T(8,128)(2,1)}), s16[4,272,256]{2,1,0:T(8,128)(2,1)}, u32[]{:S(2)}, u32[]{:S(2)}) async-start(s16[4,272,256]{2,1,0:T(8,128)(2,1)} %copy-done.2), calls=%async_computation | async-start | bytes 1114112 | tf_op jit(solution)/shard_map/all_to_all | solution.py:401
  42.3 1.8 %collective-permute-start.3 = (bf16[1024,128]{1,0:T(8,128)(2,1)}, bf16[1024,128]{1,0:T(8,128)(2,1)S(1)}, u32[]{:S(2)}, u32[]{:S(2)}) collective-permute-start(bf16[1024,128]{1,0:T(8,128)(2,1)} %get-tuple-element.50), channel_id=1, source_target_pairs={{0,1},{1,0},{2,3},{3,2},{4,5},{5,4},{6,7},{7,6},{8,9},{9,8},{10,11... | collective-permute-start | bytes 786440 | tf_op jit(solution)/shard_map/ppermute | solution.py:341
  44.1 1.5 %collective-permute-start.4 = (bf16[1024,128]{1,0:T(8,128)(2,1)}, bf16[1024,128]{1,0:T(8,128)(2,1)S(1)}, u32[]{:S(2)}, u32[]{:S(2)}) collective-permute-start(bf16[1024,128]{1,0:T(8,128)(2,1)} %get-tuple-element.51), channel_id=1, source_target_pairs={{0,2},{1,3},{2,0},{3,1},{4,6},{5,7},{6,4},{7,5},{8,10},{9,11},{10,... | collective-permute-start | bytes 786440 | tf_op jit(solution)/shard_map/ppermute | solution.py:341
  46.1 2.8 %collective-permute-start.6 = (s16[1040,128]{1,0:T(8,128)(2,1)}, s16[1040,128]{1,0:T(8,128)(2,1)S(1)}, u32[]{:S(2)}, u32[]{:S(2)}) collective-permute-start(s16[1040,128]{1,0:T(8,128)(2,1)} %copy-done.16), channel_id=1, source_target_pairs={{0,4},{1,5},{2,6},{3,7},{4,0},{5,1},{6,2},{7,3},{8,12},{9,13},{10,... | collective-permute-start | bytes 798728 | tf_op jit(solution)/shard_map/ppermute | solution.py:341
  49.0 6.4 %collective-permute-done.3.refs_1_ = bf16[1024,128]{1,0:T(8,128)(2,1)S(1)} collective-permute-done((bf16[1024,128]{1,0:T(8,128)(2,1)}, bf16[1024,128]{1,0:T(8,128)(2,1)S(1)}, u32[]{:S(2)}, u32[]{:S(2)}) %collective-permute-start.3) | collective-permute-done | bytes 262176 | tf_op jit(solution)/shard_map/ppermute | solution.py:341
  55.4 7.9 %collective-permute-done.4.refs_2_ = bf16[1024,128]{1,0:T(8,128)(2,1)S(1)} collective-permute-done((bf16[1024,128]{1,0:T(8,128)(2,1)}, bf16[1024,128]{1,0:T(8,128)(2,1)S(1)}, u32[]{:S(2)}, u32[]{:S(2)}) %collective-permute-start.4) | collective-permute-done | bytes 262176 | tf_op jit(solution)/shard_map/ppermute | solution.py:341
  63.2 4.5 %collective-permute-done.5.refs_3_ = bf16[1024,128]{1,0:T(8,128)(2,1)S(1)} collective-permute-done((bf16[1024,128]{1,0:T(8,128)(2,1)}, bf16[1024,128]{1,0:T(8,128)(2,1)S(1)}, u32[]{:S(2)}, u32[]{:S(2)}) %collective-permute-start.5) | collective-permute-done | bytes 262176 | tf_op jit(solution)/shard_map/ppermute | solution.py:341
  67.7 0.9 copy-done.13
  68.7 3.5 %sums1.1 = (f32[2048,128]{1,0:T(8,128)S(1)}, s16[1040,128]{1,0:T(8,128)(2,1)}, s32[1]{0:T(128)}) custom-call(s32[32]{0:T(128)S(1)} %get-tuple-element.43.place_ref.before_ref, s32[1]{0:T(128)} %get-tuple-element.46.after_ref.before_ref, bf16[4096,128]{1,0:T(8,128)(2,1)S(1)} %get-tuple-element.44.member_ref, s32[8,128]{1,0:T(8,128)S(1)} %get-tuple-element.45.far_count_ref, ...), custom_call_target="tpu_custom_call" | custom-call | tf_op jit(solution)/shard_map/sums1/pallas_call | solution.py:377
  72.2 1.0 copy-done.6
  73.2 1.6 %previous.1 = (f32[1024,256]{1,0:T(8,128)S(1)}, bf16[512,1024]{1,0:T(8,128)(2,1)S(1)}) custom-call(s32[3]{0:T(128)S(1)} %pad_add_fusion.me_ref, s16[4,272,256]{2,1,0:T(8,128)(2,1)} %all-to-all-done.arrived_ref), custom_call_target="tpu_custom_call" | custom-call | tf_op jit(solution)/shard_map/previous/pallas_call | solution.py:402
  74.8 1.0 copy-done.8
  76.3 3.3 %fusion = f32[2048]{0:T(1024)S(1)} fusion(bf16[2048,1024]{1,0:T(8,128)(2,1)} %all-gather.2.cloned.1.call-done), kind=kLoop, calls=%fused_computation.2 | loop fusion | flops 6289408 | bytes 4202496 | tf_op jit(solution)/shard_map/reduce_sum | solution.py:412
  79.7 5.4 %fusion.2 = f32[1024]{0:T(1024)S(1)} fusion(bf16[2048,1024]{1,0:T(8,128)(2,1)S(1)} %copy-done.17, f32[8,2048]{1,0:T(8,128)S(1)} %convert_element_type.25, f32[2048]{0:T(1024)S(1)} %add_rsqrt_fusion, bf16[1024,1024]{1,0:T(8,128)(2,1)S(1)} %copy-done.1, f32[1024]{0:T(1024)S(1)} %add_rsqrt_fusion.1), kind=kOutput, calls=%fused_computation.5 | convolution fusion | flops 4310694912 | bytes 6373376 | tf_op jit(solution)/shard_map/dot_general | solution.py:414
  85.9 2.1 %refresh.1 = (f32[1024,256]{1,0:T(8,128)S(1)}, s16[272,256]{1,0:T(8,128)(2,1)S(1)}, s16[272,256]{1,0:T(8,128)(2,1)S(1)}, s16[272,256]{1,0:T(8,128)(2,1)S(1)}, s16[272,256]{1,0:T(8,128)(2,1)S(1)}) custom-call(f32[1024,128]{1,0:T(8,128)S(1)} %copy-done.11, f32[1024,256]{1,0:T(8,128)S(1)} %copy-done.9, f32[2048,128]{1,0:T(8,128)S(1)} %copy-done.5, ...), custom_call_target="tpu_custom_call" | custom-call | tf_op jit(solution)/shard_map/refresh/pallas_call | solution.py:424
  88.0 1.0 collective-permute-start.8
  88.9 2.3 %collective-permute-start.9 = (s16[272,256]{1,0:T(8,128)(2,1)S(1)}, s16[272,256]{1,0:T(8,128)(2,1)S(1)}, u32[]{:S(2)}, u32[]{:S(2)}) collective-permute-start(s16[272,256]{1,0:T(8,128)(2,1)S(1)} %get-tuple-element.58), channel_id=1, source_target_pairs={{0,2},{1,3},{2,0},{3,1},{4,6},{5,7},{6,4},{7,5},{8,10},{9,11},{10,... | collective-permute-start | bytes 417800 | tf_op jit(solution)/shard_map/ppermute | solution.py:341
  91.2 1.0 collective-permute-start.10
  92.2 2.2 %collective-permute-done.8.refs_1_ = s16[272,256]{1,0:T(8,128)(2,1)S(1)} collective-permute-done((s16[272,256]{1,0:T(8,128)(2,1)S(1)}, s16[272,256]{1,0:T(8,128)(2,1)S(1)}, u32[]{:S(2)}, u32[]{:S(2)}) %collective-permute-start.8) | collective-permute-done | bytes 139296 | tf_op jit(solution)/shard_map/ppermute | solution.py:341
  94.4 1.2 collective-permute-done.9.refs_2_
  95.6 2.2 %collective-permute-done.10.refs_3_ = s16[272,256]{1,0:T(8,128)(2,1)S(1)} collective-permute-done((s16[272,256]{1,0:T(8,128)(2,1)S(1)}, s16[272,256]{1,0:T(8,128)(2,1)S(1)}, u32[]{:S(2)}, u32[]{:S(2)}) %collective-permute-start.10) | collective-permute-done | bytes 139296 | tf_op jit(solution)/shard_map/ppermute | solution.py:341
  97.8 1.9 %upper.1 = (s16[272,256]{1,0:T(8,128)(2,1)S(1)}, s16[272,256]{1,0:T(8,128)(2,1)S(1)}) custom-call(bf16[512,1024]{1,0:T(8,128)(2,1)S(1)} %get-tuple-element.62.member_ref, f32[1024,256]{1,0:T(8,128)S(1)} %get-tuple-element.63.x_ref, s16[272,256]{1,0:T(8,128)(2,1)S(1)} %get-tuple-element.56.refs_0_, s16[272,256]{1,0:T(8,128)(2,1)S(1)} %collective-permute-done.8.refs_1_, ...), custom_call_target="tpu_custom_call" | custom-call | tf_op jit(solution)/shard_map/upper/pallas_call | solution.py:438
  99.6 1.0 collective-permute-start.11
  100.6 1.9 %collective-permute-start.15 = (s16[272,256]{1,0:T(8,128)(2,1)S(1)}, s16[272,256]{1,0:T(8,128)(2,1)S(1)}, u32[]{:S(2)}, u32[]{:S(2)}) collective-permute-start(s16[272,256]{1,0:T(8,128)(2,1)S(1)} %get-tuple-element.65.own), channel_id=1, source_target_pairs={{0,4},{1,5},{2,6},{3,7},{4,0},{5,1},{6,2},{7,3},{8,12},{9,13},{10,... | collective-permute-start | bytes 417800 | tf_op jit(solution)/shard_map/ppermute | solution.py:341
  102.6 7.9 %collective-permute-done.11.far = s16[272,256]{1,0:T(8,128)(2,1)S(1)} collective-permute-done((s16[272,256]{1,0:T(8,128)(2,1)S(1)}, s16[272,256]{1,0:T(8,128)(2,1)S(1)}, u32[]{:S(2)}, u32[]{:S(2)}) %collective-permute-start.11) | collective-permute-done | bytes 139296 | tf_op jit(solution)/shard_map/ppermute | solution.py:341
  110.9 2.1 %collective-permute-start.13 = (s16[272,256]{1,0:T(8,128)(2,1)S(1)}, s16[272,256]{1,0:T(8,128)(2,1)S(1)}, u32[]{:S(2)}, u32[]{:S(2)}) collective-permute-start(s16[272,256]{1,0:T(8,128)(2,1)S(1)} %both0.1.refs_0_), channel_id=1, source_target_pairs={{0,2},{1,3},{2,0},{3,1},{4,6},{5,7},{6,4},{7,5},{8,10},{9,11},{10,... | collective-permute-start | bytes 417800 | tf_op jit(solution)/shard_map/ppermute | solution.py:341
  113.0 1.4 %collective-permute-start.12 = (s16[272,256]{1,0:T(8,128)(2,1)S(1)}, s16[272,256]{1,0:T(8,128)(2,1)S(1)}, u32[]{:S(2)}, u32[]{:S(2)}) collective-permute-start(s16[272,256]{1,0:T(8,128)(2,1)S(1)} %both0.1.refs_0_), channel_id=1, source_target_pairs={{0,1},{1,0},{2,3},{3,2},{4,5},{5,4},{6,7},{7,6},{8,9},{9,8},{10,11... | collective-permute-start | bytes 417800 | tf_op jit(solution)/shard_map/ppermute | solution.py:341
  114.9 2.0 %collective-permute-start.17 = (s16[272,256]{1,0:T(8,128)(2,1)S(1)}, s16[272,256]{1,0:T(8,128)(2,1)S(1)}, u32[]{:S(2)}, u32[]{:S(2)}) collective-permute-start(s16[272,256]{1,0:T(8,128)(2,1)S(1)} %both1.1.refs_4_), channel_id=1, source_target_pairs={{0,2},{1,3},{2,0},{3,1},{4,6},{5,7},{6,4},{7,5},{8,10},{9,11},{10,... | collective-permute-start | bytes 417800 | tf_op jit(solution)/shard_map/ppermute | solution.py:341
  116.9 1.6 %collective-permute-done.14.refs_3_ = s16[272,256]{1,0:T(8,128)(2,1)S(1)} collective-permute-done((s16[272,256]{1,0:T(8,128)(2,1)S(1)}, s16[272,256]{1,0:T(8,128)(2,1)S(1)}, u32[]{:S(2)}, u32[]{:S(2)}) %collective-permute-start.14) | collective-permute-done | bytes 139296 | tf_op jit(solution)/shard_map/ppermute | solution.py:341
  119.1 1.9 %decode.1 = f32[256,1024]{1,0:T(8,128)} custom-call(s32[3]{0:T(128)S(1)} %pad_add_fusion.me_ref, s16[272,256]{1,0:T(8,128)(2,1)S(1)} %get-tuple-element.56.refs_0_, s16[272,256]{1,0:T(8,128)(2,1)S(1)} %collective-permute-done.8.refs_1_, s16[272,256]{1,0:T(8,128)(2,1)S(1)} %collective-permute-done.9.refs_2_, s16[272,256]{1,0:T(8,128)(2,1)S(1)} %collective-permute-done.10.refs_3_), custom_call_target="tpu_custom_call" | custom-call | tf_op jit(solution)/shard_map/decode/pallas_call | solution.py:461
  121.0 1.0 collective-permute-done.12.refs_1_
  122.0 1.4 %collective-permute-done.18.refs_7_ = s16[272,256]{1,0:T(8,128)(2,1)S(1)} collective-permute-done((s16[272,256]{1,0:T(8,128)(2,1)S(1)}, s16[272,256]{1,0:T(8,128)(2,1)S(1)}, u32[]{:S(2)}, u32[]{:S(2)}) %collective-permute-start.18) | collective-permute-done | bytes 139296 | tf_op jit(solution)/shard_map/ppermute | solution.py:341
  123.4 1.0 collective-permute-done.17.refs_6_
  124.8 2.3 %join.1 = f32[512,1024]{1,0:T(8,128)} custom-call(s32[3]{0:T(128)S(1)} %pad_add_fusion.me_ref, s16[272,256]{1,0:T(8,128)(2,1)S(1)} %both0.1.refs_0_, s16[272,256]{1,0:T(8,128)(2,1)S(1)} %collective-permute-done.12.refs_1_, s16[272,256]{1,0:T(8,128)(2,1)S(1)} %collective-permute-done.13.refs_2_, s16[272,256]{1,0:T(8,128)(2,1)S(1)} %collective-permute-done.14.refs_3_, ...), custom_call_target="tpu_custom_call" | custom-call | tf_op jit(solution)/shard_map/join/pallas_call | solution.py:469
  (55 shorter events, 5.2 us)
Async XLA Ops:
  7.2 28.3 %copy-start.15 = (s32[256]{0:T(256)S(1)}, s32[256]{0:T(256)}, u32[]{:S(2)}) copy-start(s32[256]{0:T(256)} %param.10) | copy-start | bytes 3076
  7.2 68.6 %all-gather.2.cloned.1.call-start = ((), (), s32[]{:S(2)}) async-start(), calls=%async_computation.1 | async-start | bytes 5242880 | tf_op jit(solution)/shard_map/all_gather | solution.py:347
  7.9 38.0 %copy-start.18 = (s32[8,8]{1,0:T(8,128)S(1)}, s32[8,8]{1,0:T(8,128)}, u32[]{:S(2)}) copy-start(s32[8,8]{1,0:T(8,128)} %param.8) | copy-start | bytes 772
  8.0 1.6 %copy-start = (bf16[1024,1024]{1,0:T(8,128)(2,1)S(1)}, bf16[1024,1024]{1,0:T(8,128)(2,1)}, u32[]{:S(2)}) copy-start(bf16[1024,1024]{1,0:T(8,128)(2,1)} %points_ref.1) | copy-start | bytes 6291460
  9.6 0.7 copy-start.14
  10.3 25.2 %copy-start.3 = (f32[256,1024]{1,0:T(8,128)S(1)}, f32[256,1024]{1,0:T(8,128)}, u32[]{:S(2)}) copy-start(f32[256,1024]{1,0:T(8,128)} %prev_ref.1) | copy-start | bytes 3145732
  12.1 23.4 %copy-start.12 = (bf16[1024,128]{1,0:T(8,128)(2,1)}, bf16[1024,128]{1,0:T(8,128)(2,1)S(1)}, u32[]{:S(2)}) copy-start(bf16[1024,128]{1,0:T(8,128)(2,1)S(1)} %get-tuple-element.49.refs_0_) | copy-start | bytes 786436
  12.1 9.4 %collective-permute-start = (bf16[1040,128]{1,0:T(8,128)(2,1)S(1)}, bf16[1040,128]{1,0:T(8,128)(2,1)S(1)}, u32[]{:S(2)}, u32[]{:S(2)}) collective-permute-start(bf16[1040,128]{1,0:T(8,128)(2,1)S(1)} %get-tuple-element.38), channel_id=1, source_target_pairs={{0,1},{1,0},{2,3},{3,2},{4,5},{5,4},{6,7},{7,6},{8,9},{9,8},{10,11... | collective-permute-start | bytes 798728 | tf_op jit(solution)/shard_map/ppermute | solution.py:341
  15.1 9.3 %collective-permute-start.1 = (bf16[1040,128]{1,0:T(8,128)(2,1)S(1)}, bf16[1040,128]{1,0:T(8,128)(2,1)S(1)}, u32[]{:S(2)}, u32[]{:S(2)}) collective-permute-start(bf16[1040,128]{1,0:T(8,128)(2,1)S(1)} %get-tuple-element.39), channel_id=1, source_target_pairs={{0,2},{1,3},{2,0},{3,1},{4,6},{5,7},{6,4},{7,5},{8,10},{9,11},{10,... | collective-permute-start | bytes 798728 | tf_op jit(solution)/shard_map/ppermute | solution.py:341
  16.7 11.8 %collective-permute-start.2 = (bf16[1040,128]{1,0:T(8,128)(2,1)S(1)}, bf16[1040,128]{1,0:T(8,128)(2,1)S(1)}, u32[]{:S(2)}, u32[]{:S(2)}) collective-permute-start(bf16[1040,128]{1,0:T(8,128)(2,1)S(1)} %get-tuple-element.40), channel_id=1, source_target_pairs={{0,3},{1,2},{2,1},{3,0},{4,7},{5,6},{6,5},{7,4},{8,11},{9,10},{10,... | collective-permute-start | bytes 798728 | tf_op jit(solution)/shard_map/ppermute | solution.py:341
  28.5 47.3 %copy-start.1 = (bf16[1024,1024]{1,0:T(8,128)(2,1)S(1)}, bf16[1024,1024]{1,0:T(8,128)(2,1)}, u32[]{:S(2)}) copy-start(bf16[1024,1024]{1,0:T(8,128)(2,1)} %points_ref.1) | copy-start | bytes 6291460
  30.8 0.8 copy-start.10
  33.8 1.0 copy-start.4
  34.8 0.7 copy-start.16
  37.2 0.8 copy-start.2
  38.0 35.2 %all-to-all-start = ((s16[4,272,256]{2,1,0:T(8,128)(2,1)}), s16[4,272,256]{2,1,0:T(8,128)(2,1)}, u32[]{:S(2)}, u32[]{:S(2)}) async-start(s16[4,272,256]{2,1,0:T(8,128)(2,1)} %copy-done.2), calls=%async_computation | async-start | bytes 1114112 | tf_op jit(solution)/shard_map/all_to_all | solution.py:401
  42.3 13.0 %collective-permute-start.3 = (bf16[1024,128]{1,0:T(8,128)(2,1)}, bf16[1024,128]{1,0:T(8,128)(2,1)S(1)}, u32[]{:S(2)}, u32[]{:S(2)}) collective-permute-start(bf16[1024,128]{1,0:T(8,128)(2,1)} %get-tuple-element.50), channel_id=1, source_target_pairs={{0,1},{1,0},{2,3},{3,2},{4,5},{5,4},{6,7},{7,6},{8,9},{9,8},{10,11... | collective-permute-start | bytes 786440 | tf_op jit(solution)/shard_map/ppermute | solution.py:341
  44.1 19.1 %collective-permute-start.4 = (bf16[1024,128]{1,0:T(8,128)(2,1)}, bf16[1024,128]{1,0:T(8,128)(2,1)S(1)}, u32[]{:S(2)}, u32[]{:S(2)}) collective-permute-start(bf16[1024,128]{1,0:T(8,128)(2,1)} %get-tuple-element.51), channel_id=1, source_target_pairs={{0,2},{1,3},{2,0},{3,1},{4,6},{5,7},{6,4},{7,5},{8,10},{9,11},{10,... | collective-permute-start | bytes 786440 | tf_op jit(solution)/shard_map/ppermute | solution.py:341
  45.6 22.1 %collective-permute-start.5 = (bf16[1024,128]{1,0:T(8,128)(2,1)}, bf16[1024,128]{1,0:T(8,128)(2,1)S(1)}, u32[]{:S(2)}, u32[]{:S(2)}) collective-permute-start(bf16[1024,128]{1,0:T(8,128)(2,1)} %get-tuple-element.52), channel_id=1, source_target_pairs={{0,3},{1,2},{2,1},{3,0},{4,7},{5,6},{6,5},{7,4},{8,11},{9,10},{10,... | collective-permute-start | bytes 786440 | tf_op jit(solution)/shard_map/ppermute | solution.py:341
  46.1 39.5 %collective-permute-start.6 = (s16[1040,128]{1,0:T(8,128)(2,1)}, s16[1040,128]{1,0:T(8,128)(2,1)S(1)}, u32[]{:S(2)}, u32[]{:S(2)}) collective-permute-start(s16[1040,128]{1,0:T(8,128)(2,1)} %copy-done.16), channel_id=1, source_target_pairs={{0,4},{1,5},{2,6},{3,7},{4,0},{5,1},{6,2},{7,3},{8,12},{9,13},{10,... | collective-permute-start | bytes 798728 | tf_op jit(solution)/shard_map/ppermute | solution.py:341
  67.7 1.0 copy-start.13
  72.2 1.0 copy-start.6
  73.2 12.7 %collective-permute-start.7 = (s16[1040,128]{1,0:T(8,128)(2,1)}, s16[1040,128]{1,0:T(8,128)(2,1)}, u32[]{:S(2)}, u32[]{:S(2)}) collective-permute-start(s16[1040,128]{1,0:T(8,128)(2,1)} %get-tuple-element.55), channel_id=1, source_target_pairs={{0,4},{1,5},{2,6},{3,7},{4,0},{5,1},{6,2},{7,3},{8,12},{9,13},{10,... | collective-permute-start | bytes 798728 | tf_op jit(solution)/shard_map/ppermute | solution.py:341
  74.8 1.0 copy-start.8
  75.8 3.8 %copy-start.17 = (bf16[2048,1024]{1,0:T(8,128)(2,1)S(1)}, bf16[2048,1024]{1,0:T(8,128)(2,1)}, u32[]{:S(2)}) copy-start(bf16[2048,1024]{1,0:T(8,128)(2,1)} %all-gather.2.cloned.1.call-done) | copy-start | bytes 12582916
  79.6 6.3 %copy-start.5 = (f32[2048,128]{1,0:T(8,128)S(1)}, f32[2048,128]{1,0:T(8,128)}, u32[]{:S(2)}) copy-start(f32[2048,128]{1,0:T(8,128)} %copy-done.4) | copy-start | bytes 3145732
  79.6 6.3 %copy-start.7 = (f32[2048,128]{1,0:T(8,128)S(1)}, f32[2048,128]{1,0:T(8,128)}, u32[]{:S(2)}) copy-start(f32[2048,128]{1,0:T(8,128)} %copy-done.6) | copy-start | bytes 3145732
  79.6 6.3 %copy-start.9 = (f32[1024,256]{1,0:T(8,128)S(1)}, f32[1024,256]{1,0:T(8,128)}, u32[]{:S(2)}) copy-start(f32[1024,256]{1,0:T(8,128)} %copy-done.8) | copy-start | bytes 3145732
  79.6 6.3 %copy-start.11 = (f32[1024,128]{1,0:T(8,128)S(1)}, f32[1024,128]{1,0:T(8,128)}, u32[]{:S(2)}) copy-start(f32[1024,128]{1,0:T(8,128)} %copy-done.10) | copy-start | bytes 1572868
  88.0 6.5 %collective-permute-start.8 = (s16[272,256]{1,0:T(8,128)(2,1)S(1)}, s16[272,256]{1,0:T(8,128)(2,1)S(1)}, u32[]{:S(2)}, u32[]{:S(2)}) collective-permute-start(s16[272,256]{1,0:T(8,128)(2,1)S(1)} %get-tuple-element.57), channel_id=1, source_target_pairs={{0,1},{1,0},{2,3},{3,2},{4,5},{5,4},{6,7},{7,6},{8,9},{9,8},{10,11... | collective-permute-start | bytes 417800 | tf_op jit(solution)/shard_map/ppermute | solution.py:341
  88.9 6.7 %collective-permute-start.9 = (s16[272,256]{1,0:T(8,128)(2,1)S(1)}, s16[272,256]{1,0:T(8,128)(2,1)S(1)}, u32[]{:S(2)}, u32[]{:S(2)}) collective-permute-start(s16[272,256]{1,0:T(8,128)(2,1)S(1)} %get-tuple-element.58), channel_id=1, source_target_pairs={{0,2},{1,3},{2,0},{3,1},{4,6},{5,7},{6,4},{7,5},{8,10},{9,11},{10,... | collective-permute-start | bytes 417800 | tf_op jit(solution)/shard_map/ppermute | solution.py:341
  91.2 6.5 %collective-permute-start.10 = (s16[272,256]{1,0:T(8,128)(2,1)S(1)}, s16[272,256]{1,0:T(8,128)(2,1)S(1)}, u32[]{:S(2)}, u32[]{:S(2)}) collective-permute-start(s16[272,256]{1,0:T(8,128)(2,1)S(1)} %get-tuple-element.59), channel_id=1, source_target_pairs={{0,3},{1,2},{2,1},{3,0},{4,7},{5,6},{6,5},{7,4},{8,11},{9,10},{10,... | collective-permute-start | bytes 417800 | tf_op jit(solution)/shard_map/ppermute | solution.py:341
  99.6 10.9 %collective-permute-start.11 = (s16[272,256]{1,0:T(8,128)(2,1)S(1)}, s16[272,256]{1,0:T(8,128)(2,1)S(1)}, u32[]{:S(2)}, u32[]{:S(2)}) collective-permute-start(s16[272,256]{1,0:T(8,128)(2,1)S(1)} %get-tuple-element.64.own), channel_id=1, source_target_pairs={{0,4},{1,5},{2,6},{3,7},{4,0},{5,1},{6,2},{7,3},{8,12},{9,13},{10,... | collective-permute-start | bytes 417800 | tf_op jit(solution)/shard_map/ppermute | solution.py:341
  100.6 13.8 %collective-permute-start.15 = (s16[272,256]{1,0:T(8,128)(2,1)S(1)}, s16[272,256]{1,0:T(8,128)(2,1)S(1)}, u32[]{:S(2)}, u32[]{:S(2)}) collective-permute-start(s16[272,256]{1,0:T(8,128)(2,1)S(1)} %get-tuple-element.65.own), channel_id=1, source_target_pairs={{0,4},{1,5},{2,6},{3,7},{4,0},{5,1},{6,2},{7,3},{8,12},{9,13},{10,... | collective-permute-start | bytes 417800 | tf_op jit(solution)/shard_map/ppermute | solution.py:341
  110.9 7.6 %collective-permute-start.14 = (s16[272,256]{1,0:T(8,128)(2,1)S(1)}, s16[272,256]{1,0:T(8,128)(2,1)S(1)}, u32[]{:S(2)}, u32[]{:S(2)}) collective-permute-start(s16[272,256]{1,0:T(8,128)(2,1)S(1)} %both0.1.refs_0_), channel_id=1, source_target_pairs={{0,3},{1,2},{2,1},{3,0},{4,7},{5,6},{6,5},{7,4},{8,11},{9,10},{10,... | collective-permute-start | bytes 417800 | tf_op jit(solution)/shard_map/ppermute | solution.py:341
  110.9 10.1 %collective-permute-start.13 = (s16[272,256]{1,0:T(8,128)(2,1)S(1)}, s16[272,256]{1,0:T(8,128)(2,1)S(1)}, u32[]{:S(2)}, u32[]{:S(2)}) collective-permute-start(s16[272,256]{1,0:T(8,128)(2,1)S(1)} %both0.1.refs_0_), channel_id=1, source_target_pairs={{0,2},{1,3},{2,0},{3,1},{4,6},{5,7},{6,4},{7,5},{8,10},{9,11},{10,... | collective-permute-start | bytes 417800 | tf_op jit(solution)/shard_map/ppermute | solution.py:341
  113.0 9.0 %collective-permute-start.12 = (s16[272,256]{1,0:T(8,128)(2,1)S(1)}, s16[272,256]{1,0:T(8,128)(2,1)S(1)}, u32[]{:S(2)}, u32[]{:S(2)}) collective-permute-start(s16[272,256]{1,0:T(8,128)(2,1)S(1)} %both0.1.refs_0_), channel_id=1, source_target_pairs={{0,1},{1,0},{2,3},{3,2},{4,5},{5,4},{6,7},{7,6},{8,9},{9,8},{10,11... | collective-permute-start | bytes 417800 | tf_op jit(solution)/shard_map/ppermute | solution.py:341
  114.8 8.6 %collective-permute-start.18 = (s16[272,256]{1,0:T(8,128)(2,1)S(1)}, s16[272,256]{1,0:T(8,128)(2,1)S(1)}, u32[]{:S(2)}, u32[]{:S(2)}) collective-permute-start(s16[272,256]{1,0:T(8,128)(2,1)S(1)} %both1.1.refs_4_), channel_id=1, source_target_pairs={{0,3},{1,2},{2,1},{3,0},{4,7},{5,6},{6,5},{7,4},{8,11},{9,10},{10,... | collective-permute-start | bytes 417800 | tf_op jit(solution)/shard_map/ppermute | solution.py:341
  114.9 9.5 %collective-permute-start.17 = (s16[272,256]{1,0:T(8,128)(2,1)S(1)}, s16[272,256]{1,0:T(8,128)(2,1)S(1)}, u32[]{:S(2)}, u32[]{:S(2)}) collective-permute-start(s16[272,256]{1,0:T(8,128)(2,1)S(1)} %both1.1.refs_4_), channel_id=1, source_target_pairs={{0,2},{1,3},{2,0},{3,1},{4,6},{5,7},{6,4},{7,5},{8,10},{9,11},{10,... | collective-permute-start | bytes 417800 | tf_op jit(solution)/shard_map/ppermute | solution.py:341
  118.5 6.2 %collective-permute-start.16 = (s16[272,256]{1,0:T(8,128)(2,1)S(1)}, s16[272,256]{1,0:T(8,128)(2,1)S(1)}, u32[]{:S(2)}, u32[]{:S(2)}) collective-permute-start(s16[272,256]{1,0:T(8,128)(2,1)S(1)} %both1.1.refs_4_), channel_id=1, source_target_pairs={{0,1},{1,0},{2,3},{3,2},{4,5},{5,4},{6,7},{7,6},{8,9},{9,8},{10,11... | collective-permute-start | bytes 417800 | tf_op jit(solution)/shard_map/ppermute | solution.py:341
Sparse Core Ops, SparseCore 0:
  9.6 37.1 all-gather.1

commit v9 on v7

--- a/solution.py
+++ b/solution.py
@@ -84,17 +84,22 @@
         copy.wait()
 
 
-def pack_kernel(chunks, me_ref, points_ref, cluster_ref, *refs):
+def pack_kernel(chunks, me_ref, points_ref, cluster_ref, first_ref, *refs):
     outs, (after_ref, head, sems, head_sems) = refs[:-4], refs[-4:]
     after_ref[0] = me_ref[0]
     rows = points_ref.shape[0]
-    h = len(outs) // chunks
+    h = first_ref.shape[0]
     q = me_ref[0] & (h - 1)
-    sources = [points_ref.at[:, chunk((q ^ (k // chunks)) * chunks + k % chunks, BLOCK)] for k in range(len(outs))]
-    copies = start_all(sources, [out.at[0:rows, :] for out in outs], sems)
+    copies = []
+    for d in range(h):
+        source = points_ref.at[:, d * chunks * BLOCK : (d * chunks + 1) * BLOCK]
+        copies.append(start(source, first_ref.at[d, 0:rows, :], head_sems.at[d]))
     cluster = cluster_ref[...]
     head[...] = jnp.concatenate([cluster & (BLOCK - 1), (cluster - me_ref[1]) // BLOCK]).astype(f32).astype(bf16)
-    copies += start_all([head] * h, [out.at[rows:, :] for out in outs[::chunks]], head_sems)
+    copies += [start(head, first_ref.at[d, rows:, :], head_sems.at[h + d]) for d in range(h)]
+    for k, out in enumerate(outs):
+        m, c = k // (chunks - 1), k % (chunks - 1) + 1
+        copies.append(start(points_ref.at[:, chunk((q ^ m) * chunks + c, BLOCK)], out, sems.at[k]))
     wait_all(copies)
 
 
@@ -122,11 +127,12 @@
 
 
 def prepare_kernel(per, me_ref, *refs):
-    arrived, (member_ref, place_ref, near_ref, far_ref, count, heads, sems) = refs[:-7], refs[-7:]
-    h = len(arrived)
+    arrived, member_ref, place_ref, near_ref, far_ref, count, heads, sems = refs
+    h = arrived.shape[0]
+    q = me_ref[0] & (h - 1)
     rows = near_ref.shape[0]
     blocks = place_ref.shape[0] // h
-    copies = start_all([a.at[blocks * BLOCK :, :] for a in arrived], [heads.at[m] for m in range(h)], sems)
+    copies = start_all([arrived.at[q ^ m, blocks * BLOCK :, :] for m in range(h)], [heads.at[m] for m in range(h)], sems)
     count[...] = jnp.zeros_like(count)
     centroid = lax.broadcasted_iota(i32, (BLOCK, BLOCK), 0)
     ones = jnp.ones((BLOCK, BLOCK), bf16)
@@ -164,9 +170,11 @@
             prev_ref[at, :] = decode(arrived[m][j * w : (j + 1) * w, :], exponent)
 
 
-def sums_kernel(place_ref, before_ref, member_ref, far_count_ref, *refs):
-    h = (len(refs) - 5) // 2
-    points, (acc_ref, code, after_ref, head, sem), held = refs[:h], refs[h : h + 5], refs[h + 5 :]
+def sums_kernel(h, me_ref, place_ref, before_ref, member_ref, far_count_ref, *refs):
+    points, (acc_ref, code, after_ref, head, sem), held = refs[: -h - 5], refs[-h - 5 : -h], refs[-h:]
+    q = me_ref[0] & (h - 1)
+    if len(points) == 1:
+        points = [points[0].at[q ^ m] for m in range(h)]
     after_ref[0] = before_ref[0]
     rows = acc_ref.shape[0] // 2
     blocks = held[0].shape[0] // BLOCK
@@ -351,16 +359,20 @@
 
     table_rows = lax.all_gather(cent2_prev, "dp", axis=0, tiled=True)
 
-    first_shape = shape((point_rows + 2 * blocks, BLOCK), bf16)
-    *packed, after_pack = call(
+    others = h * (chunks - 1)
+    first, *packed, after_pack = call(
         functools.partial(pack_kernel, chunks),
-        ([first_shape] + [shape((point_rows, BLOCK), bf16)] * (chunks - 1)) * h + [shape((1,), i32)],
+        [shape((h, point_rows + 2 * blocks, BLOCK), bf16)]
+        + [shape((point_rows, BLOCK), bf16)] * others
+        + [shape((1,), i32)],
         in_specs=[SMEM, HBM, VMEM],
-        out_specs=[HBM] * (h * chunks) + [SMEM],
-        scratch_shapes=[pltpu.VMEM((2 * blocks, BLOCK), bf16), dma(h * chunks), dma(h)],
+        out_specs=[HBM] * (others + 1) + [SMEM],
+        scratch_shapes=[pltpu.VMEM((2 * blocks, BLOCK), bf16), dma(max(others, 1)), dma(2 * h)],
         name="pack",
     )(me, points, point_cluster.reshape(blocks, BLOCK))
-    arrived = [swap_half(packed[c::chunks]) for c in range(chunks)]
+    halves = [list(range(k * h, (k + 1) * h)) for k in range(2)]
+    first = lax.all_to_all(first, "cent", split_axis=0, concat_axis=0, axis_index_groups=halves, tiled=True)
+    arrived = [[first]] + [swap_half(packed[c :: chunks - 1]) for c in range(chunks - 1)]
 
     member, place, near, far_count = call(
         functools.partial(prepare_kernel, owned // BLOCK),
@@ -370,24 +382,24 @@
             shape((rows, BLOCK), f32),
             shape((rows // BLOCK, BLOCK), i32),
         ],
-        in_specs=[SMEM] + [HBM] * h,
+        in_specs=[SMEM, HBM],
         out_specs=[VMEM, SMEM] + [VMEM] * 2,
         scratch_shapes=[pltpu.VMEM((2 * rows, BLOCK), f32), pltpu.VMEM((h, 2 * blocks, BLOCK), bf16), dma(h)],
         name="prepare",
-    )(me, *arrived[0])
+    )(me, first)
 
     lines = rows + 2 * rows // BLOCK
     accs, crossed, after = [], [], place
     for c in range(chunks):
         acc, code, ended = call(
-            sums_kernel,
+            functools.partial(sums_kernel, h),
             [shape((2 * rows, BLOCK), f32), shape((lines, BLOCK), i16), shape((1,), i32)],
-            in_specs=[SMEM, SMEM, VMEM, VMEM] + [HBM] * h,
+            in_specs=[SMEM] * 3 + [VMEM, VMEM] + [HBM] * len(arrived[c]),
             out_specs=[VMEM, VMEM, SMEM],
             scratch_shapes=[pltpu.VMEM((2 * rows // BLOCK, BLOCK), i32), dma(h)]
             + [pltpu.VMEM((point_rows, BLOCK), bf16)] * h,
             name=f"sums{c}",
-        )(place, after, member, far_count, *arrived[c])
+        )(me, place, after, member, far_count, *arrived[c])
         accs.append(acc)
         crossed.append(swap(code, h))
         after = ended

time: 121 us -> 135 us (1.12)
  waiting for transfers between devices: 33.2 us -> 48.6 us
  starting transfers between devices: 31.5 us -> 28.5 us
    ppermute x22 -> x19, waiting for transfers between devices: 32.5 us -> 48 us  [swap(): return lax.ppermute(value, 'cent', [(i, i ^ mask) for i in range(n)])]
    ppermute x22 -> x19, starting transfers between devices: 31.5 us -> 23.2 us  [swap(): return lax.ppermute(value, 'cent', [(i, i ^ mask) for i in range(n)])]
    all_to_all x0 -> x1, starting transfers between devices: none -> 5.25 us  [shards(): lax.all_to_all(first, 'cent', split_axis=0, concat_axis=0, axis_index_gro...]
    unnamed x30 -> x34, local copies, waits for them, and re-layouts: 9.25 us -> 9.94 us
  transfers between devices with their start and end apart: 23 -> 21, of which waited for: 13 -> 12; matrix products, arithmetic and copies ran while one was open for 8% -> 7% of each run, Pallas kernels for 13% -> 12%
where the time goes in v9:
time: 135 us; the launch traced here: 134 us
  waiting for transfers between devices  48.6 us (36%)
  starting transfers between devices  28.5 us (21%)
  Pallas kernels  23 us (17%)
  between operations  14.2 us (11%)
  local copies, waits for them, and re-layouts  10.5 us (8%)
  matrix products  5.38 us (4%)
  other arithmetic  4.05 us (3%)
    ppermute x19, waiting for transfers between devices, swap(): return lax.ppermute(value, 'cent', [(i, i ^ mask) for i in range(n)])  48 us
    ppermute x19, starting transfers between devices, swap(): return lax.ppermute(value, 'cent', [(i, i ^ mask) for i in range(n)])  23.2 us
    unnamed x34, local copies, waits for them, and re-layouts  9.94 us
    pallas_call x2, Pallas kernels, shards(): call(functools.partial(sums_kernel, h), [shape((2 * rows, BLOCK), f32), s...  6.31 us
    dot_general x1, matrix products, shards(): lax.dot_general(unit_points, table_units, (((1,), (1,)), ((), ())), prefe...  5.38 us
    all_to_all x1, starting transfers between devices, shards(): lax.all_to_all(first, 'cent', split_axis=0, concat_axis=0, axis_index_gro...  5.25 us
    reduce_sum x1, other arithmetic, shards(): jnp.mean(jnp.square(table_rows.astype(f32)), axis=-1) + EPSILON  3.24 us
  transfers between devices with their start and end apart: 21, of which 12 were waited for; matrix products, arithmetic and copies ran while one was open for 7% of the time, Pallas kernels for 12%

profile of v9, /device:TPU:0, one launch (start us, length us, event | category | flops | bytes accessed | tf_op | source)
XLA Modules:
  0.0 134.4 jit_solution(11864873213782451902)
XLA Ops:
  7.2 0.7 all-gather.2.cloned.1.call-update
  8.0 1.6 %copy-done = bf16[1024,1024]{1,0:T(8,128)(2,1)S(1)} copy-done((bf16[1024,1024]{1,0:T(8,128)(2,1)S(1)}, bf16[1024,1024]{1,0:T(8,128)(2,1)}, u32[]{:S(2)}) %copy-start) | copy-done | bytes 2097176
  9.6 0.7 copy-done.13
  10.3 2.4 %pack.1 = (bf16[4,1040,128]{2,1,0:T(8,128)(2,1)}, bf16[1024,128]{1,0:T(8,128)(2,1)S(1)}, bf16[1024,128]{1,0:T(8,128)(2,1)}, bf16[1024,128]{1,0:T(8,128)(2,1)}, bf16[1024,128]{1,0:T(8,128)(2,1)}, /*index=5*/s32[1]{0:T(128)}) custom-call(s32[3]{0:T(128)S(1)} %pad_add_fusion.me_ref, bf16[1024,1024]{1,0:T(8,128)(2,1)S(1)} %copy-done, s32[8,128]{1,0:T(8,128)S(1)} %bitcast.9), custom_call_target="tpu_custom_call" | custom-call | tf_op jit(solution)/shard_map/pack/pallas_call | solution.py:363
  12.7 0.7 copy-done.11
  13.4 5.2 %all-to-all-start = ((bf16[4,1040,128]{2,1,0:T(8,128)(2,1)}), bf16[4,1040,128]{2,1,0:T(8,128)(2,1)S(1)}, u32[]{:S(2)}, u32[]{:S(2)}) async-start(bf16[4,1040,128]{2,1,0:T(8,128)(2,1)} %get-tuple-element.40), calls=%async_computation | async-start | bytes 2129920 | tf_op jit(solution)/shard_map/all_to_all | solution.py:374
  18.6 2.5 %prev.1 = (s16[272,256]{1,0:T(8,128)(2,1)S(1)}, s16[272,256]{1,0:T(8,128)(2,1)S(1)}, s16[272,256]{1,0:T(8,128)(2,1)S(1)}, s16[272,256]{1,0:T(8,128)(2,1)S(1)}) custom-call(s32[3]{0:T(128)S(1)} %pad_add_fusion.me_ref, s32[1]{0:T(128)} %get-tuple-element.43.after_ref, f32[256,1024]{1,0:T(8,128)S(1)} %copy-done.2, s32[1,256]{1,0:T(1,128)S(1)} %bitcast.10), custom_call_target="tpu_custom_call" | custom-call | tf_op jit(solution)/shard_map/prev/pallas_call | solution.py:408
  21.1 2.1 %collective-permute-start = (s16[272,256]{1,0:T(8,128)(2,1)S(1)}, s16[272,256]{1,0:T(8,128)(2,1)S(1)}, u32[]{:S(2)}, u32[]{:S(2)}) collective-permute-start(s16[272,256]{1,0:T(8,128)(2,1)S(1)} %get-tuple-element.45), channel_id=1, source_target_pairs={{0,1},{1,0},{2,3},{3,2},{4,5},{5,4},{6,7},{7,6},{8,9},{9,8},{10,11... | collective-permute-start | bytes 417800 | tf_op jit(solution)/shard_map/ppermute | solution.py:354
  23.3 2.0 %collective-permute-start.4 = (bf16[1024,128]{1,0:T(8,128)(2,1)}, bf16[1024,128]{1,0:T(8,128)(2,1)S(1)}, u32[]{:S(2)}, u32[]{:S(2)}) collective-permute-start(bf16[1024,128]{1,0:T(8,128)(2,1)} %get-tuple-element.56), channel_id=1, source_target_pairs={{0,2},{1,3},{2,0},{3,1},{4,6},{5,7},{6,4},{7,5},{8,10},{9,11},{10,... | collective-permute-start | bytes 786440 | tf_op jit(solution)/shard_map/ppermute | solution.py:354
  25.2 1.5 %collective-permute-start.5 = (bf16[1024,128]{1,0:T(8,128)(2,1)}, bf16[1024,128]{1,0:T(8,128)(2,1)S(1)}, u32[]{:S(2)}, u32[]{:S(2)}) collective-permute-start(bf16[1024,128]{1,0:T(8,128)(2,1)} %get-tuple-element.57), channel_id=1, source_target_pairs={{0,3},{1,2},{2,1},{3,0},{4,7},{5,6},{6,5},{7,4},{8,11},{9,10},{10,... | collective-permute-start | bytes 786440 | tf_op jit(solution)/shard_map/ppermute | solution.py:354
  26.7 1.5 %collective-permute-start.1 = (s16[272,256]{1,0:T(8,128)(2,1)S(1)}, s16[272,256]{1,0:T(8,128)(2,1)S(1)}, u32[]{:S(2)}, u32[]{:S(2)}) collective-permute-start(s16[272,256]{1,0:T(8,128)(2,1)S(1)} %get-tuple-element.46), channel_id=1, source_target_pairs={{0,2},{1,3},{2,0},{3,1},{4,6},{5,7},{6,4},{7,5},{8,10},{9,11},{10,... | collective-permute-start | bytes 417800 | tf_op jit(solution)/shard_map/ppermute | solution.py:354
  28.2 8.3 %collective-permute-done.refs_1_ = s16[272,256]{1,0:T(8,128)(2,1)S(1)} collective-permute-done((s16[272,256]{1,0:T(8,128)(2,1)S(1)}, s16[272,256]{1,0:T(8,128)(2,1)S(1)}, u32[]{:S(2)}, u32[]{:S(2)}) %collective-permute-start) | collective-permute-done | bytes 139296 | tf_op jit(solution)/shard_map/ppermute | solution.py:354
  36.9 11.2 %collective-permute-done.1.refs_2_ = s16[272,256]{1,0:T(8,128)(2,1)S(1)} collective-permute-done((s16[272,256]{1,0:T(8,128)(2,1)S(1)}, s16[272,256]{1,0:T(8,128)(2,1)S(1)}, u32[]{:S(2)}, u32[]{:S(2)}) %collective-permute-start.1) | collective-permute-done | bytes 139296 | tf_op jit(solution)/shard_map/ppermute | solution.py:354
  48.1 2.5 %collective-permute-done.2.refs_3_ = s16[272,256]{1,0:T(8,128)(2,1)S(1)} collective-permute-done((s16[272,256]{1,0:T(8,128)(2,1)S(1)}, s16[272,256]{1,0:T(8,128)(2,1)S(1)}, u32[]{:S(2)}, u32[]{:S(2)}) %collective-permute-start.2) | collective-permute-done | bytes 139296 | tf_op jit(solution)/shard_map/ppermute | solution.py:354
  51.1 1.0 copy-done.3
  52.1 2.3 %prepare.1 = (bf16[4096,128]{1,0:T(8,128)(2,1)S(1)}, s32[32]{0:T(128)S(1)}, f32[1024,128]{1,0:T(8,128)S(1)}, s32[8,128]{1,0:T(8,128)S(1)}) custom-call(s32[3]{0:T(128)S(1)} %pad_add_fusion.me_ref, bf16[4,1040,128]{2,1,0:T(8,128)(2,1)S(1)} %all-to-all-done.refs_0_), custom_call_target="tpu_custom_call" | custom-call | tf_op jit(solution)/shard_map/prepare/pallas_call | solution.py:377
  54.4 0.8 copy-done.9
  55.2 2.8 %sums0.1 = (f32[2048,128]{1,0:T(8,128)S(1)}, s16[1040,128]{1,0:T(8,128)(2,1)}, s32[1]{0:T(128)}) custom-call(s32[3]{0:T(128)S(1)} %pad_add_fusion.me_ref, s32[32]{0:T(128)S(1)} %get-tuple-element.49.place_ref.before_ref, s32[32]{0:T(128)S(1)} %get-tuple-element.49.place_ref.before_ref, bf16[4096,128]{1,0:T(8,128)(2,1)S(1)} %get-tuple-element.50.member_ref, ...), custom_call_target="tpu_custom_call" | custom-call | tf_op jit(solution)/shard_map/sums0/pallas_call | solution.py:394
  58.0 1.0 copy-done.5
  59.0 2.6 %collective-permute-start.6 = (s16[1040,128]{1,0:T(8,128)(2,1)}, s16[1040,128]{1,0:T(8,128)(2,1)S(1)}, u32[]{:S(2)}, u32[]{:S(2)}) collective-permute-start(s16[1040,128]{1,0:T(8,128)(2,1)} %get-tuple-element.59), channel_id=1, source_target_pairs={{0,4},{1,5},{2,6},{3,7},{4,0},{5,1},{6,2},{7,3},{8,12},{9,13},{10,... | collective-permute-start | bytes 798728 | tf_op jit(solution)/shard_map/ppermute | solution.py:354
  61.6 0.9 copy-done.12
  62.5 3.5 %sums1.1 = (f32[2048,128]{1,0:T(8,128)S(1)}, s16[1040,128]{1,0:T(8,128)(2,1)}, s32[1]{0:T(128)}) custom-call(s32[3]{0:T(128)S(1)} %pad_add_fusion.me_ref, s32[32]{0:T(128)S(1)} %get-tuple-element.49.place_ref.before_ref, s32[1]{0:T(128)} %get-tuple-element.53.before_ref, bf16[4096,128]{1,0:T(8,128)(2,1)S(1)} %get-tuple-element.50.member_ref, ...), custom_call_target="tpu_custom_call" | custom-call | tf_op jit(solution)/shard_map/sums1/pallas_call | solution.py:394
  66.0 1.0 copy-done.7
  67.4 3.2 %fusion = f32[2048]{0:T(1024)S(1)} fusion(bf16[2048,1024]{1,0:T(8,128)(2,1)} %all-gather.2.cloned.1.call-done), kind=kLoop, calls=%fused_computation.2 | loop fusion | flops 6289408 | bytes 4202496 | tf_op jit(solution)/shard_map/reduce_sum | solution.py:427
  70.6 7.9 %collective-permute-done.6.refs_2_ = s16[1040,128]{1,0:T(8,128)(2,1)S(1)} collective-permute-done((s16[1040,128]{1,0:T(8,128)(2,1)}, s16[1040,128]{1,0:T(8,128)(2,1)S(1)}, u32[]{:S(2)}, u32[]{:S(2)}) %collective-permute-start.6) | collective-permute-done | bytes 266272 | tf_op jit(solution)/shard_map/ppermute | solution.py:354
  78.5 5.7 %collective-permute-done.7.refs_3_ = s16[1040,128]{1,0:T(8,128)(2,1)} collective-permute-done((s16[1040,128]{1,0:T(8,128)(2,1)}, s16[1040,128]{1,0:T(8,128)(2,1)}, u32[]{:S(2)}, u32[]{:S(2)}) %collective-permute-start.7) | collective-permute-done | bytes 266272 | tf_op jit(solution)/shard_map/ppermute | solution.py:354
  84.2 1.2 copy-done.8
  85.5 1.0 copy-done.10
  86.5 2.2 %refresh.1 = (f32[1024,256]{1,0:T(8,128)S(1)}, s16[272,256]{1,0:T(8,128)(2,1)S(1)}, s16[272,256]{1,0:T(8,128)(2,1)S(1)}, s16[272,256]{1,0:T(8,128)(2,1)S(1)}, s16[272,256]{1,0:T(8,128)(2,1)S(1)}) custom-call(f32[1024,128]{1,0:T(8,128)S(1)} %copy-done.10, f32[1024,256]{1,0:T(8,128)S(1)} %copy-done.4, f32[2048,128]{1,0:T(8,128)S(1)} %copy-done.6, ...), custom_call_target="tpu_custom_call" | custom-call | tf_op jit(solution)/shard_map/refresh/pallas_call | solution.py:440
  88.7 0.7 collective-permute-start.8
  89.4 2.9 %collective-permute-start.10 = (s16[272,256]{1,0:T(8,128)(2,1)S(1)}, s16[272,256]{1,0:T(8,128)(2,1)S(1)}, u32[]{:S(2)}, u32[]{:S(2)}) collective-permute-start(s16[272,256]{1,0:T(8,128)(2,1)S(1)} %get-tuple-element.64), channel_id=1, source_target_pairs={{0,3},{1,2},{2,1},{3,0},{4,7},{5,6},{6,5},{7,4},{8,11},{9,10},{10,... | collective-permute-start | bytes 417800 | tf_op jit(solution)/shard_map/ppermute | solution.py:354
  92.7 1.7 %collective-permute-done.8.refs_1_ = s16[272,256]{1,0:T(8,128)(2,1)S(1)} collective-permute-done((s16[272,256]{1,0:T(8,128)(2,1)S(1)}, s16[272,256]{1,0:T(8,128)(2,1)S(1)}, u32[]{:S(2)}, u32[]{:S(2)}) %collective-permute-start.8) | collective-permute-done | bytes 139296 | tf_op jit(solution)/shard_map/ppermute | solution.py:354
  94.4 1.5 %collective-permute-done.9.refs_2_ = s16[272,256]{1,0:T(8,128)(2,1)S(1)} collective-permute-done((s16[272,256]{1,0:T(8,128)(2,1)S(1)}, s16[272,256]{1,0:T(8,128)(2,1)S(1)}, u32[]{:S(2)}, u32[]{:S(2)}) %collective-permute-start.9) | collective-permute-done | bytes 139296 | tf_op jit(solution)/shard_map/ppermute | solution.py:354
  95.9 2.6 %collective-permute-done.10.refs_3_ = s16[272,256]{1,0:T(8,128)(2,1)S(1)} collective-permute-done((s16[272,256]{1,0:T(8,128)(2,1)S(1)}, s16[272,256]{1,0:T(8,128)(2,1)S(1)}, u32[]{:S(2)}, u32[]{:S(2)}) %collective-permute-start.10) | collective-permute-done | bytes 139296 | tf_op jit(solution)/shard_map/ppermute | solution.py:354
  98.5 1.9 %upper.1 = (s16[272,256]{1,0:T(8,128)(2,1)S(1)}, s16[272,256]{1,0:T(8,128)(2,1)S(1)}) custom-call(bf16[512,1024]{1,0:T(8,128)(2,1)S(1)} %get-tuple-element.67.member_ref, f32[1024,256]{1,0:T(8,128)S(1)} %get-tuple-element.68.x_ref, s16[272,256]{1,0:T(8,128)(2,1)S(1)} %get-tuple-element.61.refs_0_, s16[272,256]{1,0:T(8,128)(2,1)S(1)} %collective-permute-done.8.refs_1_, ...), custom_call_target="tpu_custom_call" | custom-call | tf_op jit(solution)/shard_map/upper/pallas_call | solution.py:454
  100.9 5.4 %fusion.2 = f32[1024]{0:T(1024)S(1)} fusion(bf16[2048,1024]{1,0:T(8,128)(2,1)S(1)} %copy-done.15, f32[8,2048]{1,0:T(8,128)S(1)} %convert_element_type.25, f32[2048]{0:T(1024)S(1)} %add_rsqrt_fusion, bf16[1024,1024]{1,0:T(8,128)(2,1)S(1)} %copy-done.1, f32[1024]{0:T(1024)S(1)} %add_rsqrt_fusion.1), kind=kOutput, calls=%fused_computation.5 | convolution fusion | flops 4310694912 | bytes 6373376 | tf_op jit(solution)/shard_map/dot_general | solution.py:430
  106.3 0.6 log.3
  106.9 2.5 %collective-permute-start.15 = (s16[272,256]{1,0:T(8,128)(2,1)S(1)}, s16[272,256]{1,0:T(8,128)(2,1)S(1)}, u32[]{:S(2)}, u32[]{:S(2)}) collective-permute-start(s16[272,256]{1,0:T(8,128)(2,1)S(1)} %get-tuple-element.73.own), channel_id=1, source_target_pairs={{0,4},{1,5},{2,6},{3,7},{4,0},{5,1},{6,2},{7,3},{8,12},{9,13},{10,... | collective-permute-start | bytes 417800 | tf_op jit(solution)/shard_map/ppermute | solution.py:354
  110.1 1.7 %collective-permute-start.13 = (s16[272,256]{1,0:T(8,128)(2,1)S(1)}, s16[272,256]{1,0:T(8,128)(2,1)S(1)}, u32[]{:S(2)}, u32[]{:S(2)}) collective-permute-start(s16[272,256]{1,0:T(8,128)(2,1)S(1)} %both0.1.refs_0_), channel_id=1, source_target_pairs={{0,2},{1,3},{2,0},{3,1},{4,6},{5,7},{6,4},{7,5},{8,10},{9,11},{10,... | collective-permute-start | bytes 417800 | tf_op jit(solution)/shard_map/ppermute | solution.py:354
  111.8 1.4 %collective-permute-start.12 = (s16[272,256]{1,0:T(8,128)(2,1)S(1)}, s16[272,256]{1,0:T(8,128)(2,1)S(1)}, u32[]{:S(2)}, u32[]{:S(2)}) collective-permute-start(s16[272,256]{1,0:T(8,128)(2,1)S(1)} %both0.1.refs_0_), channel_id=1, source_target_pairs={{0,1},{1,0},{2,3},{3,2},{4,5},{5,4},{6,7},{7,6},{8,9},{9,8},{10,11... | collective-permute-start | bytes 417800 | tf_op jit(solution)/shard_map/ppermute | solution.py:354
  113.2 0.7 collective-permute-done.15.far
  114.3 2.2 %collective-permute-start.18 = (s16[272,256]{1,0:T(8,128)(2,1)S(1)}, s16[272,256]{1,0:T(8,128)(2,1)S(1)}, u32[]{:S(2)}, u32[]{:S(2)}) collective-permute-start(s16[272,256]{1,0:T(8,128)(2,1)S(1)} %both1.1.refs_4_), channel_id=1, source_target_pairs={{0,3},{1,2},{2,1},{3,0},{4,7},{5,6},{6,5},{7,4},{8,11},{9,10},{10,... | collective-permute-start | bytes 417800 | tf_op jit(solution)/shard_map/ppermute | solution.py:354
  116.5 0.8 collective-permute-done.14.refs_3_
  117.3 0.9 collective-permute-start.16
  118.2 1.9 %decode.1 = f32[256,1024]{1,0:T(8,128)} custom-call(s32[3]{0:T(128)S(1)} %pad_add_fusion.me_ref, s16[272,256]{1,0:T(8,128)(2,1)S(1)} %get-tuple-element.61.refs_0_, s16[272,256]{1,0:T(8,128)(2,1)S(1)} %collective-permute-done.8.refs_1_, s16[272,256]{1,0:T(8,128)(2,1)S(1)} %collective-permute-done.9.refs_2_, s16[272,256]{1,0:T(8,128)(2,1)S(1)} %collective-permute-done.10.refs_3_), custom_call_target="tpu_custom_call" | custom-call | tf_op jit(solution)/shard_map/decode/pallas_call | solution.py:479
  120.1 3.2 %collective-permute-done.18.refs_7_ = s16[272,256]{1,0:T(8,128)(2,1)S(1)} collective-permute-done((s16[272,256]{1,0:T(8,128)(2,1)S(1)}, s16[272,256]{1,0:T(8,128)(2,1)S(1)}, u32[]{:S(2)}, u32[]{:S(2)}) %collective-permute-start.18) | collective-permute-done | bytes 139296 | tf_op jit(solution)/shard_map/ppermute | solution.py:354
  123.3 2.0 %collective-permute-done.17.refs_6_ = s16[272,256]{1,0:T(8,128)(2,1)S(1)} collective-permute-done((s16[272,256]{1,0:T(8,128)(2,1)S(1)}, s16[272,256]{1,0:T(8,128)(2,1)S(1)}, u32[]{:S(2)}, u32[]{:S(2)}) %collective-permute-start.17) | collective-permute-done | bytes 139296 | tf_op jit(solution)/shard_map/ppermute | solution.py:354
  125.3 2.3 %join.1 = f32[512,1024]{1,0:T(8,128)} custom-call(s32[3]{0:T(128)S(1)} %pad_add_fusion.me_ref, s16[272,256]{1,0:T(8,128)(2,1)S(1)} %both0.1.refs_0_, s16[272,256]{1,0:T(8,128)(2,1)S(1)} %collective-permute-done.12.refs_1_, s16[272,256]{1,0:T(8,128)(2,1)S(1)} %collective-permute-done.13.refs_2_, s16[272,256]{1,0:T(8,128)(2,1)S(1)} %collective-permute-done.14.refs_3_, ...), custom_call_target="tpu_custom_call" | custom-call | tf_op jit(solution)/shard_map/join/pallas_call | solution.py:487
  (51 shorter events, 3.7 us)
Async XLA Ops:
  7.2 11.5 %copy-start.14 = (s32[256]{0:T(256)S(1)}, s32[256]{0:T(256)}, u32[]{:S(2)}) copy-start(s32[256]{0:T(256)} %param.10) | copy-start | bytes 3076
  7.2 11.5 %copy-start.2 = (f32[256,1024]{1,0:T(8,128)S(1)}, f32[256,1024]{1,0:T(8,128)}, u32[]{:S(2)}) copy-start(f32[256,1024]{1,0:T(8,128)} %prev_ref.1) | copy-start | bytes 3145732
  7.2 29.5 %copy-start.16 = (s32[8,8]{1,0:T(8,128)S(1)}, s32[8,8]{1,0:T(8,128)}, u32[]{:S(2)}) copy-start(s32[8,8]{1,0:T(8,128)} %param.8) | copy-start | bytes 772
  7.2 60.2 %all-gather.2.cloned.1.call-start = ((), (), s32[]{:S(2)}) async-start(), calls=%async_computation.1 | async-start | bytes 5242880 | tf_op jit(solution)/shard_map/all_gather | solution.py:360
  8.0 1.6 %copy-start = (bf16[1024,1024]{1,0:T(8,128)(2,1)S(1)}, bf16[1024,1024]{1,0:T(8,128)(2,1)}, u32[]{:S(2)}) copy-start(bf16[1024,1024]{1,0:T(8,128)(2,1)} %points_ref.1) | copy-start | bytes 6291460
  9.6 0.7 copy-start.13
  12.7 0.7 copy-start.11
  13.4 38.7 %all-to-all-start = ((bf16[4,1040,128]{2,1,0:T(8,128)(2,1)}), bf16[4,1040,128]{2,1,0:T(8,128)(2,1)S(1)}, u32[]{:S(2)}, u32[]{:S(2)}) async-start(bf16[4,1040,128]{2,1,0:T(8,128)(2,1)} %get-tuple-element.40), calls=%async_computation | async-start | bytes 2129920 | tf_op jit(solution)/shard_map/all_to_all | solution.py:374
  21.1 15.3 %collective-permute-start = (s16[272,256]{1,0:T(8,128)(2,1)S(1)}, s16[272,256]{1,0:T(8,128)(2,1)S(1)}, u32[]{:S(2)}, u32[]{:S(2)}) collective-permute-start(s16[272,256]{1,0:T(8,128)(2,1)S(1)} %get-tuple-element.45), channel_id=1, source_target_pairs={{0,1},{1,0},{2,3},{3,2},{4,5},{5,4},{6,7},{7,6},{8,9},{9,8},{10,11... | collective-permute-start | bytes 417800 | tf_op jit(solution)/shard_map/ppermute | solution.py:354
  23.2 38.3 %collective-permute-start.3 = (bf16[1024,128]{1,0:T(8,128)(2,1)}, bf16[1024,128]{1,0:T(8,128)(2,1)S(1)}, u32[]{:S(2)}, u32[]{:S(2)}) collective-permute-start(bf16[1024,128]{1,0:T(8,128)(2,1)} %get-tuple-element.55), channel_id=1, source_target_pairs={{0,1},{1,0},{2,3},{3,2},{4,5},{5,4},{6,7},{7,6},{8,9},{9,8},{10,11... | collective-permute-start | bytes 786440 | tf_op jit(solution)/shard_map/ppermute | solution.py:354
  23.3 38.3 %collective-permute-start.4 = (bf16[1024,128]{1,0:T(8,128)(2,1)}, bf16[1024,128]{1,0:T(8,128)(2,1)S(1)}, u32[]{:S(2)}, u32[]{:S(2)}) collective-permute-start(bf16[1024,128]{1,0:T(8,128)(2,1)} %get-tuple-element.56), channel_id=1, source_target_pairs={{0,2},{1,3},{2,0},{3,1},{4,6},{5,7},{6,4},{7,5},{8,10},{9,11},{10,... | collective-permute-start | bytes 786440 | tf_op jit(solution)/shard_map/ppermute | solution.py:354
  25.2 36.3 %collective-permute-start.5 = (bf16[1024,128]{1,0:T(8,128)(2,1)}, bf16[1024,128]{1,0:T(8,128)(2,1)S(1)}, u32[]{:S(2)}, u32[]{:S(2)}) collective-permute-start(bf16[1024,128]{1,0:T(8,128)(2,1)} %get-tuple-element.57), channel_id=1, source_target_pairs={{0,3},{1,2},{2,1},{3,0},{4,7},{5,6},{6,5},{7,4},{8,11},{9,10},{10,... | collective-permute-start | bytes 786440 | tf_op jit(solution)/shard_map/ppermute | solution.py:354
  26.7 21.4 %collective-permute-start.1 = (s16[272,256]{1,0:T(8,128)(2,1)S(1)}, s16[272,256]{1,0:T(8,128)(2,1)S(1)}, u32[]{:S(2)}, u32[]{:S(2)}) collective-permute-start(s16[272,256]{1,0:T(8,128)(2,1)S(1)} %get-tuple-element.46), channel_id=1, source_target_pairs={{0,2},{1,3},{2,0},{3,1},{4,6},{5,7},{6,4},{7,5},{8,10},{9,11},{10,... | collective-permute-start | bytes 417800 | tf_op jit(solution)/shard_map/ppermute | solution.py:354
  36.4 14.2 %collective-permute-start.2 = (s16[272,256]{1,0:T(8,128)(2,1)S(1)}, s16[272,256]{1,0:T(8,128)(2,1)S(1)}, u32[]{:S(2)}, u32[]{:S(2)}) collective-permute-start(s16[272,256]{1,0:T(8,128)(2,1)S(1)} %get-tuple-element.47), channel_id=1, source_target_pairs={{0,3},{1,2},{2,1},{3,0},{4,7},{5,6},{6,5},{7,4},{8,11},{9,10},{10,... | collective-permute-start | bytes 417800 | tf_op jit(solution)/shard_map/ppermute | solution.py:354
  51.1 1.0 copy-start.3
  54.4 0.8 copy-start.9
  58.0 1.0 copy-start.5
  59.0 19.5 %collective-permute-start.6 = (s16[1040,128]{1,0:T(8,128)(2,1)}, s16[1040,128]{1,0:T(8,128)(2,1)S(1)}, u32[]{:S(2)}, u32[]{:S(2)}) collective-permute-start(s16[1040,128]{1,0:T(8,128)(2,1)} %get-tuple-element.59), channel_id=1, source_target_pairs={{0,4},{1,5},{2,6},{3,7},{4,0},{5,1},{6,2},{7,3},{8,12},{9,13},{10,... | collective-permute-start | bytes 798728 | tf_op jit(solution)/shard_map/ppermute | solution.py:354
  61.6 1.0 copy-start.12
  66.0 1.0 copy-start.7
  67.0 25.2 %copy-start.1 = (bf16[1024,1024]{1,0:T(8,128)(2,1)S(1)}, bf16[1024,1024]{1,0:T(8,128)(2,1)}, u32[]{:S(2)}) copy-start(bf16[1024,1024]{1,0:T(8,128)(2,1)} %points_ref.1) | copy-start | bytes 6291460
  67.0 17.2 %collective-permute-start.7 = (s16[1040,128]{1,0:T(8,128)(2,1)}, s16[1040,128]{1,0:T(8,128)(2,1)}, u32[]{:S(2)}, u32[]{:S(2)}) collective-permute-start(s16[1040,128]{1,0:T(8,128)(2,1)} %get-tuple-element.60), channel_id=1, source_target_pairs={{0,4},{1,5},{2,6},{3,7},{4,0},{5,1},{6,2},{7,3},{8,12},{9,13},{10,... | collective-permute-start | bytes 798728 | tf_op jit(solution)/shard_map/ppermute | solution.py:354
  67.4 16.8 %copy-start.4 = (f32[1024,256]{1,0:T(8,128)S(1)}, f32[1024,256]{1,0:T(8,128)}, u32[]{:S(2)}) copy-start(f32[1024,256]{1,0:T(8,128)} %copy-done.3) | copy-start | bytes 3145732
  67.4 16.8 %copy-start.6 = (f32[2048,128]{1,0:T(8,128)S(1)}, f32[2048,128]{1,0:T(8,128)}, u32[]{:S(2)}) copy-start(f32[2048,128]{1,0:T(8,128)} %copy-done.5) | copy-start | bytes 3145732
  84.2 1.2 copy-start.8
  85.5 1.0 copy-start.10
  86.5 14.4 %copy-start.15 = (bf16[2048,1024]{1,0:T(8,128)(2,1)S(1)}, bf16[2048,1024]{1,0:T(8,128)(2,1)}, u32[]{:S(2)}) copy-start(bf16[2048,1024]{1,0:T(8,128)(2,1)} %all-gather.2.cloned.1.call-done) | copy-start | bytes 12582916
  88.7 5.7 %collective-permute-start.8 = (s16[272,256]{1,0:T(8,128)(2,1)S(1)}, s16[272,256]{1,0:T(8,128)(2,1)S(1)}, u32[]{:S(2)}, u32[]{:S(2)}) collective-permute-start(s16[272,256]{1,0:T(8,128)(2,1)S(1)} %get-tuple-element.62), channel_id=1, source_target_pairs={{0,1},{1,0},{2,3},{3,2},{4,5},{5,4},{6,7},{7,6},{8,9},{9,8},{10,11... | collective-permute-start | bytes 417800 | tf_op jit(solution)/shard_map/ppermute | solution.py:354
  89.4 6.6 %collective-permute-start.9 = (s16[272,256]{1,0:T(8,128)(2,1)S(1)}, s16[272,256]{1,0:T(8,128)(2,1)S(1)}, u32[]{:S(2)}, u32[]{:S(2)}) collective-permute-start(s16[272,256]{1,0:T(8,128)(2,1)S(1)} %get-tuple-element.63), channel_id=1, source_target_pairs={{0,2},{1,3},{2,0},{3,1},{4,6},{5,7},{6,4},{7,5},{8,10},{9,11},{10,... | collective-permute-start | bytes 417800 | tf_op jit(solution)/shard_map/ppermute | solution.py:354
  89.4 9.2 %collective-permute-start.10 = (s16[272,256]{1,0:T(8,128)(2,1)S(1)}, s16[272,256]{1,0:T(8,128)(2,1)S(1)}, u32[]{:S(2)}, u32[]{:S(2)}) collective-permute-start(s16[272,256]{1,0:T(8,128)(2,1)S(1)} %get-tuple-element.64), channel_id=1, source_target_pairs={{0,3},{1,2},{2,1},{3,0},{4,7},{5,6},{6,5},{7,4},{8,11},{9,10},{10,... | collective-permute-start | bytes 417800 | tf_op jit(solution)/shard_map/ppermute | solution.py:354
  100.4 8.9 %collective-permute-start.11 = (s16[272,256]{1,0:T(8,128)(2,1)S(1)}, s16[272,256]{1,0:T(8,128)(2,1)S(1)}, u32[]{:S(2)}, u32[]{:S(2)}) collective-permute-start(s16[272,256]{1,0:T(8,128)(2,1)S(1)} %get-tuple-element.72.own), channel_id=1, source_target_pairs={{0,4},{1,5},{2,6},{3,7},{4,0},{5,1},{6,2},{7,3},{8,12},{9,13},{10,... | collective-permute-start | bytes 417800 | tf_op jit(solution)/shard_map/ppermute | solution.py:354
  106.9 7.1 %collective-permute-start.15 = (s16[272,256]{1,0:T(8,128)(2,1)S(1)}, s16[272,256]{1,0:T(8,128)(2,1)S(1)}, u32[]{:S(2)}, u32[]{:S(2)}) collective-permute-start(s16[272,256]{1,0:T(8,128)(2,1)S(1)} %get-tuple-element.73.own), channel_id=1, source_target_pairs={{0,4},{1,5},{2,6},{3,7},{4,0},{5,1},{6,2},{7,3},{8,12},{9,13},{10,... | collective-permute-start | bytes 417800 | tf_op jit(solution)/shard_map/ppermute | solution.py:354
  109.7 7.6 %collective-permute-start.14 = (s16[272,256]{1,0:T(8,128)(2,1)S(1)}, s16[272,256]{1,0:T(8,128)(2,1)S(1)}, u32[]{:S(2)}, u32[]{:S(2)}) collective-permute-start(s16[272,256]{1,0:T(8,128)(2,1)S(1)} %both0.1.refs_0_), channel_id=1, source_target_pairs={{0,3},{1,2},{2,1},{3,0},{4,7},{5,6},{6,5},{7,4},{8,11},{9,10},{10,... | collective-permute-start | bytes 417800 | tf_op jit(solution)/shard_map/ppermute | solution.py:354
  110.1 10.0 %collective-permute-start.13 = (s16[272,256]{1,0:T(8,128)(2,1)S(1)}, s16[272,256]{1,0:T(8,128)(2,1)S(1)}, u32[]{:S(2)}, u32[]{:S(2)}) collective-permute-start(s16[272,256]{1,0:T(8,128)(2,1)S(1)} %both0.1.refs_0_), channel_id=1, source_target_pairs={{0,2},{1,3},{2,0},{3,1},{4,6},{5,7},{6,4},{7,5},{8,10},{9,11},{10,... | collective-permute-start | bytes 417800 | tf_op jit(solution)/shard_map/ppermute | solution.py:354
  111.8 8.3 %collective-permute-start.12 = (s16[272,256]{1,0:T(8,128)(2,1)S(1)}, s16[272,256]{1,0:T(8,128)(2,1)S(1)}, u32[]{:S(2)}, u32[]{:S(2)}) collective-permute-start(s16[272,256]{1,0:T(8,128)(2,1)S(1)} %both0.1.refs_0_), channel_id=1, source_target_pairs={{0,1},{1,0},{2,3},{3,2},{4,5},{5,4},{6,7},{7,6},{8,9},{9,8},{10,11... | collective-permute-start | bytes 417800 | tf_op jit(solution)/shard_map/ppermute | solution.py:354
  114.3 9.0 %collective-permute-start.18 = (s16[272,256]{1,0:T(8,128)(2,1)S(1)}, s16[272,256]{1,0:T(8,128)(2,1)S(1)}, u32[]{:S(2)}, u32[]{:S(2)}) collective-permute-start(s16[272,256]{1,0:T(8,128)(2,1)S(1)} %both1.1.refs_4_), channel_id=1, source_target_pairs={{0,3},{1,2},{2,1},{3,0},{4,7},{5,6},{6,5},{7,4},{8,11},{9,10},{10,... | collective-permute-start | bytes 417800 | tf_op jit(solution)/shard_map/ppermute | solution.py:354
  116.5 8.7 %collective-permute-start.17 = (s16[272,256]{1,0:T(8,128)(2,1)S(1)}, s16[272,256]{1,0:T(8,128)(2,1)S(1)}, u32[]{:S(2)}, u32[]{:S(2)}) collective-permute-start(s16[272,256]{1,0:T(8,128)(2,1)S(1)} %both1.1.refs_4_), channel_id=1, source_target_pairs={{0,2},{1,3},{2,0},{3,1},{4,6},{5,7},{6,4},{7,5},{8,10},{9,11},{10,... | collective-permute-start | bytes 417800 | tf_op jit(solution)/shard_map/ppermute | solution.py:354
  117.3 8.0 %collective-permute-start.16 = (s16[272,256]{1,0:T(8,128)(2,1)S(1)}, s16[272,256]{1,0:T(8,128)(2,1)S(1)}, u32[]{:S(2)}, u32[]{:S(2)}) collective-permute-start(s16[272,256]{1,0:T(8,128)(2,1)S(1)} %both1.1.refs_4_), channel_id=1, source_target_pairs={{0,1},{1,0},{2,3},{3,2},{4,5},{5,4},{6,7},{7,6},{8,9},{9,8},{10,11... | collective-permute-start | bytes 417800 | tf_op jit(solution)/shard_map/ppermute | solution.py:354
Sparse Core Ops, SparseCore 0:
  9.6 37.1 all-gather.1

commit v10 on v7

--- a/solution.py
+++ b/solution.py
@@ -148,25 +148,9 @@
         far_ref[j : j + 1, :] = (to_lanes(high) * 64.0 + to_lanes(far - high * 64.0)).astype(i32)
 
 
-def previous_kernel(*refs):
-    arrived, (prev_ref, upper_ref) = refs[:-2], refs[-2:]
-    h = len(arrived)
-    rows, w = prev_ref.shape
-    owned = rows // h
-    each = owned // w
-    parent_at = lax.broadcasted_iota(i32, (upper_ref.shape[0], w), 0)
-    for m in range(h):
-        head = arrived[m][owned:, :].astype(i32)
-        for j in range(each):
-            at = slice(m * owned + j * w, m * owned + (j + 1) * w)
-            upper_ref[:, at] = jnp.where(parent_at == head[j : j + 1, :], 1.0, 0.0).astype(bf16)
-            exponent = to_column(head[each + j : each + j + 1, :].astype(f32))
-            prev_ref[at, :] = decode(arrived[m][j * w : (j + 1) * w, :], exponent)
-
-
 def sums_kernel(place_ref, before_ref, member_ref, far_count_ref, *refs):
-    h = (len(refs) - 5) // 2
-    points, (acc_ref, code, after_ref, head, sem), held = refs[:h], refs[h : h + 5], refs[h + 5 :]
+    h = (len(refs) - 6) // 2
+    points, (near_ref, code, after_ref, acc_ref, head, sem), held = refs[:h], refs[h : h + 6], refs[h + 6 :]
     after_ref[0] = before_ref[0]
     rows = acc_ref.shape[0] // 2
     blocks = held[0].shape[0] // BLOCK
@@ -189,6 +173,7 @@
             row = j * (step // BLOCK) + k
             head[row : row + 1, :] = lanes[:, k * BLOCK : (k + 1) * BLOCK]
     head[lines:, :] = far_count_ref[...]
+    near_ref[...] = acc_ref[0:rows, :]
     code[rows:, :] = head[...].astype(i16)
 
 
@@ -196,11 +181,19 @@
     return slice(index * BLOCK // w, index * BLOCK // w + 1), slice(index * BLOCK % w, index * BLOCK % w + BLOCK)
 
 
-def refresh_kernel(chunks, near_ref, prev_ref, *refs):
-    accs, crossed, x_ref, outs, tail = refs[:chunks], refs[chunks : 2 * chunks], refs[2 * chunks], refs[2 * chunks + 1 : -1], refs[-1]
-    h = len(outs)
+def refresh_kernel(chunks, h, near_ref, *refs):
+    accs, crossed, prevs, x_ref, outs, tail = (
+        refs[:chunks],
+        refs[chunks : 2 * chunks],
+        refs[2 * chunks : -h - 2],
+        refs[-h - 2],
+        refs[-h - 1 : -1],
+        refs[-1],
+    )
     rows, w = x_ref.shape
     owned = rows // h
+    per = owned // BLOCK
+    prev_heads = [prev[owned:, :].astype(i32).astype(f32) for prev in prevs]
     lines = rows // BLOCK
     heads = [crossed[c][rows:, :].astype(i32).astype(f32) for c in range(chunks)]
     unit = jnp.ones((8, BLOCK), bf16)
@@ -209,10 +202,12 @@
         count = near_ref[at, :] + to_column(heads[0][lines + j : lines + j + 1, :])
         inverse = 1.0 / jnp.maximum(count, 1.0)
         square, top = None, None
+        owner, here = j // per, slice(j % per * BLOCK, (j % per + 1) * BLOCK)
+        prev_exponent = to_column(prev_heads[owner][spot(per + j % per, w)])
         for c in range(chunks):
             lanes = slice(c * BLOCK, (c + 1) * BLOCK)
             far = decode(crossed[c][at, :], to_column(heads[c][j : j + 1, :]))
-            x = (accs[c][at, :] + far) * inverse + prev_ref[at, lanes]
+            x = (accs[c][at, :] + far) * inverse + decode(prevs[owner][here, lanes], prev_exponent)
             x_ref[at, lanes] = x
             square = x * x if c == 0 else square + x * x
             top = jnp.abs(x) if c == 0 else jnp.maximum(top, jnp.abs(x))
@@ -224,8 +219,7 @@
         exponent = exponent_of(jnp.max(top, axis=1, keepdims=True))
         for k, value in enumerate((sums_exponent, whole, jnp.floor((scaled - whole) * 16384.0), to_lanes(exponent))):
             tail[spot(k * lines + j, w)] = value.astype(i32)
-        here = slice(j * BLOCK % owned, j * BLOCK % owned + BLOCK)
-        outs[j * BLOCK // owned][here, :] = encode(x_ref[at, :], exponent)
+        outs[owner][here, :] = encode(x_ref[at, :], exponent)
     for out in outs:
         out[owned:, :] = tail[...].astype(i16)
 
@@ -249,9 +243,8 @@
     return decode(code[j * size : (j + 1) * size, :], to_column(lanes))
 
 
-def upper_kernel(width, member_ref, x_ref, *refs):
-    backs, outs, (high, low, sums), heads = refs[:-7], refs[-7:-5], refs[-5:-2], refs[-2:]
-    h = len(backs)
+def upper_kernel(width, h, x_ref, *refs):
+    backs, prevs, outs, (high, low, sums, member), heads = refs[:h], refs[h:-8], refs[-8:-6], refs[-6:-2], refs[-2:]
     total, w = x_ref.shape
     owned = total // h
     lines, per = total // BLOCK, owned // BLOCK
@@ -268,9 +261,13 @@
             at = slice(p * owned + j * BLOCK, p * owned + (j + 1) * BLOCK)
             high[at, :], low[at, :] = split(x_ref[at, :] * to_column(factor))
     rows = sums.shape[0]
+    parent_at = lax.broadcasted_iota(i32, (rows, BLOCK), 0)
+    parents = [prev[owned:, :].astype(i32) for prev in prevs]
     for k in range(2):
-        member = member_ref[k * rows : (k + 1) * rows, :]
-        sums[...] = dot(member, high[...]) + dot(member, low[...])
+        for j in range(lines):
+            row = parents[j // per][spot(j % per, w)] - k * rows
+            member[:, j * BLOCK : (j + 1) * BLOCK] = jnp.where(parent_at == row, 1.0, 0.0).astype(bf16)
+        sums[...] = dot(member[...], high[...]) + dot(member[...], low[...])
         put_codes(sums, outs[k], heads[k])
 
 
@@ -381,10 +378,10 @@
     for c in range(chunks):
         acc, code, ended = call(
             sums_kernel,
-            [shape((2 * rows, BLOCK), f32), shape((lines, BLOCK), i16), shape((1,), i32)],
+            [shape((rows, BLOCK), f32), shape((lines, BLOCK), i16), shape((1,), i32)],
             in_specs=[SMEM, SMEM, VMEM, VMEM] + [HBM] * h,
             out_specs=[VMEM, VMEM, SMEM],
-            scratch_shapes=[pltpu.VMEM((2 * rows // BLOCK, BLOCK), i32), dma(h)]
+            scratch_shapes=[pltpu.VMEM((2 * rows, BLOCK), f32), pltpu.VMEM((2 * rows // BLOCK, BLOCK), i32), dma(h)]
             + [pltpu.VMEM((point_rows, BLOCK), bf16)] * h,
             name=f"sums{c}",
         )(place, after, member, far_count, *arrived[c])
@@ -402,13 +399,8 @@
         + [pltpu.VMEM((owned + head, w), i16)] * h,
         name="prev",
     )(me, after_pack, cent1_prev, parent.reshape(owned // w, w))
-    prev, upper_member = call(
-        previous_kernel,
-        [shape((rows, w), f32), shape((upper_rows, rows), bf16)],
-        in_specs=[VMEM] * h,
-        out_specs=[VMEM] * 2,
-        name="previous",
-    )(*swap_half(prevs))
+    prevs, crossed[0] = lax.optimization_barrier((prevs, crossed[0]))
+    prevs = swap_half(prevs)
 
     points, table_rows = lax.optimization_barrier((points, table_rows))
     unit_points = rms_norm(points.astype(f32)).astype(bf16)
@@ -426,13 +418,13 @@
 
     tail = 4 * rows // w
     x, *backs = call(
-        functools.partial(refresh_kernel, chunks),
+        functools.partial(refresh_kernel, chunks, h),
         [shape((rows, w), f32)] + [shape((owned + tail, w), i16)] * h,
-        in_specs=[VMEM] * (2 + 2 * chunks),
+        in_specs=[VMEM] * (1 + 2 * chunks + h),
         out_specs=[VMEM] * (h + 1),
         scratch_shapes=[pltpu.VMEM((tail, w), i32)],
         name="refresh",
-    )(near, prev, *accs, *crossed)
+    )(near, *accs, *crossed, *prevs)
     backs = swap_half(backs)
 
     part = upper_rows // 2
@@ -440,14 +432,15 @@
     code_shape = shape((part + tail, w), i16)
     held_head = pltpu.VMEM((tail, w), i32)
     codes = call(
-        functools.partial(upper_kernel, width),
+        functools.partial(upper_kernel, width, h),
         [code_shape] * 2,
-        in_specs=[VMEM] * (h + 2),
+        in_specs=[VMEM] * (2 * h + 1),
         out_specs=[VMEM] * 2,
         scratch_shapes=[pltpu.VMEM((rows, w), bf16), pltpu.VMEM((rows, w), bf16), pltpu.VMEM((part, w), f32)]
+        + [pltpu.VMEM((part, rows), bf16)]
         + [held_head] * 2,
         name="upper",
-    )(upper_member, x, *backs)
+    )(x, *backs, *prevs)
     far_codes = [swap(code, h) for code in codes]
     parts = []
     for k in range(2):

time: 121 us -> 125 us (1.033)
  waiting for transfers between devices: 33.2 us -> 45.8 us
  local copies, waits for them, and re-layouts: 9.86 us -> 3.7 us
  starting transfers between devices: 31.5 us -> 29.8 us
    ppermute x22, waiting for transfers between devices: 32.5 us -> 45.1 us  [swap(): return lax.ppermute(value, 'cent', [(i, i ^ mask) for i in range(n)])]
    unnamed x30 -> x22, local copies, waits for them, and re-layouts: 9.25 us -> 3.1 us
    ppermute x22, starting transfers between devices: 31.5 us -> 29.8 us  [swap(): return lax.ppermute(value, 'cent', [(i, i ^ mask) for i in range(n)])]
    pallas_call x5 -> x4, Pallas kernels: 10.9 us -> 9.96 us  [the longest x2 5.67 us: shards(): call(sums_kernel, [shape((rows, BLOCK), f32), shape((lines, BLOCK), i16),...]
  transfers between devices with their start and end apart: 23 -> 23, of which waited for: 13 -> 16; matrix products, arithmetic and copies ran while one was open for 8% -> 8% of each run, Pallas kernels for 13% -> 12%
where the time goes in v10:
time: 125 us
  waiting for transfers between devices  45.8 us (37%)
  starting transfers between devices  29.8 us (24%)
  Pallas kernels  21.6 us (17%)
  between operations  14.2 us (11%)
  matrix products  5.53 us (4%)
  other arithmetic  3.97 us (3%)
  local copies, waits for them, and re-layouts  3.7 us (3%)
    ppermute x22, waiting for transfers between devices, swap(): return lax.ppermute(value, 'cent', [(i, i ^ mask) for i in range(n)])  45.1 us
    ppermute x22, starting transfers between devices, swap(): return lax.ppermute(value, 'cent', [(i, i ^ mask) for i in range(n)])  29.8 us
    pallas_call x2, Pallas kernels, shards(): call(sums_kernel, [shape((rows, BLOCK), f32), shape((lines, BLOCK), i16),...  5.67 us
    dot_general x1, matrix products, shards(): lax.dot_general(unit_points, table_units, (((1,), (1,)), ((), ())), prefe...  5.53 us
    reduce_sum x1, other arithmetic, shards(): jnp.mean(jnp.square(table_rows.astype(f32)), axis=-1) + EPSILON  3.16 us
    unnamed x22, local copies, waits for them, and re-layouts  3.1 us
    pallas_call x1, Pallas kernels, shards(): call(prev_kernel, [shape((owned + head, w), i16)] * h, in_specs=[SMEM, SM...  2.61 us
  transfers between devices with their start and end apart: 23, of which 16 were waited for; matrix products, arithmetic and copies ran while one was open for 8% of the time, Pallas kernels for 12%

profile of v10, /device:TPU:0, one launch (start us, length us, event | category | flops | bytes accessed | tf_op | source)
XLA Modules:
  0.0 124.6 jit_solution(18100094640017080145)
XLA Ops:
  7.2 0.7 all-gather.2.cloned.1.call-update
  8.0 1.6 %copy-done = bf16[1024,1024]{1,0:T(8,128)(2,1)S(1)} copy-done((bf16[1024,1024]{1,0:T(8,128)(2,1)S(1)}, bf16[1024,1024]{1,0:T(8,128)(2,1)}, u32[]{:S(2)}) %copy-start) | copy-done | bytes 2097176
  9.6 0.7 copy-done.7
  10.3 1.8 %pack.1 = (bf16[1040,128]{1,0:T(8,128)(2,1)S(1)}, bf16[1024,128]{1,0:T(8,128)(2,1)S(1)}, bf16[1040,128]{1,0:T(8,128)(2,1)S(1)}, bf16[1024,128]{1,0:T(8,128)(2,1)...) custom-call(s32[3]{0:T(128)S(1)} %pad_add_fusion.me_ref, ...), custom_call_target="tpu_custom_call" | custom-call | tf_op jit(solution)/shard_map/pack/pallas_call | solution.py:352
  12.1 3.0 %collective-permute-start = (bf16[1040,128]{1,0:T(8,128)(2,1)S(1)}, bf16[1040,128]{1,0:T(8,128)(2,1)S(1)}, u32[]{:S(2)}, u32[]{:S(2)}) collective-permute-start(bf16[1040,128]{1,0:T(8,128)(2,1)S(1)} %get-tuple-element.47), channel_id=1, source_target_pairs={{0,1},{1,0},{2,3},{3,2},{4,5},{5,4},{6,7},{7,6},{8,9},{9,8},{10,11... | collective-permute-start | bytes 798728 | tf_op jit(solution)/shard_map/ppermute | solution.py:343
  15.1 1.6 %collective-permute-start.1 = (bf16[1040,128]{1,0:T(8,128)(2,1)S(1)}, bf16[1040,128]{1,0:T(8,128)(2,1)S(1)}, u32[]{:S(2)}, u32[]{:S(2)}) collective-permute-start(bf16[1040,128]{1,0:T(8,128)(2,1)S(1)} %get-tuple-element.48), channel_id=1, source_target_pairs={{0,2},{1,3},{2,0},{3,1},{4,6},{5,7},{6,4},{7,5},{8,10},{9,11},{10,... | collective-permute-start | bytes 798728 | tf_op jit(solution)/shard_map/ppermute | solution.py:343
  16.7 4.8 %collective-permute-done.refs_1_ = bf16[1040,128]{1,0:T(8,128)(2,1)S(1)} collective-permute-done((bf16[1040,128]{1,0:T(8,128)(2,1)S(1)}, bf16[1040,128]{1,0:T(8,128)(2,1)S(1)}, u32[]{:S(2)}, u32[]{:S(2)}) %collective-permute-start) | collective-permute-done | bytes 266272 | tf_op jit(solution)/shard_map/ppermute | solution.py:343
  21.5 2.9 %collective-permute-done.1.refs_2_ = bf16[1040,128]{1,0:T(8,128)(2,1)S(1)} collective-permute-done((bf16[1040,128]{1,0:T(8,128)(2,1)S(1)}, bf16[1040,128]{1,0:T(8,128)(2,1)S(1)}, u32[]{:S(2)}, u32[]{:S(2)}) %collective-permute-start.1) | collective-permute-done | bytes 266272 | tf_op jit(solution)/shard_map/ppermute | solution.py:343
  24.4 4.0 %collective-permute-done.2.refs_3_ = bf16[1040,128]{1,0:T(8,128)(2,1)S(1)} collective-permute-done((bf16[1040,128]{1,0:T(8,128)(2,1)S(1)}, bf16[1040,128]{1,0:T(8,128)(2,1)S(1)}, u32[]{:S(2)}, u32[]{:S(2)}) %collective-permute-start.2) | collective-permute-done | bytes 266272 | tf_op jit(solution)/shard_map/ppermute | solution.py:343
  28.5 2.3 %prepare.1 = (bf16[4096,128]{1,0:T(8,128)(2,1)S(1)}, s32[32]{0:T(128)S(1)}, f32[1024,128]{1,0:T(8,128)S(1)}, s32[8,128]{1,0:T(8,128)S(1)}) custom-call(s32[3]{0:T(128)S(1)} %pad_add_fusion.me_ref, bf16[1040,128]{1,0:T(8,128)(2,1)S(1)} %get-tuple-element.46.refs_0_, bf16[1040,128]{1,0:T(8,128)(2,1)S(1)} %collective-permute-done.refs_1_, ...), custom_call_target="tpu_custom_call" | custom-call | tf_op jit(solution)/shard_map/prepare/pallas_call | solution.py:362
  30.7 2.2 %sums0.1 = (f32[1024,128]{1,0:T(8,128)S(1)}, s16[1040,128]{1,0:T(8,128)(2,1)S(1)}, s32[1]{0:T(128)}) custom-call(s32[32]{0:T(128)S(1)} %get-tuple-element.52.place_ref.before_ref, s32[32]{0:T(128)S(1)} %get-tuple-element.52.place_ref.before_ref, bf16[4096,128]{1,0:T(8,128)(2,1)S(1)} %get-tuple-element.53.member_ref, ...), custom_call_target="tpu_custom_call" | custom-call | tf_op jit(solution)/shard_map/sums0/pallas_call | solution.py:379
  32.9 2.8 %collective-permute-start.6 = (s16[1040,128]{1,0:T(8,128)(2,1)S(1)}, s16[1040,128]{1,0:T(8,128)(2,1)S(1)}, u32[]{:S(2)}, u32[]{:S(2)}) collective-permute-start(s16[1040,128]{1,0:T(8,128)(2,1)S(1)} %get-tuple-element.67), channel_id=1, source_target_pairs={{0,4},{1,5},{2,6},{3,7},{4,0},{5,1},{6,2},{7,3},{8,12},{9,13},{10,... | collective-permute-start | bytes 798728 | tf_op jit(solution)/shard_map/ppermute | solution.py:343
  35.7 1.5 %collective-permute-start.3 = (bf16[1024,128]{1,0:T(8,128)(2,1)S(1)}, bf16[1024,128]{1,0:T(8,128)(2,1)S(1)}, u32[]{:S(2)}, u32[]{:S(2)}) collective-permute-start(bf16[1024,128]{1,0:T(8,128)(2,1)S(1)} %get-tuple-element.58), channel_id=1, source_target_pairs={{0,1},{1,0},{2,3},{3,2},{4,5},{5,4},{6,7},{7,6},{8,9},{9,8},{10,11... | collective-permute-start | bytes 786440 | tf_op jit(solution)/shard_map/ppermute | solution.py:343
  37.2 1.6 %collective-permute-start.4 = (bf16[1024,128]{1,0:T(8,128)(2,1)S(1)}, bf16[1024,128]{1,0:T(8,128)(2,1)S(1)}, u32[]{:S(2)}, u32[]{:S(2)}) collective-permute-start(bf16[1024,128]{1,0:T(8,128)(2,1)S(1)} %get-tuple-element.59), channel_id=1, source_target_pairs={{0,2},{1,3},{2,0},{3,1},{4,6},{5,7},{6,4},{7,5},{8,10},{9,11},{10,... | collective-permute-start | bytes 786440 | tf_op jit(solution)/shard_map/ppermute | solution.py:343
  39.2 2.6 %prev.1 = (s16[272,256]{1,0:T(8,128)(2,1)S(1)}, s16[272,256]{1,0:T(8,128)(2,1)}, s16[272,256]{1,0:T(8,128)(2,1)}, s16[272,256]{1,0:T(8,128)(2,1)}) custom-call(s32[3]{0:T(128)S(1)} %pad_add_fusion.me_ref, s32[1]{0:T(128)} %get-tuple-element.62.after_ref, f32[256,1024]{1,0:T(8,128)S(1)} %copy-done.2, s32[1,256]{1,0:T(1,128)S(1)} %bitcast.10), custom_call_target="tpu_custom_call" | custom-call | tf_op jit(solution)/shard_map/prev/pallas_call | solution.py:393
  41.8 1.1 collective-permute-done.3.refs_1_
  43.0 7.8 %collective-permute-done.4.refs_2_ = bf16[1024,128]{1,0:T(8,128)(2,1)S(1)} collective-permute-done((bf16[1024,128]{1,0:T(8,128)(2,1)S(1)}, bf16[1024,128]{1,0:T(8,128)(2,1)S(1)}, u32[]{:S(2)}, u32[]{:S(2)}) %collective-permute-start.4) | collective-permute-done | bytes 262176 | tf_op jit(solution)/shard_map/ppermute | solution.py:343
  50.8 3.0 %collective-permute-done.5.refs_3_ = bf16[1024,128]{1,0:T(8,128)(2,1)S(1)} collective-permute-done((bf16[1024,128]{1,0:T(8,128)(2,1)S(1)}, bf16[1024,128]{1,0:T(8,128)(2,1)S(1)}, u32[]{:S(2)}, u32[]{:S(2)}) %collective-permute-start.5) | collective-permute-done | bytes 262176 | tf_op jit(solution)/shard_map/ppermute | solution.py:343
  53.7 3.5 %sums1.1 = (f32[1024,128]{1,0:T(8,128)S(1)}, s16[1040,128]{1,0:T(8,128)(2,1)}, s32[1]{0:T(128)}) custom-call(s32[32]{0:T(128)S(1)} %get-tuple-element.52.place_ref.before_ref, s32[1]{0:T(128)} %get-tuple-element.56.before_ref, bf16[4096,128]{1,0:T(8,128)(2,1)S(1)} %get-tuple-element.53.member_ref, s32[8,128]{1,0:T(8,128)S(1)} %get-tuple-element.54.far_count_ref, ...), custom_call_target="tpu_custom_call" | custom-call | tf_op jit(solution)/shard_map/sums1/pallas_call | solution.py:379
  57.2 0.8 copy-done.5
  58.0 1.1 collective-permute-start.7
  59.1 2.9 %collective-permute-start.10 = (s16[272,256]{1,0:T(8,128)(2,1)}, s16[272,256]{1,0:T(8,128)(2,1)S(1)}, u32[]{:S(2)}, u32[]{:S(2)}) collective-permute-start(s16[272,256]{1,0:T(8,128)(2,1)} %get-tuple-element.73), channel_id=1, source_target_pairs={{0,3},{1,2},{2,1},{3,0},{4,7},{5,6},{6,5},{7,4},{8,11},{9,10},{10,... | collective-permute-start | bytes 417800 | tf_op jit(solution)/shard_map/ppermute | solution.py:343
  62.0 0.5 collective-permute-start.8
  62.6 3.2 %fusion = f32[2048]{0:T(1024)S(1)} fusion(bf16[2048,1024]{1,0:T(8,128)(2,1)} %all-gather.2.cloned.1.call-done), kind=kLoop, calls=%fused_computation.2 | loop fusion | flops 6289408 | bytes 4202496 | tf_op jit(solution)/shard_map/reduce_sum | solution.py:407
  65.8 4.4 %collective-permute-done.7.refs_3_ = s16[1040,128]{1,0:T(8,128)(2,1)} collective-permute-done((s16[1040,128]{1,0:T(8,128)(2,1)}, s16[1040,128]{1,0:T(8,128)(2,1)}, u32[]{:S(2)}, u32[]{:S(2)}) %collective-permute-start.7) | collective-permute-done | bytes 266272 | tf_op jit(solution)/shard_map/ppermute | solution.py:343
  70.4 2.2 %refresh.1 = (f32[1024,256]{1,0:T(8,128)S(1)}, s16[272,256]{1,0:T(8,128)(2,1)S(1)}, s16[272,256]{1,0:T(8,128)(2,1)S(1)}, s16[272,256]{1,0:T(8,128)(2,1)S(1)}, s16[272,256]{1,0:T(8,128)(2,1)S(1)}) custom-call(f32[1024,128]{1,0:T(8,128)S(1)} %get-tuple-element.51.near_ref, f32[1024,128]{1,0:T(8,128)S(1)} %copy-done.4, f32[1024,128]{1,0:T(8,128)S(1)} %copy-done.6, ...), custom_call_target="tpu_custom_call" | custom-call | tf_op jit(solution)/shard_map/refresh/pallas_call | solution.py:420
  72.6 2.7 %collective-permute-start.11 = (s16[272,256]{1,0:T(8,128)(2,1)S(1)}, s16[272,256]{1,0:T(8,128)(2,1)S(1)}, u32[]{:S(2)}, u32[]{:S(2)}) collective-permute-start(s16[272,256]{1,0:T(8,128)(2,1)S(1)} %get-tuple-element.75), channel_id=1, source_target_pairs={{0,1},{1,0},{2,3},{3,2},{4,5},{5,4},{6,7},{7,6},{8,9},{9,8},{10,11... | collective-permute-start | bytes 417800 | tf_op jit(solution)/shard_map/ppermute | solution.py:343
  75.3 1.5 %collective-permute-start.13 = (s16[272,256]{1,0:T(8,128)(2,1)S(1)}, s16[272,256]{1,0:T(8,128)(2,1)S(1)}, u32[]{:S(2)}, u32[]{:S(2)}) collective-permute-start(s16[272,256]{1,0:T(8,128)(2,1)S(1)} %get-tuple-element.77), channel_id=1, source_target_pairs={{0,3},{1,2},{2,1},{3,0},{4,7},{5,6},{6,5},{7,4},{8,11},{9,10},{10,... | collective-permute-start | bytes 417800 | tf_op jit(solution)/shard_map/ppermute | solution.py:343
  77.1 2.7 %collective-permute-done.11.refs_1_ = s16[272,256]{1,0:T(8,128)(2,1)S(1)} collective-permute-done((s16[272,256]{1,0:T(8,128)(2,1)S(1)}, s16[272,256]{1,0:T(8,128)(2,1)S(1)}, u32[]{:S(2)}, u32[]{:S(2)}) %collective-permute-start.11) | collective-permute-done | bytes 139296 | tf_op jit(solution)/shard_map/ppermute | solution.py:343
  79.9 0.9 collective-permute-done.12.refs_2_
  80.8 1.2 collective-permute-done.13.refs_3_
  82.0 2.1 %upper.1 = (s16[272,256]{1,0:T(8,128)(2,1)S(1)}, s16[272,256]{1,0:T(8,128)(2,1)S(1)}) custom-call(f32[1024,256]{1,0:T(8,128)S(1)} %get-tuple-element.80.x_ref, s16[272,256]{1,0:T(8,128)(2,1)S(1)} %get-tuple-element.74.refs_0_, s16[272,256]{1,0:T(8,128)(2,1)S(1)} %collective-permute-done.11.refs_1_, s16[272,256]{1,0:T(8,128)(2,1)S(1)} %collective-permute-done.12.refs_2_, ...), custom_call_target="tpu_custom_call" | custom-call | tf_op jit(solution)/shard_map/upper/pallas_call | solution.py:434
  84.1 2.0 %collective-permute-start.18 = (s16[272,256]{1,0:T(8,128)(2,1)S(1)}, s16[272,256]{1,0:T(8,128)(2,1)S(1)}, u32[]{:S(2)}, u32[]{:S(2)}) collective-permute-start(s16[272,256]{1,0:T(8,128)(2,1)S(1)} %get-tuple-element.85.own), channel_id=1, source_target_pairs={{0,4},{1,5},{2,6},{3,7},{4,0},{5,1},{6,2},{7,3},{8,12},{9,13},{10,... | collective-permute-start | bytes 417800 | tf_op jit(solution)/shard_map/ppermute | solution.py:343
  86.2 0.5 fusion.3
  86.7 0.9 collective-permute-start.14
  87.6 7.9 %collective-permute-done.18.far = s16[272,256]{1,0:T(8,128)(2,1)S(1)} collective-permute-done((s16[272,256]{1,0:T(8,128)(2,1)S(1)}, s16[272,256]{1,0:T(8,128)(2,1)S(1)}, u32[]{:S(2)}, u32[]{:S(2)}) %collective-permute-start.18) | collective-permute-done | bytes 139296 | tf_op jit(solution)/shard_map/ppermute | solution.py:343
  95.9 0.6 collective-permute-start.19
  96.5 5.5 %fusion.2 = f32[1024]{0:T(1024)S(1)} fusion(bf16[2048,1024]{1,0:T(8,128)(2,1)S(1)} %copy-done.9, f32[8,2048]{1,0:T(8,128)S(1)} %convert_element_type.25, f32[2048]{0:T(1024)S(1)} %add_rsqrt_fusion, bf16[1024,1024]{1,0:T(8,128)(2,1)S(1)} %copy-done.1, f32[1024]{0:T(1024)S(1)} %add_rsqrt_fusion.1), kind=kOutput, calls=%fused_computation.5 | convolution fusion | flops 4310694912 | bytes 6373376 | tf_op jit(solution)/shard_map/dot_general | solution.py:410
  102.1 0.6 log.3
  102.7 2.9 %collective-permute-start.21 = (s16[272,256]{1,0:T(8,128)(2,1)S(1)}, s16[272,256]{1,0:T(8,128)(2,1)S(1)}, u32[]{:S(2)}, u32[]{:S(2)}) collective-permute-start(s16[272,256]{1,0:T(8,128)(2,1)S(1)} %both1.1.refs_4_), channel_id=1, source_target_pairs={{0,3},{1,2},{2,1},{3,0},{4,7},{5,6},{6,5},{7,4},{8,11},{9,10},{10,... | collective-permute-start | bytes 417800 | tf_op jit(solution)/shard_map/ppermute | solution.py:343
  106.0 0.6 collective-permute-start.15
  106.6 2.9 %collective-permute-start.17 = (s16[272,256]{1,0:T(8,128)(2,1)S(1)}, s16[272,256]{1,0:T(8,128)(2,1)S(1)}, u32[]{:S(2)}, u32[]{:S(2)}) collective-permute-start(s16[272,256]{1,0:T(8,128)(2,1)S(1)} %both0.1.refs_0_), channel_id=1, source_target_pairs={{0,3},{1,2},{2,1},{3,0},{4,7},{5,6},{6,5},{7,4},{8,11},{9,10},{10,... | collective-permute-start | bytes 417800 | tf_op jit(solution)/shard_map/ppermute | solution.py:343
  109.5 1.9 %decode.1 = f32[256,1024]{1,0:T(8,128)} custom-call(s32[3]{0:T(128)S(1)} %pad_add_fusion.me_ref, s16[272,256]{1,0:T(8,128)(2,1)S(1)} %get-tuple-element.74.refs_0_, s16[272,256]{1,0:T(8,128)(2,1)S(1)} %collective-permute-done.11.refs_1_, s16[272,256]{1,0:T(8,128)(2,1)S(1)} %collective-permute-done.12.refs_2_, s16[272,256]{1,0:T(8,128)(2,1)S(1)} %collective-permute-done.13.refs_3_), custom_call_target="tpu_custom_call" | custom-call | tf_op jit(solution)/shard_map/decode/pallas_call | solution.py:460
  111.4 1.2 collective-permute-done.21.refs_7_
  112.5 1.1 collective-permute-done.15.refs_1_
  113.7 0.4 collective-permute-done.16.refs_2_
  114.1 1.3 %collective-permute-done.17.refs_3_ = s16[272,256]{1,0:T(8,128)(2,1)S(1)} collective-permute-done((s16[272,256]{1,0:T(8,128)(2,1)S(1)}, s16[272,256]{1,0:T(8,128)(2,1)S(1)}, u32[]{:S(2)}, u32[]{:S(2)}) %collective-permute-start.17) | collective-permute-done | bytes 139296 | tf_op jit(solution)/shard_map/ppermute | solution.py:343
  115.5 2.3 %join.1 = f32[512,1024]{1,0:T(8,128)} custom-call(s32[3]{0:T(128)S(1)} %pad_add_fusion.me_ref, s16[272,256]{1,0:T(8,128)(2,1)S(1)} %both0.1.refs_0_, s16[272,256]{1,0:T(8,128)(2,1)S(1)} %collective-permute-done.15.refs_1_, s16[272,256]{1,0:T(8,128)(2,1)S(1)} %collective-permute-done.16.refs_2_, s16[272,256]{1,0:T(8,128)(2,1)S(1)} %collective-permute-done.17.refs_3_, ...), custom_call_target="tpu_custom_call" | custom-call | tf_op jit(solution)/shard_map/join/pallas_call | solution.py:468
  (42 shorter events, 1.9 us)
Async XLA Ops:
  7.2 32.0 %copy-start.8 = (s32[256]{0:T(256)S(1)}, s32[256]{0:T(256)}, u32[]{:S(2)}) copy-start(s32[256]{0:T(256)} %param.10) | copy-start | bytes 3076
  7.2 32.0 %copy-start.2 = (f32[256,1024]{1,0:T(8,128)S(1)}, f32[256,1024]{1,0:T(8,128)}, u32[]{:S(2)}) copy-start(f32[256,1024]{1,0:T(8,128)} %prev_ref.1) | copy-start | bytes 3145732
  7.2 55.5 %all-gather.2.cloned.1.call-start = ((), (), s32[]{:S(2)}) async-start(), calls=%async_computation | async-start | bytes 5242880 | tf_op jit(solution)/shard_map/all_gather | solution.py:349
  8.0 1.6 %copy-start = (bf16[1024,1024]{1,0:T(8,128)(2,1)S(1)}, bf16[1024,1024]{1,0:T(8,128)(2,1)}, u32[]{:S(2)}) copy-start(bf16[1024,1024]{1,0:T(8,128)(2,1)} %points_ref.1) | copy-start | bytes 6291460
  9.6 0.7 copy-start.7
  12.1 9.4 %collective-permute-start = (bf16[1040,128]{1,0:T(8,128)(2,1)S(1)}, bf16[1040,128]{1,0:T(8,128)(2,1)S(1)}, u32[]{:S(2)}, u32[]{:S(2)}) collective-permute-start(bf16[1040,128]{1,0:T(8,128)(2,1)S(1)} %get-tuple-element.47), channel_id=1, source_target_pairs={{0,1},{1,0},{2,3},{3,2},{4,5},{5,4},{6,7},{7,6},{8,9},{9,8},{10,11... | collective-permute-start | bytes 798728 | tf_op jit(solution)/shard_map/ppermute | solution.py:343
  15.1 9.3 %collective-permute-start.1 = (bf16[1040,128]{1,0:T(8,128)(2,1)S(1)}, bf16[1040,128]{1,0:T(8,128)(2,1)S(1)}, u32[]{:S(2)}, u32[]{:S(2)}) collective-permute-start(bf16[1040,128]{1,0:T(8,128)(2,1)S(1)} %get-tuple-element.48), channel_id=1, source_target_pairs={{0,2},{1,3},{2,0},{3,1},{4,6},{5,7},{6,4},{7,5},{8,10},{9,11},{10,... | collective-permute-start | bytes 798728 | tf_op jit(solution)/shard_map/ppermute | solution.py:343
  16.7 11.8 %collective-permute-start.2 = (bf16[1040,128]{1,0:T(8,128)(2,1)S(1)}, bf16[1040,128]{1,0:T(8,128)(2,1)S(1)}, u32[]{:S(2)}, u32[]{:S(2)}) collective-permute-start(bf16[1040,128]{1,0:T(8,128)(2,1)S(1)} %get-tuple-element.49), channel_id=1, source_target_pairs={{0,3},{1,2},{2,1},{3,0},{4,7},{5,6},{6,5},{7,4},{8,11},{9,10},{10,... | collective-permute-start | bytes 798728 | tf_op jit(solution)/shard_map/ppermute | solution.py:343
  32.9 8.9 %copy-start.3 = (f32[1024,128]{1,0:T(8,128)}, f32[1024,128]{1,0:T(8,128)S(1)}, u32[]{:S(2)}) copy-start(f32[1024,128]{1,0:T(8,128)S(1)} %get-tuple-element.55.refs_0_) | copy-start | bytes 1572868
  32.9 26.2 %collective-permute-start.6 = (s16[1040,128]{1,0:T(8,128)(2,1)S(1)}, s16[1040,128]{1,0:T(8,128)(2,1)S(1)}, u32[]{:S(2)}, u32[]{:S(2)}) collective-permute-start(s16[1040,128]{1,0:T(8,128)(2,1)S(1)} %get-tuple-element.67), channel_id=1, source_target_pairs={{0,4},{1,5},{2,6},{3,7},{4,0},{5,1},{6,2},{7,3},{8,12},{9,13},{10,... | collective-permute-start | bytes 798728 | tf_op jit(solution)/shard_map/ppermute | solution.py:343
  35.7 7.3 %collective-permute-start.3 = (bf16[1024,128]{1,0:T(8,128)(2,1)S(1)}, bf16[1024,128]{1,0:T(8,128)(2,1)S(1)}, u32[]{:S(2)}, u32[]{:S(2)}) collective-permute-start(bf16[1024,128]{1,0:T(8,128)(2,1)S(1)} %get-tuple-element.58), channel_id=1, source_target_pairs={{0,1},{1,0},{2,3},{3,2},{4,5},{5,4},{6,7},{7,6},{8,9},{9,8},{10,11... | collective-permute-start | bytes 786440 | tf_op jit(solution)/shard_map/ppermute | solution.py:343
  37.2 13.5 %collective-permute-start.4 = (bf16[1024,128]{1,0:T(8,128)(2,1)S(1)}, bf16[1024,128]{1,0:T(8,128)(2,1)S(1)}, u32[]{:S(2)}, u32[]{:S(2)}) collective-permute-start(bf16[1024,128]{1,0:T(8,128)(2,1)S(1)} %get-tuple-element.59), channel_id=1, source_target_pairs={{0,2},{1,3},{2,0},{3,1},{4,6},{5,7},{6,4},{7,5},{8,10},{9,11},{10,... | collective-permute-start | bytes 786440 | tf_op jit(solution)/shard_map/ppermute | solution.py:343
  38.8 14.9 %collective-permute-start.5 = (bf16[1024,128]{1,0:T(8,128)(2,1)S(1)}, bf16[1024,128]{1,0:T(8,128)(2,1)S(1)}, u32[]{:S(2)}, u32[]{:S(2)}) collective-permute-start(bf16[1024,128]{1,0:T(8,128)(2,1)S(1)} %get-tuple-element.60), channel_id=1, source_target_pairs={{0,3},{1,2},{2,1},{3,0},{4,7},{5,6},{6,5},{7,4},{8,11},{9,10},{10,... | collective-permute-start | bytes 786440 | tf_op jit(solution)/shard_map/ppermute | solution.py:343
  53.7 23.2 %copy-start.10 = (s32[8,8]{1,0:T(8,128)S(1)}, s32[8,8]{1,0:T(8,128)}, u32[]{:S(2)}) copy-start(s32[8,8]{1,0:T(8,128)} %param.8) | copy-start | bytes 772
  57.2 0.8 copy-start.5
  58.0 12.2 %collective-permute-start.7 = (s16[1040,128]{1,0:T(8,128)(2,1)}, s16[1040,128]{1,0:T(8,128)(2,1)}, u32[]{:S(2)}, u32[]{:S(2)}) collective-permute-start(s16[1040,128]{1,0:T(8,128)(2,1)} %get-tuple-element.69), channel_id=1, source_target_pairs={{0,4},{1,5},{2,6},{3,7},{4,0},{5,1},{6,2},{7,3},{8,12},{9,13},{10,... | collective-permute-start | bytes 798728 | tf_op jit(solution)/shard_map/ppermute | solution.py:343
  59.1 27.1 %copy-start.1 = (bf16[1024,1024]{1,0:T(8,128)(2,1)S(1)}, bf16[1024,1024]{1,0:T(8,128)(2,1)}, u32[]{:S(2)}) copy-start(bf16[1024,1024]{1,0:T(8,128)(2,1)} %points_ref.1) | copy-start | bytes 6291460
  59.1 11.1 %collective-permute-start.10 = (s16[272,256]{1,0:T(8,128)(2,1)}, s16[272,256]{1,0:T(8,128)(2,1)S(1)}, u32[]{:S(2)}, u32[]{:S(2)}) collective-permute-start(s16[272,256]{1,0:T(8,128)(2,1)} %get-tuple-element.73), channel_id=1, source_target_pairs={{0,3},{1,2},{2,1},{3,0},{4,7},{5,6},{6,5},{7,4},{8,11},{9,10},{10,... | collective-permute-start | bytes 417800 | tf_op jit(solution)/shard_map/ppermute | solution.py:343
  62.0 8.2 %collective-permute-start.8 = (s16[272,256]{1,0:T(8,128)(2,1)}, s16[272,256]{1,0:T(8,128)(2,1)S(1)}, u32[]{:S(2)}, u32[]{:S(2)}) collective-permute-start(s16[272,256]{1,0:T(8,128)(2,1)} %get-tuple-element.71), channel_id=1, source_target_pairs={{0,1},{1,0},{2,3},{3,2},{4,5},{5,4},{6,7},{7,6},{8,9},{9,8},{10,11... | collective-permute-start | bytes 417800 | tf_op jit(solution)/shard_map/ppermute | solution.py:343
  62.5 7.8 %collective-permute-start.9 = (s16[272,256]{1,0:T(8,128)(2,1)}, s16[272,256]{1,0:T(8,128)(2,1)S(1)}, u32[]{:S(2)}, u32[]{:S(2)}) collective-permute-start(s16[272,256]{1,0:T(8,128)(2,1)} %get-tuple-element.72), channel_id=1, source_target_pairs={{0,2},{1,3},{2,0},{3,1},{4,6},{5,7},{6,4},{7,5},{8,10},{9,11},{10,... | collective-permute-start | bytes 417800 | tf_op jit(solution)/shard_map/ppermute | solution.py:343
  62.6 7.7 %copy-start.4 = (f32[1024,128]{1,0:T(8,128)S(1)}, f32[1024,128]{1,0:T(8,128)}, u32[]{:S(2)}) copy-start(f32[1024,128]{1,0:T(8,128)} %copy-done.3) | copy-start | bytes 1572868
  62.6 7.7 %copy-start.6 = (f32[1024,128]{1,0:T(8,128)S(1)}, f32[1024,128]{1,0:T(8,128)}, u32[]{:S(2)}) copy-start(f32[1024,128]{1,0:T(8,128)} %copy-done.5) | copy-start | bytes 1572868
  65.8 30.7 %copy-start.9 = (bf16[2048,1024]{1,0:T(8,128)(2,1)S(1)}, bf16[2048,1024]{1,0:T(8,128)(2,1)}, u32[]{:S(2)}) copy-start(bf16[2048,1024]{1,0:T(8,128)(2,1)} %all-gather.2.cloned.1.call-done) | copy-start | bytes 12582916
  72.6 7.3 %collective-permute-start.11 = (s16[272,256]{1,0:T(8,128)(2,1)S(1)}, s16[272,256]{1,0:T(8,128)(2,1)S(1)}, u32[]{:S(2)}, u32[]{:S(2)}) collective-permute-start(s16[272,256]{1,0:T(8,128)(2,1)S(1)} %get-tuple-element.75), channel_id=1, source_target_pairs={{0,1},{1,0},{2,3},{3,2},{4,5},{5,4},{6,7},{7,6},{8,9},{9,8},{10,11... | collective-permute-start | bytes 417800 | tf_op jit(solution)/shard_map/ppermute | solution.py:343
  75.3 5.5 %collective-permute-start.12 = (s16[272,256]{1,0:T(8,128)(2,1)S(1)}, s16[272,256]{1,0:T(8,128)(2,1)S(1)}, u32[]{:S(2)}, u32[]{:S(2)}) collective-permute-start(s16[272,256]{1,0:T(8,128)(2,1)S(1)} %get-tuple-element.76), channel_id=1, source_target_pairs={{0,2},{1,3},{2,0},{3,1},{4,6},{5,7},{6,4},{7,5},{8,10},{9,11},{10,... | collective-permute-start | bytes 417800 | tf_op jit(solution)/shard_map/ppermute | solution.py:343
  75.3 6.7 %collective-permute-start.13 = (s16[272,256]{1,0:T(8,128)(2,1)S(1)}, s16[272,256]{1,0:T(8,128)(2,1)S(1)}, u32[]{:S(2)}, u32[]{:S(2)}) collective-permute-start(s16[272,256]{1,0:T(8,128)(2,1)S(1)} %get-tuple-element.77), channel_id=1, source_target_pairs={{0,3},{1,2},{2,1},{3,0},{4,7},{5,6},{6,5},{7,4},{8,11},{9,10},{10,... | collective-permute-start | bytes 417800 | tf_op jit(solution)/shard_map/ppermute | solution.py:343
  84.1 11.4 %collective-permute-start.18 = (s16[272,256]{1,0:T(8,128)(2,1)S(1)}, s16[272,256]{1,0:T(8,128)(2,1)S(1)}, u32[]{:S(2)}, u32[]{:S(2)}) collective-permute-start(s16[272,256]{1,0:T(8,128)(2,1)S(1)} %get-tuple-element.85.own), channel_id=1, source_target_pairs={{0,4},{1,5},{2,6},{3,7},{4,0},{5,1},{6,2},{7,3},{8,12},{9,13},{10,... | collective-permute-start | bytes 417800 | tf_op jit(solution)/shard_map/ppermute | solution.py:343
  86.7 18.9 %collective-permute-start.14 = (s16[272,256]{1,0:T(8,128)(2,1)S(1)}, s16[272,256]{1,0:T(8,128)(2,1)S(1)}, u32[]{:S(2)}, u32[]{:S(2)}) collective-permute-start(s16[272,256]{1,0:T(8,128)(2,1)S(1)} %get-tuple-element.84.own), channel_id=1, source_target_pairs={{0,4},{1,5},{2,6},{3,7},{4,0},{5,1},{6,2},{7,3},{8,12},{9,13},{10,... | collective-permute-start | bytes 417800 | tf_op jit(solution)/shard_map/ppermute | solution.py:343
  95.9 10.7 %collective-permute-start.19 = (s16[272,256]{1,0:T(8,128)(2,1)S(1)}, s16[272,256]{1,0:T(8,128)(2,1)S(1)}, u32[]{:S(2)}, u32[]{:S(2)}) collective-permute-start(s16[272,256]{1,0:T(8,128)(2,1)S(1)} %both1.1.refs_4_), channel_id=1, source_target_pairs={{0,1},{1,0},{2,3},{3,2},{4,5},{5,4},{6,7},{7,6},{8,9},{9,8},{10,11... | collective-permute-start | bytes 417800 | tf_op jit(solution)/shard_map/ppermute | solution.py:343
  102.7 8.7 %collective-permute-start.20 = (s16[272,256]{1,0:T(8,128)(2,1)S(1)}, s16[272,256]{1,0:T(8,128)(2,1)S(1)}, u32[]{:S(2)}, u32[]{:S(2)}) collective-permute-start(s16[272,256]{1,0:T(8,128)(2,1)S(1)} %both1.1.refs_4_), channel_id=1, source_target_pairs={{0,2},{1,3},{2,0},{3,1},{4,6},{5,7},{6,4},{7,5},{8,10},{9,11},{10,... | collective-permute-start | bytes 417800 | tf_op jit(solution)/shard_map/ppermute | solution.py:343
  102.7 9.9 %collective-permute-start.21 = (s16[272,256]{1,0:T(8,128)(2,1)S(1)}, s16[272,256]{1,0:T(8,128)(2,1)S(1)}, u32[]{:S(2)}, u32[]{:S(2)}) collective-permute-start(s16[272,256]{1,0:T(8,128)(2,1)S(1)} %both1.1.refs_4_), channel_id=1, source_target_pairs={{0,3},{1,2},{2,1},{3,0},{4,7},{5,6},{6,5},{7,4},{8,11},{9,10},{10,... | collective-permute-start | bytes 417800 | tf_op jit(solution)/shard_map/ppermute | solution.py:343
  106.0 7.7 %collective-permute-start.15 = (s16[272,256]{1,0:T(8,128)(2,1)S(1)}, s16[272,256]{1,0:T(8,128)(2,1)S(1)}, u32[]{:S(2)}, u32[]{:S(2)}) collective-permute-start(s16[272,256]{1,0:T(8,128)(2,1)S(1)} %both0.1.refs_0_), channel_id=1, source_target_pairs={{0,1},{1,0},{2,3},{3,2},{4,5},{5,4},{6,7},{7,6},{8,9},{9,8},{10,11... | collective-permute-start | bytes 417800 | tf_op jit(solution)/shard_map/ppermute | solution.py:343
  106.6 7.5 %collective-permute-start.16 = (s16[272,256]{1,0:T(8,128)(2,1)S(1)}, s16[272,256]{1,0:T(8,128)(2,1)S(1)}, u32[]{:S(2)}, u32[]{:S(2)}) collective-permute-start(s16[272,256]{1,0:T(8,128)(2,1)S(1)} %both0.1.refs_0_), channel_id=1, source_target_pairs={{0,2},{1,3},{2,0},{3,1},{4,6},{5,7},{6,4},{7,5},{8,10},{9,11},{10,... | collective-permute-start | bytes 417800 | tf_op jit(solution)/shard_map/ppermute | solution.py:343
  106.6 8.9 %collective-permute-start.17 = (s16[272,256]{1,0:T(8,128)(2,1)S(1)}, s16[272,256]{1,0:T(8,128)(2,1)S(1)}, u32[]{:S(2)}, u32[]{:S(2)}) collective-permute-start(s16[272,256]{1,0:T(8,128)(2,1)S(1)} %both0.1.refs_0_), channel_id=1, source_target_pairs={{0,3},{1,2},{2,1},{3,0},{4,7},{5,6},{6,5},{7,4},{8,11},{9,10},{10,... | collective-permute-start | bytes 417800 | tf_op jit(solution)/shard_map/ppermute | solution.py:343
Sparse Core Ops, SparseCore 0:
  9.6 37.1 all-gather.1

commit v11 on v10

--- a/solution.py
+++ b/solution.py
@@ -442,11 +442,10 @@
         name="upper",
     )(x, *backs, *prevs)
     far_codes = [swap(code, h) for code in codes]
+    *codes, point_score = lax.optimization_barrier((*codes, point_score))
     parts = []
     for k in range(2):
         code = codes[k]
-        if k == 0:
-            code, point_score = lax.optimization_barrier((code, point_score))
         code = call(
             both_kernel,
             code_shape,

time: 125 us -> 118 us (0.944)
  waiting for transfers between devices: 45.8 us -> 39.3 us
    ppermute x22, waiting for transfers between devices: 45.1 us -> 38.6 us  [swap(): return lax.ppermute(value, 'cent', [(i, i ^ mask) for i in range(n)])]
  transfers between devices with their start and end apart: 23 -> 23, of which waited for: 16 -> 14; matrix products, arithmetic and copies ran while one was open for 8% -> 8% of each run, Pallas kernels for 12% -> 13%
where the time goes in v11:
time: 118 us
  waiting for transfers between devices  39.3 us (33%)
  starting transfers between devices  29.8 us (25%)
  Pallas kernels  21.7 us (18%)
  between operations  14.2 us (12%)
  matrix products  5.44 us (5%)
  other arithmetic  3.97 us (3%)
  local copies, waits for them, and re-layouts  3.7 us (3%)
    ppermute x22, waiting for transfers between devices, swap(): return lax.ppermute(value, 'cent', [(i, i ^ mask) for i in range(n)])  38.6 us
    ppermute x22, starting transfers between devices, swap(): return lax.ppermute(value, 'cent', [(i, i ^ mask) for i in range(n)])  29.7 us
    pallas_call x2, Pallas kernels, shards(): call(sums_kernel, [shape((rows, BLOCK), f32), shape((lines, BLOCK), i16),...  5.8 us
    dot_general x1, matrix products, shards(): lax.dot_general(unit_points, table_units, (((1,), (1,)), ((), ())), prefe...  5.44 us
    reduce_sum x1, other arithmetic, shards(): jnp.mean(jnp.square(table_rows.astype(f32)), axis=-1) + EPSILON  3.16 us
    unnamed x22, local copies, waits for them, and re-layouts  3.1 us
    pallas_call x1, Pallas kernels, shards(): call(prev_kernel, [shape((owned + head, w), i16)] * h, in_specs=[SMEM, SM...  2.62 us
  transfers between devices with their start and end apart: 23, of which 14 were waited for; matrix products, arithmetic and copies ran while one was open for 8% of the time, Pallas kernels for 13%

profile of v11, /device:TPU:0, one launch (start us, length us, event | category | flops | bytes accessed | tf_op | source)
XLA Modules:
  0.0 118.1 jit_solution(6455343772068921243)
XLA Ops:
  7.2 0.7 all-gather.2.cloned.1.call-update
  8.0 1.6 %copy-done = bf16[1024,1024]{1,0:T(8,128)(2,1)S(1)} copy-done((bf16[1024,1024]{1,0:T(8,128)(2,1)S(1)}, bf16[1024,1024]{1,0:T(8,128)(2,1)}, u32[]{:S(2)}) %copy-start) | copy-done | bytes 2097176
  9.6 0.7 copy-done.7
  10.3 1.8 %pack.1 = (bf16[1040,128]{1,0:T(8,128)(2,1)S(1)}, bf16[1024,128]{1,0:T(8,128)(2,1)S(1)}, bf16[1040,128]{1,0:T(8,128)(2,1)S(1)}, bf16[1024,128]{1,0:T(8,128)(2,1)...) custom-call(s32[3]{0:T(128)S(1)} %pad_add_fusion.me_ref, ...), custom_call_target="tpu_custom_call" | custom-call | tf_op jit(solution)/shard_map/pack/pallas_call | solution.py:352
  12.1 3.0 %collective-permute-start = (bf16[1040,128]{1,0:T(8,128)(2,1)S(1)}, bf16[1040,128]{1,0:T(8,128)(2,1)S(1)}, u32[]{:S(2)}, u32[]{:S(2)}) collective-permute-start(bf16[1040,128]{1,0:T(8,128)(2,1)S(1)} %get-tuple-element.48), channel_id=1, source_target_pairs={{0,1},{1,0},{2,3},{3,2},{4,5},{5,4},{6,7},{7,6},{8,9},{9,8},{10,11... | collective-permute-start | bytes 798728 | tf_op jit(solution)/shard_map/ppermute | solution.py:343
  15.1 1.6 %collective-permute-start.1 = (bf16[1040,128]{1,0:T(8,128)(2,1)S(1)}, bf16[1040,128]{1,0:T(8,128)(2,1)S(1)}, u32[]{:S(2)}, u32[]{:S(2)}) collective-permute-start(bf16[1040,128]{1,0:T(8,128)(2,1)S(1)} %get-tuple-element.49), channel_id=1, source_target_pairs={{0,2},{1,3},{2,0},{3,1},{4,6},{5,7},{6,4},{7,5},{8,10},{9,11},{10,... | collective-permute-start | bytes 798728 | tf_op jit(solution)/shard_map/ppermute | solution.py:343
  16.7 4.8 %collective-permute-done.refs_1_ = bf16[1040,128]{1,0:T(8,128)(2,1)S(1)} collective-permute-done((bf16[1040,128]{1,0:T(8,128)(2,1)S(1)}, bf16[1040,128]{1,0:T(8,128)(2,1)S(1)}, u32[]{:S(2)}, u32[]{:S(2)}) %collective-permute-start) | collective-permute-done | bytes 266272 | tf_op jit(solution)/shard_map/ppermute | solution.py:343
  21.5 2.9 %collective-permute-done.1.refs_2_ = bf16[1040,128]{1,0:T(8,128)(2,1)S(1)} collective-permute-done((bf16[1040,128]{1,0:T(8,128)(2,1)S(1)}, bf16[1040,128]{1,0:T(8,128)(2,1)S(1)}, u32[]{:S(2)}, u32[]{:S(2)}) %collective-permute-start.1) | collective-permute-done | bytes 266272 | tf_op jit(solution)/shard_map/ppermute | solution.py:343
  24.4 4.0 %collective-permute-done.2.refs_3_ = bf16[1040,128]{1,0:T(8,128)(2,1)S(1)} collective-permute-done((bf16[1040,128]{1,0:T(8,128)(2,1)S(1)}, bf16[1040,128]{1,0:T(8,128)(2,1)S(1)}, u32[]{:S(2)}, u32[]{:S(2)}) %collective-permute-start.2) | collective-permute-done | bytes 266272 | tf_op jit(solution)/shard_map/ppermute | solution.py:343
  28.5 2.3 %prepare.1 = (bf16[4096,128]{1,0:T(8,128)(2,1)S(1)}, s32[32]{0:T(128)S(1)}, f32[1024,128]{1,0:T(8,128)S(1)}, s32[8,128]{1,0:T(8,128)S(1)}) custom-call(s32[3]{0:T(128)S(1)} %pad_add_fusion.me_ref, bf16[1040,128]{1,0:T(8,128)(2,1)S(1)} %get-tuple-element.47.refs_0_, bf16[1040,128]{1,0:T(8,128)(2,1)S(1)} %collective-permute-done.refs_1_, ...), custom_call_target="tpu_custom_call" | custom-call | tf_op jit(solution)/shard_map/prepare/pallas_call | solution.py:362
  30.8 2.2 %sums0.1 = (f32[1024,128]{1,0:T(8,128)S(1)}, s16[1040,128]{1,0:T(8,128)(2,1)S(1)}, s32[1]{0:T(128)}) custom-call(s32[32]{0:T(128)S(1)} %get-tuple-element.53.place_ref.before_ref, s32[32]{0:T(128)S(1)} %get-tuple-element.53.place_ref.before_ref, bf16[4096,128]{1,0:T(8,128)(2,1)S(1)} %get-tuple-element.54.member_ref, ...), custom_call_target="tpu_custom_call" | custom-call | tf_op jit(solution)/shard_map/sums0/pallas_call | solution.py:379
  32.9 2.8 %collective-permute-start.6 = (s16[1040,128]{1,0:T(8,128)(2,1)S(1)}, s16[1040,128]{1,0:T(8,128)(2,1)S(1)}, u32[]{:S(2)}, u32[]{:S(2)}) collective-permute-start(s16[1040,128]{1,0:T(8,128)(2,1)S(1)} %get-tuple-element.68), channel_id=1, source_target_pairs={{0,4},{1,5},{2,6},{3,7},{4,0},{5,1},{6,2},{7,3},{8,12},{9,13},{10,... | collective-permute-start | bytes 798728 | tf_op jit(solution)/shard_map/ppermute | solution.py:343
  35.7 1.5 %collective-permute-start.3 = (bf16[1024,128]{1,0:T(8,128)(2,1)S(1)}, bf16[1024,128]{1,0:T(8,128)(2,1)S(1)}, u32[]{:S(2)}, u32[]{:S(2)}) collective-permute-start(bf16[1024,128]{1,0:T(8,128)(2,1)S(1)} %get-tuple-element.59), channel_id=1, source_target_pairs={{0,1},{1,0},{2,3},{3,2},{4,5},{5,4},{6,7},{7,6},{8,9},{9,8},{10,11... | collective-permute-start | bytes 786440 | tf_op jit(solution)/shard_map/ppermute | solution.py:343
  37.3 1.6 %collective-permute-start.4 = (bf16[1024,128]{1,0:T(8,128)(2,1)S(1)}, bf16[1024,128]{1,0:T(8,128)(2,1)S(1)}, u32[]{:S(2)}, u32[]{:S(2)}) collective-permute-start(bf16[1024,128]{1,0:T(8,128)(2,1)S(1)} %get-tuple-element.60), channel_id=1, source_target_pairs={{0,2},{1,3},{2,0},{3,1},{4,6},{5,7},{6,4},{7,5},{8,10},{9,11},{10,... | collective-permute-start | bytes 786440 | tf_op jit(solution)/shard_map/ppermute | solution.py:343
  39.5 2.6 %prev.1 = (s16[272,256]{1,0:T(8,128)(2,1)S(1)}, s16[272,256]{1,0:T(8,128)(2,1)}, s16[272,256]{1,0:T(8,128)(2,1)}, s16[272,256]{1,0:T(8,128)(2,1)}) custom-call(s32[3]{0:T(128)S(1)} %pad_add_fusion.me_ref, s32[1]{0:T(128)} %get-tuple-element.63.after_ref, f32[256,1024]{1,0:T(8,128)S(1)} %copy-done.2, s32[1,256]{1,0:T(1,128)S(1)} %bitcast.10), custom_call_target="tpu_custom_call" | custom-call | tf_op jit(solution)/shard_map/prev/pallas_call | solution.py:393
  42.1 0.9 collective-permute-done.3.refs_1_
  43.0 7.8 %collective-permute-done.4.refs_2_ = bf16[1024,128]{1,0:T(8,128)(2,1)S(1)} collective-permute-done((bf16[1024,128]{1,0:T(8,128)(2,1)S(1)}, bf16[1024,128]{1,0:T(8,128)(2,1)S(1)}, u32[]{:S(2)}, u32[]{:S(2)}) %collective-permute-start.4) | collective-permute-done | bytes 262176 | tf_op jit(solution)/shard_map/ppermute | solution.py:343
  50.8 2.9 %collective-permute-done.5.refs_3_ = bf16[1024,128]{1,0:T(8,128)(2,1)S(1)} collective-permute-done((bf16[1024,128]{1,0:T(8,128)(2,1)S(1)}, bf16[1024,128]{1,0:T(8,128)(2,1)S(1)}, u32[]{:S(2)}, u32[]{:S(2)}) %collective-permute-start.5) | collective-permute-done | bytes 262176 | tf_op jit(solution)/shard_map/ppermute | solution.py:343
  53.7 3.6 %sums1.1 = (f32[1024,128]{1,0:T(8,128)S(1)}, s16[1040,128]{1,0:T(8,128)(2,1)}, s32[1]{0:T(128)}) custom-call(s32[32]{0:T(128)S(1)} %get-tuple-element.53.place_ref.before_ref, s32[1]{0:T(128)} %get-tuple-element.57.before_ref, bf16[4096,128]{1,0:T(8,128)(2,1)S(1)} %get-tuple-element.54.member_ref, s32[8,128]{1,0:T(8,128)S(1)} %get-tuple-element.55.far_count_ref, ...), custom_call_target="tpu_custom_call" | custom-call | tf_op jit(solution)/shard_map/sums1/pallas_call | solution.py:379
  57.4 0.8 copy-done.5
  58.2 1.1 collective-permute-start.7
  59.3 2.9 %collective-permute-start.10 = (s16[272,256]{1,0:T(8,128)(2,1)}, s16[272,256]{1,0:T(8,128)(2,1)S(1)}, u32[]{:S(2)}, u32[]{:S(2)}) collective-permute-start(s16[272,256]{1,0:T(8,128)(2,1)} %get-tuple-element.74), channel_id=1, source_target_pairs={{0,3},{1,2},{2,1},{3,0},{4,7},{5,6},{6,5},{7,4},{8,11},{9,10},{10,... | collective-permute-start | bytes 417800 | tf_op jit(solution)/shard_map/ppermute | solution.py:343
  62.1 0.5 collective-permute-start.8
  62.8 3.2 %fusion = f32[2048]{0:T(1024)S(1)} fusion(bf16[2048,1024]{1,0:T(8,128)(2,1)} %all-gather.2.cloned.1.call-done), kind=kLoop, calls=%fused_computation.2 | loop fusion | flops 6289408 | bytes 4202496 | tf_op jit(solution)/shard_map/reduce_sum | solution.py:407
  66.0 4.4 %collective-permute-done.7.refs_3_ = s16[1040,128]{1,0:T(8,128)(2,1)} collective-permute-done((s16[1040,128]{1,0:T(8,128)(2,1)}, s16[1040,128]{1,0:T(8,128)(2,1)}, u32[]{:S(2)}, u32[]{:S(2)}) %collective-permute-start.7) | collective-permute-done | bytes 266272 | tf_op jit(solution)/shard_map/ppermute | solution.py:343
  70.4 2.2 %refresh.1 = (f32[1024,256]{1,0:T(8,128)S(1)}, s16[272,256]{1,0:T(8,128)(2,1)S(1)}, s16[272,256]{1,0:T(8,128)(2,1)S(1)}, s16[272,256]{1,0:T(8,128)(2,1)S(1)}, s16[272,256]{1,0:T(8,128)(2,1)S(1)}) custom-call(f32[1024,128]{1,0:T(8,128)S(1)} %get-tuple-element.52.near_ref, f32[1024,128]{1,0:T(8,128)S(1)} %copy-done.4, f32[1024,128]{1,0:T(8,128)S(1)} %copy-done.6, ...), custom_call_target="tpu_custom_call" | custom-call | tf_op jit(solution)/shard_map/refresh/pallas_call | solution.py:420
  72.6 2.8 %collective-permute-start.11 = (s16[272,256]{1,0:T(8,128)(2,1)S(1)}, s16[272,256]{1,0:T(8,128)(2,1)S(1)}, u32[]{:S(2)}, u32[]{:S(2)}) collective-permute-start(s16[272,256]{1,0:T(8,128)(2,1)S(1)} %get-tuple-element.76), channel_id=1, source_target_pairs={{0,1},{1,0},{2,3},{3,2},{4,5},{5,4},{6,7},{7,6},{8,9},{9,8},{10,11... | collective-permute-start | bytes 417800 | tf_op jit(solution)/shard_map/ppermute | solution.py:343
  75.4 1.5 %collective-permute-start.13 = (s16[272,256]{1,0:T(8,128)(2,1)S(1)}, s16[272,256]{1,0:T(8,128)(2,1)S(1)}, u32[]{:S(2)}, u32[]{:S(2)}) collective-permute-start(s16[272,256]{1,0:T(8,128)(2,1)S(1)} %get-tuple-element.78), channel_id=1, source_target_pairs={{0,3},{1,2},{2,1},{3,0},{4,7},{5,6},{6,5},{7,4},{8,11},{9,10},{10,... | collective-permute-start | bytes 417800 | tf_op jit(solution)/shard_map/ppermute | solution.py:343
  77.0 0.5 fusion.3
  77.4 2.5 %collective-permute-done.11.refs_1_ = s16[272,256]{1,0:T(8,128)(2,1)S(1)} collective-permute-done((s16[272,256]{1,0:T(8,128)(2,1)S(1)}, s16[272,256]{1,0:T(8,128)(2,1)S(1)}, u32[]{:S(2)}, u32[]{:S(2)}) %collective-permute-start.11) | collective-permute-done | bytes 139296 | tf_op jit(solution)/shard_map/ppermute | solution.py:343
  79.9 1.0 collective-permute-done.12.refs_2_
  80.9 1.2 %collective-permute-done.13.refs_3_ = s16[272,256]{1,0:T(8,128)(2,1)S(1)} collective-permute-done((s16[272,256]{1,0:T(8,128)(2,1)S(1)}, s16[272,256]{1,0:T(8,128)(2,1)S(1)}, u32[]{:S(2)}, u32[]{:S(2)}) %collective-permute-start.13) | collective-permute-done | bytes 139296 | tf_op jit(solution)/shard_map/ppermute | solution.py:343
  82.1 2.1 %upper.1 = (s16[272,256]{1,0:T(8,128)(2,1)S(1)}, s16[272,256]{1,0:T(8,128)(2,1)S(1)}) custom-call(f32[1024,256]{1,0:T(8,128)S(1)} %get-tuple-element.81.x_ref, s16[272,256]{1,0:T(8,128)(2,1)S(1)} %get-tuple-element.75.refs_0_, s16[272,256]{1,0:T(8,128)(2,1)S(1)} %collective-permute-done.11.refs_1_, s16[272,256]{1,0:T(8,128)(2,1)S(1)} %collective-permute-done.12.refs_2_, ...), custom_call_target="tpu_custom_call" | custom-call | tf_op jit(solution)/shard_map/upper/pallas_call | solution.py:434
  84.2 2.0 %collective-permute-start.18 = (s16[272,256]{1,0:T(8,128)(2,1)S(1)}, s16[272,256]{1,0:T(8,128)(2,1)S(1)}, u32[]{:S(2)}, u32[]{:S(2)}) collective-permute-start(s16[272,256]{1,0:T(8,128)(2,1)S(1)} %get-tuple-element.87.own), channel_id=1, source_target_pairs={{0,4},{1,5},{2,6},{3,7},{4,0},{5,1},{6,2},{7,3},{8,12},{9,13},{10,... | collective-permute-start | bytes 417800 | tf_op jit(solution)/shard_map/ppermute | solution.py:343
  86.3 5.4 %fusion.2 = f32[1024]{0:T(1024)S(1)} fusion(bf16[2048,1024]{1,0:T(8,128)(2,1)S(1)} %copy-done.9, f32[8,2048]{1,0:T(8,128)S(1)} %convert_element_type.25, f32[2048]{0:T(1024)S(1)} %add_rsqrt_fusion, bf16[1024,1024]{1,0:T(8,128)(2,1)S(1)} %copy-done.1, f32[1024]{0:T(1024)S(1)} %add_rsqrt_fusion.1), kind=kOutput, calls=%fused_computation.5 | convolution fusion | flops 4310694912 | bytes 6373376 | tf_op jit(solution)/shard_map/dot_general | solution.py:410
  91.7 0.6 log.3
  92.3 0.9 collective-permute-start.14
  93.2 0.4 both1.1.refs_4_
  93.6 1.7 %collective-permute-start.19 = (s16[272,256]{1,0:T(8,128)(2,1)S(1)}, s16[272,256]{1,0:T(8,128)(2,1)S(1)}, u32[]{:S(2)}, u32[]{:S(2)}) collective-permute-start(s16[272,256]{1,0:T(8,128)(2,1)S(1)} %both1.1.refs_4_), channel_id=1, source_target_pairs={{0,1},{1,0},{2,3},{3,2},{4,5},{5,4},{6,7},{7,6},{8,9},{9,8},{10,11... | collective-permute-start | bytes 417800 | tf_op jit(solution)/shard_map/ppermute | solution.py:343
  95.6 1.5 %collective-permute-start.21 = (s16[272,256]{1,0:T(8,128)(2,1)S(1)}, s16[272,256]{1,0:T(8,128)(2,1)S(1)}, u32[]{:S(2)}, u32[]{:S(2)}) collective-permute-start(s16[272,256]{1,0:T(8,128)(2,1)S(1)} %both1.1.refs_4_), channel_id=1, source_target_pairs={{0,3},{1,2},{2,1},{3,0},{4,7},{5,6},{6,5},{7,4},{8,11},{9,10},{10,... | collective-permute-start | bytes 417800 | tf_op jit(solution)/shard_map/ppermute | solution.py:343
  97.1 2.7 %collective-permute-done.14.far = s16[272,256]{1,0:T(8,128)(2,1)S(1)} collective-permute-done((s16[272,256]{1,0:T(8,128)(2,1)S(1)}, s16[272,256]{1,0:T(8,128)(2,1)S(1)}, u32[]{:S(2)}, u32[]{:S(2)}) %collective-permute-start.14) | collective-permute-done | bytes 139296 | tf_op jit(solution)/shard_map/ppermute | solution.py:343
  99.8 0.4 both0.1.refs_0_
  100.5 0.4 collective-permute-start.16
  100.9 2.8 %collective-permute-start.17 = (s16[272,256]{1,0:T(8,128)(2,1)S(1)}, s16[272,256]{1,0:T(8,128)(2,1)S(1)}, u32[]{:S(2)}, u32[]{:S(2)}) collective-permute-start(s16[272,256]{1,0:T(8,128)(2,1)S(1)} %both0.1.refs_0_), channel_id=1, source_target_pairs={{0,3},{1,2},{2,1},{3,0},{4,7},{5,6},{6,5},{7,4},{8,11},{9,10},{10,... | collective-permute-start | bytes 417800 | tf_op jit(solution)/shard_map/ppermute | solution.py:343
  103.7 1.9 %decode.1 = f32[256,1024]{1,0:T(8,128)} custom-call(s32[3]{0:T(128)S(1)} %pad_add_fusion.me_ref, s16[272,256]{1,0:T(8,128)(2,1)S(1)} %get-tuple-element.75.refs_0_, s16[272,256]{1,0:T(8,128)(2,1)S(1)} %collective-permute-done.11.refs_1_, s16[272,256]{1,0:T(8,128)(2,1)S(1)} %collective-permute-done.12.refs_2_, s16[272,256]{1,0:T(8,128)(2,1)S(1)} %collective-permute-done.13.refs_3_), custom_call_target="tpu_custom_call" | custom-call | tf_op jit(solution)/shard_map/decode/pallas_call | solution.py:459
  105.6 1.6 %collective-permute-done.15.refs_1_ = s16[272,256]{1,0:T(8,128)(2,1)S(1)} collective-permute-done((s16[272,256]{1,0:T(8,128)(2,1)S(1)}, s16[272,256]{1,0:T(8,128)(2,1)S(1)}, u32[]{:S(2)}, u32[]{:S(2)}) %collective-permute-start.15) | collective-permute-done | bytes 139296 | tf_op jit(solution)/shard_map/ppermute | solution.py:343
  107.3 1.7 %collective-permute-done.17.refs_3_ = s16[272,256]{1,0:T(8,128)(2,1)S(1)} collective-permute-done((s16[272,256]{1,0:T(8,128)(2,1)S(1)}, s16[272,256]{1,0:T(8,128)(2,1)S(1)}, u32[]{:S(2)}, u32[]{:S(2)}) %collective-permute-start.17) | collective-permute-done | bytes 139296 | tf_op jit(solution)/shard_map/ppermute | solution.py:343
  109.0 2.3 %join.1 = f32[512,1024]{1,0:T(8,128)} custom-call(s32[3]{0:T(128)S(1)} %pad_add_fusion.me_ref, s16[272,256]{1,0:T(8,128)(2,1)S(1)} %both0.1.refs_0_, s16[272,256]{1,0:T(8,128)(2,1)S(1)} %collective-permute-done.15.refs_1_, s16[272,256]{1,0:T(8,128)(2,1)S(1)} %collective-permute-done.16.refs_2_, s16[272,256]{1,0:T(8,128)(2,1)S(1)} %collective-permute-done.17.refs_3_, ...), custom_call_target="tpu_custom_call" | custom-call | tf_op jit(solution)/shard_map/join/pallas_call | solution.py:467
  (42 shorter events, 1.5 us)
Async XLA Ops:
  7.2 32.1 %copy-start.10 = (s32[8,8]{1,0:T(8,128)S(1)}, s32[8,8]{1,0:T(8,128)}, u32[]{:S(2)}) copy-start(s32[8,8]{1,0:T(8,128)} %param.8) | copy-start | bytes 772
  7.2 32.3 %copy-start.8 = (s32[256]{0:T(256)S(1)}, s32[256]{0:T(256)}, u32[]{:S(2)}) copy-start(s32[256]{0:T(256)} %param.10) | copy-start | bytes 3076
  7.2 32.3 %copy-start.2 = (f32[256,1024]{1,0:T(8,128)S(1)}, f32[256,1024]{1,0:T(8,128)}, u32[]{:S(2)}) copy-start(f32[256,1024]{1,0:T(8,128)} %prev_ref.1) | copy-start | bytes 3145732
  7.2 55.6 %all-gather.2.cloned.1.call-start = ((), (), s32[]{:S(2)}) async-start(), calls=%async_computation | async-start | bytes 5242880 | tf_op jit(solution)/shard_map/all_gather | solution.py:349
  8.0 1.6 %copy-start = (bf16[1024,1024]{1,0:T(8,128)(2,1)S(1)}, bf16[1024,1024]{1,0:T(8,128)(2,1)}, u32[]{:S(2)}) copy-start(bf16[1024,1024]{1,0:T(8,128)(2,1)} %points_ref.1) | copy-start | bytes 6291460
  9.6 0.7 copy-start.7
  12.1 9.4 %collective-permute-start = (bf16[1040,128]{1,0:T(8,128)(2,1)S(1)}, bf16[1040,128]{1,0:T(8,128)(2,1)S(1)}, u32[]{:S(2)}, u32[]{:S(2)}) collective-permute-start(bf16[1040,128]{1,0:T(8,128)(2,1)S(1)} %get-tuple-element.48), channel_id=1, source_target_pairs={{0,1},{1,0},{2,3},{3,2},{4,5},{5,4},{6,7},{7,6},{8,9},{9,8},{10,11... | collective-permute-start | bytes 798728 | tf_op jit(solution)/shard_map/ppermute | solution.py:343
  15.1 9.3 %collective-permute-start.1 = (bf16[1040,128]{1,0:T(8,128)(2,1)S(1)}, bf16[1040,128]{1,0:T(8,128)(2,1)S(1)}, u32[]{:S(2)}, u32[]{:S(2)}) collective-permute-start(bf16[1040,128]{1,0:T(8,128)(2,1)S(1)} %get-tuple-element.49), channel_id=1, source_target_pairs={{0,2},{1,3},{2,0},{3,1},{4,6},{5,7},{6,4},{7,5},{8,10},{9,11},{10,... | collective-permute-start | bytes 798728 | tf_op jit(solution)/shard_map/ppermute | solution.py:343
  16.7 11.8 %collective-permute-start.2 = (bf16[1040,128]{1,0:T(8,128)(2,1)S(1)}, bf16[1040,128]{1,0:T(8,128)(2,1)S(1)}, u32[]{:S(2)}, u32[]{:S(2)}) collective-permute-start(bf16[1040,128]{1,0:T(8,128)(2,1)S(1)} %get-tuple-element.50), channel_id=1, source_target_pairs={{0,3},{1,2},{2,1},{3,0},{4,7},{5,6},{6,5},{7,4},{8,11},{9,10},{10,... | collective-permute-start | bytes 798728 | tf_op jit(solution)/shard_map/ppermute | solution.py:343
  32.9 20.8 %copy-start.3 = (f32[1024,128]{1,0:T(8,128)}, f32[1024,128]{1,0:T(8,128)S(1)}, u32[]{:S(2)}) copy-start(f32[1024,128]{1,0:T(8,128)S(1)} %get-tuple-element.56.refs_0_) | copy-start | bytes 1572868
  32.9 26.3 %collective-permute-start.6 = (s16[1040,128]{1,0:T(8,128)(2,1)S(1)}, s16[1040,128]{1,0:T(8,128)(2,1)S(1)}, u32[]{:S(2)}, u32[]{:S(2)}) collective-permute-start(s16[1040,128]{1,0:T(8,128)(2,1)S(1)} %get-tuple-element.68), channel_id=1, source_target_pairs={{0,4},{1,5},{2,6},{3,7},{4,0},{5,1},{6,2},{7,3},{8,12},{9,13},{10,... | collective-permute-start | bytes 798728 | tf_op jit(solution)/shard_map/ppermute | solution.py:343
  35.7 7.3 %collective-permute-start.3 = (bf16[1024,128]{1,0:T(8,128)(2,1)S(1)}, bf16[1024,128]{1,0:T(8,128)(2,1)S(1)}, u32[]{:S(2)}, u32[]{:S(2)}) collective-permute-start(bf16[1024,128]{1,0:T(8,128)(2,1)S(1)} %get-tuple-element.59), channel_id=1, source_target_pairs={{0,1},{1,0},{2,3},{3,2},{4,5},{5,4},{6,7},{7,6},{8,9},{9,8},{10,11... | collective-permute-start | bytes 786440 | tf_op jit(solution)/shard_map/ppermute | solution.py:343
  37.3 13.5 %collective-permute-start.4 = (bf16[1024,128]{1,0:T(8,128)(2,1)S(1)}, bf16[1024,128]{1,0:T(8,128)(2,1)S(1)}, u32[]{:S(2)}, u32[]{:S(2)}) collective-permute-start(bf16[1024,128]{1,0:T(8,128)(2,1)S(1)} %get-tuple-element.60), channel_id=1, source_target_pairs={{0,2},{1,3},{2,0},{3,1},{4,6},{5,7},{6,4},{7,5},{8,10},{9,11},{10,... | collective-permute-start | bytes 786440 | tf_op jit(solution)/shard_map/ppermute | solution.py:343
  38.8 14.9 %collective-permute-start.5 = (bf16[1024,128]{1,0:T(8,128)(2,1)S(1)}, bf16[1024,128]{1,0:T(8,128)(2,1)S(1)}, u32[]{:S(2)}, u32[]{:S(2)}) collective-permute-start(bf16[1024,128]{1,0:T(8,128)(2,1)S(1)} %get-tuple-element.61), channel_id=1, source_target_pairs={{0,3},{1,2},{2,1},{3,0},{4,7},{5,6},{6,5},{7,4},{8,11},{9,10},{10,... | collective-permute-start | bytes 786440 | tf_op jit(solution)/shard_map/ppermute | solution.py:343
  53.7 23.2 %copy-start.1 = (bf16[1024,1024]{1,0:T(8,128)(2,1)S(1)}, bf16[1024,1024]{1,0:T(8,128)(2,1)}, u32[]{:S(2)}) copy-start(bf16[1024,1024]{1,0:T(8,128)(2,1)} %points_ref.1) | copy-start | bytes 6291460
  57.4 0.8 copy-start.5
  58.2 12.2 %collective-permute-start.7 = (s16[1040,128]{1,0:T(8,128)(2,1)}, s16[1040,128]{1,0:T(8,128)(2,1)}, u32[]{:S(2)}, u32[]{:S(2)}) collective-permute-start(s16[1040,128]{1,0:T(8,128)(2,1)} %get-tuple-element.70), channel_id=1, source_target_pairs={{0,4},{1,5},{2,6},{3,7},{4,0},{5,1},{6,2},{7,3},{8,12},{9,13},{10,... | collective-permute-start | bytes 798728 | tf_op jit(solution)/shard_map/ppermute | solution.py:343
  59.3 11.1 %collective-permute-start.10 = (s16[272,256]{1,0:T(8,128)(2,1)}, s16[272,256]{1,0:T(8,128)(2,1)S(1)}, u32[]{:S(2)}, u32[]{:S(2)}) collective-permute-start(s16[272,256]{1,0:T(8,128)(2,1)} %get-tuple-element.74), channel_id=1, source_target_pairs={{0,3},{1,2},{2,1},{3,0},{4,7},{5,6},{6,5},{7,4},{8,11},{9,10},{10,... | collective-permute-start | bytes 417800 | tf_op jit(solution)/shard_map/ppermute | solution.py:343
  62.1 8.2 %collective-permute-start.8 = (s16[272,256]{1,0:T(8,128)(2,1)}, s16[272,256]{1,0:T(8,128)(2,1)S(1)}, u32[]{:S(2)}, u32[]{:S(2)}) collective-permute-start(s16[272,256]{1,0:T(8,128)(2,1)} %get-tuple-element.72), channel_id=1, source_target_pairs={{0,1},{1,0},{2,3},{3,2},{4,5},{5,4},{6,7},{7,6},{8,9},{9,8},{10,11... | collective-permute-start | bytes 417800 | tf_op jit(solution)/shard_map/ppermute | solution.py:343
  62.7 7.8 %collective-permute-start.9 = (s16[272,256]{1,0:T(8,128)(2,1)}, s16[272,256]{1,0:T(8,128)(2,1)S(1)}, u32[]{:S(2)}, u32[]{:S(2)}) collective-permute-start(s16[272,256]{1,0:T(8,128)(2,1)} %get-tuple-element.73), channel_id=1, source_target_pairs={{0,2},{1,3},{2,0},{3,1},{4,6},{5,7},{6,4},{7,5},{8,10},{9,11},{10,... | collective-permute-start | bytes 417800 | tf_op jit(solution)/shard_map/ppermute | solution.py:343
  62.8 7.7 %copy-start.4 = (f32[1024,128]{1,0:T(8,128)S(1)}, f32[1024,128]{1,0:T(8,128)}, u32[]{:S(2)}) copy-start(f32[1024,128]{1,0:T(8,128)} %copy-done.3) | copy-start | bytes 1572868
  62.8 7.7 %copy-start.6 = (f32[1024,128]{1,0:T(8,128)S(1)}, f32[1024,128]{1,0:T(8,128)}, u32[]{:S(2)}) copy-start(f32[1024,128]{1,0:T(8,128)} %copy-done.5) | copy-start | bytes 1572868
  65.9 20.3 %copy-start.9 = (bf16[2048,1024]{1,0:T(8,128)(2,1)S(1)}, bf16[2048,1024]{1,0:T(8,128)(2,1)}, u32[]{:S(2)}) copy-start(bf16[2048,1024]{1,0:T(8,128)(2,1)} %all-gather.2.cloned.1.call-done) | copy-start | bytes 12582916
  72.6 7.3 %collective-permute-start.11 = (s16[272,256]{1,0:T(8,128)(2,1)S(1)}, s16[272,256]{1,0:T(8,128)(2,1)S(1)}, u32[]{:S(2)}, u32[]{:S(2)}) collective-permute-start(s16[272,256]{1,0:T(8,128)(2,1)S(1)} %get-tuple-element.76), channel_id=1, source_target_pairs={{0,1},{1,0},{2,3},{3,2},{4,5},{5,4},{6,7},{7,6},{8,9},{9,8},{10,11... | collective-permute-start | bytes 417800 | tf_op jit(solution)/shard_map/ppermute | solution.py:343
  75.4 5.5 %collective-permute-start.12 = (s16[272,256]{1,0:T(8,128)(2,1)S(1)}, s16[272,256]{1,0:T(8,128)(2,1)S(1)}, u32[]{:S(2)}, u32[]{:S(2)}) collective-permute-start(s16[272,256]{1,0:T(8,128)(2,1)S(1)} %get-tuple-element.77), channel_id=1, source_target_pairs={{0,2},{1,3},{2,0},{3,1},{4,6},{5,7},{6,4},{7,5},{8,10},{9,11},{10,... | collective-permute-start | bytes 417800 | tf_op jit(solution)/shard_map/ppermute | solution.py:343
  75.4 6.7 %collective-permute-start.13 = (s16[272,256]{1,0:T(8,128)(2,1)S(1)}, s16[272,256]{1,0:T(8,128)(2,1)S(1)}, u32[]{:S(2)}, u32[]{:S(2)}) collective-permute-start(s16[272,256]{1,0:T(8,128)(2,1)S(1)} %get-tuple-element.78), channel_id=1, source_target_pairs={{0,3},{1,2},{2,1},{3,0},{4,7},{5,6},{6,5},{7,4},{8,11},{9,10},{10,... | collective-permute-start | bytes 417800 | tf_op jit(solution)/shard_map/ppermute | solution.py:343
  84.2 9.0 %collective-permute-start.18 = (s16[272,256]{1,0:T(8,128)(2,1)S(1)}, s16[272,256]{1,0:T(8,128)(2,1)S(1)}, u32[]{:S(2)}, u32[]{:S(2)}) collective-permute-start(s16[272,256]{1,0:T(8,128)(2,1)S(1)} %get-tuple-element.87.own), channel_id=1, source_target_pairs={{0,4},{1,5},{2,6},{3,7},{4,0},{5,1},{6,2},{7,3},{8,12},{9,13},{10,... | collective-permute-start | bytes 417800 | tf_op jit(solution)/shard_map/ppermute | solution.py:343
  92.3 7.5 %collective-permute-start.14 = (s16[272,256]{1,0:T(8,128)(2,1)S(1)}, s16[272,256]{1,0:T(8,128)(2,1)S(1)}, u32[]{:S(2)}, u32[]{:S(2)}) collective-permute-start(s16[272,256]{1,0:T(8,128)(2,1)S(1)} %get-tuple-element.86.own), channel_id=1, source_target_pairs={{0,4},{1,5},{2,6},{3,7},{4,0},{5,1},{6,2},{7,3},{8,12},{9,13},{10,... | collective-permute-start | bytes 417800 | tf_op jit(solution)/shard_map/ppermute | solution.py:343
  93.6 7.3 %collective-permute-start.19 = (s16[272,256]{1,0:T(8,128)(2,1)S(1)}, s16[272,256]{1,0:T(8,128)(2,1)S(1)}, u32[]{:S(2)}, u32[]{:S(2)}) collective-permute-start(s16[272,256]{1,0:T(8,128)(2,1)S(1)} %both1.1.refs_4_), channel_id=1, source_target_pairs={{0,1},{1,0},{2,3},{3,2},{4,5},{5,4},{6,7},{7,6},{8,9},{9,8},{10,11... | collective-permute-start | bytes 417800 | tf_op jit(solution)/shard_map/ppermute | solution.py:343
  95.3 10.3 %collective-permute-start.20 = (s16[272,256]{1,0:T(8,128)(2,1)S(1)}, s16[272,256]{1,0:T(8,128)(2,1)S(1)}, u32[]{:S(2)}, u32[]{:S(2)}) collective-permute-start(s16[272,256]{1,0:T(8,128)(2,1)S(1)} %both1.1.refs_4_), channel_id=1, source_target_pairs={{0,2},{1,3},{2,0},{3,1},{4,6},{5,7},{6,4},{7,5},{8,10},{9,11},{10,... | collective-permute-start | bytes 417800 | tf_op jit(solution)/shard_map/ppermute | solution.py:343
  95.6 10.0 %collective-permute-start.21 = (s16[272,256]{1,0:T(8,128)(2,1)S(1)}, s16[272,256]{1,0:T(8,128)(2,1)S(1)}, u32[]{:S(2)}, u32[]{:S(2)}) collective-permute-start(s16[272,256]{1,0:T(8,128)(2,1)S(1)} %both1.1.refs_4_), channel_id=1, source_target_pairs={{0,3},{1,2},{2,1},{3,0},{4,7},{5,6},{6,5},{7,4},{8,11},{9,10},{10,... | collective-permute-start | bytes 417800 | tf_op jit(solution)/shard_map/ppermute | solution.py:343
  100.2 7.0 %collective-permute-start.15 = (s16[272,256]{1,0:T(8,128)(2,1)S(1)}, s16[272,256]{1,0:T(8,128)(2,1)S(1)}, u32[]{:S(2)}, u32[]{:S(2)}) collective-permute-start(s16[272,256]{1,0:T(8,128)(2,1)S(1)} %both0.1.refs_0_), channel_id=1, source_target_pairs={{0,1},{1,0},{2,3},{3,2},{4,5},{5,4},{6,7},{7,6},{8,9},{9,8},{10,11... | collective-permute-start | bytes 417800 | tf_op jit(solution)/shard_map/ppermute | solution.py:343
  100.5 6.8 %collective-permute-start.16 = (s16[272,256]{1,0:T(8,128)(2,1)S(1)}, s16[272,256]{1,0:T(8,128)(2,1)S(1)}, u32[]{:S(2)}, u32[]{:S(2)}) collective-permute-start(s16[272,256]{1,0:T(8,128)(2,1)S(1)} %both0.1.refs_0_), channel_id=1, source_target_pairs={{0,2},{1,3},{2,0},{3,1},{4,6},{5,7},{6,4},{7,5},{8,10},{9,11},{10,... | collective-permute-start | bytes 417800 | tf_op jit(solution)/shard_map/ppermute | solution.py:343
  100.9 8.1 %collective-permute-start.17 = (s16[272,256]{1,0:T(8,128)(2,1)S(1)}, s16[272,256]{1,0:T(8,128)(2,1)S(1)}, u32[]{:S(2)}, u32[]{:S(2)}) collective-permute-start(s16[272,256]{1,0:T(8,128)(2,1)S(1)} %both0.1.refs_0_), channel_id=1, source_target_pairs={{0,3},{1,2},{2,1},{3,0},{4,7},{5,6},{6,5},{7,4},{8,11},{9,10},{10,... | collective-permute-start | bytes 417800 | tf_op jit(solution)/shard_map/ppermute | solution.py:343
Sparse Core Ops, SparseCore 0:
  9.6 37.1 all-gather.1
